TPU v7x, 32 devices: a whole 2x2x4 slice. The times are simulated.
32 devices in a mesh: wide: 8 (over z, y), narrow: 4 (over x, core).
Axes of the slice: x: 2, y: 2, z: 4, core: 2. Of those that a mesh axis runs over, the one named last changes fastest.
Arguments:
- hidden_in: bfloat16 [128, 16384], P('narrow', 'wide'), may hold values from -6 to 6
- attn_gain: float32 [16384], P('wide'), may hold values from 0.1 to 1.9
- w_query: bfloat16 [16384, 16384], P('wide', 'narrow'), may hold values from -0.046875 to 0.046875
- w_key: bfloat16 [16384, 1024], P('wide', 'narrow'), may hold values from -0.046875 to 0.046875
- w_value: bfloat16 [16384, 1024], P('wide', 'narrow'), may hold values from -0.046875 to 0.046875
- w_out: bfloat16 [16384, 16384], P('narrow', 'wide'), may hold values from -0.046875 to 0.046875
- ffn_gain: float32 [16384], P('wide'), may hold values from 0.1 to 1.9
- w_gate: bfloat16 [16384, 8192], P('wide', 'narrow'), may hold values from -0.046875 to 0.046875
- w_up: bfloat16 [16384, 8192], P('wide', 'narrow'), may hold values from -0.046875 to 0.046875
- w_down: bfloat16 [8192, 16384], P('narrow', 'wide'), may hold values from -0.0625 to 0.0625
- key_cache: bfloat16 [128, 512, 1024], P(('wide', 'narrow')), may hold values from -192 to 192
- value_cache: bfloat16 [128, 512, 1024], P(('wide', 'narrow')), may hold values from -6 to 6
- cache_len: int32 [128], P(('wide', 'narrow')), may hold values from 1 to 512, as said below
- bank_row: int32 [128], replicated, may hold values from 0 to 127, each once
Outputs:
- layer_out: bfloat16 [128, 16384], P('narrow', 'wide')
Inputs may be any that keep to these rules, and one draw needn't show every extreme that they name: cache_len[b] counts the valid leading positions of bank row b; some row is full.
All inputs are finite; a program needn't handle non-finite values.
Results may differ from a plain program's by a relative error of at most 0.006.
The roundings to bfloat16 on the way count: a program that leaves them out, or rounds other values in their place, can miss the bound.
Values may be sent and summed in bfloat16 or wider, within the bound.
No kernel may reach another device: no remote copies, remote signals or barrier semaphores. Data moves between devices by JAX's collectives and lax.ppermute only.
A program may use at most 192 MiB of HBM per device.

v0:
```python
import math

import jax
import jax.numpy as jnp
from jax import lax
from jax.sharding import PartitionSpec as P

HEAD_DIM = 128


NORM_EPSILON = 1e-05
ROPE_BASE = 500000.0


def product(left, right):
    return jnp.dot(left, right, preferred_element_type=jnp.float32)


def normalize(values_in, gain_row, sum_sq, model_width):
    mean_sq = sum_sq / model_width
    scaled = values_in.astype(jnp.float32) * lax.rsqrt(mean_sq + NORM_EPSILON)[:, None]
    return (scaled * gain_row[None, :]).astype(jnp.bfloat16)


def rotate(head_rows, lengths):
    head_size = head_rows.shape[-1]
    half_size = head_size // 2
    inverse_freq = jnp.exp(
        jnp.arange(half_size, dtype=jnp.float32) * (-2.0 * math.log(ROPE_BASE) / head_size)
    )
    angles = lengths.astype(jnp.float32)[:, None] * inverse_freq[None, :]
    cos_part = jnp.cos(angles)[:, None, :]
    sin_part = jnp.sin(angles)[:, None, :]
    front_half = head_rows[..., :half_size].astype(jnp.float32)
    back_half = head_rows[..., half_size:].astype(jnp.float32)
    turned = jnp.concatenate(
        [
            front_half * cos_part - back_half * sin_part,
            back_half * cos_part + front_half * sin_part,
        ],
        axis=-1,
    )
    return turned.astype(jnp.bfloat16)


def attend(queries, fresh_key, fresh_value, key_cache, value_cache, lengths):
    row_count, length, kv_width = key_cache.shape
    groups = kv_width // HEAD_DIM
    group_size = queries.shape[1] // kv_width
    score_scale = 1.0 / math.sqrt(HEAD_DIM)
    query_heads = queries.reshape(row_count, groups, group_size, HEAD_DIM)
    cache_keys = key_cache.reshape(row_count, length, groups, HEAD_DIM)
    cache_values = value_cache.reshape(row_count, length, groups, HEAD_DIM)
    own_key = fresh_key.reshape(row_count, groups, HEAD_DIM)
    own_value = fresh_value.reshape(row_count, groups, HEAD_DIM)
    scores = (
        jnp.einsum("rgqd,rlgd->rgql", query_heads, cache_keys, preferred_element_type=jnp.float32)
        * score_scale
    )
    own_score = (
        jnp.einsum("rgqd,rgd->rgq", query_heads, own_key, preferred_element_type=jnp.float32)
        * score_scale
    )
    valid_pos = jnp.arange(length, dtype=jnp.int32)[None, :] < lengths[:, None]
    scores = jnp.where(valid_pos[:, None, None, :], scores, -jnp.inf)
    row_max = jnp.maximum(jnp.max(scores, axis=3), own_score)
    weights = jnp.exp(scores - row_max[..., None])
    own_weight = jnp.exp(own_score - row_max)
    weight_sum = jnp.sum(weights, axis=3) + own_weight
    probs = (weights / weight_sum[..., None]).astype(jnp.bfloat16)
    own_prob = (own_weight / weight_sum).astype(jnp.bfloat16)
    context = jnp.einsum("rgql,rlgd->rgqd", probs, cache_values, preferred_element_type=jnp.float32)
    context = (
        context
        + own_prob.astype(jnp.float32)[..., None] * own_value.astype(jnp.float32)[:, :, None, :]
    )
    return context.reshape(row_count, groups * group_size * HEAD_DIM).astype(jnp.bfloat16)


def shards(
    hidden_in,
    attn_gain,
    w_query,
    w_key,
    w_value,
    w_out,
    ffn_gain,
    w_gate,
    w_up,
    w_down,
    key_cache,
    value_cache,
    cache_len,
    bank_row,
):
    wide_count = lax.axis_size("wide")
    model_width = hidden_in.shape[1] * wide_count
    local_rows = cache_len.shape[0]
    all_rows = bank_row.shape[0]
    served_by = (
        jnp.zeros((all_rows,), jnp.int32).at[bank_row].set(jnp.arange(all_rows, dtype=jnp.int32))
    )
    rows_in = hidden_in.astype(jnp.float32)
    first_sq = lax.psum(jnp.sum(rows_in * rows_in, axis=1), "wide")
    normed = normalize(hidden_in, attn_gain, first_sq, model_width)
    gathered = lax.all_gather(normed, "narrow", axis=0, tiled=True)
    q_cols = w_query.shape[1]
    k_cols = w_key.shape[1]
    in_bank = gathered[served_by]
    row_block = in_bank
    summed = lax.psum_scatter(
        jnp.concatenate(
            [product(row_block, w_query), product(row_block, w_key), product(row_block, w_value)],
            axis=1,
        ),
        "wide",
        scatter_dimension=0,
        tiled=True,
    ).astype(jnp.bfloat16)
    qkv_parts = (
        summed[:, :q_cols],
        summed[:, q_cols : q_cols + k_cols],
        summed[:, q_cols + k_cols :],
    )
    queries, key_new, value_new = (
        lax.all_to_all(qkv_parts[0], "narrow", split_axis=0, concat_axis=1, tiled=True),
        lax.all_to_all(qkv_parts[1], "narrow", split_axis=0, concat_axis=1, tiled=True),
        lax.all_to_all(qkv_parts[2], "narrow", split_axis=0, concat_axis=1, tiled=True),
    )
    query_rot = rotate(queries.reshape(local_rows, -1, HEAD_DIM), cache_len).reshape(local_rows, -1)
    key_rot = rotate(key_new.reshape(local_rows, -1, HEAD_DIM), cache_len).reshape(local_rows, -1)
    context = attend(query_rot, key_rot, value_new, key_cache, value_cache, cache_len)
    by_heads = lax.all_to_all(context, "narrow", split_axis=1, concat_axis=0, tiled=True)
    every_row = lax.all_gather(by_heads, "wide", axis=0, tiled=True)
    in_hypothesis = every_row[bank_row]
    row_block = in_hypothesis
    attn_out = lax.psum_scatter(
        product(row_block, w_out), "narrow", scatter_dimension=0, tiled=True
    )
    resid = (rows_in + attn_out).astype(jnp.bfloat16)
    resid_wide = resid.astype(jnp.float32)
    second_sq = lax.psum(jnp.sum(resid_wide * resid_wide, axis=1), "wide")
    normed_two = normalize(resid, ffn_gain, second_sq, model_width)
    gathered_two = lax.all_gather(normed_two, "narrow", axis=0, tiled=True)
    gate_sum, up_sum = lax.psum(
        (product(gathered_two, w_gate), product(gathered_two, w_up)), "wide"
    )
    hidden_act = (jax.nn.silu(gate_sum) * up_sum).astype(jnp.bfloat16)
    row_block = hidden_act
    ffn_out = lax.psum_scatter(
        product(row_block, w_down), "narrow", scatter_dimension=0, tiled=True
    )
    return (resid_wide + ffn_out).astype(jnp.bfloat16)


def solution(mesh):
    return jax.shard_map(
        shards,
        mesh=mesh,
        in_specs=(
            P("narrow", "wide"),
            P("wide"),
            P("wide", "narrow"),
            P("wide", "narrow"),
            P("wide", "narrow"),
            P("narrow", "wide"),
            P("wide"),
            P("wide", "narrow"),
            P("wide", "narrow"),
            P("narrow", "wide"),
            P(("wide", "narrow"), None, None),
            P(("wide", "narrow"), None, None),
            P(("wide", "narrow")),
            P(),
        ),
        out_specs=P("narrow", "wide"),
        check_vma=False,
    )
```

profile of v0, /device:TPU:0, one launch (start us, length us, event | category | flops | bytes accessed | tf_op | source)
XLA Modules:
  0.0 409.3 jit_solution(17071868195461537711)
XLA Ops:
  9.3 23.1 %psum.28 = f32[32]{0:T(128)S(1)} all-reduce(f32[32]{0:T(128)S(1)} %fusion.27), channel_id=1, replica_groups=mesh['wide'=8,'narrow'=4] {'wide'}, use_global_device_ids=true, to_apply=%region_1.0 | all-reduce | flops 32 | bytes 256 | tf_op jit(solution)/shard_map/psum | solution.py:104
  33.5 7.2 %all_gather.9 = bf16[128,2048]{1,0:T(8,128)(2,1)S(1)} all-gather(bf16[32,2048]{1,0:T(8,128)(2,1)S(1)} %fusion.29), channel_id=1, replica_groups=mesh['wide'=8,'narrow'=4] {'narrow'}, dimensions={0}, use_global_device_ids=true | all-gather | bytes 655360 | tf_op jit(solution)/shard_map/all_gather | solution.py:106
  41.6 8.2 %fusion.51 = f32[128,4096]{1,0:T(8,128)S(1)} fusion(bf16[128,2048]{1,0:T(8,128)(2,1)S(1)} %gather_fusion, bf16[2048,4096]{1,0:T(8,128)(2,1)} %param.16), kind=kOutput, calls=%fused_computation.79 | convolution fusion | flops 2147483648 | bytes 19398656 | tf_op jit(solution)/shard_map/dot_general | solution.py:16
  52.1 65.7 %reduce-scatter.4.cloned.1.call-done = f32[16,4608]{1,0:T(8,128)} async-done(((f32[128,4608]{1,0:T(8,128)}), f32[16,4608]{1,0:T(8,128)}) %reduce-scatter.4.cloned.1.call-update) | async-done | bytes 294928 | tf_op jit(solution)/shard_map/reduce_scatter | solution.py:111
  119.4 3.2 all-to-all-start.1
  123.4 3.1 all-to-all-done.1
  126.5 3.2 all-to-all-start.2
  130.5 3.0 all-to-all-done.2
  133.5 3.3 all-to-all-start
  137.1 4.3 %all-to-all-done = bf16[4,4,4096]{2,1,0:T(4,128)(2,1)S(1)} async-done(((bf16[4,4,4096]{2,1,0:T(4,128)(2,1)}), bf16[4,4,4096]{2,1,0:T(4,128)(2,1)S(1)}, u32[]{:S(2)}, u32[]{:S(2)}) %all-to-all-start) | async-done | bytes 131104 | tf_op jit(solution)/shard_map/all_to_all | solution.py:126
  142.1 3.7 fusion.50
  147.5 7.0 %all_to_all.61 = bf16[4,4,4096]{2,0,1:T(4,128)(2,1)S(1)} all-to-all(bf16[4,4,4096]{2,0,1:T(4,128)(2,1)S(1)} %copy.29), channel_id=1, replica_groups=mesh['wide'=8,'narrow'=4] {'narrow'}, dimensions={1} | all-to-all | bytes 262144 | tf_op jit(solution)/shard_map/all_to_all | solution.py:133
  155.5 38.2 %all-gather.2.cloned.1.call-done = bf16[128,4096]{1,0:T(8,128)(2,1)} async-done(((bf16[16,4096]{1,0:T(8,128)(2,1)}), bf16[128,4096]{1,0:T(8,128)(2,1)}) %all-gather.2.cloned.1.call-update) | async-done | bytes 1048592 | tf_op jit(solution)/shard_map/all_gather | solution.py:134
  193.7 3.6 gather_fusion.1
  197.3 9.1 %fusion.54 = f32[128,2048]{1,0:T(8,128)} fusion(bf16[128,4096]{1,0:T(8,128)(2,1)S(1)} %gather_fusion.1, bf16[4096,2048]{1,0:T(8,128)(2,1)} %param.19), kind=kOutput, calls=%fused_computation.82 | convolution fusion | flops 2147483648 | bytes 18874368 | tf_op jit(solution)/shard_map/dot_general | solution.py:16
  206.5 23.8 %reduce-scatter.6.cloned.1.call-done = f32[32,2048]{1,0:T(8,128)} async-done(((f32[128,2048]{1,0:T(8,128)}), f32[32,2048]{1,0:T(8,128)}) %reduce-scatter.6.cloned.1.call-update) | async-done | bytes 262160 | tf_op jit(solution)/shard_map/reduce_scatter | solution.py:137
  231.3 21.3 %psum.29 = f32[32]{0:T(128)S(1)} all-reduce(f32[32]{0:T(128)S(1)} %get-tuple-element.7), channel_id=1, replica_groups=mesh['wide'=8,'narrow'=4] {'wide'}, use_global_device_ids=true, to_apply=%region_8.9 | all-reduce | flops 32 | bytes 256 | tf_op jit(solution)/shard_map/psum | solution.py:142
  252.8 6.5 %all_gather.11 = bf16[128,2048]{1,0:T(8,128)(2,1)S(1)} all-gather(bf16[32,2048]{1,0:T(8,128)(2,1)S(1)} %fusion.33), channel_id=1, replica_groups=mesh['wide'=8,'narrow'=4] {'narrow'}, dimensions={0}, use_global_device_ids=true | all-gather | bytes 655360 | tf_op jit(solution)/shard_map/all_gather | solution.py:144
  259.3 5.6 %fusion.55 = f32[128,2048]{1,0:T(8,128)} fusion(bf16[128,2048]{1,0:T(8,128)(2,1)S(1)} %all_gather.11, bf16[2048,2048]{1,0:T(8,128)(2,1)} %param.21), kind=kOutput, calls=%fused_computation.83 | convolution fusion | flops 1073741824 | bytes 9961472 | tf_op jit(solution)/shard_map/dot_general | solution.py:16
  264.9 5.6 %fusion.56 = f32[128,2048]{1,0:T(8,128)} fusion(bf16[128,2048]{1,0:T(8,128)(2,1)S(1)} %all_gather.11, bf16[2048,2048]{1,0:T(8,128)(2,1)} %param.22), kind=kOutput, calls=%fused_computation.84 | convolution fusion | flops 1073741824 | bytes 9961472 | tf_op jit(solution)/shard_map/dot_general | solution.py:16
  270.6 99.3 %all-reduce.3.cloned.1.call-done = (f32[128,2048]{1,0:T(8,128)}, f32[128,2048]{1,0:T(8,128)}) async-done(((f32[128,2048]{1,0:T(8,128)}, f32[128,2048]{1,0:T(8,128)}), (f32[128,2048]{1,0:T(8,128)}, f32[128,2048]{1,0:T(8,128)})) %all-reduce.3.cloned.1.call-update) | async-done | bytes 2097168 | tf_op jit(solution)/shard_map/psum | solution.py:145
  369.9 6.4 %fusion.19 = f32[128,2048]{1,0:T(8,128)} fusion(bf16[2048,2048]{1,0:T(8,128)(2,1)} %param.23, f32[128,2048]{1,0:T(8,128)} %get-tuple-element.5, f32[128,2048]{1,0:T(8,128)} %get-tuple-element.6), kind=kOutput, calls=%fused_computation.18 | convolution fusion | flops 1075314688 | bytes 11534336 | tf_op jit(solution)/shard_map/dot_general | solution.py:16
  376.3 24.8 %reduce-scatter.8.cloned.1.call-done = f32[32,2048]{1,0:T(8,128)} async-done(((f32[128,2048]{1,0:T(8,128)}), f32[32,2048]{1,0:T(8,128)}) %reduce-scatter.8.cloned.1.call-update) | async-done | bytes 262160 | tf_op jit(solution)/shard_map/reduce_scatter | solution.py:150
  401.1 1.6 fusion.34
  (68 shorter events, 14.9 us)
Async XLA Ops:
  6.5 43.3 %copy-start = (bf16[2048,256]{1,0:T(8,128)(2,1)S(1)}, bf16[2048,256]{1,0:T(8,128)(2,1)}, u32[]{:S(2)}) copy-start(bf16[2048,256]{1,0:T(8,128)(2,1)} %param.17) | copy-start | bytes 3145732
  6.5 111.3 %reduce-scatter.4.cloned.1.call-start = ((), (), s32[]{:S(2)}) async-start(), calls=%async_computation.7 | async-start | bytes 2654208 | tf_op jit(solution)/shard_map/reduce_scatter | solution.py:111
  41.6 8.5 %copy-start.3 = (bf16[2048,256]{1,0:T(8,128)(2,1)S(1)}, bf16[2048,256]{1,0:T(8,128)(2,1)}, u32[]{:S(2)}) copy-start(bf16[2048,256]{1,0:T(8,128)(2,1)} %param.18) | copy-start | bytes 3145732
  50.1 2.0 copy-start.5
  119.4 7.0 %all-to-all-start.1 = ((bf16[4,4,256]{2,1,0:T(4,128)(2,1)}), bf16[4,4,256]{2,1,0:T(4,128)(2,1)S(1)}, u32[]{:S(2)}, u32[]{:S(2)}) async-start(bf16[4,4,256]{2,1,0:T(4,128)(2,1)} %all_to_all.49), calls=%async_computation.2 | async-start | bytes 16384 | tf_op jit(solution)/shard_map/all_to_all | solution.py:127
  126.5 7.0 %all-to-all-start.2 = ((bf16[4,4,256]{2,1,0:T(4,128)(2,1)}), bf16[4,4,256]{2,1,0:T(4,128)(2,1)S(1)}, u32[]{:S(2)}, u32[]{:S(2)}) async-start(bf16[4,4,256]{2,1,0:T(4,128)(2,1)} %all_to_all.52), calls=%async_computation.3 | async-start | bytes 16384 | tf_op jit(solution)/shard_map/all_to_all | solution.py:128
  133.5 7.9 %all-to-all-start = ((bf16[4,4,4096]{2,1,0:T(4,128)(2,1)}), bf16[4,4,4096]{2,1,0:T(4,128)(2,1)S(1)}, u32[]{:S(2)}, u32[]{:S(2)}) async-start(bf16[4,4,4096]{2,1,0:T(4,128)(2,1)} %all_to_all.46), calls=%async_computation.1 | async-start | bytes 262144 | tf_op jit(solution)/shard_map/all_to_all | solution.py:126
  136.8 56.9 %all-gather.2.cloned.1.call-start = ((), (), s32[]{:S(2)}) async-start(), calls=%async_computation.8 | async-start | bytes 1179648 | tf_op jit(solution)/shard_map/all_gather | solution.py:134
  141.7 4.5 %copy-start.6 = (bf16[4,512,1024]{2,1,0:T(8,128)(2,1)S(1)}, bf16[4,512,1024]{2,1,0:T(8,128)(2,1)}, u32[]{:S(2)}) copy-start(bf16[4,512,1024]{2,1,0:T(8,128)(2,1)} %param.25) | copy-start | bytes 12582916
  155.2 75.0 %reduce-scatter.6.cloned.1.call-start = ((), (), s32[]{:S(2)}) async-start(), calls=%async_computation.9 | async-start | bytes 1310720 | tf_op jit(solution)/shard_map/reduce_scatter | solution.py:137
  197.2 33.0 %copy-start.2 = (bf16[32,2048]{1,0:T(8,128)(2,1)S(1)}, bf16[32,2048]{1,0:T(8,128)(2,1)}, u32[]{:S(2)}) copy-start(bf16[32,2048]{1,0:T(8,128)(2,1)} %param.14) | copy-start | bytes 393220
  197.3 55.4 %copy-start.4 = (f32[2048]{0:T(1024)S(1)}, f32[2048]{0:T(1024)}, u32[]{:S(2)}) copy-start(f32[2048]{0:T(1024)} %param.20) | copy-start | bytes 24580
  206.4 163.5 %all-reduce.3.cloned.1.call-start = ((), (), s32[]{:S(2)}) async-start(), calls=%async_computation.11 | async-start | bytes 4194304 | tf_op jit(solution)/shard_map/psum | solution.py:145
  270.6 130.5 %reduce-scatter.8.cloned.1.call-start = ((), (), s32[]{:S(2)}) async-start(), calls=%async_computation.10 | async-start | bytes 1310720 | tf_op jit(solution)/shard_map/reduce_scatter | solution.py:150
  369.9 32.9 %copy-start.1 = (bf16[2048,256]{1,0:T(8,128)(2,1)S(1)}, bf16[2048,256]{1,0:T(8,128)(2,1)}, u32[]{:S(2)}) copy-start(bf16[2048,256]{1,0:T(8,128)(2,1)} %param.17) | copy-start | bytes 3145732
Sparse Core Ops, SparseCore 0:
  52.2 65.5 reduce-scatter.3
  155.3 38.3 all-gather.1
  206.5 23.6 reduce-scatter.5
  270.7 99.1 all-reduce.2
  376.5 24.6 reduce-scatter.7
where the time goes:
time: 410 us; the launch traced here: 409 us
  waiting for transfers between devices  262 us (64%)
  blocking collectives  65.2 us (16%)
  matrix products  40.7 us (10%)
  between operations  13.4 us (3%)
  starting transfers between devices  10.2 us (2%)
  other arithmetic  9.08 us (2%)
  local copies, waits for them, and re-layouts  8.59 us (2%)
    psum x1, waiting for transfers between devices, shards(): lax.psum((product(gathered_two, w_gate), product(gathered_two, w_up)), 'w...  99.3 us
    reduce_scatter x1, waiting for transfers between devices, shards(): lax.psum_scatter(jnp.concatenate([product(row_block, w_query), product(ro...  65.7 us
    all_gather x1, waiting for transfers between devices, shards(): every_row = lax.all_gather(by_heads, 'wide', axis=0, tiled=True)  38.2 us
    dot_general x7, matrix products, product(): return jnp.dot(left, right, preferred_element_type=jnp.float32)  35.6 us
    reduce_scatter x1, waiting for transfers between devices, shards(): lax.psum_scatter(product(row_block, w_down), 'narrow', scatter_dimension=...  24.8 us
    reduce_scatter x1, waiting for transfers between devices, shards(): lax.psum_scatter(product(row_block, w_out), 'narrow', scatter_dimension=0...  23.8 us
    psum x1, blocking collectives, shards(): first_sq = lax.psum(jnp.sum(rows_in * rows_in, axis=1), 'wide')  23.1 us
    psum x1, blocking collectives, shards(): second_sq = lax.psum(jnp.sum(resid_wide * resid_wide, axis=1), 'wide')  21.3 us
  transfers between devices with their start and end apart: 8, of which 8 were waited for; matrix products, arithmetic and copies ran while one was open for 0% of the time, Pallas kernels for 0%

commit v1 on v0

--- a/solution.py
+++ b/solution.py
@@ -3,6 +3,8 @@
 import jax
 import jax.numpy as jnp
 from jax import lax
+from jax.experimental import pallas as pl
+from jax.experimental.pallas import tpu as pltpu
 from jax.sharding import PartitionSpec as P
 
 HEAD_DIM = 128
@@ -75,6 +77,134 @@
         + own_prob.astype(jnp.float32)[..., None] * own_value.astype(jnp.float32)[:, :, None, :]
     )
     return context.reshape(row_count, groups * group_size * HEAD_DIM).astype(jnp.bfloat16)
+
+
+QKV_CHUNKS = 3
+FFN_CHUNKS = 4
+CONTEXT_CHUNKS = 2
+DOWN_CHUNKS = 2
+VMEM_LIMIT = 32 * 1024 * 1024
+
+
+def swap(block, axis, offset):
+    count = lax.axis_size(axis)
+    return lax.ppermute(block, axis, [(i, i ^ offset) for i in range(count)])
+
+
+def project(blocks, order, segments, tile, split, total=None):
+    rows = order.shape[0]
+    depth = blocks[0].shape[1]
+    starts = []
+    steps = 0
+    for _, _, _, tiles in segments:
+        starts.append(steps)
+        steps += tiles
+    width = steps * tile
+    part = rows // split
+
+    def body(*refs):
+        block_refs = refs[: len(blocks)]
+        order_ref = refs[len(blocks)]
+        weight_refs = refs[len(blocks) + 1 : len(blocks) + 1 + len(segments)]
+        rest = refs[len(blocks) + 1 + len(segments) :]
+        if total is not None:
+            total_ref, rest = rest[0], rest[1:]
+        out_refs, left_ref = rest[:split], rest[split]
+        step = pl.program_id(0)
+
+        @pl.when(step == 0)
+        def _():
+            stacked = jnp.concatenate([ref[...] for ref in block_refs], axis=0)
+            left_ref[...] = jnp.dot(
+                order_ref[...], stacked, preferred_element_type=jnp.float32
+            ).astype(jnp.bfloat16)
+
+        columns = pl.ds(pl.multiple_of(step * tile, tile), tile)
+        for start, (_, _, _, tiles), weight_ref in zip(starts, segments, weight_refs):
+
+            @pl.when((step >= start) & (step < start + tiles))
+            def _(weight_ref=weight_ref):
+                result = jnp.dot(
+                    left_ref[...], weight_ref[...], preferred_element_type=jnp.float32
+                )
+                if total is not None:
+                    result = result + total_ref[:, columns]
+                for index, out_ref in enumerate(out_refs):
+                    out_ref[:, columns] = result[index * part : (index + 1) * part]
+
+    def whole(array):
+        return pl.BlockSpec(array.shape, lambda j: (0,) * array.ndim)
+
+    def weight_spec(start, row_block, first, tiles):
+        return pl.BlockSpec(
+            (depth, tile),
+            lambda j: (row_block, first + jnp.clip(j - start, 0, tiles - 1)),
+        )
+
+    operands = list(blocks) + [order] + [segment[0] for segment in segments]
+    specs = [whole(block) for block in blocks] + [whole(order)]
+    specs += [
+        weight_spec(start, row_block, first, tiles)
+        for start, (_, row_block, first, tiles) in zip(starts, segments)
+    ]
+    if total is not None:
+        operands.append(total)
+        specs.append(whole(total))
+    out_shape = [jax.ShapeDtypeStruct((part, width), jnp.float32)] * split
+    return pl.pallas_call(
+        body,
+        grid=(steps,),
+        in_specs=specs,
+        out_specs=[pl.BlockSpec((part, width), lambda j: (0, 0))] * split,
+        out_shape=out_shape,
+        scratch_shapes=[pltpu.VMEM((rows, depth), jnp.bfloat16)],
+        compiler_params=pltpu.CompilerParams(vmem_limit_bytes=VMEM_LIMIT),
+        cost_estimate=pl.CostEstimate(
+            flops=2 * rows * depth * (width + rows),
+            bytes_accessed=2 * depth * width + 4 * rows * width,
+            transcendentals=0,
+        ),
+    )(*operands)
+
+
+def one_hot(left, right):
+    return (left[:, None] == right[None, :]).astype(jnp.bfloat16)
+
+
+def wide_scatter(parts, low, high):
+    half = jnp.float16
+    mine = parts[0]
+    for i in range(1, low):
+        mine = mine + swap(parts[i].astype(half), "wide", i).astype(jnp.float32)
+    rows = mine.shape[0] // high
+    mine = mine.reshape(high, rows, -1)
+    total = mine[0]
+    for j in range(1, high):
+        total = total + swap(mine[j].astype(half), "wide", low * j).astype(jnp.float32)
+    return total
+
+
+def wide_gather(block, low, high):
+    held = [block] + [swap(block, "wide", low * j) for j in range(1, high)]
+    result = list(held)
+    for i in range(1, low):
+        result += [swap(piece, "wide", i) for piece in held]
+    return result
+
+
+def narrow_scatter(parts, far):
+    mine = parts[0] + swap(parts[1], "narrow", 1)
+    rows = mine.shape[0] // far
+    mine = mine.reshape(far, rows, -1)
+    total = mine[0]
+    for j in range(1, far):
+        total = total + swap(mine[j], "narrow", 2 * j)
+    return total
+
+
+def narrow_gather(block, far):
+    held = [block] + [swap(block, "narrow", 2 * j) for j in range(1, far)]
+    return held + [swap(piece, "narrow", 1) for piece in held]
 
 
 def shards(
@@ -94,62 +224,128 @@
     bank_row,
 ):
     wide_count = lax.axis_size("wide")
+    narrow_count = lax.axis_size("narrow")
+    me_wide = lax.axis_index("wide")
+    me_narrow = lax.axis_index("narrow")
+    high = 4
+    low = wide_count // high
+    far = narrow_count // 2
     model_width = hidden_in.shape[1] * wide_count
+    own_rows = hidden_in.shape[0]
     local_rows = cache_len.shape[0]
     all_rows = bank_row.shape[0]
-    served_by = (
-        jnp.zeros((all_rows,), jnp.int32).at[bank_row].set(jnp.arange(all_rows, dtype=jnp.int32))
-    )
+    wide_rows = all_rows // wide_count
+
+    position = jnp.arange(all_rows, dtype=jnp.int32)
+    narrow_offset = position // own_rows
+    narrow_offset = narrow_offset // far + 2 * (narrow_offset % far)
+    hypothesis = (me_narrow ^ narrow_offset) * own_rows + position % own_rows
+    wide_offset = position // wide_rows
+    wide_offset = wide_offset // high + low * (wide_offset % high)
+    wide_block = me_wide ^ wide_offset
+    inner = position % wide_rows
+    bank = (wide_block * narrow_count + (me_narrow ^ (inner // local_rows))) * local_rows
+    bank = bank + inner % local_rows
+    hypothesis_bank = bank_row[hypothesis]
+    to_bank = one_hot(bank, hypothesis_bank)
+    to_hypothesis = one_hot(hypothesis_bank, bank)
+    to_wide = one_hot(wide_block * wide_rows + inner, position)
+    from_wide = one_hot(position, wide_block * wide_rows + inner)
+
+    def wide_sum(rows_sq):
+        for i in (range(1, low),):
+            pair = rows_sq + sum(swap(rows_sq, "wide", j) for j in i)
+        return pair + sum(swap(pair, "wide", low * j) for j in range(1, high))
+
     rows_in = hidden_in.astype(jnp.float32)
-    first_sq = lax.psum(jnp.sum(rows_in * rows_in, axis=1), "wide")
+    first_sq = wide_sum(jnp.sum(rows_in * rows_in, axis=1))
     normed = normalize(hidden_in, attn_gain, first_sq, model_width)
-    gathered = lax.all_gather(normed, "narrow", axis=0, tiled=True)
+    row_blocks = narrow_gather(normed, far)
+
     q_cols = w_query.shape[1]
     k_cols = w_key.shape[1]
-    in_bank = gathered[served_by]
-    row_block = in_bank
-    summed = lax.psum_scatter(
-        jnp.concatenate(
-            [product(row_block, w_query), product(row_block, w_key), product(row_block, w_value)],
-            axis=1,
-        ),
-        "wide",
-        scatter_dimension=0,
-        tiled=True,
-    ).astype(jnp.bfloat16)
-    qkv_parts = (
-        summed[:, :q_cols],
-        summed[:, q_cols : q_cols + k_cols],
-        summed[:, q_cols + k_cols :],
-    )
-    queries, key_new, value_new = (
-        lax.all_to_all(qkv_parts[0], "narrow", split_axis=0, concat_axis=1, tiled=True),
-        lax.all_to_all(qkv_parts[1], "narrow", split_axis=0, concat_axis=1, tiled=True),
-        lax.all_to_all(qkv_parts[2], "narrow", split_axis=0, concat_axis=1, tiled=True),
-    )
-    query_rot = rotate(queries.reshape(local_rows, -1, HEAD_DIM), cache_len).reshape(local_rows, -1)
-    key_rot = rotate(key_new.reshape(local_rows, -1, HEAD_DIM), cache_len).reshape(local_rows, -1)
+    tile = k_cols
+    q_tiles = q_cols // tile
+    tiles = (q_tiles + 2) // QKV_CHUNKS
+    pieces = []
+    for chunk in range(QKV_CHUNKS):
+        first = chunk * tiles
+        segments = [(w_query, 0, first, min(tiles, q_tiles - first))]
+        if chunk == QKV_CHUNKS - 1:
+            segments += [(w_key, 0, 0, 1), (w_value, 0, 0, 1)]
+        pieces.append(wide_scatter(project(row_blocks, to_bank, segments, tile, low), low, high))
+    summed = jnp.concatenate(pieces, axis=1).astype(jnp.bfloat16)
+    summed = summed.reshape(narrow_count, local_rows, -1, HEAD_DIM)
+    turned = [summed[0]] + [swap(summed[j], "narrow", j) for j in range(1, narrow_count)]
+    ranks = me_narrow ^ jnp.arange(narrow_count, dtype=jnp.int32)
+    turned = jnp.stack(turned)[ranks].transpose(1, 0, 2, 3)
+    q_heads = q_cols // HEAD_DIM
+    k_heads = k_cols // HEAD_DIM
+    query_rot = rotate(
+        turned[:, :, :q_heads].reshape(local_rows, -1, HEAD_DIM), cache_len
+    ).reshape(local_rows, -1)
+    key_rot = rotate(
+        turned[:, :, q_heads : q_heads + k_heads].reshape(local_rows, -1, HEAD_DIM), cache_len
+    ).reshape(local_rows, -1)
+    value_new = turned[:, :, q_heads + k_heads :].reshape(local_rows, -1)
     context = attend(query_rot, key_rot, value_new, key_cache, value_cache, cache_len)
-    by_heads = lax.all_to_all(context, "narrow", split_axis=1, concat_axis=0, tiled=True)
-    every_row = lax.all_gather(by_heads, "wide", axis=0, tiled=True)
-    in_hypothesis = every_row[bank_row]
-    row_block = in_hypothesis
-    attn_out = lax.psum_scatter(
-        product(row_block, w_out), "narrow", scatter_dimension=0, tiled=True
-    )
+    context = context.reshape(local_rows, narrow_count, -1).transpose(1, 0, 2)[ranks]
+    by_heads = [context[0]] + [swap(context[j], "narrow", j) for j in range(1, narrow_count)]
+
+    out_tile = 512
+    out_tiles = w_out.shape[1] // out_tile
+    depth = w_out.shape[0] // CONTEXT_CHUNKS
+    total = None
+    for chunk in range(CONTEXT_CHUNKS):
+        columns = slice(chunk * depth, (chunk + 1) * depth)
+        block = jnp.concatenate([piece[:, columns] for piece in by_heads], axis=0)
+        last = chunk == CONTEXT_CHUNKS - 1
+        total = project(
+            wide_gather(block, low, high),
+            to_hypothesis,
+            [(w_out, chunk, 0, out_tiles)],
+            out_tile,
+            2 if last else 1,
+            total if total is None else total[0],
+        )
+    attn_out = narrow_scatter(total, far)
     resid = (rows_in + attn_out).astype(jnp.bfloat16)
     resid_wide = resid.astype(jnp.float32)
-    second_sq = lax.psum(jnp.sum(resid_wide * resid_wide, axis=1), "wide")
+    second_sq = wide_sum(jnp.sum(resid_wide * resid_wide, axis=1))
     normed_two = normalize(resid, ffn_gain, second_sq, model_width)
-    gathered_two = lax.all_gather(normed_two, "narrow", axis=0, tiled=True)
-    gate_sum, up_sum = lax.psum(
-        (product(gathered_two, w_gate), product(gathered_two, w_up)), "wide"
-    )
-    hidden_act = (jax.nn.silu(gate_sum) * up_sum).astype(jnp.bfloat16)
-    row_block = hidden_act
-    ffn_out = lax.psum_scatter(
-        product(row_block, w_down), "narrow", scatter_dimension=0, tiled=True
-    )
+    row_blocks = narrow_gather(normed_two, far)
+
+    f_cols = w_gate.shape[1] // FFN_CHUNKS
+    acts = []
+    for chunk in range(FFN_CHUNKS):
+        sums = wide_scatter(
+            project(
+                row_blocks,
+                to_wide,
+                [(w_gate, 0, chunk, 1), (w_up, 0, chunk, 1)],
+                f_cols,
+                low,
+            ),
+            low,
+            high,
+        )
+        acts.append((jax.nn.silu(sums[:, :f_cols]) * sums[:, f_cols:]).astype(jnp.bfloat16))
+    each = FFN_CHUNKS // DOWN_CHUNKS
+    down_tile = 512
+    down_tiles = w_down.shape[1] // down_tile
+    total = None
+    for chunk in range(DOWN_CHUNKS):
+        block = jnp.concatenate(acts[chunk * each : (chunk + 1) * each], axis=1)
+        last = chunk == DOWN_CHUNKS - 1
+        total = project(
+            wide_gather(block, low, high),
+            from_wide,
+            [(w_down, chunk, 0, down_tiles)],
+            down_tile,
+            2 if last else 1,
+            total if total is None else total[0],
+        )
+    ffn_out = narrow_scatter(total, far)
     return (resid_wide + ffn_out).astype(jnp.bfloat16)
 
 

time: 410 us -> 214 us (0.52)
  waiting for transfers between devices: 262 us -> 51.3 us
  starting transfers between devices: 10.2 us -> 93.8 us
  blocking collectives: 65.2 us -> 0 us
  matrix products: 40.7 us -> 5.16 us
  Pallas kernels: 0 us -> 25.1 us
  local copies, waits for them, and re-layouts: 8.59 us -> 30.9 us
  between operations: 13.4 us -> 0.89 us
    reduce_scatter x3 -> x0, waiting for transfers between devices: 114 us -> none  [the longest x1 65.7 us: shards(): lax.psum_scatter(jnp.concatenate([product(row_block, w_query), product(ro...]
    psum x1 -> x0, waiting for transfers between devices: 99.3 us -> none  [shards(): lax.psum((product(gathered_two, w_gate), product(gathered_two, w_up)), 'w...]
    ppermute x0 -> x80, starting transfers between devices: none -> 93.8 us  [swap(): return lax.ppermute(block, axis, [(i, i ^ offset) for i in range(count)])]
    ppermute x0 -> x80, waiting for transfers between devices: none -> 51.3 us  [swap(): return lax.ppermute(block, axis, [(i, i ^ offset) for i in range(count)])]
    psum x2 -> x0, blocking collectives: 44.5 us -> none  [the longest x1 23.1 us: shards(): first_sq = lax.psum(jnp.sum(rows_in * rows_in, axis=1), 'wide')]
    all_gather x1 -> x0, waiting for transfers between devices: 38.2 us -> none  [shards(): every_row = lax.all_gather(by_heads, 'wide', axis=0, tiled=True)]
    dot_general x7 -> x0, matrix products: 35.6 us -> none  [product(): return jnp.dot(left, right, preferred_element_type=jnp.float32)]
    unnamed x14 -> x30, local copies, waits for them, and re-layouts: 0.04 us -> 27.6 us
  transfers between devices with their start and end apart: 8 -> 80, of which waited for: 8 -> 26; matrix products, arithmetic and copies ran while one was open for 0% -> 2% of each run, Pallas kernels for 0% -> 7%
where the time goes in v1:
time: 214 us
  starting transfers between devices  93.8 us (44%)
  waiting for transfers between devices  51.3 us (24%)
  local copies, waits for them, and re-layouts  30.9 us (14%)
  Pallas kernels  25.1 us (12%)
  other arithmetic  6.51 us (3%)
  matrix products  5.16 us (2%)
    ppermute x80, starting transfers between devices, swap(): return lax.ppermute(block, axis, [(i, i ^ offset) for i in range(count)])  93.8 us
    ppermute x80, waiting for transfers between devices, swap(): return lax.ppermute(block, axis, [(i, i ^ offset) for i in range(count)])  51.3 us
    unnamed x30, local copies, waits for them, and re-layouts  27.6 us
    pallas_call x11, Pallas kernels, project(): pl.pallas_call(body, grid=(steps,), in_specs=specs, out_specs=[pl.BlockSp...  25.1 us
  transfers between devices with their start and end apart: 80, of which 26 were waited for; matrix products, arithmetic and copies ran while one was open for 2% of the time, Pallas kernels for 7%

profile of v1, /device:TPU:0, one launch (start us, length us, event | category | flops | bytes accessed | tf_op | source)
XLA Modules:
  0.0 213.6 jit_solution(13640966196854575291)
XLA Ops:
  1.1 3.0 %collective-permute-start = (f32[32]{0:T(128)S(1)}, f32[32]{0:T(128)S(1)}, u32[]{:S(2)}, u32[]{:S(2)}) collective-permute-start(f32[32]{0:T(128)S(1)} %fusion.25), channel_id=1, source_target_pairs={{0,4},{4,0},{8,12},{12,8},{16,20},{20,16},{24,28},{28,24},{1,5},{5... | collective-permute-start | bytes 392 | tf_op jit(solution)/shard_map/ppermute | solution.py:91
  12.2 3.5 %collective-permute-done.3 = f32[32]{0:T(128)S(1)} collective-permute-done((f32[32]{0:T(128)S(1)}, f32[32]{0:T(128)S(1)}, u32[]{:S(2)}, u32[]{:S(2)}) %collective-permute-start.3) | collective-permute-done | bytes 160 | tf_op jit(solution)/shard_map/ppermute | solution.py:91
  18.4 3.3 %collective-permute-done.4.refs_1_ = bf16[32,2048]{1,0:T(8,128)(2,1)S(1)} collective-permute-done((bf16[32,2048]{1,0:T(8,128)(2,1)S(1)}, bf16[32,2048]{1,0:T(8,128)(2,1)S(1)}, u32[]{:S(2)}, u32[]{:S(2)}) %collective-permute-start.4) | collective-permute-done | bytes 131104 | tf_op jit(solution)/shard_map/ppermute | solution.py:91
  23.1 5.8 %copy-done.2 = bf16[2048,4096]{1,0:T(8,128)(2,1)S(1)} copy-done((bf16[2048,4096]{1,0:T(8,128)(2,1)S(1)}, bf16[2048,4096]{1,0:T(8,128)(2,1)}, u32[]{:S(2)}) %copy-start.2) | copy-done | bytes 16777240
  28.8 3.1 %shard_map.136 = (f32[64,1536]{1,0:T(8,128)S(1)}, f32[64,1536]{1,0:T(8,128)S(1)}) custom-call(bf16[32,2048]{1,0:T(8,128)(2,1)S(1)} %fusion.27.refs_0_, bf16[32,2048]{1,0:T(8,128)(2,1)S(1)} %collective-permute-done.4.refs_1_, bf16[32,2048]{1,0:T(8,128)(2,1)S(1)} %collective-permute-done.5.refs_2_, bf16[32,2048]{1,0:T(8,128)(2,1)S(1)} %collective-permute-done.6.refs_3_, ...), custom_call_target="tpu_custom_call" | custom-call | flops 872415232 | bytes 7077888 | tf_op jit(solution)/shard_map/pallas_call | solution.py:154
  33.6 3.2 %shard_map.137 = (f32[64,1536]{1,0:T(8,128)S(1)}, f32[64,1536]{1,0:T(8,128)S(1)}) custom-call(bf16[32,2048]{1,0:T(8,128)(2,1)S(1)} %fusion.27.refs_0_, bf16[32,2048]{1,0:T(8,128)(2,1)S(1)} %collective-permute-done.4.refs_1_, bf16[32,2048]{1,0:T(8,128)(2,1)S(1)} %collective-permute-done.5.refs_2_, bf16[32,2048]{1,0:T(8,128)(2,1)S(1)} %collective-permute-done.6.refs_3_, ...), custom_call_target="tpu_custom_call" | custom-call | flops 872415232 | bytes 7077888 | tf_op jit(solution)/shard_map/pallas_call | solution.py:154
  37.4 2.9 %shard_map.138 = (f32[64,1536]{1,0:T(8,128)S(1)}, f32[64,1536]{1,0:T(8,128)S(1)}) custom-call(bf16[32,2048]{1,0:T(8,128)(2,1)S(1)} %fusion.27.refs_0_, bf16[32,2048]{1,0:T(8,128)(2,1)S(1)} %collective-permute-done.4.refs_1_, bf16[32,2048]{1,0:T(8,128)(2,1)S(1)} %collective-permute-done.5.refs_2_, bf16[32,2048]{1,0:T(8,128)(2,1)S(1)} %collective-permute-done.6.refs_3_, ...), custom_call_target="tpu_custom_call" | custom-call | flops 872415232 | bytes 7077888 | tf_op jit(solution)/shard_map/pallas_call | solution.py:154
  42.3 4.2 %collective-permute-start.9 = (f16[16,1536]{1,0:T(8,128)(2,1)S(1)}, f16[16,1536]{1,0:T(8,128)(2,1)S(1)}, u32[]{:S(2)}, u32[]{:S(2)}) collective-permute-start(f16[16,1536]{1,0:T(8,128)(2,1)S(1)} %get-tuple-element.59), channel_id=1, source_target_pairs={{0,16},{4,20},{8,24},{12,28},{16,0},{20,4},{24,8},{28,12},{1,17},{... | collective-permute-start | bytes 147464 | tf_op jit(solution)/shard_map/ppermute | solution.py:91
  65.8 3.9 %fusion.94 = (f32[4,8,16]{2,1,0:T(8,128)S(1)}, f32[4,8,16,512]{3,2,1,0:T(8,128)S(1)}) fusion(bf16[4,8,16,64]{3,2,1,0:T(8,128)(2,1)S(1)} %bitcast.72, bf16[4,8,16,64]{3,2,1,0:T(8,128)(2,1)S(1)} %bitcast.70, pred[4,512]{1,0:T(4,128)(4,1)S(1)} %iota_compare_fusion.2, bf16[4,512,1024]{2,1,0:T(8,128)(2,1)} %param.24), kind=kOutput, calls=%fused_computation.185 | convolution fusion | flops 68156928 | bytes 5378048 | tf_op jit(solution)/shard_map/rgqd,rlgd->rgql/dot_general | solution.py:59
  76.8 3.1 %collective-permute-start.33 = (bf16[16,2048]{1,0:T(8,128)(2,1)S(1)}, bf16[16,2048]{1,0:T(8,128)(2,1)S(1)}, u32[]{:S(2)}, u32[]{:S(2)}) collective-permute-start(bf16[16,2048]{1,0:T(8,128)(2,1)S(1)} %pad_maximum_fusion.4.refs_0_), channel_id=1, source_target_pairs={{0,16},{4,20},{8,24},{12,28},{16,0},{20,4},{24,8},{28,12},{1,17},{... | collective-permute-start | bytes 196616 | tf_op jit(solution)/shard_map/ppermute | solution.py:91
  82.1 3.0 %collective-permute-start.26 = (bf16[16,2048]{1,0:T(8,128)(2,1)S(1)}, bf16[16,2048]{1,0:T(8,128)(2,1)S(1)}, u32[]{:S(2)}, u32[]{:S(2)}) collective-permute-start(bf16[16,2048]{1,0:T(8,128)(2,1)S(1)} %pad_maximum_fusion.3.refs_0_), channel_id=1, source_target_pairs={{0,16},{4,20},{8,24},{12,28},{16,0},{20,4},{24,8},{28,12},{1,17},{... | collective-permute-start | bytes 196616 | tf_op jit(solution)/shard_map/ppermute | solution.py:91
  85.0 3.1 %collective-permute-start.27 = (bf16[16,2048]{1,0:T(8,128)(2,1)S(1)}, bf16[16,2048]{1,0:T(8,128)(2,1)S(1)}, u32[]{:S(2)}, u32[]{:S(2)}) collective-permute-start(bf16[16,2048]{1,0:T(8,128)(2,1)S(1)} %pad_maximum_fusion.3.refs_0_), channel_id=1, source_target_pairs={{0,24},{4,28},{8,16},{12,20},{16,8},{20,12},{24,0},{28,4},{1,25},{... | collective-permute-start | bytes 196616 | tf_op jit(solution)/shard_map/ppermute | solution.py:91
  95.6 5.8 %copy-done.4 = bf16[4096,2048]{1,0:T(8,128)(2,1)S(1)} copy-done((bf16[4096,2048]{1,0:T(8,128)(2,1)S(1)}, bf16[4096,2048]{1,0:T(8,128)(2,1)}, u32[]{:S(2)}) %copy-start.4) | copy-done | bytes 16777240
  101.3 2.8 %shard_map.139.refs_10_ = f32[128,2048]{1,0:T(8,128)S(1)} custom-call(bf16[16,2048]{1,0:T(8,128)(2,1)S(1)} %pad_maximum_fusion.4.refs_0_, bf16[16,2048]{1,0:T(8,128)(2,1)S(1)} %collective-permute-done.32.refs_1_, bf16[16,2048]{1,0:T(8,128)(2,1)S(1)} %collective-permute-done.33.refs_2_, bf16[16,2048]{1,0:T(8,128)(2,1)S(1)} %collective-permute-done.34.refs_3_, ...), custom_call_target="tpu_custom_call" | custom-call | flops 1140850688 | bytes 9437184 | tf_op jit(solution)/shard_map/pallas_call | solution.py:154
  104.2 5.9 %copy-done.5 = bf16[4096,2048]{1,0:T(8,128)(2,1)S(1)} copy-done((bf16[4096,2048]{1,0:T(8,128)(2,1)S(1)}, bf16[4096,2048]{1,0:T(8,128)(2,1)}, u32[]{:S(2)}) %copy-start.5) | copy-done | bytes 16777240
  110.1 3.0 %shard_map.140 = (f32[64,2048]{1,0:T(8,128)S(1)}, f32[64,2048]{1,0:T(8,128)S(1)}) custom-call(bf16[16,2048]{1,0:T(8,128)(2,1)S(1)} %pad_maximum_fusion.3.refs_0_, bf16[16,2048]{1,0:T(8,128)(2,1)S(1)} %collective-permute-done.25.refs_1_, bf16[16,2048]{1,0:T(8,128)(2,1)S(1)} %collective-permute-done.26.refs_2_, ...), custom_call_target="tpu_custom_call" | custom-call | flops 1140850688 | bytes 9437184 | tf_op jit(solution)/shard_map/pallas_call | solution.py:154
  116.3 7.3 %collective-permute-done.40 = f32[32,2048]{1,0:T(8,128)S(1)} collective-permute-done((f32[32,2048]{1,0:T(8,128)S(1)}, f32[32,2048]{1,0:T(8,128)S(1)}, u32[]{:S(2)}, u32[]{:S(2)}) %collective-permute-start.40) | collective-permute-done | bytes 262176 | tf_op jit(solution)/shard_map/ppermute | solution.py:91
  127.4 2.9 %collective-permute-start.43 = (f32[32]{0:T(128)S(1)}, f32[32]{0:T(128)S(1)}, u32[]{:S(2)}, u32[]{:S(2)}) collective-permute-start(f32[32]{0:T(128)S(1)} %add.420), channel_id=1, source_target_pairs={{0,16},{4,20},{8,24},{12,28},{16,0},{20,4},{24,8},{28,12},{1,17},{... | collective-permute-start | bytes 392 | tf_op jit(solution)/shard_map/ppermute | solution.py:91
  131.8 3.8 %collective-permute-done.44 = f32[32]{0:T(128)S(1)} collective-permute-done((f32[32]{0:T(128)S(1)}, f32[32]{0:T(128)S(1)}, u32[]{:S(2)}, u32[]{:S(2)}) %collective-permute-start.44) | collective-permute-done | bytes 160 | tf_op jit(solution)/shard_map/ppermute | solution.py:91
  136.9 3.9 %collective-permute-done.45.refs_1_ = bf16[32,2048]{1,0:T(8,128)(2,1)S(1)} collective-permute-done((bf16[32,2048]{1,0:T(8,128)(2,1)S(1)}, bf16[32,2048]{1,0:T(8,128)(2,1)S(1)}, u32[]{:S(2)}, u32[]{:S(2)}) %collective-permute-start.45) | collective-permute-done | bytes 131104 | tf_op jit(solution)/shard_map/ppermute | solution.py:91
  142.1 3.4 %copy-done.3 = bf16[2048,2048]{1,0:T(8,128)(2,1)S(1)} copy-done((bf16[2048,2048]{1,0:T(8,128)(2,1)S(1)}, bf16[2048,2048]{1,0:T(8,128)(2,1)}, u32[]{:S(2)}) %copy-start.3) | copy-done | bytes 8388632
  191.8 3.4 %copy-done.6 = bf16[2048,2048]{1,0:T(8,128)(2,1)S(1)} copy-done((bf16[2048,2048]{1,0:T(8,128)(2,1)S(1)}, bf16[2048,2048]{1,0:T(8,128)(2,1)}, u32[]{:S(2)}) %copy-start.6) | copy-done | bytes 8388632
  197.1 3.4 %copy-done.7 = bf16[2048,2048]{1,0:T(8,128)(2,1)S(1)} copy-done((bf16[2048,2048]{1,0:T(8,128)(2,1)S(1)}, bf16[2048,2048]{1,0:T(8,128)(2,1)}, u32[]{:S(2)}) %copy-start.7) | copy-done | bytes 8388632
  205.6 7.3 %collective-permute-done.79 = f32[32,2048]{1,0:T(8,128)S(1)} collective-permute-done((f32[32,2048]{1,0:T(8,128)S(1)}, f32[32,2048]{1,0:T(8,128)S(1)}, u32[]{:S(2)}, u32[]{:S(2)}) %collective-permute-start.79) | collective-permute-done | bytes 262176 | tf_op jit(solution)/shard_map/ppermute | solution.py:91
  (266 shorter events, 117.8 us)
Async XLA Ops:
  32.0 9.9 %collective-permute-start.7 = (f16[64,1536]{1,0:T(8,128)(2,1)S(1)}, f16[64,1536]{1,0:T(8,128)(2,1)S(1)}, u32[]{:S(2)}, u32[]{:S(2)}) collective-permute-start(f16[64,1536]{1,0:T(8,128)(2,1)S(1)} %convert_element_type.219), channel_id=1, source_target_pairs={{0,4},{4,0},{8,12},{12,8},{16,20},{20,16},{24,28},{28,24},{1,5},{5... | collective-permute-start | bytes 589832 | tf_op jit(solution)/shard_map/ppermute | solution.py:91
  36.8 9.7 %collective-permute-start.11 = (f16[64,1536]{1,0:T(8,128)(2,1)S(1)}, f16[64,1536]{1,0:T(8,128)(2,1)S(1)}, u32[]{:S(2)}, u32[]{:S(2)}) collective-permute-start(f16[64,1536]{1,0:T(8,128)(2,1)S(1)} %convert_element_type.224), channel_id=1, source_target_pairs={{0,4},{4,0},{8,12},{12,8},{16,20},{20,16},{24,28},{28,24},{1,5},{5... | collective-permute-start | bytes 589832 | tf_op jit(solution)/shard_map/ppermute | solution.py:91
  42.3 8.9 %collective-permute-start.8 = (f16[16,1536]{1,0:T(8,128)(2,1)S(1)}, f16[16,1536]{1,0:T(8,128)(2,1)S(1)}, u32[]{:S(2)}, u32[]{:S(2)}) collective-permute-start(f16[16,1536]{1,0:T(8,128)(2,1)S(1)} %get-tuple-element.57), channel_id=1, source_target_pairs={{0,8},{4,12},{8,0},{12,4},{16,24},{20,28},{24,16},{28,20},{1,9},{5... | collective-permute-start | bytes 147464 | tf_op jit(solution)/shard_map/ppermute | solution.py:91
  42.3 9.1 %collective-permute-start.9 = (f16[16,1536]{1,0:T(8,128)(2,1)S(1)}, f16[16,1536]{1,0:T(8,128)(2,1)S(1)}, u32[]{:S(2)}, u32[]{:S(2)}) collective-permute-start(f16[16,1536]{1,0:T(8,128)(2,1)S(1)} %get-tuple-element.59), channel_id=1, source_target_pairs={{0,16},{4,20},{8,24},{12,28},{16,0},{20,4},{24,8},{28,12},{1,17},{... | collective-permute-start | bytes 147464 | tf_op jit(solution)/shard_map/ppermute | solution.py:91
  47.7 8.0 %collective-permute-start.13 = (f16[16,1536]{1,0:T(8,128)(2,1)S(1)}, f16[16,1536]{1,0:T(8,128)(2,1)S(1)}, u32[]{:S(2)}, u32[]{:S(2)}) collective-permute-start(f16[16,1536]{1,0:T(8,128)(2,1)S(1)} %get-tuple-element.62), channel_id=1, source_target_pairs={{0,16},{4,20},{8,24},{12,28},{16,0},{20,4},{24,8},{28,12},{1,17},{... | collective-permute-start | bytes 147464 | tf_op jit(solution)/shard_map/ppermute | solution.py:91
  76.8 8.2 %collective-permute-start.33 = (bf16[16,2048]{1,0:T(8,128)(2,1)S(1)}, bf16[16,2048]{1,0:T(8,128)(2,1)S(1)}, u32[]{:S(2)}, u32[]{:S(2)}) collective-permute-start(bf16[16,2048]{1,0:T(8,128)(2,1)S(1)} %pad_maximum_fusion.4.refs_0_), channel_id=1, source_target_pairs={{0,16},{4,20},{8,24},{12,28},{16,0},{20,4},{24,8},{28,12},{1,17},{... | collective-permute-start | bytes 196616 | tf_op jit(solution)/shard_map/ppermute | solution.py:91
  79.9 8.2 %collective-permute-start.34 = (bf16[16,2048]{1,0:T(8,128)(2,1)S(1)}, bf16[16,2048]{1,0:T(8,128)(2,1)S(1)}, u32[]{:S(2)}, u32[]{:S(2)}) collective-permute-start(bf16[16,2048]{1,0:T(8,128)(2,1)S(1)} %pad_maximum_fusion.4.refs_0_), channel_id=1, source_target_pairs={{0,24},{4,28},{8,16},{12,20},{16,8},{20,12},{24,0},{28,4},{1,25},{... | collective-permute-start | bytes 196616 | tf_op jit(solution)/shard_map/ppermute | solution.py:91
  81.9 8.3 %collective-permute-start.25 = (bf16[16,2048]{1,0:T(8,128)(2,1)S(1)}, bf16[16,2048]{1,0:T(8,128)(2,1)S(1)}, u32[]{:S(2)}, u32[]{:S(2)}) collective-permute-start(bf16[16,2048]{1,0:T(8,128)(2,1)S(1)} %pad_maximum_fusion.3.refs_0_), channel_id=1, source_target_pairs={{0,8},{4,12},{8,0},{12,4},{16,24},{20,28},{24,16},{28,20},{1,9},{5... | collective-permute-start | bytes 196616 | tf_op jit(solution)/shard_map/ppermute | solution.py:91
  82.1 8.4 %collective-permute-start.26 = (bf16[16,2048]{1,0:T(8,128)(2,1)S(1)}, bf16[16,2048]{1,0:T(8,128)(2,1)S(1)}, u32[]{:S(2)}, u32[]{:S(2)}) collective-permute-start(bf16[16,2048]{1,0:T(8,128)(2,1)S(1)} %pad_maximum_fusion.3.refs_0_), channel_id=1, source_target_pairs={{0,16},{4,20},{8,24},{12,28},{16,0},{20,4},{24,8},{28,12},{1,17},{... | collective-permute-start | bytes 196616 | tf_op jit(solution)/shard_map/ppermute | solution.py:91
  90.5 13.7 %collective-permute-start.28 = (bf16[16,2048]{1,0:T(8,128)(2,1)S(1)}, bf16[16,2048]{1,0:T(8,128)(2,1)S(1)}, u32[]{:S(2)}, u32[]{:S(2)}) collective-permute-start(bf16[16,2048]{1,0:T(8,128)(2,1)S(1)} %pad_maximum_fusion.3.refs_0_), channel_id=1, source_target_pairs={{0,4},{4,0},{8,12},{12,8},{16,20},{20,16},{24,28},{28,24},{1,5},{5... | collective-permute-start | bytes 196616 | tf_op jit(solution)/shard_map/ppermute | solution.py:91
  92.2 12.0 %collective-permute-start.29 = (bf16[16,2048]{1,0:T(8,128)(2,1)S(1)}, bf16[16,2048]{1,0:T(8,128)(2,1)S(1)}, u32[]{:S(2)}, u32[]{:S(2)}) collective-permute-start(bf16[16,2048]{1,0:T(8,128)(2,1)S(1)} %collective-permute-done.25.refs_1_), channel_id=1, source_target_pairs={{0,4},{4,0},{8,12},{12,8},{16,20},{20,16},{24,28},{28,24},{1,5},{5... | collective-permute-start | bytes 196616 | tf_op jit(solution)/shard_map/ppermute | solution.py:91
  92.8 11.4 %collective-permute-start.30 = (bf16[16,2048]{1,0:T(8,128)(2,1)S(1)}, bf16[16,2048]{1,0:T(8,128)(2,1)S(1)}, u32[]{:S(2)}, u32[]{:S(2)}) collective-permute-start(bf16[16,2048]{1,0:T(8,128)(2,1)S(1)} %collective-permute-done.26.refs_2_), channel_id=1, source_target_pairs={{0,4},{4,0},{8,12},{12,8},{16,20},{20,16},{24,28},{28,24},{1,5},{5... | collective-permute-start | bytes 196616 | tf_op jit(solution)/shard_map/ppermute | solution.py:91
  94.2 9.9 %collective-permute-start.31 = (bf16[16,2048]{1,0:T(8,128)(2,1)S(1)}, bf16[16,2048]{1,0:T(8,128)(2,1)S(1)}, u32[]{:S(2)}, u32[]{:S(2)}) collective-permute-start(bf16[16,2048]{1,0:T(8,128)(2,1)S(1)} %collective-permute-done.27.refs_3_), channel_id=1, source_target_pairs={{0,4},{4,0},{8,12},{12,8},{16,20},{20,16},{24,28},{28,24},{1,5},{5... | collective-permute-start | bytes 196616 | tf_op jit(solution)/shard_map/ppermute | solution.py:91
  115.2 8.4 %collective-permute-start.40 = (f32[32,2048]{1,0:T(8,128)S(1)}, f32[32,2048]{1,0:T(8,128)S(1)}, u32[]{:S(2)}, u32[]{:S(2)}) collective-permute-start(f32[32,2048]{1,0:T(8,128)S(1)} %slice.354), channel_id=1, source_target_pairs={{0,2},{1,3},{2,0},{3,1},{4,6},{5,7},{6,4},{7,5},{8,10},{9,11},{10,... | collective-permute-start | bytes 786440 | tf_op jit(solution)/shard_map/ppermute | solution.py:91
  147.1 9.1 %collective-permute-start.63 = (f16[64,1024]{1,0:T(8,128)(2,1)S(1)}, f16[64,1024]{1,0:T(8,128)(2,1)S(1)}, u32[]{:S(2)}, u32[]{:S(2)}) collective-permute-start(f16[64,1024]{1,0:T(8,128)(2,1)S(1)} %convert_element_type.264), channel_id=1, source_target_pairs={{0,4},{4,0},{8,12},{12,8},{16,20},{20,16},{24,28},{28,24},{1,5},{5... | collective-permute-start | bytes 393224 | tf_op jit(solution)/shard_map/ppermute | solution.py:91
  149.4 9.0 %collective-permute-start.67 = (f16[64,1024]{1,0:T(8,128)(2,1)S(1)}, f16[64,1024]{1,0:T(8,128)(2,1)S(1)}, u32[]{:S(2)}, u32[]{:S(2)}) collective-permute-start(f16[64,1024]{1,0:T(8,128)(2,1)S(1)} %convert_element_type.270), channel_id=1, source_target_pairs={{0,4},{4,0},{8,12},{12,8},{16,20},{20,16},{24,28},{28,24},{1,5},{5... | collective-permute-start | bytes 393224 | tf_op jit(solution)/shard_map/ppermute | solution.py:91
  152.5 8.4 %collective-permute-start.48 = (f16[64,1024]{1,0:T(8,128)(2,1)S(1)}, f16[64,1024]{1,0:T(8,128)(2,1)S(1)}, u32[]{:S(2)}, u32[]{:S(2)}) collective-permute-start(f16[64,1024]{1,0:T(8,128)(2,1)S(1)} %convert_element_type.251), channel_id=1, source_target_pairs={{0,4},{4,0},{8,12},{12,8},{16,20},{20,16},{24,28},{28,24},{1,5},{5... | collective-permute-start | bytes 393224 | tf_op jit(solution)/shard_map/ppermute | solution.py:91
  156.6 9.0 %collective-permute-start.65 = (f16[16,1024]{1,0:T(8,128)(2,1)S(1)}, f16[16,1024]{1,0:T(8,128)(2,1)S(1)}, u32[]{:S(2)}, u32[]{:S(2)}) collective-permute-start(f16[16,1024]{1,0:T(8,128)(2,1)S(1)} %get-tuple-element.76), channel_id=1, source_target_pairs={{0,16},{4,20},{8,24},{12,28},{16,0},{20,4},{24,8},{28,12},{1,17},{... | collective-permute-start | bytes 98312 | tf_op jit(solution)/shard_map/ppermute | solution.py:91
  161.2 9.0 %collective-permute-start.69 = (f16[16,1024]{1,0:T(8,128)(2,1)S(1)}, f16[16,1024]{1,0:T(8,128)(2,1)S(1)}, u32[]{:S(2)}, u32[]{:S(2)}) collective-permute-start(f16[16,1024]{1,0:T(8,128)(2,1)S(1)} %get-tuple-element.79), channel_id=1, source_target_pairs={{0,16},{4,20},{8,24},{12,28},{16,0},{20,4},{24,8},{28,12},{1,17},{... | collective-permute-start | bytes 98312 | tf_op jit(solution)/shard_map/ppermute | solution.py:91
  165.6 9.0 %collective-permute-start.50 = (f16[16,1024]{1,0:T(8,128)(2,1)S(1)}, f16[16,1024]{1,0:T(8,128)(2,1)S(1)}, u32[]{:S(2)}, u32[]{:S(2)}) collective-permute-start(f16[16,1024]{1,0:T(8,128)(2,1)S(1)} %get-tuple-element.82), channel_id=1, source_target_pairs={{0,16},{4,20},{8,24},{12,28},{16,0},{20,4},{24,8},{28,12},{1,17},{... | collective-permute-start | bytes 98312 | tf_op jit(solution)/shard_map/ppermute | solution.py:91
  170.1 9.0 %collective-permute-start.54 = (f16[16,1024]{1,0:T(8,128)(2,1)S(1)}, f16[16,1024]{1,0:T(8,128)(2,1)S(1)}, u32[]{:S(2)}, u32[]{:S(2)}) collective-permute-start(f16[16,1024]{1,0:T(8,128)(2,1)S(1)} %get-tuple-element.85), channel_id=1, source_target_pairs={{0,16},{4,20},{8,24},{12,28},{16,0},{20,4},{24,8},{28,12},{1,17},{... | collective-permute-start | bytes 98312 | tf_op jit(solution)/shard_map/ppermute | solution.py:91
  187.8 9.3 %collective-permute-start.59 = (bf16[16,1024]{1,0:T(8,128)(2,1)S(1)}, bf16[16,1024]{1,0:T(8,128)(2,1)S(1)}, u32[]{:S(2)}, u32[]{:S(2)}) collective-permute-start(bf16[16,1024]{1,0:T(8,128)(2,1)S(1)} %pad_maximum_fusion.5.refs_0_), channel_id=1, source_target_pairs={{0,4},{4,0},{8,12},{12,8},{16,20},{20,16},{24,28},{28,24},{1,5},{5... | collective-permute-start | bytes 98312 | tf_op jit(solution)/shard_map/ppermute | solution.py:91
  188.4 8.7 %collective-permute-start.60 = (bf16[16,1024]{1,0:T(8,128)(2,1)S(1)}, bf16[16,1024]{1,0:T(8,128)(2,1)S(1)}, u32[]{:S(2)}, u32[]{:S(2)}) collective-permute-start(bf16[16,1024]{1,0:T(8,128)(2,1)S(1)} %collective-permute-done.56.refs_1_), channel_id=1, source_target_pairs={{0,4},{4,0},{8,12},{12,8},{16,20},{20,16},{24,28},{28,24},{1,5},{5... | collective-permute-start | bytes 98312 | tf_op jit(solution)/shard_map/ppermute | solution.py:91
  204.5 8.4 %collective-permute-start.79 = (f32[32,2048]{1,0:T(8,128)S(1)}, f32[32,2048]{1,0:T(8,128)S(1)}, u32[]{:S(2)}, u32[]{:S(2)}) collective-permute-start(f32[32,2048]{1,0:T(8,128)S(1)} %slice.380), channel_id=1, source_target_pairs={{0,2},{1,3},{2,0},{3,1},{4,6},{5,7},{6,4},{7,5},{8,10},{9,11},{10,... | collective-permute-start | bytes 786440 | tf_op jit(solution)/shard_map/ppermute | solution.py:91
  (71 other events, 497.7 us)

commit v2 on v0

--- a/solution.py
+++ b/solution.py
@@ -3,6 +3,8 @@
 import jax
 import jax.numpy as jnp
 from jax import lax
+from jax.experimental import pallas as pl
+from jax.experimental.pallas import tpu as pltpu
 from jax.sharding import PartitionSpec as P
 
 HEAD_DIM = 128
@@ -75,6 +77,147 @@
         + own_prob.astype(jnp.float32)[..., None] * own_value.astype(jnp.float32)[:, :, None, :]
     )
     return context.reshape(row_count, groups * group_size * HEAD_DIM).astype(jnp.bfloat16)
+
+
+QKV_CHUNKS = 3
+FFN_CHUNKS = 2
+CONTEXT_CHUNKS = 2
+NARROW_KINDS = [jnp.float32] + [jnp.bfloat16] * 8
+TILE = 512
+STAND_IN = 3
+MIB = 1024 * 1024
+
+
+def swap(block, axis, offset):
+    count = lax.axis_size(axis)
+    return lax.ppermute(block, axis, [(i, i ^ offset) for i in range(count)])
+
+
+def strides_of(axis):
+    count = lax.axis_size(axis)
+    return [1 << bit for bit in range(count.bit_length() - 1)]
+
+
+def offsets_of(axis):
+    order = [0]
+    for stride in reversed(strides_of(axis)):
+        order = order + [offset ^ stride for offset in order]
+    return order
+
+
+def project(pieces, order, segments, split, room, total=None):
+    rows = order.shape[0]
+    depth = pieces[0].shape[1]
+    tiles = []
+    width = 0
+    for index, (_, first_row, first, columns) in enumerate(segments):
+        for start in range(first, first + columns, TILE):
+            tile = min(TILE, first + columns - start)
+            tiles.append((index, first_row, start, tile, width))
+            width += tile
+    part = rows // split
+    count = len(pieces)
+
+    def body(*refs):
+        piece_refs, order_ref, rest = refs[:count], refs[count], refs[count + 1 :]
+        weight_refs, rest = rest[: len(segments)], rest[len(segments) :]
+        if total is not None:
+            total_ref, rest = rest[0], rest[1:]
+        out_refs = rest[:split]
+        stacked = jnp.concatenate([ref[...] for ref in piece_refs], axis=0)
+        left = jnp.dot(order_ref[...], stacked, preferred_element_type=jnp.float32)
+        left = left.astype(jnp.bfloat16)
+        for index, first_row, start, tile, base in tiles:
+            weight = weight_refs[index][pl.ds(first_row, depth), pl.ds(start, tile)]
+            result = jnp.dot(left, weight, preferred_element_type=jnp.float32)
+            if total is not None:
+                result = result + total_ref[:, base : base + tile]
+            for index, out_ref in enumerate(out_refs):
+                out_ref[:, base : base + tile] = result[index * part : (index + 1) * part]
+
+    operands = list(pieces) + [order] + [segment[0] for segment in segments]
+    in_vmem = pl.BlockSpec(memory_space=pltpu.VMEM)
+    specs = [in_vmem] * (count + 1) + [in_vmem] * len(segments)
+    if total is not None:
+        operands.append(total)
+        specs.append(in_vmem)
+    return pl.pallas_call(
+        body,
+        in_specs=specs,
+        out_specs=[in_vmem] * split,
+        out_shape=[jax.ShapeDtypeStruct((part, width), jnp.float32)] * split,
+        compiler_params=pltpu.CompilerParams(vmem_limit_bytes=room * MIB),
+        cost_estimate=pl.CostEstimate(
+            flops=2 * rows * depth * (width + rows),
+            bytes_accessed=2 * depth * width + 4 * rows * width,
+            transcendentals=0,
+        ),
+    )(*operands)
+
+
+def stand_in(after, microseconds):
+    def body(after_ref, zero_ref):
+        zero_ref[...] = jnp.zeros_like(zero_ref)
+
+    zero = pl.pallas_call(
+        body,
+        in_specs=[pl.BlockSpec(memory_space=pl.ANY)],
+        out_specs=pl.BlockSpec(memory_space=pltpu.VMEM),
+        out_shape=jax.ShapeDtypeStruct((8, 128), jnp.float32),
+        compiler_params=pltpu.CompilerParams(vmem_limit_bytes=MIB),
+        cost_estimate=pl.CostEstimate(
+            flops=int(1.1e9 * microseconds), bytes_accessed=4096, transcendentals=0
+        ),
+    )(after)
+    return zero[0, 0]
+
+
+def one_hot(left, right):
+    return (left[:, None] == right[None, :]).astype(jnp.bfloat16)
+
+
+def wide_scatter(kept, sent, kind):
+    strides = strides_of("wide")
+    rows = 2 * kept.shape[0] // lax.axis_size("wide")
+    kept = kept + swap(sent.astype(kind), "wide", strides[0]).astype(jnp.float32)
+    total = kept[:rows] + stand_in(kept, STAND_IN)
+    for place, offset in enumerate(offsets_of("wide")[: kept.shape[0] // rows]):
+        if offset:
+            block = kept[place * rows : (place + 1) * rows].astype(kind)
+            total = total + swap(block, "wide", offset).astype(jnp.float32)
+    return total
+
+
+def narrow_scatter(kept, sent):
+    for stride, kind in zip(strides_of("narrow"), NARROW_KINDS):
+        if stride > 1:
+            half = kept.shape[0] // 2
+            kept, sent = kept[:half], kept[half:]
+        kept = kept + swap(sent.astype(kind), "narrow", stride).astype(jnp.float32)
+    return kept
+
+
+def gather(block, axis):
+    strides = strides_of(axis)[::-1]
+    for stride in strides[:-1]:
+        block = jnp.concatenate([block, swap(block, axis, stride)], axis=0)
+    return [block, swap(block, axis, strides[-1])]
+
+
+def gather_direct(block, axis):
+    offsets = offsets_of(axis)
+    held = [block] + [swap(block, axis, o) for o in offsets[1 : len(offsets) // 2]]
+    return held + [swap(piece, axis, 1) for piece in held]
+
+
+def exchange(blocks, axis):
+    blocks = list(blocks)
+    for stride in strides_of(axis)[::-1]:
+        marked = [i for i in range(len(blocks)) if i & stride]
+        arrived = swap(jnp.stack([blocks[i] for i in marked]), axis, stride)
+        for place, i in enumerate(marked):
+            blocks[i] = arrived[place]
+    return blocks
 
 
 def shards(
@@ -94,62 +237,107 @@
     bank_row,
 ):
     wide_count = lax.axis_size("wide")
+    narrow_count = lax.axis_size("narrow")
+    me_wide = lax.axis_index("wide")
+    me_narrow = lax.axis_index("narrow")
     model_width = hidden_in.shape[1] * wide_count
+    own_rows = hidden_in.shape[0]
     local_rows = cache_len.shape[0]
     all_rows = bank_row.shape[0]
-    served_by = (
-        jnp.zeros((all_rows,), jnp.int32).at[bank_row].set(jnp.arange(all_rows, dtype=jnp.int32))
-    )
+    wide_rows = all_rows // wide_count
+
+    position = jnp.arange(all_rows, dtype=jnp.int32)
+
+    def devices(axis, me):
+        offsets = jnp.array(offsets_of(axis), jnp.int32)
+        return jnp.repeat(me ^ offsets, all_rows // len(offsets_of(axis)))
+
+    hypothesis = devices("narrow", me_narrow) * own_rows + position % own_rows
+    inner = position % wide_rows
+    wide_block = devices("wide", me_wide)
+    bank = (wide_block * narrow_count + (me_narrow ^ (inner // local_rows))) * local_rows
+    bank = bank + inner % local_rows
+    hypothesis_bank = bank_row[hypothesis]
+    to_bank = one_hot(bank, hypothesis_bank)
+    to_hypothesis = one_hot(hypothesis_bank, bank)
+    to_wide = one_hot(wide_block * wide_rows + inner, position)
+    from_wide = one_hot(position, wide_block * wide_rows + inner)
+
+    def wide_sum(rows_sq):
+        for stride in strides_of("wide"):
+            arrived = swap(rows_sq, "wide", stride)
+            rows_sq = rows_sq + stand_in(rows_sq, STAND_IN) + arrived
+        return rows_sq
+
     rows_in = hidden_in.astype(jnp.float32)
-    first_sq = lax.psum(jnp.sum(rows_in * rows_in, axis=1), "wide")
-    normed = normalize(hidden_in, attn_gain, first_sq, model_width)
-    gathered = lax.all_gather(normed, "narrow", axis=0, tiled=True)
+    first_sq = wide_sum(jnp.sum(rows_in * rows_in, axis=1))
+    normed = gather(normalize(hidden_in, attn_gain, first_sq, model_width), "narrow")
+
     q_cols = w_query.shape[1]
     k_cols = w_key.shape[1]
-    in_bank = gathered[served_by]
-    row_block = in_bank
-    summed = lax.psum_scatter(
-        jnp.concatenate(
-            [product(row_block, w_query), product(row_block, w_key), product(row_block, w_value)],
-            axis=1,
-        ),
-        "wide",
-        scatter_dimension=0,
-        tiled=True,
-    ).astype(jnp.bfloat16)
-    qkv_parts = (
-        summed[:, :q_cols],
-        summed[:, q_cols : q_cols + k_cols],
-        summed[:, q_cols + k_cols :],
-    )
-    queries, key_new, value_new = (
-        lax.all_to_all(qkv_parts[0], "narrow", split_axis=0, concat_axis=1, tiled=True),
-        lax.all_to_all(qkv_parts[1], "narrow", split_axis=0, concat_axis=1, tiled=True),
-        lax.all_to_all(qkv_parts[2], "narrow", split_axis=0, concat_axis=1, tiled=True),
-    )
-    query_rot = rotate(queries.reshape(local_rows, -1, HEAD_DIM), cache_len).reshape(local_rows, -1)
-    key_rot = rotate(key_new.reshape(local_rows, -1, HEAD_DIM), cache_len).reshape(local_rows, -1)
+    chunk_cols = (q_cols + 2 * k_cols) // QKV_CHUNKS
+    pieces = []
+    for chunk in range(QKV_CHUNKS):
+        if chunk < QKV_CHUNKS - 1:
+            segments = [(w_query, 0, chunk * chunk_cols, chunk_cols)]
+        else:
+            segments = [(w_query, 0, chunk * chunk_cols, q_cols - chunk * chunk_cols)]
+            segments += [(w_key, 0, 0, k_cols), (w_value, 0, 0, k_cols)]
+        pieces.append(wide_scatter(*project(normed, to_bank, segments, 2, 24), jnp.float32))
+    summed = jnp.concatenate(pieces, axis=1).astype(jnp.bfloat16)
+    summed = summed.reshape(narrow_count, local_rows, -1, HEAD_DIM)
+    turned = exchange([summed[j] for j in range(narrow_count)], "narrow")
+    ranks = me_narrow ^ jnp.arange(narrow_count, dtype=jnp.int32)
+    turned = jnp.stack(turned)[ranks].transpose(1, 0, 2, 3)
+    q_heads = q_cols // HEAD_DIM
+    k_heads = k_cols // HEAD_DIM
+    query_rot = rotate(
+        turned[:, :, :q_heads].reshape(local_rows, -1, HEAD_DIM), cache_len
+    ).reshape(local_rows, -1)
+    key_rot = rotate(
+        turned[:, :, q_heads : q_heads + k_heads].reshape(local_rows, -1, HEAD_DIM), cache_len
+    ).reshape(local_rows, -1)
+    value_new = turned[:, :, q_heads + k_heads :].reshape(local_rows, -1)
     context = attend(query_rot, key_rot, value_new, key_cache, value_cache, cache_len)
-    by_heads = lax.all_to_all(context, "narrow", split_axis=1, concat_axis=0, tiled=True)
-    every_row = lax.all_gather(by_heads, "wide", axis=0, tiled=True)
-    in_hypothesis = every_row[bank_row]
-    row_block = in_hypothesis
-    attn_out = lax.psum_scatter(
-        product(row_block, w_out), "narrow", scatter_dimension=0, tiled=True
-    )
+    context = context.reshape(local_rows, narrow_count, -1).transpose(1, 0, 2)[ranks]
+    by_heads = exchange([context[j] for j in range(narrow_count)], "narrow")
+
+    depth = w_out.shape[0] // CONTEXT_CHUNKS
+    total = None
+    for chunk in range(CONTEXT_CHUNKS):
+        columns = slice(chunk * depth, (chunk + 1) * depth)
+        block = jnp.concatenate([piece[:, columns] for piece in by_heads], axis=0)
+        last = chunk == CONTEXT_CHUNKS - 1
+        total = project(
+            gather_direct(block, "wide"),
+            to_hypothesis,
+            [(w_out, chunk * depth, 0, w_out.shape[1])],
+            2 if last else 1,
+            24,
+            total if total is None else total[0],
+        )
+    attn_out = narrow_scatter(*total)
     resid = (rows_in + attn_out).astype(jnp.bfloat16)
     resid_wide = resid.astype(jnp.float32)
-    second_sq = lax.psum(jnp.sum(resid_wide * resid_wide, axis=1), "wide")
-    normed_two = normalize(resid, ffn_gain, second_sq, model_width)
-    gathered_two = lax.all_gather(normed_two, "narrow", axis=0, tiled=True)
-    gate_sum, up_sum = lax.psum(
-        (product(gathered_two, w_gate), product(gathered_two, w_up)), "wide"
-    )
-    hidden_act = (jax.nn.silu(gate_sum) * up_sum).astype(jnp.bfloat16)
-    row_block = hidden_act
-    ffn_out = lax.psum_scatter(
-        product(row_block, w_down), "narrow", scatter_dimension=0, tiled=True
-    )
+    second_sq = wide_sum(jnp.sum(resid_wide * resid_wide, axis=1))
+    normed_two = gather(normalize(resid, ffn_gain, second_sq, model_width), "narrow")
+
+    f_cols = w_gate.shape[1] // FFN_CHUNKS
+    total = None
+    for chunk in range(FFN_CHUNKS):
+        segments = [(w_gate, 0, chunk * f_cols, f_cols), (w_up, 0, chunk * f_cols, f_cols)]
+        sums = wide_scatter(*project(normed_two, to_wide, segments, 2, 24), jnp.float16)
+        act = (jax.nn.silu(sums[:, :f_cols]) * sums[:, f_cols:]).astype(jnp.bfloat16)
+        last = chunk == FFN_CHUNKS - 1
+        total = project(
+            gather(act, "wide"),
+            from_wide,
+            [(w_down, chunk * f_cols, 0, w_down.shape[1])],
+            2 if last else 1,
+            24,
+            total if total is None else total[0],
+        )
+    ffn_out = narrow_scatter(*total)
     return (resid_wide + ffn_out).astype(jnp.bfloat16)
 
 

time: 410 us -> 220 us (0.54)
  waiting for transfers between devices: 262 us -> 79.9 us
  starting transfers between devices: 10.2 us -> 78 us
  blocking collectives: 65.2 us -> 0 us
  matrix products: 40.7 us -> 5.17 us
  local copies, waits for them, and re-layouts: 8.59 us -> 33.6 us
  between operations: 13.4 us -> 0.87 us
  Pallas kernels: 0 us -> 10.9 us
    reduce_scatter x3 -> x0, waiting for transfers between devices: 114 us -> none  [the longest x1 65.7 us: shards(): lax.psum_scatter(jnp.concatenate([product(row_block, w_query), product(ro...]
    psum x1 -> x0, waiting for transfers between devices: 99.3 us -> none  [shards(): lax.psum((product(gathered_two, w_gate), product(gathered_two, w_up)), 'w...]
    ppermute x0 -> x58, waiting for transfers between devices: none -> 79.9 us  [swap(): return lax.ppermute(block, axis, [(i, i ^ offset) for i in range(count)])]
    ppermute x0 -> x58, starting transfers between devices: none -> 78 us  [swap(): return lax.ppermute(block, axis, [(i, i ^ offset) for i in range(count)])]
    psum x2 -> x0, blocking collectives: 44.5 us -> none  [the longest x1 23.1 us: shards(): first_sq = lax.psum(jnp.sum(rows_in * rows_in, axis=1), 'wide')]
    all_gather x1 -> x0, waiting for transfers between devices: 38.2 us -> none  [shards(): every_row = lax.all_gather(by_heads, 'wide', axis=0, tiled=True)]
    dot_general x7 -> x0, matrix products: 35.6 us -> none  [product(): return jnp.dot(left, right, preferred_element_type=jnp.float32)]
    unnamed x14 -> x36, local copies, waits for them, and re-layouts: 0.04 us -> 24.1 us
  transfers between devices with their start and end apart: 8 -> 58, of which waited for: 8 -> 35; matrix products, arithmetic and copies ran while one was open for 0% -> 5% of each run, Pallas kernels for 0% -> 3%
where the time goes in v2:
time: 220 us
  waiting for transfers between devices  79.9 us (36%)
  starting transfers between devices  78 us (35%)
  local copies, waits for them, and re-layouts  33.6 us (15%)
  other arithmetic  11.4 us (5%)
  Pallas kernels  10.9 us (5%)
  matrix products  5.17 us (2%)
    ppermute x58, waiting for transfers between devices, swap(): return lax.ppermute(block, axis, [(i, i ^ offset) for i in range(count)])  79.9 us
    ppermute x58, starting transfers between devices, swap(): return lax.ppermute(block, axis, [(i, i ^ offset) for i in range(count)])  78 us
    unnamed x36, local copies, waits for them, and re-layouts  24.1 us
    pallas_call x9, Pallas kernels, project(): pl.pallas_call(body, in_specs=specs, out_specs=[in_vmem] * split, out_sha...  10.9 us
    slice x11, local copies, waits for them, and re-layouts, stand_in(): return zero[0, 0]  5.74 us
  transfers between devices with their start and end apart: 58, of which 35 were waited for; matrix products, arithmetic and copies ran while one was open for 5% of the time, Pallas kernels for 3%

profile of v2, /device:TPU:0, one launch (start us, length us, event | category | flops | bytes accessed | tf_op | source)
XLA Modules:
  0.0 219.8 jit_solution(7298834857700732513)
XLA Ops:
  1.1 3.0 %collective-permute-start = (f32[32]{0:T(128)S(1)}, f32[32]{0:T(128)S(1)}, u32[]{:S(2)}, u32[]{:S(2)}) collective-permute-start(f32[32]{0:T(128)S(1)} %fusion.25.after_ref), channel_id=1, source_target_pairs={{0,4},{4,0},{8,12},{12,8},{16,20},{20,16},{24,28},{28,24},{1,5},{5... | collective-permute-start | bytes 392 | tf_op jit(solution)/shard_map/ppermute | solution.py:93
  10.7 3.1 %collective-permute-start.2 = (f32[32]{0:T(128)S(1)}, f32[32]{0:T(128)S(1)}, u32[]{:S(2)}, u32[]{:S(2)}) collective-permute-start(f32[32]{0:T(128)S(1)} %add_add_fusion.2.after_ref), channel_id=1, source_target_pairs={{0,16},{4,20},{8,24},{12,28},{16,0},{20,4},{24,8},{28,12},{1,17},{... | collective-permute-start | bytes 392 | tf_op jit(solution)/shard_map/ppermute | solution.py:93
  18.0 3.1 %collective-permute-done.3 = bf16[32,2048]{1,0:T(8,128)(2,1)S(1)} collective-permute-done((bf16[32,2048]{1,0:T(8,128)(2,1)S(1)}, bf16[32,2048]{1,0:T(8,128)(2,1)S(1)}, u32[]{:S(2)}, u32[]{:S(2)}) %collective-permute-start.3) | collective-permute-done | bytes 131104 | tf_op jit(solution)/shard_map/ppermute | solution.py:93
  22.7 5.8 %copy-done.2 = bf16[2048,4096]{1,0:T(8,128)(2,1)S(1)} copy-done((bf16[2048,4096]{1,0:T(8,128)(2,1)S(1)}, bf16[2048,4096]{1,0:T(8,128)(2,1)}, u32[]{:S(2)}) %copy-start.2) | copy-done | bytes 16777240
  36.1 5.5 %collective-permute-done.13 = f32[64,1536]{1,0:T(8,128)S(1)} collective-permute-done((f32[64,1536]{1,0:T(8,128)S(1)}, f32[64,1536]{1,0:T(8,128)S(1)}, u32[]{:S(2)}, u32[]{:S(2)}) %collective-permute-start.13) | collective-permute-done | bytes 393248 | tf_op jit(solution)/shard_map/ppermute | solution.py:93
  41.7 4.0 %collective-permute-start.16 = (f32[16,1536]{1,0:T(8,128)S(1)}, f32[16,1536]{1,0:T(8,128)S(1)}, u32[]{:S(2)}, u32[]{:S(2)}) collective-permute-start(f32[16,1536]{1,0:T(8,128)S(1)} %get-tuple-element.46), channel_id=1, source_target_pairs={{0,24},{4,28},{8,16},{12,20},{16,8},{20,12},{24,0},{28,4},{1,25},{... | collective-permute-start | bytes 294920 | tf_op jit(solution)/shard_map/ppermute | solution.py:93
  46.4 3.7 %collective-permute-done.9 = f32[64,1536]{1,0:T(8,128)S(1)} collective-permute-done((f32[64,1536]{1,0:T(8,128)S(1)}, f32[64,1536]{1,0:T(8,128)S(1)}, u32[]{:S(2)}, u32[]{:S(2)}) %collective-permute-start.9) | collective-permute-done | bytes 393248 | tf_op jit(solution)/shard_map/ppermute | solution.py:93
  50.1 7.9 %collective-permute-done.5 = f32[64,1536]{1,0:T(8,128)S(1)} collective-permute-done((f32[64,1536]{1,0:T(8,128)S(1)}, f32[64,1536]{1,0:T(8,128)S(1)}, u32[]{:S(2)}, u32[]{:S(2)}) %collective-permute-start.5) | collective-permute-done | bytes 393248 | tf_op jit(solution)/shard_map/ppermute | solution.py:93
  58.6 3.8 %collective-permute-start.12 = (f32[16,1536]{1,0:T(8,128)S(1)}, f32[16,1536]{1,0:T(8,128)S(1)}, u32[]{:S(2)}, u32[]{:S(2)}) collective-permute-start(f32[16,1536]{1,0:T(8,128)S(1)} %get-tuple-element.43), channel_id=1, source_target_pairs={{0,24},{4,28},{8,16},{12,20},{16,8},{20,12},{24,0},{28,4},{1,25},{... | collective-permute-start | bytes 294920 | tf_op jit(solution)/shard_map/ppermute | solution.py:93
  64.1 3.8 %collective-permute-start.8 = (f32[16,1536]{1,0:T(8,128)S(1)}, f32[16,1536]{1,0:T(8,128)S(1)}, u32[]{:S(2)}, u32[]{:S(2)}) collective-permute-start(f32[16,1536]{1,0:T(8,128)S(1)} %get-tuple-element.40), channel_id=1, source_target_pairs={{0,24},{4,28},{8,16},{12,20},{16,8},{20,12},{24,0},{28,4},{1,25},{... | collective-permute-start | bytes 294920 | tf_op jit(solution)/shard_map/ppermute | solution.py:93
  69.3 6.7 %collective-permute-done.10 = f32[16,1536]{1,0:T(8,128)S(1)} collective-permute-done((f32[16,1536]{1,0:T(8,128)S(1)}, f32[16,1536]{1,0:T(8,128)S(1)}, u32[]{:S(2)}, u32[]{:S(2)}) %collective-permute-start.10) | collective-permute-done | bytes 98336 | tf_op jit(solution)/shard_map/ppermute | solution.py:93
  81.2 2.8 %collective-permute-done.17 = bf16[2,4,36,128]{3,1,2,0:T(4,128)(2,1)S(1)} collective-permute-done((bf16[2,4,36,128]{3,1,2,0:T(4,128)(2,1)S(1)}, bf16[2,4,36,128]{3,1,2,0:T(4,128)(2,1)S(1)}, u32[]{:S(2)}, u32[]{:S(2)}) %collective-permute-start.17) | collective-permute-done | bytes 73760 | tf_op jit(solution)/shard_map/ppermute | solution.py:93
  87.1 3.9 %fusion.84 = (f32[4,8,16]{2,1,0:T(8,128)S(1)}, f32[4,8,16,512]{3,2,1,0:T(8,128)S(1)}) fusion(bf16[4,8,16,64]{3,2,1,0:T(8,128)(2,1)S(1)} %bitcast.80, bf16[4,8,16,64]{3,2,1,0:T(8,128)(2,1)S(1)} %bitcast.78, pred[4,512]{1,0:T(4,128)(4,1)S(1)} %iota_compare_fusion.2, bf16[4,512,1024]{2,1,0:T(8,128)(2,1)} %param.26), kind=kOutput, calls=%fused_computation.164 | convolution fusion | flops 68156928 | bytes 5378048 | tf_op jit(solution)/shard_map/rgqd,rlgd->rgql/dot_general | solution.py:59
  99.6 3.0 %collective-permute-start.22 = (bf16[16,2048]{1,0:T(8,128)(2,1)S(1)}, bf16[16,2048]{1,0:T(8,128)(2,1)S(1)}, u32[]{:S(2)}, u32[]{:S(2)}) collective-permute-start(bf16[16,2048]{1,0:T(8,128)(2,1)S(1)} %pad_maximum_fusion.10.refs_0_), channel_id=1, source_target_pairs={{0,8},{4,12},{8,0},{12,4},{16,24},{20,28},{24,16},{28,20},{1,9},{5... | collective-permute-start | bytes 196616 | tf_op jit(solution)/shard_map/ppermute | solution.py:93
  104.3 2.8 %collective-permute-start.30 = (bf16[16,2048]{1,0:T(8,128)(2,1)S(1)}, bf16[16,2048]{1,0:T(8,128)(2,1)S(1)}, u32[]{:S(2)}, u32[]{:S(2)}) collective-permute-start(bf16[16,2048]{1,0:T(8,128)(2,1)S(1)} %pad_maximum_fusion.11.refs_0_), channel_id=1, source_target_pairs={{0,24},{4,28},{8,16},{12,20},{16,8},{20,12},{24,0},{28,4},{1,25},{... | collective-permute-start | bytes 196616 | tf_op jit(solution)/shard_map/ppermute | solution.py:93
  117.5 5.8 %copy-done.3 = bf16[4096,2048]{1,0:T(8,128)(2,1)S(1)} copy-done((bf16[4096,2048]{1,0:T(8,128)(2,1)S(1)}, bf16[4096,2048]{1,0:T(8,128)(2,1)}, u32[]{:S(2)}) %copy-start.3) | copy-done | bytes 16777240
  124.8 5.8 %copy-done.4 = bf16[4096,2048]{1,0:T(8,128)(2,1)S(1)} copy-done((bf16[4096,2048]{1,0:T(8,128)(2,1)S(1)}, bf16[4096,2048]{1,0:T(8,128)(2,1)}, u32[]{:S(2)}) %copy-start.4) | copy-done | bytes 16777240
  135.8 4.1 %collective-permute-done.36 = bf16[32,2048]{1,0:T(8,128)(2,1)S(1)} collective-permute-done((bf16[32,2048]{1,0:T(8,128)(2,1)S(1)}, bf16[32,2048]{1,0:T(8,128)(2,1)S(1)}, u32[]{:S(2)}, u32[]{:S(2)}) %collective-permute-start.36) | collective-permute-done | bytes 131104 | tf_op jit(solution)/shard_map/ppermute | solution.py:93
  155.5 3.4 %collective-permute-done.40 = bf16[32,2048]{1,0:T(8,128)(2,1)S(1)} collective-permute-done((bf16[32,2048]{1,0:T(8,128)(2,1)S(1)}, bf16[32,2048]{1,0:T(8,128)(2,1)S(1)}, u32[]{:S(2)}, u32[]{:S(2)}) %collective-permute-start.40) | collective-permute-done | bytes 131104 | tf_op jit(solution)/shard_map/ppermute | solution.py:93
  160.5 3.4 %copy-done.5 = bf16[2048,2048]{1,0:T(8,128)(2,1)S(1)} copy-done((bf16[2048,2048]{1,0:T(8,128)(2,1)S(1)}, bf16[2048,2048]{1,0:T(8,128)(2,1)}, u32[]{:S(2)}) %copy-start.5) | copy-done | bytes 8388632
  163.9 3.4 %copy-done.6 = bf16[2048,2048]{1,0:T(8,128)(2,1)S(1)} copy-done((bf16[2048,2048]{1,0:T(8,128)(2,1)S(1)}, bf16[2048,2048]{1,0:T(8,128)(2,1)}, u32[]{:S(2)}) %copy-start.6) | copy-done | bytes 8388632
  172.3 5.6 %collective-permute-done.42 = f16[64,2048]{1,0:T(8,128)(2,1)S(1)} collective-permute-done((f16[64,2048]{1,0:T(8,128)(2,1)S(1)}, f16[64,2048]{1,0:T(8,128)(2,1)S(1)}, u32[]{:S(2)}, u32[]{:S(2)}) %collective-permute-start.42) | collective-permute-done | bytes 262176 | tf_op jit(solution)/shard_map/ppermute | solution.py:93
  178.0 2.8 %collective-permute-start.45 = (f16[16,2048]{1,0:T(8,128)(2,1)S(1)}, f16[16,2048]{1,0:T(8,128)(2,1)S(1)}, u32[]{:S(2)}, u32[]{:S(2)}) collective-permute-start(f16[16,2048]{1,0:T(8,128)(2,1)S(1)} %get-tuple-element.52), channel_id=1, source_target_pairs={{0,24},{4,28},{8,16},{12,20},{16,8},{20,12},{24,0},{28,4},{1,25},{... | collective-permute-start | bytes 196616 | tf_op jit(solution)/shard_map/ppermute | solution.py:93
  215.0 4.1 %collective-permute-done.57 = bf16[32,2048]{1,0:T(8,128)(2,1)S(1)} collective-permute-done((bf16[32,2048]{1,0:T(8,128)(2,1)S(1)}, bf16[32,2048]{1,0:T(8,128)(2,1)S(1)}, u32[]{:S(2)}, u32[]{:S(2)}) %collective-permute-start.57) | collective-permute-done | bytes 131104 | tf_op jit(solution)/shard_map/ppermute | solution.py:93
  (256 shorter events, 117.7 us)
Async XLA Ops:
  29.6 12.0 %collective-permute-start.13 = (f32[64,1536]{1,0:T(8,128)S(1)}, f32[64,1536]{1,0:T(8,128)S(1)}, u32[]{:S(2)}, u32[]{:S(2)}) collective-permute-start(f32[64,1536]{1,0:T(8,128)S(1)} %get-tuple-element.24), channel_id=1, source_target_pairs={{0,4},{4,0},{8,12},{12,8},{16,20},{20,16},{24,28},{28,24},{1,5},{5... | collective-permute-start | bytes 1179656 | tf_op jit(solution)/shard_map/ppermute | solution.py:93
  32.8 17.2 %collective-permute-start.9 = (f32[64,1536]{1,0:T(8,128)S(1)}, f32[64,1536]{1,0:T(8,128)S(1)}, u32[]{:S(2)}, u32[]{:S(2)}) collective-permute-start(f32[64,1536]{1,0:T(8,128)S(1)} %get-tuple-element.22), channel_id=1, source_target_pairs={{0,4},{4,0},{8,12},{12,8},{16,20},{20,16},{24,28},{28,24},{1,5},{5... | collective-permute-start | bytes 1179656 | tf_op jit(solution)/shard_map/ppermute | solution.py:93
  34.2 23.8 %collective-permute-start.5 = (f32[64,1536]{1,0:T(8,128)S(1)}, f32[64,1536]{1,0:T(8,128)S(1)}, u32[]{:S(2)}, u32[]{:S(2)}) collective-permute-start(f32[64,1536]{1,0:T(8,128)S(1)} %get-tuple-element.20), channel_id=1, source_target_pairs={{0,4},{4,0},{8,12},{12,8},{16,20},{20,16},{24,28},{28,24},{1,5},{5... | collective-permute-start | bytes 1179656 | tf_op jit(solution)/shard_map/ppermute | solution.py:93
  41.7 21.8 %collective-permute-start.16 = (f32[16,1536]{1,0:T(8,128)S(1)}, f32[16,1536]{1,0:T(8,128)S(1)}, u32[]{:S(2)}, u32[]{:S(2)}) collective-permute-start(f32[16,1536]{1,0:T(8,128)S(1)} %get-tuple-element.46), channel_id=1, source_target_pairs={{0,24},{4,28},{8,16},{12,20},{16,8},{20,12},{24,0},{28,4},{1,25},{... | collective-permute-start | bytes 294920 | tf_op jit(solution)/shard_map/ppermute | solution.py:93
  45.7 18.4 %collective-permute-start.15 = (f32[16,1536]{1,0:T(8,128)S(1)}, f32[16,1536]{1,0:T(8,128)S(1)}, u32[]{:S(2)}, u32[]{:S(2)}) collective-permute-start(f32[16,1536]{1,0:T(8,128)S(1)} %get-tuple-element.47), channel_id=1, source_target_pairs={{0,8},{4,12},{8,0},{12,4},{16,24},{20,28},{24,16},{28,20},{1,9},{5... | collective-permute-start | bytes 294920 | tf_op jit(solution)/shard_map/ppermute | solution.py:93
  45.7 22.2 %collective-permute-start.14 = (f32[16,1536]{1,0:T(8,128)S(1)}, f32[16,1536]{1,0:T(8,128)S(1)}, u32[]{:S(2)}, u32[]{:S(2)}) collective-permute-start(f32[16,1536]{1,0:T(8,128)S(1)} %get-tuple-element.45), channel_id=1, source_target_pairs={{0,16},{4,20},{8,24},{12,28},{16,0},{20,4},{24,8},{28,12},{1,17},{... | collective-permute-start | bytes 294920 | tf_op jit(solution)/shard_map/ppermute | solution.py:93
  58.6 10.0 %collective-permute-start.12 = (f32[16,1536]{1,0:T(8,128)S(1)}, f32[16,1536]{1,0:T(8,128)S(1)}, u32[]{:S(2)}, u32[]{:S(2)}) collective-permute-start(f32[16,1536]{1,0:T(8,128)S(1)} %get-tuple-element.43), channel_id=1, source_target_pairs={{0,24},{4,28},{8,16},{12,20},{16,8},{20,12},{24,0},{28,4},{1,25},{... | collective-permute-start | bytes 294920 | tf_op jit(solution)/shard_map/ppermute | solution.py:93
  63.5 12.5 %collective-permute-start.10 = (f32[16,1536]{1,0:T(8,128)S(1)}, f32[16,1536]{1,0:T(8,128)S(1)}, u32[]{:S(2)}, u32[]{:S(2)}) collective-permute-start(f32[16,1536]{1,0:T(8,128)S(1)} %get-tuple-element.42), channel_id=1, source_target_pairs={{0,16},{4,20},{8,24},{12,28},{16,0},{20,4},{24,8},{28,12},{1,17},{... | collective-permute-start | bytes 294920 | tf_op jit(solution)/shard_map/ppermute | solution.py:93
  64.1 12.6 %collective-permute-start.8 = (f32[16,1536]{1,0:T(8,128)S(1)}, f32[16,1536]{1,0:T(8,128)S(1)}, u32[]{:S(2)}, u32[]{:S(2)}) collective-permute-start(f32[16,1536]{1,0:T(8,128)S(1)} %get-tuple-element.40), channel_id=1, source_target_pairs={{0,24},{4,28},{8,16},{12,20},{16,8},{20,12},{24,0},{28,4},{1,25},{... | collective-permute-start | bytes 294920 | tf_op jit(solution)/shard_map/ppermute | solution.py:93
  67.9 8.8 %collective-permute-start.7 = (f32[16,1536]{1,0:T(8,128)S(1)}, f32[16,1536]{1,0:T(8,128)S(1)}, u32[]{:S(2)}, u32[]{:S(2)}) collective-permute-start(f32[16,1536]{1,0:T(8,128)S(1)} %get-tuple-element.41), channel_id=1, source_target_pairs={{0,8},{4,12},{8,0},{12,4},{16,24},{20,28},{24,16},{28,20},{1,9},{5... | collective-permute-start | bytes 294920 | tf_op jit(solution)/shard_map/ppermute | solution.py:93
  68.6 10.3 %collective-permute-start.6 = (f32[16,1536]{1,0:T(8,128)S(1)}, f32[16,1536]{1,0:T(8,128)S(1)}, u32[]{:S(2)}, u32[]{:S(2)}) collective-permute-start(f32[16,1536]{1,0:T(8,128)S(1)} %get-tuple-element.39), channel_id=1, source_target_pairs={{0,16},{4,20},{8,24},{12,28},{16,0},{20,4},{24,8},{28,12},{1,17},{... | collective-permute-start | bytes 294920 | tf_op jit(solution)/shard_map/ppermute | solution.py:93
  99.1 7.9 %collective-permute-start.21 = (bf16[16,2048]{1,0:T(8,128)(2,1)S(1)}, bf16[16,2048]{1,0:T(8,128)(2,1)S(1)}, u32[]{:S(2)}, u32[]{:S(2)}) collective-permute-start(bf16[16,2048]{1,0:T(8,128)(2,1)S(1)} %pad_maximum_fusion.10.refs_0_), channel_id=1, source_target_pairs={{0,16},{4,20},{8,24},{12,28},{16,0},{20,4},{24,8},{28,12},{1,17},{... | collective-permute-start | bytes 196616 | tf_op jit(solution)/shard_map/ppermute | solution.py:93
  99.6 8.5 %collective-permute-start.22 = (bf16[16,2048]{1,0:T(8,128)(2,1)S(1)}, bf16[16,2048]{1,0:T(8,128)(2,1)S(1)}, u32[]{:S(2)}, u32[]{:S(2)}) collective-permute-start(bf16[16,2048]{1,0:T(8,128)(2,1)S(1)} %pad_maximum_fusion.10.refs_0_), channel_id=1, source_target_pairs={{0,8},{4,12},{8,0},{12,4},{16,24},{20,28},{24,16},{28,20},{1,9},{5... | collective-permute-start | bytes 196616 | tf_op jit(solution)/shard_map/ppermute | solution.py:93
  102.7 8.3 %collective-permute-start.29 = (bf16[16,2048]{1,0:T(8,128)(2,1)S(1)}, bf16[16,2048]{1,0:T(8,128)(2,1)S(1)}, u32[]{:S(2)}, u32[]{:S(2)}) collective-permute-start(bf16[16,2048]{1,0:T(8,128)(2,1)S(1)} %pad_maximum_fusion.11.refs_0_), channel_id=1, source_target_pairs={{0,8},{4,12},{8,0},{12,4},{16,24},{20,28},{24,16},{28,20},{1,9},{5... | collective-permute-start | bytes 196616 | tf_op jit(solution)/shard_map/ppermute | solution.py:93
  104.3 7.4 %collective-permute-start.30 = (bf16[16,2048]{1,0:T(8,128)(2,1)S(1)}, bf16[16,2048]{1,0:T(8,128)(2,1)S(1)}, u32[]{:S(2)}, u32[]{:S(2)}) collective-permute-start(bf16[16,2048]{1,0:T(8,128)(2,1)S(1)} %pad_maximum_fusion.11.refs_0_), channel_id=1, source_target_pairs={{0,24},{4,28},{8,16},{12,20},{16,8},{20,12},{24,0},{28,4},{1,25},{... | collective-permute-start | bytes 196616 | tf_op jit(solution)/shard_map/ppermute | solution.py:93
  113.2 11.5 %collective-permute-start.24 = (bf16[16,2048]{1,0:T(8,128)(2,1)S(1)}, bf16[16,2048]{1,0:T(8,128)(2,1)S(1)}, u32[]{:S(2)}, u32[]{:S(2)}) collective-permute-start(bf16[16,2048]{1,0:T(8,128)(2,1)S(1)} %pad_maximum_fusion.10.refs_0_), channel_id=1, source_target_pairs={{0,4},{4,0},{8,12},{12,8},{16,20},{20,16},{24,28},{28,24},{1,5},{5... | collective-permute-start | bytes 196616 | tf_op jit(solution)/shard_map/ppermute | solution.py:93
  114.8 10.0 %collective-permute-start.25 = (bf16[16,2048]{1,0:T(8,128)(2,1)S(1)}, bf16[16,2048]{1,0:T(8,128)(2,1)S(1)}, u32[]{:S(2)}, u32[]{:S(2)}) collective-permute-start(bf16[16,2048]{1,0:T(8,128)(2,1)S(1)} %collective-permute-done.21.refs_1_), channel_id=1, source_target_pairs={{0,4},{4,0},{8,12},{12,8},{16,20},{20,16},{24,28},{28,24},{1,5},{5... | collective-permute-start | bytes 196616 | tf_op jit(solution)/shard_map/ppermute | solution.py:93
  115.3 9.5 %collective-permute-start.26 = (bf16[16,2048]{1,0:T(8,128)(2,1)S(1)}, bf16[16,2048]{1,0:T(8,128)(2,1)S(1)}, u32[]{:S(2)}, u32[]{:S(2)}) collective-permute-start(bf16[16,2048]{1,0:T(8,128)(2,1)S(1)} %collective-permute-done.22.refs_2_), channel_id=1, source_target_pairs={{0,4},{4,0},{8,12},{12,8},{16,20},{20,16},{24,28},{28,24},{1,5},{5... | collective-permute-start | bytes 196616 | tf_op jit(solution)/shard_map/ppermute | solution.py:93
  116.8 8.0 %collective-permute-start.27 = (bf16[16,2048]{1,0:T(8,128)(2,1)S(1)}, bf16[16,2048]{1,0:T(8,128)(2,1)S(1)}, u32[]{:S(2)}, u32[]{:S(2)}) collective-permute-start(bf16[16,2048]{1,0:T(8,128)(2,1)S(1)} %collective-permute-done.23.refs_3_), channel_id=1, source_target_pairs={{0,4},{4,0},{8,12},{12,8},{16,20},{20,16},{24,28},{28,24},{1,5},{5... | collective-permute-start | bytes 196616 | tf_op jit(solution)/shard_map/ppermute | solution.py:93
  168.7 9.2 %collective-permute-start.42 = (f16[64,2048]{1,0:T(8,128)(2,1)S(1)}, f16[64,2048]{1,0:T(8,128)(2,1)S(1)}, u32[]{:S(2)}, u32[]{:S(2)}) collective-permute-start(f16[64,2048]{1,0:T(8,128)(2,1)S(1)} %convert_element_type.149), channel_id=1, source_target_pairs={{0,4},{4,0},{8,12},{12,8},{16,20},{20,16},{24,28},{28,24},{1,5},{5... | collective-permute-start | bytes 786440 | tf_op jit(solution)/shard_map/ppermute | solution.py:93
  171.6 11.1 %collective-permute-start.49 = (f16[64,2048]{1,0:T(8,128)(2,1)S(1)}, f16[64,2048]{1,0:T(8,128)(2,1)S(1)}, u32[]{:S(2)}, u32[]{:S(2)}) collective-permute-start(f16[64,2048]{1,0:T(8,128)(2,1)S(1)} %convert_element_type.156), channel_id=1, source_target_pairs={{0,4},{4,0},{8,12},{12,8},{16,20},{20,16},{24,28},{28,24},{1,5},{5... | collective-permute-start | bytes 786440 | tf_op jit(solution)/shard_map/ppermute | solution.py:93
  178.0 16.2 %collective-permute-start.45 = (f16[16,2048]{1,0:T(8,128)(2,1)S(1)}, f16[16,2048]{1,0:T(8,128)(2,1)S(1)}, u32[]{:S(2)}, u32[]{:S(2)}) collective-permute-start(f16[16,2048]{1,0:T(8,128)(2,1)S(1)} %get-tuple-element.52), channel_id=1, source_target_pairs={{0,24},{4,28},{8,16},{12,20},{16,8},{20,12},{24,0},{28,4},{1,25},{... | collective-permute-start | bytes 196616 | tf_op jit(solution)/shard_map/ppermute | solution.py:93
  180.8 13.4 %collective-permute-start.44 = (f16[16,2048]{1,0:T(8,128)(2,1)S(1)}, f16[16,2048]{1,0:T(8,128)(2,1)S(1)}, u32[]{:S(2)}, u32[]{:S(2)}) collective-permute-start(f16[16,2048]{1,0:T(8,128)(2,1)S(1)} %get-tuple-element.53), channel_id=1, source_target_pairs={{0,8},{4,12},{8,0},{12,4},{16,24},{20,28},{24,16},{28,20},{1,9},{5... | collective-permute-start | bytes 196616 | tf_op jit(solution)/shard_map/ppermute | solution.py:93
  185.7 7.2 %collective-permute-start.50 = (f16[16,2048]{1,0:T(8,128)(2,1)S(1)}, f16[16,2048]{1,0:T(8,128)(2,1)S(1)}, u32[]{:S(2)}, u32[]{:S(2)}) collective-permute-start(f16[16,2048]{1,0:T(8,128)(2,1)S(1)} %get-tuple-element.48), channel_id=1, source_target_pairs={{0,16},{4,20},{8,24},{12,28},{16,0},{20,4},{24,8},{28,12},{1,17},{... | collective-permute-start | bytes 196616 | tf_op jit(solution)/shard_map/ppermute | solution.py:93
  (52 other events, 315.1 us)

commit v3 on v2

--- a/solution.py
+++ b/solution.py
@@ -84,7 +84,8 @@
 CONTEXT_CHUNKS = 2
 NARROW_KINDS = [jnp.float32] + [jnp.bfloat16] * 8
 TILE = 512
-STAND_IN = 3
+ROOM = 24
+STAND_IN = 4
 MIB = 1024 * 1024
 
 
@@ -105,9 +106,9 @@
     return order
 
 
-def project(pieces, order, segments, split, room, total=None):
+def project(groups, order, turned, segments, split, total=None):
     rows = order.shape[0]
-    depth = pieces[0].shape[1]
+    depth = groups[0][0].shape[1]
     tiles = []
     width = 0
     for index, (_, first_row, first, columns) in enumerate(segments):
@@ -116,7 +117,9 @@
             tiles.append((index, first_row, start, tile, width))
             width += tile
     part = rows // split
+    pieces = [piece for group in groups for piece in group]
     count = len(pieces)
+    each = count // len(groups)
 
     def body(*refs):
         piece_refs, order_ref, rest = refs[:count], refs[count], refs[count + 1 :]
@@ -124,63 +127,69 @@
         if total is not None:
             total_ref, rest = rest[0], rest[1:]
         out_refs = rest[:split]
-        stacked = jnp.concatenate([ref[...] for ref in piece_refs], axis=0)
-        left = jnp.dot(order_ref[...], stacked, preferred_element_type=jnp.float32)
-        left = left.astype(jnp.bfloat16)
+        lefts = []
+        for group in range(len(groups)):
+            group_refs = piece_refs[group * each : (group + 1) * each]
+            left = lax.dot_general(
+                order_ref[...],
+                jnp.concatenate([ref[...] for ref in group_refs], axis=0),
+                (((0 if turned else 1,), (0,)), ((), ())),
+                preferred_element_type=jnp.float32,
+            )
+            lefts.append(left.astype(jnp.bfloat16))
         for index, first_row, start, tile, base in tiles:
-            weight = weight_refs[index][pl.ds(first_row, depth), pl.ds(start, tile)]
-            result = jnp.dot(left, weight, preferred_element_type=jnp.float32)
+            result = None
+            for group, left in enumerate(lefts):
+                weight = weight_refs[index][
+                    pl.ds(first_row + group * depth, depth), pl.ds(start, tile)
+                ]
+                product = jnp.dot(left, weight, preferred_element_type=jnp.float32)
+                result = product if result is None else result + product
             if total is not None:
                 result = result + total_ref[:, base : base + tile]
-            for index, out_ref in enumerate(out_refs):
-                out_ref[:, base : base + tile] = result[index * part : (index + 1) * part]
-
-    operands = list(pieces) + [order] + [segment[0] for segment in segments]
-    in_vmem = pl.BlockSpec(memory_space=pltpu.VMEM)
-    specs = [in_vmem] * (count + 1) + [in_vmem] * len(segments)
+            for place, out_ref in enumerate(out_refs):
+                out_ref[:, base : base + tile] = result[place * part : (place + 1) * part]
+
+    operands = pieces + [order] + [segment[0] for segment in segments]
     if total is not None:
         operands.append(total)
-        specs.append(in_vmem)
+    in_vmem = pl.BlockSpec(memory_space=pltpu.VMEM)
     return pl.pallas_call(
         body,
-        in_specs=specs,
+        in_specs=[in_vmem] * len(operands),
         out_specs=[in_vmem] * split,
         out_shape=[jax.ShapeDtypeStruct((part, width), jnp.float32)] * split,
-        compiler_params=pltpu.CompilerParams(vmem_limit_bytes=room * MIB),
+        compiler_params=pltpu.CompilerParams(vmem_limit_bytes=ROOM * MIB),
         cost_estimate=pl.CostEstimate(
-            flops=2 * rows * depth * (width + rows),
-            bytes_accessed=2 * depth * width + 4 * rows * width,
+            flops=2 * rows * len(groups) * depth * (width + rows),
+            bytes_accessed=2 * len(groups) * depth * width + 4 * rows * width,
             transcendentals=0,
         ),
     )(*operands)
 
 
-def stand_in(after, microseconds):
-    def body(after_ref, zero_ref):
-        zero_ref[...] = jnp.zeros_like(zero_ref)
-
-    zero = pl.pallas_call(
+def stand_in(array):
+    def body(array_ref, copy_ref):
+        copy_ref[...] = array_ref[...]
+
+    in_vmem = pl.BlockSpec(memory_space=pltpu.VMEM)
+    return pl.pallas_call(
         body,
-        in_specs=[pl.BlockSpec(memory_space=pl.ANY)],
-        out_specs=pl.BlockSpec(memory_space=pltpu.VMEM),
-        out_shape=jax.ShapeDtypeStruct((8, 128), jnp.float32),
+        in_specs=[in_vmem],
+        out_specs=in_vmem,
+        out_shape=jax.ShapeDtypeStruct(array.shape, array.dtype),
         compiler_params=pltpu.CompilerParams(vmem_limit_bytes=MIB),
         cost_estimate=pl.CostEstimate(
-            flops=int(1.1e9 * microseconds), bytes_accessed=4096, transcendentals=0
+            flops=int(1.1e9 * STAND_IN), bytes_accessed=4096, transcendentals=0
         ),
-    )(after)
-    return zero[0, 0]
-
-
-def one_hot(left, right):
-    return (left[:, None] == right[None, :]).astype(jnp.bfloat16)
+    )(array)
 
 
 def wide_scatter(kept, sent, kind):
     strides = strides_of("wide")
     rows = 2 * kept.shape[0] // lax.axis_size("wide")
     kept = kept + swap(sent.astype(kind), "wide", strides[0]).astype(jnp.float32)
-    total = kept[:rows] + stand_in(kept, STAND_IN)
+    total = kept[:rows]
     for place, offset in enumerate(offsets_of("wide")[: kept.shape[0] // rows]):
         if offset:
             block = kept[place * rows : (place + 1) * rows].astype(kind)
@@ -207,7 +216,7 @@
 def gather_direct(block, axis):
     offsets = offsets_of(axis)
     held = [block] + [swap(block, axis, o) for o in offsets[1 : len(offsets) // 2]]
-    return held + [swap(piece, axis, 1) for piece in held]
+    return [stand_in(block)] + held[1:] + [swap(piece, axis, 1) for piece in held]
 
 
 def exchange(blocks, axis):
@@ -217,6 +226,15 @@
         arrived = swap(jnp.stack([blocks[i] for i in marked]), axis, stride)
         for place, i in enumerate(marked):
             blocks[i] = arrived[place]
+    return blocks
+
+
+def by_rank(blocks, me):
+    stride = 1
+    while stride < len(blocks):
+        other = (me & stride) != 0
+        blocks = [jnp.where(other, blocks[i ^ stride], block) for i, block in enumerate(blocks)]
+        stride *= 2
     return blocks
 
 
@@ -246,27 +264,36 @@
     all_rows = bank_row.shape[0]
     wide_rows = all_rows // wide_count
 
-    position = jnp.arange(all_rows, dtype=jnp.int32)
-
-    def devices(axis, me):
-        offsets = jnp.array(offsets_of(axis), jnp.int32)
-        return jnp.repeat(me ^ offsets, all_rows // len(offsets_of(axis)))
-
-    hypothesis = devices("narrow", me_narrow) * own_rows + position % own_rows
-    inner = position % wide_rows
-    wide_block = devices("wide", me_wide)
-    bank = (wide_block * narrow_count + (me_narrow ^ (inner // local_rows))) * local_rows
-    bank = bank + inner % local_rows
-    hypothesis_bank = bank_row[hypothesis]
-    to_bank = one_hot(bank, hypothesis_bank)
-    to_hypothesis = one_hot(hypothesis_bank, bank)
-    to_wide = one_hot(wide_block * wide_rows + inner, position)
-    from_wide = one_hot(position, wide_block * wide_rows + inner)
+    def device(block, axis, me):
+        bits = len(strides_of(axis))
+        for bit in range(bits):
+            me = me ^ (((block >> bit) & 1) << (bits - 1 - bit))
+        return me
+
+    def hypothesis(place):
+        return device(place // own_rows, "narrow", me_narrow) * own_rows + place % own_rows
+
+    def wide_row(place):
+        return device(place // wide_rows, "wide", me_wide) * wide_rows + place % wide_rows
+
+    def bank(place):
+        inner = place % wide_rows
+        owner = device(place // wide_rows, "wide", me_wide) * narrow_count
+        owner = owner + (me_narrow ^ (inner // local_rows))
+        return owner * local_rows + inner % local_rows
+
+    down = lax.broadcasted_iota(jnp.int32, (all_rows, all_rows), 0)
+    across = lax.broadcasted_iota(jnp.int32, (all_rows, all_rows), 1)
+    banks = jnp.broadcast_to(bank_row[None, :], (all_rows, all_rows))
+    hypothesis_bank = jnp.sum(
+        jnp.where(hypothesis(down) == across, banks, 0), axis=1, keepdims=True
+    )
+    to_hypothesis = (hypothesis_bank == bank(across)).astype(jnp.bfloat16)
+    to_wide = (wide_row(down) == across).astype(jnp.bfloat16)
 
     def wide_sum(rows_sq):
         for stride in strides_of("wide"):
-            arrived = swap(rows_sq, "wide", stride)
-            rows_sq = rows_sq + stand_in(rows_sq, STAND_IN) + arrived
+            rows_sq = stand_in(rows_sq) + swap(rows_sq, "wide", stride)
         return rows_sq
 
     rows_in = hidden_in.astype(jnp.float32)
@@ -283,12 +310,11 @@
         else:
             segments = [(w_query, 0, chunk * chunk_cols, q_cols - chunk * chunk_cols)]
             segments += [(w_key, 0, 0, k_cols), (w_value, 0, 0, k_cols)]
-        pieces.append(wide_scatter(*project(normed, to_bank, segments, 2, 24), jnp.float32))
+        pieces.append(wide_scatter(*project([normed], to_hypothesis, True, segments, 2), jnp.float32))
     summed = jnp.concatenate(pieces, axis=1).astype(jnp.bfloat16)
     summed = summed.reshape(narrow_count, local_rows, -1, HEAD_DIM)
     turned = exchange([summed[j] for j in range(narrow_count)], "narrow")
-    ranks = me_narrow ^ jnp.arange(narrow_count, dtype=jnp.int32)
-    turned = jnp.stack(turned)[ranks].transpose(1, 0, 2, 3)
+    turned = jnp.stack(by_rank(turned, me_narrow), axis=1)
     q_heads = q_cols // HEAD_DIM
     k_heads = k_cols // HEAD_DIM
     query_rot = rotate(
@@ -299,23 +325,17 @@
     ).reshape(local_rows, -1)
     value_new = turned[:, :, q_heads + k_heads :].reshape(local_rows, -1)
     context = attend(query_rot, key_rot, value_new, key_cache, value_cache, cache_len)
-    context = context.reshape(local_rows, narrow_count, -1).transpose(1, 0, 2)[ranks]
-    by_heads = exchange([context[j] for j in range(narrow_count)], "narrow")
+    context = context.reshape(local_rows, narrow_count, -1)
+    context = by_rank([context[:, j] for j in range(narrow_count)], me_narrow)
+    by_heads = exchange(context, "narrow")
 
     depth = w_out.shape[0] // CONTEXT_CHUNKS
-    total = None
+    groups = []
     for chunk in range(CONTEXT_CHUNKS):
         columns = slice(chunk * depth, (chunk + 1) * depth)
         block = jnp.concatenate([piece[:, columns] for piece in by_heads], axis=0)
-        last = chunk == CONTEXT_CHUNKS - 1
-        total = project(
-            gather_direct(block, "wide"),
-            to_hypothesis,
-            [(w_out, chunk * depth, 0, w_out.shape[1])],
-            2 if last else 1,
-            24,
-            total if total is None else total[0],
-        )
+        groups.append(gather_direct(block, "wide"))
+    total = project(groups, to_hypothesis, False, [(w_out, 0, 0, w_out.shape[1])], 2)
     attn_out = narrow_scatter(*total)
     resid = (rows_in + attn_out).astype(jnp.bfloat16)
     resid_wide = resid.astype(jnp.float32)
@@ -326,15 +346,15 @@
     total = None
     for chunk in range(FFN_CHUNKS):
         segments = [(w_gate, 0, chunk * f_cols, f_cols), (w_up, 0, chunk * f_cols, f_cols)]
-        sums = wide_scatter(*project(normed_two, to_wide, segments, 2, 24), jnp.float16)
+        sums = wide_scatter(*project([normed_two], to_wide, False, segments, 2), jnp.float16)
         act = (jax.nn.silu(sums[:, :f_cols]) * sums[:, f_cols:]).astype(jnp.bfloat16)
         last = chunk == FFN_CHUNKS - 1
         total = project(
-            gather(act, "wide"),
-            from_wide,
+            [gather(act, "wide")],
+            to_wide,
+            True,
             [(w_down, chunk * f_cols, 0, w_down.shape[1])],
             2 if last else 1,
-            24,
             total if total is None else total[0],
         )
     ffn_out = narrow_scatter(*total)

time: 220 us -> 191 us (0.87)
  local copies, waits for them, and re-layouts: 33.6 us -> 6.7 us
  other arithmetic: 11.4 us -> 5.4 us
  waiting for transfers between devices: 79.9 us -> 85.1 us
    unnamed x36 -> x38, local copies, waits for them, and re-layouts: 24.1 us -> 5.86 us
    slice x11 -> x1, local copies, waits for them, and re-layouts: 5.74 us -> 0.24 us  [shards(): context = by_rank([context[:, j] for j in range(narrow_count)], me_narrow)]
    ppermute x58, waiting for transfers between devices: 79.9 us -> 85.1 us  [swap(): return lax.ppermute(block, axis, [(i, i ^ offset) for i in range(count)])]
    gather x4 -> x0, local copies, waits for them, and re-layouts: 2.62 us -> none  [the longest x1 1.23 us: shards(): hypothesis_bank = bank_row[hypothesis]]
    add x6, other arithmetic: 2.61 us -> 0.02 us  [the longest x4 0.01 us: wide_sum(): rows_sq = stand_in(rows_sq) + swap(rows_sq, 'wide', stride)]
    pallas_call x20 -> x16, Pallas kernels: 10.9 us -> 10.7 us  [the longest x8 10.7 us: project(): pl.pallas_call(body, in_specs=[in_vmem] * len(operands), out_specs=[in_vm...]
  transfers between devices with their start and end apart: 58 -> 58, of which waited for: 35 -> 42; matrix products, arithmetic and copies ran while one was open for 5% -> 1% of each run, Pallas kernels for 3% -> 2%
where the time goes in v3:
time: 191 us; the launch traced here: 190 us
  waiting for transfers between devices  85.1 us (45%)
  starting transfers between devices  76.5 us (40%)
  Pallas kernels  10.7 us (6%)
  local copies, waits for them, and re-layouts  6.7 us (4%)
  other arithmetic  5.4 us (3%)
  matrix products  5.16 us (3%)
    ppermute x58, waiting for transfers between devices, swap(): return lax.ppermute(block, axis, [(i, i ^ offset) for i in range(count)])  85.1 us
    ppermute x58, starting transfers between devices, swap(): return lax.ppermute(block, axis, [(i, i ^ offset) for i in range(count)])  76.5 us
    pallas_call x8, Pallas kernels, project(): pl.pallas_call(body, in_specs=[in_vmem] * len(operands), out_specs=[in_vm...  10.7 us
    unnamed x38, local copies, waits for them, and re-layouts  5.86 us
    dot_general x1, matrix products, attend(): jnp.einsum('rgqd,rlgd->rgql', query_heads, cache_keys, preferred_element_...  3.85 us
  transfers between devices with their start and end apart: 58, of which 42 were waited for; matrix products, arithmetic and copies ran while one was open for 1% of the time, Pallas kernels for 2%

profile of v3, /device:TPU:0, one launch (start us, length us, event | category | flops | bytes accessed | tf_op | source)
XLA Modules:
  0.0 190.4 jit_solution(8501895745917605919)
XLA Ops:
  1.0 3.0 %collective-permute-start = (f32[32]{0:T(128)S(1)}, f32[32]{0:T(128)S(1)}, u32[]{:S(2)}, u32[]{:S(2)}) collective-permute-start(f32[32]{0:T(128)S(1)} %fusion.25.array_ref), channel_id=1, source_target_pairs={{0,4},{4,0},{8,12},{12,8},{16,20},{20,16},{24,28},{28,24},{1,5},{5... | collective-permute-start | bytes 392 | tf_op jit(solution)/shard_map/ppermute | solution.py:94
  9.2 3.1 %collective-permute-start.2 = (f32[32]{0:T(128)S(1)}, f32[32]{0:T(128)S(1)}, u32[]{:S(2)}, u32[]{:S(2)}) collective-permute-start(f32[32]{0:T(128)S(1)} %add.164.array_ref), channel_id=1, source_target_pairs={{0,16},{4,20},{8,24},{12,28},{16,0},{20,4},{24,8},{28,12},{1,17},{... | collective-permute-start | bytes 392 | tf_op jit(solution)/shard_map/ppermute | solution.py:94
  16.1 2.9 %collective-permute-done.3 = bf16[32,2048]{1,0:T(8,128)(2,1)S(1)} collective-permute-done((bf16[32,2048]{1,0:T(8,128)(2,1)S(1)}, bf16[32,2048]{1,0:T(8,128)(2,1)S(1)}, u32[]{:S(2)}, u32[]{:S(2)}) %collective-permute-start.3) | collective-permute-done | bytes 131104 | tf_op jit(solution)/shard_map/ppermute | solution.py:94
  20.6 5.8 %copy-done = bf16[2048,4096]{1,0:T(8,128)(2,1)S(1)} copy-done((bf16[2048,4096]{1,0:T(8,128)(2,1)S(1)}, bf16[2048,4096]{1,0:T(8,128)(2,1)}, u32[]{:S(2)}) %copy-start) | copy-done | bytes 16777240
  33.9 5.7 %collective-permute-done.13 = f32[64,1536]{1,0:T(8,128)S(1)} collective-permute-done((f32[64,1536]{1,0:T(8,128)S(1)}, f32[64,1536]{1,0:T(8,128)S(1)}, u32[]{:S(2)}, u32[]{:S(2)}) %collective-permute-start.13) | collective-permute-done | bytes 393248 | tf_op jit(solution)/shard_map/ppermute | solution.py:94
  39.6 3.0 %collective-permute-start.14 = (f32[16,1536]{1,0:T(8,128)S(1)}, f32[16,1536]{1,0:T(8,128)S(1)}, u32[]{:S(2)}, u32[]{:S(2)}) collective-permute-start(f32[16,1536]{1,0:T(8,128)S(1)} %get-tuple-element.51), channel_id=1, source_target_pairs={{0,16},{4,20},{8,24},{12,28},{16,0},{20,4},{24,8},{28,12},{1,17},{... | collective-permute-start | bytes 294920 | tf_op jit(solution)/shard_map/ppermute | solution.py:94
  44.2 3.8 %collective-permute-done.5 = f32[64,1536]{1,0:T(8,128)S(1)} collective-permute-done((f32[64,1536]{1,0:T(8,128)S(1)}, f32[64,1536]{1,0:T(8,128)S(1)}, u32[]{:S(2)}, u32[]{:S(2)}) %collective-permute-start.5) | collective-permute-done | bytes 393248 | tf_op jit(solution)/shard_map/ppermute | solution.py:94
  48.1 3.0 %collective-permute-start.6 = (f32[16,1536]{1,0:T(8,128)S(1)}, f32[16,1536]{1,0:T(8,128)S(1)}, u32[]{:S(2)}, u32[]{:S(2)}) collective-permute-start(f32[16,1536]{1,0:T(8,128)S(1)} %get-tuple-element.45), channel_id=1, source_target_pairs={{0,16},{4,20},{8,24},{12,28},{16,0},{20,4},{24,8},{28,12},{1,17},{... | collective-permute-start | bytes 294920 | tf_op jit(solution)/shard_map/ppermute | solution.py:94
  51.0 4.7 %collective-permute-done.9 = f32[64,1536]{1,0:T(8,128)S(1)} collective-permute-done((f32[64,1536]{1,0:T(8,128)S(1)}, f32[64,1536]{1,0:T(8,128)S(1)}, u32[]{:S(2)}, u32[]{:S(2)}) %collective-permute-start.9) | collective-permute-done | bytes 393248 | tf_op jit(solution)/shard_map/ppermute | solution.py:94
  55.7 3.8 %collective-permute-start.8 = (f32[16,1536]{1,0:T(8,128)S(1)}, f32[16,1536]{1,0:T(8,128)S(1)}, u32[]{:S(2)}, u32[]{:S(2)}) collective-permute-start(f32[16,1536]{1,0:T(8,128)S(1)} %get-tuple-element.46), channel_id=1, source_target_pairs={{0,24},{4,28},{8,16},{12,20},{16,8},{20,12},{24,0},{28,4},{1,25},{... | collective-permute-start | bytes 294920 | tf_op jit(solution)/shard_map/ppermute | solution.py:94
  60.3 3.8 %collective-permute-start.12 = (f32[16,1536]{1,0:T(8,128)S(1)}, f32[16,1536]{1,0:T(8,128)S(1)}, u32[]{:S(2)}, u32[]{:S(2)}) collective-permute-start(f32[16,1536]{1,0:T(8,128)S(1)} %get-tuple-element.49), channel_id=1, source_target_pairs={{0,24},{4,28},{8,16},{12,20},{16,8},{20,12},{24,0},{28,4},{1,25},{... | collective-permute-start | bytes 294920 | tf_op jit(solution)/shard_map/ppermute | solution.py:94
  64.2 2.8 %collective-permute-done.7 = f32[16,1536]{1,0:T(8,128)S(1)} collective-permute-done((f32[16,1536]{1,0:T(8,128)S(1)}, f32[16,1536]{1,0:T(8,128)S(1)}, u32[]{:S(2)}, u32[]{:S(2)}) %collective-permute-start.7) | collective-permute-done | bytes 98336 | tf_op jit(solution)/shard_map/ppermute | solution.py:94
  67.0 3.2 %collective-permute-done.10 = f32[16,1536]{1,0:T(8,128)S(1)} collective-permute-done((f32[16,1536]{1,0:T(8,128)S(1)}, f32[16,1536]{1,0:T(8,128)S(1)}, u32[]{:S(2)}, u32[]{:S(2)}) %collective-permute-start.10) | collective-permute-done | bytes 98336 | tf_op jit(solution)/shard_map/ppermute | solution.py:94
  72.7 2.7 %collective-permute-done.17 = bf16[2,4,36,128]{3,2,1,0:T(8,128)(2,1)S(1)} collective-permute-done((bf16[2,4,36,128]{3,2,1,0:T(8,128)(2,1)S(1)}, bf16[2,4,36,128]{3,2,1,0:T(8,128)(2,1)S(1)}, u32[]{:S(2)}, u32[]{:S(2)}) %collective-permute-start.17) | collective-permute-done | bytes 73760 | tf_op jit(solution)/shard_map/ppermute | solution.py:94
  78.3 3.9 %fusion.114 = (f32[4,8,16]{2,1,0:T(8,128)S(1)}, f32[4,8,16,512]{3,2,1,0:T(8,128)S(1)}) fusion(bf16[4,8,16,64]{3,2,1,0:T(8,128)(2,1)S(1)} %bitcast.70, bf16[4,8,16,64]{3,2,1,0:T(8,128)(2,1)S(1)} %bitcast.68, pred[4,512]{1,0:T(4,128)(4,1)S(1)} %iota_compare_fusion, bf16[4,512,1024]{2,1,0:T(8,128)(2,1)} %param.24), kind=kOutput, calls=%fused_computation.213 | convolution fusion | flops 68156928 | bytes 5378048 | tf_op jit(solution)/shard_map/rgqd,rlgd->rgql/dot_general | solution.py:59
  99.6 3.0 %collective-permute-start.28 = (bf16[16,2048]{1,0:T(8,128)(2,1)S(1)}, bf16[16,2048]{1,0:T(8,128)(2,1)S(1)}, u32[]{:S(2)}, u32[]{:S(2)}) collective-permute-start(bf16[16,2048]{1,0:T(8,128)(2,1)S(1)} %pad_maximum_fusion.12.array_ref), channel_id=1, source_target_pairs={{0,16},{4,20},{8,24},{12,28},{16,0},{20,4},{24,8},{28,12},{1,17},{... | collective-permute-start | bytes 196616 | tf_op jit(solution)/shard_map/ppermute | solution.py:94
  113.3 2.8 %shard_map.144 = (f32[64,2048]{1,0:T(8,128)S(1)}, f32[64,2048]{1,0:T(8,128)S(1)}) custom-call(bf16[16,2048]{1,0:T(8,128)(2,1)S(1)} %shard_map.142.refs_0_, bf16[16,2048]{1,0:T(8,128)(2,1)S(1)} %collective-permute-done.21.refs_1_, bf16[16,2048]{1,0:T(8,128)(2,1)S(1)} %collective-permute-done.22.refs_2_, bf16[16,2048]{1,0:T(8,128)(2,1)S(1)} %collective-permute-done.23.refs_3_, ...), custom_call_target="tpu_custom_call" | custom-call | flops 2281701376 | bytes 17825792 | tf_op jit(solution)/shard_map/pallas_call | solution.py:157
  119.7 4.1 %collective-permute-done.36 = bf16[32,2048]{1,0:T(8,128)(2,1)S(1)} collective-permute-done((bf16[32,2048]{1,0:T(8,128)(2,1)S(1)}, bf16[32,2048]{1,0:T(8,128)(2,1)S(1)}, u32[]{:S(2)}, u32[]{:S(2)}) %collective-permute-start.36) | collective-permute-done | bytes 131104 | tf_op jit(solution)/shard_map/ppermute | solution.py:94
  128.3 2.8 %collective-permute-done.38 = f32[32]{0:T(128)S(1)} collective-permute-done((f32[32]{0:T(128)S(1)}, f32[32]{0:T(128)S(1)}, u32[]{:S(2)}, u32[]{:S(2)}) %collective-permute-start.38) | collective-permute-done | bytes 160 | tf_op jit(solution)/shard_map/ppermute | solution.py:94
  132.3 3.3 %collective-permute-done.39 = f32[32]{0:T(128)S(1)} collective-permute-done((f32[32]{0:T(128)S(1)}, f32[32]{0:T(128)S(1)}, u32[]{:S(2)}, u32[]{:S(2)}) %collective-permute-start.39) | collective-permute-done | bytes 160 | tf_op jit(solution)/shard_map/ppermute | solution.py:94
  137.3 3.5 %collective-permute-done.40 = bf16[32,2048]{1,0:T(8,128)(2,1)S(1)} collective-permute-done((bf16[32,2048]{1,0:T(8,128)(2,1)S(1)}, bf16[32,2048]{1,0:T(8,128)(2,1)S(1)}, u32[]{:S(2)}, u32[]{:S(2)}) %collective-permute-start.40) | collective-permute-done | bytes 131104 | tf_op jit(solution)/shard_map/ppermute | solution.py:94
  147.5 5.6 %collective-permute-done.49 = f16[64,2048]{1,0:T(8,128)(2,1)S(1)} collective-permute-done((f16[64,2048]{1,0:T(8,128)(2,1)S(1)}, f16[64,2048]{1,0:T(8,128)(2,1)S(1)}, u32[]{:S(2)}, u32[]{:S(2)}) %collective-permute-start.49) | collective-permute-done | bytes 262176 | tf_op jit(solution)/shard_map/ppermute | solution.py:94
  163.7 2.8 %collective-permute-done.43 = f16[16,2048]{1,0:T(8,128)(2,1)S(1)} collective-permute-done((f16[16,2048]{1,0:T(8,128)(2,1)S(1)}, f16[16,2048]{1,0:T(8,128)(2,1)S(1)}, u32[]{:S(2)}, u32[]{:S(2)}) %collective-permute-start.43) | collective-permute-done | bytes 65568 | tf_op jit(solution)/shard_map/ppermute | solution.py:94
  185.7 4.1 %collective-permute-done.57 = bf16[32,2048]{1,0:T(8,128)(2,1)S(1)} collective-permute-done((bf16[32,2048]{1,0:T(8,128)(2,1)S(1)}, bf16[32,2048]{1,0:T(8,128)(2,1)S(1)}, u32[]{:S(2)}, u32[]{:S(2)}) %collective-permute-start.57) | collective-permute-done | bytes 131104 | tf_op jit(solution)/shard_map/ppermute | solution.py:94
  (246 shorter events, 102.5 us)
Async XLA Ops:
  27.5 12.0 %collective-permute-start.13 = (f32[64,1536]{1,0:T(8,128)S(1)}, f32[64,1536]{1,0:T(8,128)S(1)}, u32[]{:S(2)}, u32[]{:S(2)}) collective-permute-start(f32[64,1536]{1,0:T(8,128)S(1)} %get-tuple-element.24), channel_id=1, source_target_pairs={{0,4},{4,0},{8,12},{12,8},{16,20},{20,16},{24,28},{28,24},{1,5},{5... | collective-permute-start | bytes 1179656 | tf_op jit(solution)/shard_map/ppermute | solution.py:94
  30.6 17.4 %collective-permute-start.5 = (f32[64,1536]{1,0:T(8,128)S(1)}, f32[64,1536]{1,0:T(8,128)S(1)}, u32[]{:S(2)}, u32[]{:S(2)}) collective-permute-start(f32[64,1536]{1,0:T(8,128)S(1)} %get-tuple-element.20), channel_id=1, source_target_pairs={{0,4},{4,0},{8,12},{12,8},{16,20},{20,16},{24,28},{28,24},{1,5},{5... | collective-permute-start | bytes 1179656 | tf_op jit(solution)/shard_map/ppermute | solution.py:94
  32.0 23.7 %collective-permute-start.9 = (f32[64,1536]{1,0:T(8,128)S(1)}, f32[64,1536]{1,0:T(8,128)S(1)}, u32[]{:S(2)}, u32[]{:S(2)}) collective-permute-start(f32[64,1536]{1,0:T(8,128)S(1)} %get-tuple-element.22), channel_id=1, source_target_pairs={{0,4},{4,0},{8,12},{12,8},{16,20},{20,16},{24,28},{28,24},{1,5},{5... | collective-permute-start | bytes 1179656 | tf_op jit(solution)/shard_map/ppermute | solution.py:94
  39.6 20.0 %collective-permute-start.14 = (f32[16,1536]{1,0:T(8,128)S(1)}, f32[16,1536]{1,0:T(8,128)S(1)}, u32[]{:S(2)}, u32[]{:S(2)}) collective-permute-start(f32[16,1536]{1,0:T(8,128)S(1)} %get-tuple-element.51), channel_id=1, source_target_pairs={{0,16},{4,20},{8,24},{12,28},{16,0},{20,4},{24,8},{28,12},{1,17},{... | collective-permute-start | bytes 294920 | tf_op jit(solution)/shard_map/ppermute | solution.py:94
  42.6 17.1 %collective-permute-start.16 = (f32[16,1536]{1,0:T(8,128)S(1)}, f32[16,1536]{1,0:T(8,128)S(1)}, u32[]{:S(2)}, u32[]{:S(2)}) collective-permute-start(f32[16,1536]{1,0:T(8,128)S(1)} %get-tuple-element.52), channel_id=1, source_target_pairs={{0,24},{4,28},{8,16},{12,20},{16,8},{20,12},{24,0},{28,4},{1,25},{... | collective-permute-start | bytes 294920 | tf_op jit(solution)/shard_map/ppermute | solution.py:94
  44.0 16.3 %collective-permute-start.15 = (f32[16,1536]{1,0:T(8,128)S(1)}, f32[16,1536]{1,0:T(8,128)S(1)}, u32[]{:S(2)}, u32[]{:S(2)}) collective-permute-start(f32[16,1536]{1,0:T(8,128)S(1)} %get-tuple-element.53), channel_id=1, source_target_pairs={{0,8},{4,12},{8,0},{12,4},{16,24},{20,28},{24,16},{28,20},{1,9},{5... | collective-permute-start | bytes 294920 | tf_op jit(solution)/shard_map/ppermute | solution.py:94
  48.1 16.1 %collective-permute-start.6 = (f32[16,1536]{1,0:T(8,128)S(1)}, f32[16,1536]{1,0:T(8,128)S(1)}, u32[]{:S(2)}, u32[]{:S(2)}) collective-permute-start(f32[16,1536]{1,0:T(8,128)S(1)} %get-tuple-element.45), channel_id=1, source_target_pairs={{0,16},{4,20},{8,24},{12,28},{16,0},{20,4},{24,8},{28,12},{1,17},{... | collective-permute-start | bytes 294920 | tf_op jit(solution)/shard_map/ppermute | solution.py:94
  55.7 8.5 %collective-permute-start.8 = (f32[16,1536]{1,0:T(8,128)S(1)}, f32[16,1536]{1,0:T(8,128)S(1)}, u32[]{:S(2)}, u32[]{:S(2)}) collective-permute-start(f32[16,1536]{1,0:T(8,128)S(1)} %get-tuple-element.46), channel_id=1, source_target_pairs={{0,24},{4,28},{8,16},{12,20},{16,8},{20,12},{24,0},{28,4},{1,25},{... | collective-permute-start | bytes 294920 | tf_op jit(solution)/shard_map/ppermute | solution.py:94
  59.6 7.3 %collective-permute-start.7 = (f32[16,1536]{1,0:T(8,128)S(1)}, f32[16,1536]{1,0:T(8,128)S(1)}, u32[]{:S(2)}, u32[]{:S(2)}) collective-permute-start(f32[16,1536]{1,0:T(8,128)S(1)} %get-tuple-element.47), channel_id=1, source_target_pairs={{0,8},{4,12},{8,0},{12,4},{16,24},{20,28},{24,16},{28,20},{1,9},{5... | collective-permute-start | bytes 294920 | tf_op jit(solution)/shard_map/ppermute | solution.py:94
  59.7 10.5 %collective-permute-start.10 = (f32[16,1536]{1,0:T(8,128)S(1)}, f32[16,1536]{1,0:T(8,128)S(1)}, u32[]{:S(2)}, u32[]{:S(2)}) collective-permute-start(f32[16,1536]{1,0:T(8,128)S(1)} %get-tuple-element.48), channel_id=1, source_target_pairs={{0,16},{4,20},{8,24},{12,28},{16,0},{20,4},{24,8},{28,12},{1,17},{... | collective-permute-start | bytes 294920 | tf_op jit(solution)/shard_map/ppermute | solution.py:94
  60.3 10.0 %collective-permute-start.12 = (f32[16,1536]{1,0:T(8,128)S(1)}, f32[16,1536]{1,0:T(8,128)S(1)}, u32[]{:S(2)}, u32[]{:S(2)}) collective-permute-start(f32[16,1536]{1,0:T(8,128)S(1)} %get-tuple-element.49), channel_id=1, source_target_pairs={{0,24},{4,28},{8,16},{12,20},{16,8},{20,12},{24,0},{28,4},{1,25},{... | collective-permute-start | bytes 294920 | tf_op jit(solution)/shard_map/ppermute | solution.py:94
  91.8 7.5 %collective-permute-start.23 = (bf16[16,2048]{1,0:T(8,128)(2,1)S(1)}, bf16[16,2048]{1,0:T(8,128)(2,1)S(1)}, u32[]{:S(2)}, u32[]{:S(2)}) collective-permute-start(bf16[16,2048]{1,0:T(8,128)(2,1)S(1)} %pad_maximum_fusion.11.array_ref), channel_id=1, source_target_pairs={{0,24},{4,28},{8,16},{12,20},{16,8},{20,12},{24,0},{28,4},{1,25},{... | collective-permute-start | bytes 196616 | tf_op jit(solution)/shard_map/ppermute | solution.py:94
  95.2 8.8 %collective-permute-start.21 = (bf16[16,2048]{1,0:T(8,128)(2,1)S(1)}, bf16[16,2048]{1,0:T(8,128)(2,1)S(1)}, u32[]{:S(2)}, u32[]{:S(2)}) collective-permute-start(bf16[16,2048]{1,0:T(8,128)(2,1)S(1)} %pad_maximum_fusion.11.array_ref), channel_id=1, source_target_pairs={{0,16},{4,20},{8,24},{12,28},{16,0},{20,4},{24,8},{28,12},{1,17},{... | collective-permute-start | bytes 196616 | tf_op jit(solution)/shard_map/ppermute | solution.py:94
  96.2 7.8 %collective-permute-start.31 = (bf16[16,2048]{1,0:T(8,128)(2,1)S(1)}, bf16[16,2048]{1,0:T(8,128)(2,1)S(1)}, u32[]{:S(2)}, u32[]{:S(2)}) collective-permute-start(bf16[16,2048]{1,0:T(8,128)(2,1)S(1)} %pad_maximum_fusion.12.array_ref), channel_id=1, source_target_pairs={{0,4},{4,0},{8,12},{12,8},{16,20},{20,16},{24,28},{28,24},{1,5},{5... | collective-permute-start | bytes 196616 | tf_op jit(solution)/shard_map/ppermute | solution.py:94
  96.7 9.4 %collective-permute-start.30 = (bf16[16,2048]{1,0:T(8,128)(2,1)S(1)}, bf16[16,2048]{1,0:T(8,128)(2,1)S(1)}, u32[]{:S(2)}, u32[]{:S(2)}) collective-permute-start(bf16[16,2048]{1,0:T(8,128)(2,1)S(1)} %pad_maximum_fusion.12.array_ref), channel_id=1, source_target_pairs={{0,24},{4,28},{8,16},{12,20},{16,8},{20,12},{24,0},{28,4},{1,25},{... | collective-permute-start | bytes 196616 | tf_op jit(solution)/shard_map/ppermute | solution.py:94
  99.2 7.0 %collective-permute-start.29 = (bf16[16,2048]{1,0:T(8,128)(2,1)S(1)}, bf16[16,2048]{1,0:T(8,128)(2,1)S(1)}, u32[]{:S(2)}, u32[]{:S(2)}) collective-permute-start(bf16[16,2048]{1,0:T(8,128)(2,1)S(1)} %pad_maximum_fusion.12.array_ref), channel_id=1, source_target_pairs={{0,8},{4,12},{8,0},{12,4},{16,24},{20,28},{24,16},{28,20},{1,9},{5... | collective-permute-start | bytes 196616 | tf_op jit(solution)/shard_map/ppermute | solution.py:94
  99.6 8.6 %collective-permute-start.28 = (bf16[16,2048]{1,0:T(8,128)(2,1)S(1)}, bf16[16,2048]{1,0:T(8,128)(2,1)S(1)}, u32[]{:S(2)}, u32[]{:S(2)}) collective-permute-start(bf16[16,2048]{1,0:T(8,128)(2,1)S(1)} %pad_maximum_fusion.12.array_ref), channel_id=1, source_target_pairs={{0,16},{4,20},{8,24},{12,28},{16,0},{20,4},{24,8},{28,12},{1,17},{... | collective-permute-start | bytes 196616 | tf_op jit(solution)/shard_map/ppermute | solution.py:94
  143.9 9.2 %collective-permute-start.49 = (f16[64,2048]{1,0:T(8,128)(2,1)S(1)}, f16[64,2048]{1,0:T(8,128)(2,1)S(1)}, u32[]{:S(2)}, u32[]{:S(2)}) collective-permute-start(f16[64,2048]{1,0:T(8,128)(2,1)S(1)} %convert_element_type.148), channel_id=1, source_target_pairs={{0,4},{4,0},{8,12},{12,8},{16,20},{20,16},{24,28},{28,24},{1,5},{5... | collective-permute-start | bytes 786440 | tf_op jit(solution)/shard_map/ppermute | solution.py:94
  146.6 11.3 %collective-permute-start.42 = (f16[64,2048]{1,0:T(8,128)(2,1)S(1)}, f16[64,2048]{1,0:T(8,128)(2,1)S(1)}, u32[]{:S(2)}, u32[]{:S(2)}) collective-permute-start(f16[64,2048]{1,0:T(8,128)(2,1)S(1)} %convert_element_type.142), channel_id=1, source_target_pairs={{0,4},{4,0},{8,12},{12,8},{16,20},{20,16},{24,28},{28,24},{1,5},{5... | collective-permute-start | bytes 786440 | tf_op jit(solution)/shard_map/ppermute | solution.py:94
  153.2 8.0 %collective-permute-start.50 = (f16[16,2048]{1,0:T(8,128)(2,1)S(1)}, f16[16,2048]{1,0:T(8,128)(2,1)S(1)}, u32[]{:S(2)}, u32[]{:S(2)}) collective-permute-start(f16[16,2048]{1,0:T(8,128)(2,1)S(1)} %get-tuple-element.56), channel_id=1, source_target_pairs={{0,16},{4,20},{8,24},{12,28},{16,0},{20,4},{24,8},{28,12},{1,17},{... | collective-permute-start | bytes 196616 | tf_op jit(solution)/shard_map/ppermute | solution.py:94
  154.4 7.2 %collective-permute-start.52 = (f16[16,2048]{1,0:T(8,128)(2,1)S(1)}, f16[16,2048]{1,0:T(8,128)(2,1)S(1)}, u32[]{:S(2)}, u32[]{:S(2)}) collective-permute-start(f16[16,2048]{1,0:T(8,128)(2,1)S(1)} %get-tuple-element.57), channel_id=1, source_target_pairs={{0,24},{4,28},{8,16},{12,20},{16,8},{20,12},{24,0},{28,4},{1,25},{... | collective-permute-start | bytes 196616 | tf_op jit(solution)/shard_map/ppermute | solution.py:94
  158.0 8.5 %collective-permute-start.43 = (f16[16,2048]{1,0:T(8,128)(2,1)S(1)}, f16[16,2048]{1,0:T(8,128)(2,1)S(1)}, u32[]{:S(2)}, u32[]{:S(2)}) collective-permute-start(f16[16,2048]{1,0:T(8,128)(2,1)S(1)} %get-tuple-element.59), channel_id=1, source_target_pairs={{0,16},{4,20},{8,24},{12,28},{16,0},{20,4},{24,8},{28,12},{1,17},{... | collective-permute-start | bytes 196616 | tf_op jit(solution)/shard_map/ppermute | solution.py:94
  159.2 7.3 %collective-permute-start.45 = (f16[16,2048]{1,0:T(8,128)(2,1)S(1)}, f16[16,2048]{1,0:T(8,128)(2,1)S(1)}, u32[]{:S(2)}, u32[]{:S(2)}) collective-permute-start(f16[16,2048]{1,0:T(8,128)(2,1)S(1)} %get-tuple-element.60), channel_id=1, source_target_pairs={{0,24},{4,28},{8,16},{12,20},{16,8},{20,12},{24,0},{28,4},{1,25},{... | collective-permute-start | bytes 196616 | tf_op jit(solution)/shard_map/ppermute | solution.py:94
  161.7 7.2 %collective-permute-start.53 = (bf16[16,1024]{1,0:T(8,128)(2,1)S(1)}, bf16[16,1024]{1,0:T(8,128)(2,1)S(1)}, u32[]{:S(2)}, u32[]{:S(2)}) collective-permute-start(bf16[16,1024]{1,0:T(8,128)(2,1)S(1)} %fusion.85), channel_id=1, source_target_pairs={{0,16},{4,20},{8,24},{12,28},{16,0},{20,4},{24,8},{28,12},{1,17},{... | collective-permute-start | bytes 98312 | tf_op jit(solution)/shard_map/ppermute | solution.py:94
  (53 other events, 358.8 us)

commit v4 on v3

--- a/solution.py
+++ b/solution.py
@@ -79,7 +79,7 @@
     return context.reshape(row_count, groups * group_size * HEAD_DIM).astype(jnp.bfloat16)
 
 
-QKV_CHUNKS = 3
+QKV_CHUNKS = 4
 FFN_CHUNKS = 2
 CONTEXT_CHUNKS = 2
 NARROW_KINDS = [jnp.float32] + [jnp.bfloat16] * 8
@@ -206,11 +206,12 @@
     return kept
 
 
-def gather(block, axis):
+def gather(block, axis, paired=False):
     strides = strides_of(axis)[::-1]
+    kept = stand_in if paired else lambda held: held
     for stride in strides[:-1]:
-        block = jnp.concatenate([block, swap(block, axis, stride)], axis=0)
-    return [block, swap(block, axis, strides[-1])]
+        block = jnp.concatenate([kept(block), swap(block, axis, stride)], axis=0)
+    return [kept(block), swap(block, axis, strides[-1])]
 
 
 def gather_direct(block, axis):
@@ -229,12 +230,10 @@
     return blocks
 
 
-def by_rank(blocks, me):
-    stride = 1
-    while stride < len(blocks):
-        other = (me & stride) != 0
-        blocks = [jnp.where(other, blocks[i ^ stride], block) for i, block in enumerate(blocks)]
-        stride *= 2
+def by_rank(blocks, flags):
+    for bit, flag in enumerate(flags):
+        other = 1 << bit
+        blocks = [jnp.where(flag, blocks[i ^ other], block) for i, block in enumerate(blocks)]
     return blocks
 
 
@@ -258,6 +257,10 @@
     narrow_count = lax.axis_size("narrow")
     me_wide = lax.axis_index("wide")
     me_narrow = lax.axis_index("narrow")
+    flags = [(me_narrow & stride) != 0 for stride in strides_of("narrow")]
+    hidden_in, me_wide, me_narrow, flags = lax.optimization_barrier(
+        (hidden_in, me_wide, me_narrow, flags)
+    )
     model_width = hidden_in.shape[1] * wide_count
     own_rows = hidden_in.shape[0]
     local_rows = cache_len.shape[0]
@@ -291,30 +294,46 @@
     to_hypothesis = (hypothesis_bank == bank(across)).astype(jnp.bfloat16)
     to_wide = (wide_row(down) == across).astype(jnp.bfloat16)
 
-    def wide_sum(rows_sq):
-        for stride in strides_of("wide"):
-            rows_sq = stand_in(rows_sq) + swap(rows_sq, "wide", stride)
-        return rows_sq
+    def normalized_rows(values, gain_row):
+        wide_values = values.astype(jnp.float32)
+        rows_sq = jnp.sum(wide_values * wide_values, axis=1)
+        sent = jnp.broadcast_to(rows_sq[None, :], (wide_count * narrow_count, own_rows))
+        landed = lax.all_to_all(sent, ("wide", "narrow"), 0, 0, tiled=True)
+        pieces = gather(values, "narrow", paired=True)
+        sums = jnp.sum(landed.reshape(wide_count, narrow_count, own_rows), axis=0)
+        sums = by_rank([sums[j] for j in range(narrow_count)], flags)
+        order = offsets_of("narrow")
+        half = narrow_count // 2
+        result = []
+        for piece, offsets in zip(pieces, (order[:half], order[half:])):
+            sum_sq = jnp.concatenate([sums[offset] for offset in offsets])
+            result.append(normalize(piece, gain_row, sum_sq, model_width))
+        return result
 
     rows_in = hidden_in.astype(jnp.float32)
-    first_sq = wide_sum(jnp.sum(rows_in * rows_in, axis=1))
-    normed = gather(normalize(hidden_in, attn_gain, first_sq, model_width), "narrow")
+    normed = normalized_rows(hidden_in, attn_gain)
 
     q_cols = w_query.shape[1]
     k_cols = w_key.shape[1]
-    chunk_cols = (q_cols + 2 * k_cols) // QKV_CHUNKS
+    stacked = [(w_query, q_cols), (w_key, k_cols), (w_value, k_cols)]
+    heads = (q_cols + 2 * k_cols) // HEAD_DIM
+    edges = [heads * chunk // QKV_CHUNKS for chunk in range(QKV_CHUNKS)] + [heads]
     pieces = []
     for chunk in range(QKV_CHUNKS):
-        if chunk < QKV_CHUNKS - 1:
-            segments = [(w_query, 0, chunk * chunk_cols, chunk_cols)]
-        else:
-            segments = [(w_query, 0, chunk * chunk_cols, q_cols - chunk * chunk_cols)]
-            segments += [(w_key, 0, 0, k_cols), (w_value, 0, 0, k_cols)]
-        pieces.append(wide_scatter(*project([normed], to_hypothesis, True, segments, 2), jnp.float32))
+        first, last = edges[chunk] * HEAD_DIM, edges[chunk + 1] * HEAD_DIM
+        segments = []
+        start = 0
+        for weight, columns in stacked:
+            low, high = max(first, start), min(last, start + columns)
+            if low < high:
+                segments.append((weight, 0, low - start, high - low))
+            start += columns
+        sums = project([normed], to_hypothesis, True, segments, 2)
+        pieces.append(wide_scatter(*sums, jnp.float32))
     summed = jnp.concatenate(pieces, axis=1).astype(jnp.bfloat16)
     summed = summed.reshape(narrow_count, local_rows, -1, HEAD_DIM)
     turned = exchange([summed[j] for j in range(narrow_count)], "narrow")
-    turned = jnp.stack(by_rank(turned, me_narrow), axis=1)
+    turned = jnp.stack(by_rank(turned, flags), axis=1)
     q_heads = q_cols // HEAD_DIM
     k_heads = k_cols // HEAD_DIM
     query_rot = rotate(
@@ -326,7 +345,7 @@
     value_new = turned[:, :, q_heads + k_heads :].reshape(local_rows, -1)
     context = attend(query_rot, key_rot, value_new, key_cache, value_cache, cache_len)
     context = context.reshape(local_rows, narrow_count, -1)
-    context = by_rank([context[:, j] for j in range(narrow_count)], me_narrow)
+    context = by_rank([context[:, j] for j in range(narrow_count)], flags)
     by_heads = exchange(context, "narrow")
 
     depth = w_out.shape[0] // CONTEXT_CHUNKS
@@ -339,8 +358,7 @@
     attn_out = narrow_scatter(*total)
     resid = (rows_in + attn_out).astype(jnp.bfloat16)
     resid_wide = resid.astype(jnp.float32)
-    second_sq = wide_sum(jnp.sum(resid_wide * resid_wide, axis=1))
-    normed_two = gather(normalize(resid, ffn_gain, second_sq, model_width), "narrow")
+    normed_two = normalized_rows(resid, ffn_gain)
 
     f_cols = w_gate.shape[1] // FFN_CHUNKS
     total = None

time: 191 us -> 188 us (0.984)
  starting transfers between devices: 76.5 us -> 67.5 us
  local copies, waits for them, and re-layouts: 6.7 us -> 13.3 us
  waiting for transfers between devices: 85.1 us -> 83 us
    ppermute x58 -> x56, starting transfers between devices: 76.5 us -> 60 us  [swap(): return lax.ppermute(block, axis, [(i, i ^ offset) for i in range(count)])]
    ppermute x58 -> x56, waiting for transfers between devices: 85.1 us -> 72.7 us  [swap(): return lax.ppermute(block, axis, [(i, i ^ offset) for i in range(count)])]
    all_to_all x0 -> x2, waiting for transfers between devices: none -> 10.3 us  [normalized_rows(): landed = lax.all_to_all(sent, ('wide', 'narrow'), 0, 0, tiled=True)]
    all_to_all x0 -> x2, starting transfers between devices: none -> 7.47 us  [normalized_rows(): landed = lax.all_to_all(sent, ('wide', 'narrow'), 0, 0, tiled=True)]
    unnamed x38 -> x42, local copies, waits for them, and re-layouts: 5.86 us -> 11.2 us
    pallas_call x8 -> x9, Pallas kernels: 10.7 us -> 11.2 us  [project(): pl.pallas_call(body, in_specs=[in_vmem] * len(operands), out_specs=[in_vm...]
  transfers between devices with their start and end apart: 58 -> 58, of which waited for: 42 -> 35; matrix products, arithmetic and copies ran while one was open for 1% -> 2% of each run, Pallas kernels for 2% -> 3%
where the time goes in v4:
time: 188 us; the launch traced here: 187 us
  waiting for transfers between devices  83 us (44%)
  starting transfers between devices  67.5 us (36%)
  local copies, waits for them, and re-layouts  13.3 us (7%)
  Pallas kernels  11.3 us (6%)
  other arithmetic  6.02 us (3%)
  matrix products  5.17 us (3%)
    ppermute x56, waiting for transfers between devices, swap(): return lax.ppermute(block, axis, [(i, i ^ offset) for i in range(count)])  72.7 us
    ppermute x56, starting transfers between devices, swap(): return lax.ppermute(block, axis, [(i, i ^ offset) for i in range(count)])  60 us
    unnamed x42, local copies, waits for them, and re-layouts  11.2 us
    pallas_call x9, Pallas kernels, project(): pl.pallas_call(body, in_specs=[in_vmem] * len(operands), out_specs=[in_vm...  11.2 us
    all_to_all x2, waiting for transfers between devices, normalized_rows(): landed = lax.all_to_all(sent, ('wide', 'narrow'), 0, 0, tiled=True)  10.3 us
    all_to_all x2, starting transfers between devices, normalized_rows(): landed = lax.all_to_all(sent, ('wide', 'narrow'), 0, 0, tiled=True)  7.47 us
    dot_general x1, matrix products, attend(): jnp.einsum('rgqd,rlgd->rgql', query_heads, cache_keys, preferred_element_...  3.86 us
  transfers between devices with their start and end apart: 58, of which 35 were waited for; matrix products, arithmetic and copies ran while one was open for 2% of the time, Pallas kernels for 3%

profile of v4, /device:TPU:0, one launch (start us, length us, event | category | flops | bytes accessed | tf_op | source)
XLA Modules:
  0.0 187.4 jit_solution(17933823952795684013)
XLA Ops:
  0.0 2.9 %collective-permute-start = (bf16[32,2048]{1,0:T(8,128)(2,1)}, bf16[32,2048]{1,0:T(8,128)(2,1)S(1)}, u32[]{:S(2)}, u32[]{:S(2)}) collective-permute-start(bf16[32,2048]{1,0:T(8,128)(2,1)} %array_ref), channel_id=1, source_target_pairs={{0,2},{1,3},{2,0},{3,1},{4,6},{5,7},{6,4},{7,5},{8,10},{9,11},{10,... | collective-permute-start | bytes 393224 | tf_op jit(solution)/shard_map/ppermute | solution.py:94
  4.6 4.9 %all-to-all-start = ((f32[32,1,32]{2,1,0:T(1,128)}), f32[32,1,32]{2,1,0:T(1,128)S(1)}, u32[]{:S(2)}, u32[]{:S(2)}) async-start(f32[32,1,32]{2,1,0:T(1,128)} %broadcast_in_dim.17), calls=%async_computation | async-start | bytes 32768 | tf_op jit(solution)/shard_map/all_to_all | solution.py:301
  11.7 4.9 %all-to-all-done = f32[32,1,32]{2,1,0:T(1,128)S(1)} async-done(((f32[32,1,32]{2,1,0:T(1,128)}), f32[32,1,32]{2,1,0:T(1,128)S(1)}, u32[]{:S(2)}, u32[]{:S(2)}) %all-to-all-start) | async-done | bytes 4128 | tf_op jit(solution)/shard_map/all_to_all | solution.py:301
  18.7 4.3 %copy-done = bf16[2048,4096]{1,0:T(8,128)(2,1)S(1)} copy-done((bf16[2048,4096]{1,0:T(8,128)(2,1)S(1)}, bf16[2048,4096]{1,0:T(8,128)(2,1)}, u32[]{:S(2)}) %copy-start) | copy-done | bytes 16777240
  31.4 2.5 %collective-permute-done.14 = f32[64,1152]{1,0:T(8,128)S(1)} collective-permute-done((f32[64,1152]{1,0:T(8,128)S(1)}, f32[64,1152]{1,0:T(8,128)S(1)}, u32[]{:S(2)}, u32[]{:S(2)}) %collective-permute-start.14) | collective-permute-done | bytes 294944 | tf_op jit(solution)/shard_map/ppermute | solution.py:94
  37.0 3.3 %collective-permute-done.10 = f32[64,1152]{1,0:T(8,128)S(1)} collective-permute-done((f32[64,1152]{1,0:T(8,128)S(1)}, f32[64,1152]{1,0:T(8,128)S(1)}, u32[]{:S(2)}, u32[]{:S(2)}) %collective-permute-start.10) | collective-permute-done | bytes 294944 | tf_op jit(solution)/shard_map/ppermute | solution.py:94
  40.9 5.7 %collective-permute-done.2 = f32[64,1152]{1,0:T(8,128)S(1)} collective-permute-done((f32[64,1152]{1,0:T(8,128)S(1)}, f32[64,1152]{1,0:T(8,128)S(1)}, u32[]{:S(2)}, u32[]{:S(2)}) %collective-permute-start.2) | collective-permute-done | bytes 294944 | tf_op jit(solution)/shard_map/ppermute | solution.py:94
  47.2 5.1 %collective-permute-done.6 = f32[64,1152]{1,0:T(8,128)S(1)} collective-permute-done((f32[64,1152]{1,0:T(8,128)S(1)}, f32[64,1152]{1,0:T(8,128)S(1)}, u32[]{:S(2)}, u32[]{:S(2)}) %collective-permute-start.6) | collective-permute-done | bytes 294944 | tf_op jit(solution)/shard_map/ppermute | solution.py:94
  53.6 3.2 %collective-permute-start.3 = (f32[16,1152]{1,0:T(8,128)S(1)}, f32[16,1152]{1,0:T(8,128)S(1)}, u32[]{:S(2)}, u32[]{:S(2)}) collective-permute-start(f32[16,1152]{1,0:T(8,128)S(1)} %get-tuple-element.61), channel_id=1, source_target_pairs={{0,16},{4,20},{8,24},{12,28},{16,0},{20,4},{24,8},{28,12},{1,17},{... | collective-permute-start | bytes 221192 | tf_op jit(solution)/shard_map/ppermute | solution.py:94
  64.0 5.8 %collective-permute-done.7 = f32[16,1152]{1,0:T(8,128)S(1)} collective-permute-done((f32[16,1152]{1,0:T(8,128)S(1)}, f32[16,1152]{1,0:T(8,128)S(1)}, u32[]{:S(2)}, u32[]{:S(2)}) %collective-permute-start.7) | collective-permute-done | bytes 73760 | tf_op jit(solution)/shard_map/ppermute | solution.py:94
  70.9 3.8 %collective-permute-done.18 = bf16[2,4,36,128]{3,2,1,0:T(8,128)(2,1)S(1)} collective-permute-done((bf16[2,4,36,128]{3,2,1,0:T(8,128)(2,1)S(1)}, bf16[2,4,36,128]{3,2,1,0:T(8,128)(2,1)S(1)}, u32[]{:S(2)}, u32[]{:S(2)}) %collective-permute-start.18) | collective-permute-done | bytes 73760 | tf_op jit(solution)/shard_map/ppermute | solution.py:94
  77.6 3.9 %fusion.130 = (f32[4,8,16]{2,1,0:T(8,128)S(1)}, f32[4,8,16,512]{3,2,1,0:T(8,128)S(1)}) fusion(bf16[4,8,16,64]{3,2,1,0:T(8,128)(2,1)S(1)} %bitcast.88, bf16[4,8,16,64]{3,2,1,0:T(8,128)(2,1)S(1)} %bitcast.86, pred[4,512]{1,0:T(4,128)(4,1)S(1)} %iota_compare_fusion, bf16[4,512,1024]{2,1,0:T(8,128)(2,1)} %param.24), kind=kOutput, calls=%fused_computation.250 | convolution fusion | flops 68156928 | bytes 5378048 | tf_op jit(solution)/shard_map/rgqd,rlgd->rgql/dot_general | solution.py:59
  84.1 3.7 %collective-permute-done.20 = bf16[2,4,4096]{2,1,0:T(4,128)(2,1)S(1)} collective-permute-done((bf16[2,4,4096]{2,1,0:T(4,128)(2,1)S(1)}, bf16[2,4,4096]{2,1,0:T(4,128)(2,1)S(1)}, u32[]{:S(2)}, u32[]{:S(2)}) %collective-permute-start.20) | collective-permute-done | bytes 65568 | tf_op jit(solution)/shard_map/ppermute | solution.py:94
  91.6 2.7 %collective-permute-start.22 = (bf16[16,2048]{1,0:T(8,128)(2,1)S(1)}, bf16[16,2048]{1,0:T(8,128)(2,1)S(1)}, u32[]{:S(2)}, u32[]{:S(2)}) collective-permute-start(bf16[16,2048]{1,0:T(8,128)(2,1)S(1)} %pad_maximum_fusion.11.array_ref), channel_id=1, source_target_pairs={{0,16},{4,20},{8,24},{12,28},{16,0},{20,4},{24,8},{28,12},{1,17},{... | collective-permute-start | bytes 196616 | tf_op jit(solution)/shard_map/ppermute | solution.py:94
  100.5 2.9 %collective-permute-start.28 = (bf16[16,2048]{1,0:T(8,128)(2,1)S(1)}, bf16[16,2048]{1,0:T(8,128)(2,1)S(1)}, u32[]{:S(2)}, u32[]{:S(2)}) collective-permute-start(bf16[16,2048]{1,0:T(8,128)(2,1)S(1)} %collective-permute-done.24.refs_3_), channel_id=1, source_target_pairs={{0,4},{4,0},{8,12},{12,8},{16,20},{20,16},{24,28},{28,24},{1,5},{5... | collective-permute-start | bytes 196616 | tf_op jit(solution)/shard_map/ppermute | solution.py:94
  111.9 2.6 %shard_map.144 = (f32[64,2048]{1,0:T(8,128)S(1)}, f32[64,2048]{1,0:T(8,128)S(1)}) custom-call(bf16[16,2048]{1,0:T(8,128)(2,1)S(1)} %shard_map.142.refs_0_, bf16[16,2048]{1,0:T(8,128)(2,1)S(1)} %collective-permute-done.22.refs_1_, bf16[16,2048]{1,0:T(8,128)(2,1)S(1)} %collective-permute-done.23.refs_2_, bf16[16,2048]{1,0:T(8,128)(2,1)S(1)} %collective-permute-done.24.refs_3_, ...), custom_call_target="tpu_custom_call" | custom-call | flops 2281701376 | bytes 17825792 | tf_op jit(solution)/shard_map/pallas_call | solution.py:157
  117.2 5.0 %collective-permute-done.37 = bf16[32,2048]{1,0:T(8,128)(2,1)S(1)} collective-permute-done((bf16[32,2048]{1,0:T(8,128)(2,1)S(1)}, bf16[32,2048]{1,0:T(8,128)(2,1)S(1)}, u32[]{:S(2)}, u32[]{:S(2)}) %collective-permute-start.37) | collective-permute-done | bytes 131104 | tf_op jit(solution)/shard_map/ppermute | solution.py:94
  123.0 2.5 %all-to-all-start.1 = ((f32[32,1,32]{2,1,0:T(1,128)}), f32[32,1,32]{2,1,0:T(1,128)S(1)}, u32[]{:S(2)}, u32[]{:S(2)}) async-start(f32[32,1,32]{2,1,0:T(1,128)} %broadcast_in_dim.20), calls=%async_computation.1 | async-start | bytes 32768 | tf_op jit(solution)/shard_map/all_to_all | solution.py:301
  127.3 5.4 %all-to-all-done.1 = f32[32,1,32]{2,1,0:T(1,128)S(1)} async-done(((f32[32,1,32]{2,1,0:T(1,128)}), f32[32,1,32]{2,1,0:T(1,128)S(1)}, u32[]{:S(2)}, u32[]{:S(2)}) %all-to-all-start.1) | async-done | bytes 4128 | tf_op jit(solution)/shard_map/all_to_all | solution.py:301
  136.3 3.6 %copy-done.1 = bf16[2048,2048]{1,0:T(8,128)(2,1)S(1)} copy-done((bf16[2048,2048]{1,0:T(8,128)(2,1)S(1)}, bf16[2048,2048]{1,0:T(8,128)(2,1)}, u32[]{:S(2)}) %copy-start.1) | copy-done | bytes 8388632
  144.9 5.7 %collective-permute-done.47 = f16[64,2048]{1,0:T(8,128)(2,1)S(1)} collective-permute-done((f16[64,2048]{1,0:T(8,128)(2,1)S(1)}, f16[64,2048]{1,0:T(8,128)(2,1)S(1)}, u32[]{:S(2)}, u32[]{:S(2)}) %collective-permute-start.47) | collective-permute-done | bytes 262176 | tf_op jit(solution)/shard_map/ppermute | solution.py:94
  158.9 2.5 %collective-permute-start.51 = (bf16[16,1024]{1,0:T(8,128)(2,1)S(1)}, bf16[16,1024]{1,0:T(8,128)(2,1)S(1)}, u32[]{:S(2)}, u32[]{:S(2)}) collective-permute-start(bf16[16,1024]{1,0:T(8,128)(2,1)S(1)} %fusion.84), channel_id=1, source_target_pairs={{0,16},{4,20},{8,24},{12,28},{16,0},{20,4},{24,8},{28,12},{1,17},{... | collective-permute-start | bytes 98312 | tf_op jit(solution)/shard_map/ppermute | solution.py:94
  166.2 2.6 %collective-permute-done.44 = bf16[16,1024]{1,0:T(8,128)(2,1)S(1)} collective-permute-done((bf16[16,1024]{1,0:T(8,128)(2,1)S(1)}, bf16[16,1024]{1,0:T(8,128)(2,1)S(1)}, u32[]{:S(2)}, u32[]{:S(2)}) %collective-permute-start.44) | collective-permute-done | bytes 32800 | tf_op jit(solution)/shard_map/ppermute | solution.py:94
  182.2 4.5 %collective-permute-done.55 = bf16[32,2048]{1,0:T(8,128)(2,1)S(1)} collective-permute-done((bf16[32,2048]{1,0:T(8,128)(2,1)S(1)}, bf16[32,2048]{1,0:T(8,128)(2,1)S(1)}, u32[]{:S(2)}, u32[]{:S(2)}) %collective-permute-start.55) | collective-permute-done | bytes 131104 | tf_op jit(solution)/shard_map/ppermute | solution.py:94
  (261 shorter events, 92.5 us)
Async XLA Ops:
  0.0 16.8 %collective-permute-start = (bf16[32,2048]{1,0:T(8,128)(2,1)}, bf16[32,2048]{1,0:T(8,128)(2,1)S(1)}, u32[]{:S(2)}, u32[]{:S(2)}) collective-permute-start(bf16[32,2048]{1,0:T(8,128)(2,1)} %array_ref), channel_id=1, source_target_pairs={{0,2},{1,3},{2,0},{3,1},{4,6},{5,7},{6,4},{7,5},{8,10},{9,11},{10,... | collective-permute-start | bytes 393224 | tf_op jit(solution)/shard_map/ppermute | solution.py:94
  4.6 12.0 %all-to-all-start = ((f32[32,1,32]{2,1,0:T(1,128)}), f32[32,1,32]{2,1,0:T(1,128)S(1)}, u32[]{:S(2)}, u32[]{:S(2)}) async-start(f32[32,1,32]{2,1,0:T(1,128)} %broadcast_in_dim.17), calls=%async_computation | async-start | bytes 32768 | tf_op jit(solution)/shard_map/all_to_all | solution.py:301
  24.0 9.9 %collective-permute-start.14 = (f32[64,1152]{1,0:T(8,128)S(1)}, f32[64,1152]{1,0:T(8,128)S(1)}, u32[]{:S(2)}, u32[]{:S(2)}) collective-permute-start(f32[64,1152]{1,0:T(8,128)S(1)} %get-tuple-element.38), channel_id=1, source_target_pairs={{0,4},{4,0},{8,12},{12,8},{16,20},{20,16},{24,28},{28,24},{1,5},{5... | collective-permute-start | bytes 884744 | tf_op jit(solution)/shard_map/ppermute | solution.py:94
  25.7 14.6 %collective-permute-start.10 = (f32[64,1152]{1,0:T(8,128)S(1)}, f32[64,1152]{1,0:T(8,128)S(1)}, u32[]{:S(2)}, u32[]{:S(2)}) collective-permute-start(f32[64,1152]{1,0:T(8,128)S(1)} %get-tuple-element.36), channel_id=1, source_target_pairs={{0,4},{4,0},{8,12},{12,8},{16,20},{20,16},{24,28},{28,24},{1,5},{5... | collective-permute-start | bytes 884744 | tf_op jit(solution)/shard_map/ppermute | solution.py:94
  28.3 18.3 %collective-permute-start.2 = (f32[64,1152]{1,0:T(8,128)S(1)}, f32[64,1152]{1,0:T(8,128)S(1)}, u32[]{:S(2)}, u32[]{:S(2)}) collective-permute-start(f32[64,1152]{1,0:T(8,128)S(1)} %get-tuple-element.32), channel_id=1, source_target_pairs={{0,4},{4,0},{8,12},{12,8},{16,20},{20,16},{24,28},{28,24},{1,5},{5... | collective-permute-start | bytes 884744 | tf_op jit(solution)/shard_map/ppermute | solution.py:94
  29.9 22.4 %collective-permute-start.6 = (f32[64,1152]{1,0:T(8,128)S(1)}, f32[64,1152]{1,0:T(8,128)S(1)}, u32[]{:S(2)}, u32[]{:S(2)}) collective-permute-start(f32[64,1152]{1,0:T(8,128)S(1)} %get-tuple-element.34), channel_id=1, source_target_pairs={{0,4},{4,0},{8,12},{12,8},{16,20},{20,16},{24,28},{28,24},{1,5},{5... | collective-permute-start | bytes 884744 | tf_op jit(solution)/shard_map/ppermute | solution.py:94
  34.0 18.9 %collective-permute-start.15 = (f32[16,1152]{1,0:T(8,128)S(1)}, f32[16,1152]{1,0:T(8,128)S(1)}, u32[]{:S(2)}, u32[]{:S(2)}) collective-permute-start(f32[16,1152]{1,0:T(8,128)S(1)} %get-tuple-element.70), channel_id=1, source_target_pairs={{0,16},{4,20},{8,24},{12,28},{16,0},{20,4},{24,8},{28,12},{1,17},{... | collective-permute-start | bytes 221192 | tf_op jit(solution)/shard_map/ppermute | solution.py:94
  34.6 18.9 %collective-permute-start.17 = (f32[16,1152]{1,0:T(8,128)S(1)}, f32[16,1152]{1,0:T(8,128)S(1)}, u32[]{:S(2)}, u32[]{:S(2)}) collective-permute-start(f32[16,1152]{1,0:T(8,128)S(1)} %get-tuple-element.71), channel_id=1, source_target_pairs={{0,24},{4,28},{8,16},{12,20},{16,8},{20,12},{24,0},{28,4},{1,25},{... | collective-permute-start | bytes 221192 | tf_op jit(solution)/shard_map/ppermute | solution.py:94
  40.2 16.6 %collective-permute-start.16 = (f32[16,1152]{1,0:T(8,128)S(1)}, f32[16,1152]{1,0:T(8,128)S(1)}, u32[]{:S(2)}, u32[]{:S(2)}) collective-permute-start(f32[16,1152]{1,0:T(8,128)S(1)} %get-tuple-element.72), channel_id=1, source_target_pairs={{0,8},{4,12},{8,0},{12,4},{16,24},{20,28},{24,16},{28,20},{1,9},{5... | collective-permute-start | bytes 221192 | tf_op jit(solution)/shard_map/ppermute | solution.py:94
  46.6 10.8 %collective-permute-start.11 = (f32[16,1152]{1,0:T(8,128)S(1)}, f32[16,1152]{1,0:T(8,128)S(1)}, u32[]{:S(2)}, u32[]{:S(2)}) collective-permute-start(f32[16,1152]{1,0:T(8,128)S(1)} %get-tuple-element.67), channel_id=1, source_target_pairs={{0,16},{4,20},{8,24},{12,28},{16,0},{20,4},{24,8},{28,12},{1,17},{... | collective-permute-start | bytes 221192 | tf_op jit(solution)/shard_map/ppermute | solution.py:94
  52.9 8.4 %collective-permute-start.12 = (f32[16,1152]{1,0:T(8,128)S(1)}, f32[16,1152]{1,0:T(8,128)S(1)}, u32[]{:S(2)}, u32[]{:S(2)}) collective-permute-start(f32[16,1152]{1,0:T(8,128)S(1)} %get-tuple-element.69), channel_id=1, source_target_pairs={{0,8},{4,12},{8,0},{12,4},{16,24},{20,28},{24,16},{28,20},{1,9},{5... | collective-permute-start | bytes 221192 | tf_op jit(solution)/shard_map/ppermute | solution.py:94
  53.6 10.4 %collective-permute-start.3 = (f32[16,1152]{1,0:T(8,128)S(1)}, f32[16,1152]{1,0:T(8,128)S(1)}, u32[]{:S(2)}, u32[]{:S(2)}) collective-permute-start(f32[16,1152]{1,0:T(8,128)S(1)} %get-tuple-element.61), channel_id=1, source_target_pairs={{0,16},{4,20},{8,24},{12,28},{16,0},{20,4},{24,8},{28,12},{1,17},{... | collective-permute-start | bytes 221192 | tf_op jit(solution)/shard_map/ppermute | solution.py:94
  59.4 10.4 %collective-permute-start.7 = (f32[16,1152]{1,0:T(8,128)S(1)}, f32[16,1152]{1,0:T(8,128)S(1)}, u32[]{:S(2)}, u32[]{:S(2)}) collective-permute-start(f32[16,1152]{1,0:T(8,128)S(1)} %get-tuple-element.64), channel_id=1, source_target_pairs={{0,16},{4,20},{8,24},{12,28},{16,0},{20,4},{24,8},{28,12},{1,17},{... | collective-permute-start | bytes 221192 | tf_op jit(solution)/shard_map/ppermute | solution.py:94
  61.3 8.5 %collective-permute-start.9 = (f32[16,1152]{1,0:T(8,128)S(1)}, f32[16,1152]{1,0:T(8,128)S(1)}, u32[]{:S(2)}, u32[]{:S(2)}) collective-permute-start(f32[16,1152]{1,0:T(8,128)S(1)} %get-tuple-element.65), channel_id=1, source_target_pairs={{0,24},{4,28},{8,16},{12,20},{16,8},{20,12},{24,0},{28,4},{1,25},{... | collective-permute-start | bytes 221192 | tf_op jit(solution)/shard_map/ppermute | solution.py:94
  90.0 7.6 %collective-permute-start.24 = (bf16[16,2048]{1,0:T(8,128)(2,1)S(1)}, bf16[16,2048]{1,0:T(8,128)(2,1)S(1)}, u32[]{:S(2)}, u32[]{:S(2)}) collective-permute-start(bf16[16,2048]{1,0:T(8,128)(2,1)S(1)} %pad_maximum_fusion.11.array_ref), channel_id=1, source_target_pairs={{0,24},{4,28},{8,16},{12,20},{16,8},{20,12},{24,0},{28,4},{1,25},{... | collective-permute-start | bytes 196616 | tf_op jit(solution)/shard_map/ppermute | solution.py:94
  91.6 8.9 %collective-permute-start.22 = (bf16[16,2048]{1,0:T(8,128)(2,1)S(1)}, bf16[16,2048]{1,0:T(8,128)(2,1)S(1)}, u32[]{:S(2)}, u32[]{:S(2)}) collective-permute-start(bf16[16,2048]{1,0:T(8,128)(2,1)S(1)} %pad_maximum_fusion.11.array_ref), channel_id=1, source_target_pairs={{0,16},{4,20},{8,24},{12,28},{16,0},{20,4},{24,8},{28,12},{1,17},{... | collective-permute-start | bytes 196616 | tf_op jit(solution)/shard_map/ppermute | solution.py:94
  94.4 9.1 %collective-permute-start.32 = (bf16[16,2048]{1,0:T(8,128)(2,1)S(1)}, bf16[16,2048]{1,0:T(8,128)(2,1)S(1)}, u32[]{:S(2)}, u32[]{:S(2)}) collective-permute-start(bf16[16,2048]{1,0:T(8,128)(2,1)S(1)} %pad_maximum_fusion.12.array_ref), channel_id=1, source_target_pairs={{0,4},{4,0},{8,12},{12,8},{16,20},{20,16},{24,28},{28,24},{1,5},{5... | collective-permute-start | bytes 196616 | tf_op jit(solution)/shard_map/ppermute | solution.py:94
  96.0 7.8 %collective-permute-start.31 = (bf16[16,2048]{1,0:T(8,128)(2,1)S(1)}, bf16[16,2048]{1,0:T(8,128)(2,1)S(1)}, u32[]{:S(2)}, u32[]{:S(2)}) collective-permute-start(bf16[16,2048]{1,0:T(8,128)(2,1)S(1)} %pad_maximum_fusion.12.array_ref), channel_id=1, source_target_pairs={{0,24},{4,28},{8,16},{12,20},{16,8},{20,12},{24,0},{28,4},{1,25},{... | collective-permute-start | bytes 196616 | tf_op jit(solution)/shard_map/ppermute | solution.py:94
  97.6 8.0 %collective-permute-start.30 = (bf16[16,2048]{1,0:T(8,128)(2,1)S(1)}, bf16[16,2048]{1,0:T(8,128)(2,1)S(1)}, u32[]{:S(2)}, u32[]{:S(2)}) collective-permute-start(bf16[16,2048]{1,0:T(8,128)(2,1)S(1)} %pad_maximum_fusion.12.array_ref), channel_id=1, source_target_pairs={{0,8},{4,12},{8,0},{12,4},{16,24},{20,28},{24,16},{28,20},{1,9},{5... | collective-permute-start | bytes 196616 | tf_op jit(solution)/shard_map/ppermute | solution.py:94
  123.0 9.6 %all-to-all-start.1 = ((f32[32,1,32]{2,1,0:T(1,128)}), f32[32,1,32]{2,1,0:T(1,128)S(1)}, u32[]{:S(2)}, u32[]{:S(2)}) async-start(f32[32,1,32]{2,1,0:T(1,128)} %broadcast_in_dim.20), calls=%async_computation.1 | async-start | bytes 32768 | tf_op jit(solution)/shard_map/all_to_all | solution.py:301
  141.3 9.3 %collective-permute-start.47 = (f16[64,2048]{1,0:T(8,128)(2,1)S(1)}, f16[64,2048]{1,0:T(8,128)(2,1)S(1)}, u32[]{:S(2)}, u32[]{:S(2)}) collective-permute-start(f16[64,2048]{1,0:T(8,128)(2,1)S(1)} %convert_element_type.172), channel_id=1, source_target_pairs={{0,4},{4,0},{8,12},{12,8},{16,20},{20,16},{24,28},{28,24},{1,5},{5... | collective-permute-start | bytes 786440 | tf_op jit(solution)/shard_map/ppermute | solution.py:94
  143.5 11.6 %collective-permute-start.40 = (f16[64,2048]{1,0:T(8,128)(2,1)S(1)}, f16[64,2048]{1,0:T(8,128)(2,1)S(1)}, u32[]{:S(2)}, u32[]{:S(2)}) collective-permute-start(f16[64,2048]{1,0:T(8,128)(2,1)S(1)} %convert_element_type.166), channel_id=1, source_target_pairs={{0,4},{4,0},{8,12},{12,8},{16,20},{20,16},{24,28},{28,24},{1,5},{5... | collective-permute-start | bytes 786440 | tf_op jit(solution)/shard_map/ppermute | solution.py:94
  150.7 7.6 %collective-permute-start.48 = (f16[16,2048]{1,0:T(8,128)(2,1)S(1)}, f16[16,2048]{1,0:T(8,128)(2,1)S(1)}, u32[]{:S(2)}, u32[]{:S(2)}) collective-permute-start(f16[16,2048]{1,0:T(8,128)(2,1)S(1)} %get-tuple-element.73), channel_id=1, source_target_pairs={{0,16},{4,20},{8,24},{12,28},{16,0},{20,4},{24,8},{28,12},{1,17},{... | collective-permute-start | bytes 196616 | tf_op jit(solution)/shard_map/ppermute | solution.py:94
  155.2 8.0 %collective-permute-start.41 = (f16[16,2048]{1,0:T(8,128)(2,1)S(1)}, f16[16,2048]{1,0:T(8,128)(2,1)S(1)}, u32[]{:S(2)}, u32[]{:S(2)}) collective-permute-start(f16[16,2048]{1,0:T(8,128)(2,1)S(1)} %get-tuple-element.76), channel_id=1, source_target_pairs={{0,16},{4,20},{8,24},{12,28},{16,0},{20,4},{24,8},{28,12},{1,17},{... | collective-permute-start | bytes 196616 | tf_op jit(solution)/shard_map/ppermute | solution.py:94
  (55 other events, 333.9 us)

commit v5 on v4

--- a/solution.py
+++ b/solution.py
@@ -85,6 +85,9 @@
 NARROW_KINDS = [jnp.float32] + [jnp.bfloat16] * 8
 TILE = 512
 ROOM = 24
+DIRECT_ROOM = 50
+DIRECT_TILE = 256
+IN_FLIGHT = 4
 STAND_IN = 4
 MIB = 1024 * 1024
 
@@ -106,14 +109,15 @@
     return order
 
 
-def project(groups, order, turned, segments, split, total=None):
+def project(groups, order, turned, segments, split, total=None, direct=False):
     rows = order.shape[0]
+    width_of_tile = DIRECT_TILE if direct else TILE
     depth = groups[0][0].shape[1]
     tiles = []
     width = 0
     for index, (_, first_row, first, columns) in enumerate(segments):
-        for start in range(first, first + columns, TILE):
-            tile = min(TILE, first + columns - start)
+        for start in range(first, first + columns, width_of_tile):
+            tile = min(width_of_tile, first + columns - start)
             tiles.append((index, first_row, start, tile, width))
             width += tile
     part = rows // split
@@ -126,7 +130,14 @@
         weight_refs, rest = rest[: len(segments)], rest[len(segments) :]
         if total is not None:
             total_ref, rest = rest[0], rest[1:]
-        out_refs = rest[:split]
+        out_refs, rest = rest[:split], rest[split:]
+        copies = []
+        if direct:
+            for place, (index, first_row, start, tile, _) in enumerate(tiles):
+                source = weight_refs[index].at[pl.ds(first_row, depth), pl.ds(start, tile)]
+                copies.append(pltpu.make_async_copy(source, rest[place], rest[-1].at[place]))
+        for copy in copies[:IN_FLIGHT]:
+            copy.start()
         lefts = []
         for group in range(len(groups)):
             group_refs = piece_refs[group * each : (group + 1) * each]
@@ -137,12 +148,18 @@
                 preferred_element_type=jnp.float32,
             )
             lefts.append(left.astype(jnp.bfloat16))
-        for index, first_row, start, tile, base in tiles:
+        for number, (index, first_row, start, tile, base) in enumerate(tiles):
             result = None
             for group, left in enumerate(lefts):
-                weight = weight_refs[index][
-                    pl.ds(first_row + group * depth, depth), pl.ds(start, tile)
-                ]
+                if direct:
+                    copies[number].wait()
+                    weight = rest[number][...]
+                    if number + IN_FLIGHT < len(tiles):
+                        copies[number + IN_FLIGHT].start()
+                else:
+                    weight = weight_refs[index][
+                        pl.ds(first_row + group * depth, depth), pl.ds(start, tile)
+                    ]
                 product = jnp.dot(left, weight, preferred_element_type=jnp.float32)
                 result = product if result is None else result + product
             if total is not None:
@@ -154,12 +171,20 @@
     if total is not None:
         operands.append(total)
     in_vmem = pl.BlockSpec(memory_space=pltpu.VMEM)
+    specs = [in_vmem] * len(operands)
+    scratch = []
+    if direct:
+        for place in range(count + 1, count + 1 + len(segments)):
+            specs[place] = pl.BlockSpec(memory_space=pltpu.HBM)
+        scratch = [pltpu.VMEM((depth, tile[3]), jnp.bfloat16) for tile in tiles]
+        scratch.append(pltpu.SemaphoreType.DMA((len(tiles),)))
     return pl.pallas_call(
         body,
-        in_specs=[in_vmem] * len(operands),
+        in_specs=specs,
         out_specs=[in_vmem] * split,
+        scratch_shapes=scratch,
         out_shape=[jax.ShapeDtypeStruct((part, width), jnp.float32)] * split,
-        compiler_params=pltpu.CompilerParams(vmem_limit_bytes=ROOM * MIB),
+        compiler_params=pltpu.CompilerParams(vmem_limit_bytes=(DIRECT_ROOM if direct else ROOM) * MIB),
         cost_estimate=pl.CostEstimate(
             flops=2 * rows * len(groups) * depth * (width + rows),
             bytes_accessed=2 * len(groups) * depth * width + 4 * rows * width,
@@ -206,12 +231,11 @@
     return kept
 
 
-def gather(block, axis, paired=False):
+def gather(block, axis):
     strides = strides_of(axis)[::-1]
-    kept = stand_in if paired else lambda held: held
     for stride in strides[:-1]:
-        block = jnp.concatenate([kept(block), swap(block, axis, stride)], axis=0)
-    return [kept(block), swap(block, axis, strides[-1])]
+        block = jnp.concatenate([block, swap(block, axis, stride)], axis=0)
+    return [block, swap(block, axis, strides[-1])]
 
 
 def gather_direct(block, axis):
@@ -299,7 +323,7 @@
         rows_sq = jnp.sum(wide_values * wide_values, axis=1)
         sent = jnp.broadcast_to(rows_sq[None, :], (wide_count * narrow_count, own_rows))
         landed = lax.all_to_all(sent, ("wide", "narrow"), 0, 0, tiled=True)
-        pieces = gather(values, "narrow", paired=True)
+        pieces = gather(values, "narrow")
         sums = jnp.sum(landed.reshape(wide_count, narrow_count, own_rows), axis=0)
         sums = by_rank([sums[j] for j in range(narrow_count)], flags)
         order = offsets_of("narrow")
@@ -319,6 +343,7 @@
     heads = (q_cols + 2 * k_cols) // HEAD_DIM
     edges = [heads * chunk // QKV_CHUNKS for chunk in range(QKV_CHUNKS)] + [heads]
     pieces = []
+    ordered = to_hypothesis
     for chunk in range(QKV_CHUNKS):
         first, last = edges[chunk] * HEAD_DIM, edges[chunk + 1] * HEAD_DIM
         segments = []
@@ -328,7 +353,8 @@
             if low < high:
                 segments.append((weight, 0, low - start, high - low))
             start += columns
-        sums = project([normed], to_hypothesis, True, segments, 2)
+        sums = project([normed], ordered, True, segments, 2, direct=True)
+        sums, ordered = lax.optimization_barrier((sums, ordered))
         pieces.append(wide_scatter(*sums, jnp.float32))
     summed = jnp.concatenate(pieces, axis=1).astype(jnp.bfloat16)
     summed = summed.reshape(narrow_count, local_rows, -1, HEAD_DIM)
@@ -364,7 +390,7 @@
     total = None
     for chunk in range(FFN_CHUNKS):
         segments = [(w_gate, 0, chunk * f_cols, f_cols), (w_up, 0, chunk * f_cols, f_cols)]
-        sums = wide_scatter(*project([normed_two], to_wide, False, segments, 2), jnp.float16)
+        sums = wide_scatter(*project([normed_two], to_wide, False, segments, 2, direct=True), jnp.float16)
         act = (jax.nn.silu(sums[:, :f_cols]) * sums[:, f_cols:]).astype(jnp.bfloat16)
         last = chunk == FFN_CHUNKS - 1
         total = project(
@@ -374,6 +400,7 @@
             [(w_down, chunk * f_cols, 0, w_down.shape[1])],
             2 if last else 1,
             total if total is None else total[0],
+            direct=True,
         )
     ffn_out = narrow_scatter(*total)
     return (resid_wide + ffn_out).astype(jnp.bfloat16)

time: 188 us -> 188 us (level)
  Pallas kernels: 11.3 us -> 32.7 us
  waiting for transfers between devices: 83 us -> 67.5 us
  local copies, waits for them, and re-layouts: 13.3 us -> 2.45 us
  blocking collectives: 0 us -> 9.17 us
  starting transfers between devices: 67.5 us -> 61.4 us
  other arithmetic: 6.02 us -> 8 us
    pallas_call x9, Pallas kernels: 11.2 us -> 32.7 us  [project(): pl.pallas_call(body, in_specs=specs, out_specs=[in_vmem] * split, scratch...]
    unnamed x42 -> x21, local copies, waits for them, and re-layouts: 11.2 us -> 0.97 us
    ppermute x56, waiting for transfers between devices: 72.7 us -> 63.3 us  [swap(): return lax.ppermute(block, axis, [(i, i ^ offset) for i in range(count)])]
    all_to_all x0 -> x1, blocking collectives: none -> 9.17 us  [normalized_rows(): landed = lax.all_to_all(sent, ('wide', 'narrow'), 0, 0, tiled=True)]
    all_to_all x2 -> x1, waiting for transfers between devices: 10.3 us -> 4.26 us  [normalized_rows(): landed = lax.all_to_all(sent, ('wide', 'narrow'), 0, 0, tiled=True)]
    ppermute x56, starting transfers between devices: 60 us -> 56.5 us  [swap(): return lax.ppermute(block, axis, [(i, i ^ offset) for i in range(count)])]
    all_to_all x2 -> x1, starting transfers between devices: 7.47 us -> 4.92 us  [normalized_rows(): landed = lax.all_to_all(sent, ('wide', 'narrow'), 0, 0, tiled=True)]
  transfers between devices with their start and end apart: 58 -> 57, of which waited for: 35 -> 30; matrix products, arithmetic and copies ran while one was open for 2% -> 3% of each run, Pallas kernels for 3% -> 10%
where the time goes in v5:
time: 188 us; the launch traced here: 187 us
  waiting for transfers between devices  67.5 us (36%)
  starting transfers between devices  61.4 us (33%)
  Pallas kernels  32.7 us (17%)
  blocking collectives  9.17 us (5%)
  other arithmetic  8 us (4%)
  matrix products  5.16 us (3%)
  local copies, waits for them, and re-layouts  2.45 us (1%)
    ppermute x56, waiting for transfers between devices, swap(): return lax.ppermute(block, axis, [(i, i ^ offset) for i in range(count)])  63.3 us
    ppermute x56, starting transfers between devices, swap(): return lax.ppermute(block, axis, [(i, i ^ offset) for i in range(count)])  56.5 us
    pallas_call x9, Pallas kernels, project(): pl.pallas_call(body, in_specs=specs, out_specs=[in_vmem] * split, scratch...  32.7 us
    all_to_all x1, blocking collectives, normalized_rows(): landed = lax.all_to_all(sent, ('wide', 'narrow'), 0, 0, tiled=True)  9.17 us
    all_to_all x1, starting transfers between devices, normalized_rows(): landed = lax.all_to_all(sent, ('wide', 'narrow'), 0, 0, tiled=True)  4.92 us
    all_to_all x1, waiting for transfers between devices, normalized_rows(): landed = lax.all_to_all(sent, ('wide', 'narrow'), 0, 0, tiled=True)  4.26 us
    dot_general x1, matrix products, attend(): jnp.einsum('rgqd,rlgd->rgql', query_heads, cache_keys, preferred_element_...  3.86 us
  transfers between devices with their start and end apart: 57, of which 30 were waited for; matrix products, arithmetic and copies ran while one was open for 3% of the time, Pallas kernels for 10%

profile of v5, /device:TPU:0, one launch (start us, length us, event | category | flops | bytes accessed | tf_op | source)
XLA Modules:
  0.0 187.3 jit_solution(11064393120756010028)
XLA Ops:
  0.0 2.9 %collective-permute-start = (bf16[32,2048]{1,0:T(8,128)(2,1)}, bf16[32,2048]{1,0:T(8,128)(2,1)S(1)}, u32[]{:S(2)}, u32[]{:S(2)}) collective-permute-start(bf16[32,2048]{1,0:T(8,128)(2,1)} %param.14), channel_id=1, source_target_pairs={{0,2},{1,3},{2,0},{3,1},{4,6},{5,7},{6,4},{7,5},{8,10},{9,11},{10,... | collective-permute-start | bytes 393224 | tf_op jit(solution)/shard_map/ppermute | solution.py:97
  4.6 4.9 %all-to-all-start = ((f32[32,1,32]{2,1,0:T(1,128)}), f32[32,1,32]{2,1,0:T(1,128)S(1)}, u32[]{:S(2)}, u32[]{:S(2)}) async-start(f32[32,1,32]{2,1,0:T(1,128)} %broadcast_in_dim.17), calls=%async_computation | async-start | bytes 32768 | tf_op jit(solution)/shard_map/all_to_all | solution.py:325
  12.4 4.3 %all-to-all-done = f32[32,1,32]{2,1,0:T(1,128)S(1)} async-done(((f32[32,1,32]{2,1,0:T(1,128)}), f32[32,1,32]{2,1,0:T(1,128)S(1)}, u32[]{:S(2)}, u32[]{:S(2)}) %all-to-all-start) | async-done | bytes 4128 | tf_op jit(solution)/shard_map/all_to_all | solution.py:325
  19.2 3.4 %shard_map.136 = (f32[64,1152]{1,0:T(8,128)S(1)}, f32[64,1152]{1,0:T(8,128)S(1)}) custom-call(bf16[64,2048]{1,0:T(8,128)(2,1)S(1)} %get-tuple-element.142.refs_0_, bf16[64,2048]{1,0:T(8,128)(2,1)S(1)} %get-tuple-element.141.refs_1_, bf16[128,128]{1,0:T(8,128)(2,1)S(1)} %get-tuple-element.56.refs_2_.refs_16_, bf16[2048,4096]{1,0:T(8,128)(2,1)} %refs_3_.11), custom_call_target="tpu_custom_call" | custom-call | flops 671088640 | bytes 5308416 | tf_op jit(solution)/shard_map/pallas_call | solution.py:181
  23.2 3.4 %shard_map.137 = (f32[64,1152]{1,0:T(8,128)S(1)}, f32[64,1152]{1,0:T(8,128)S(1)}) custom-call(bf16[64,2048]{1,0:T(8,128)(2,1)S(1)} %get-tuple-element.142.refs_0_, bf16[64,2048]{1,0:T(8,128)(2,1)S(1)} %get-tuple-element.141.refs_1_, bf16[128,128]{1,0:T(8,128)(2,1)S(1)} %get-tuple-element.56.refs_2_.refs_16_, bf16[2048,4096]{1,0:T(8,128)(2,1)} %refs_3_.11), custom_call_target="tpu_custom_call" | custom-call | flops 671088640 | bytes 5308416 | tf_op jit(solution)/shard_map/pallas_call | solution.py:181
  28.1 3.4 %shard_map.138 = (f32[64,1152]{1,0:T(8,128)S(1)}, f32[64,1152]{1,0:T(8,128)S(1)}) custom-call(bf16[64,2048]{1,0:T(8,128)(2,1)S(1)} %get-tuple-element.142.refs_0_, bf16[64,2048]{1,0:T(8,128)(2,1)S(1)} %get-tuple-element.141.refs_1_, bf16[128,128]{1,0:T(8,128)(2,1)S(1)} %get-tuple-element.56.refs_2_.refs_16_, bf16[2048,4096]{1,0:T(8,128)(2,1)} %refs_3_.11), custom_call_target="tpu_custom_call" | custom-call | flops 671088640 | bytes 5308416 | tf_op jit(solution)/shard_map/pallas_call | solution.py:181
  31.5 3.5 %shard_map.139 = (f32[64,1152]{1,0:T(8,128)S(1)}, f32[64,1152]{1,0:T(8,128)S(1)}) custom-call(bf16[64,2048]{1,0:T(8,128)(2,1)S(1)} %get-tuple-element.142.refs_0_, bf16[64,2048]{1,0:T(8,128)(2,1)S(1)} %get-tuple-element.141.refs_1_, bf16[128,128]{1,0:T(8,128)(2,1)S(1)} %get-tuple-element.56.refs_2_.refs_16_, bf16[2048,4096]{1,0:T(8,128)(2,1)} %refs_3_.11, ...), custom_call_target="tpu_custom_call" | custom-call | flops 671088640 | bytes 5308416 | tf_op jit(solution)/shard_map/pallas_call | solution.py:181
  40.8 4.2 %collective-permute-done.14 = f32[64,1152]{1,0:T(8,128)S(1)} collective-permute-done((f32[64,1152]{1,0:T(8,128)S(1)}, f32[64,1152]{1,0:T(8,128)S(1)}, u32[]{:S(2)}, u32[]{:S(2)}) %collective-permute-start.14) | collective-permute-done | bytes 294944 | tf_op jit(solution)/shard_map/ppermute | solution.py:97
  45.7 4.9 %collective-permute-done.10 = f32[64,1152]{1,0:T(8,128)S(1)} collective-permute-done((f32[64,1152]{1,0:T(8,128)S(1)}, f32[64,1152]{1,0:T(8,128)S(1)}, u32[]{:S(2)}, u32[]{:S(2)}) %collective-permute-start.10) | collective-permute-done | bytes 294944 | tf_op jit(solution)/shard_map/ppermute | solution.py:97
  51.9 3.2 %collective-permute-start.15 = (f32[16,1152]{1,0:T(8,128)S(1)}, f32[16,1152]{1,0:T(8,128)S(1)}, u32[]{:S(2)}, u32[]{:S(2)}) collective-permute-start(f32[16,1152]{1,0:T(8,128)S(1)} %get-tuple-element.92), channel_id=1, source_target_pairs={{0,16},{4,20},{8,24},{12,28},{16,0},{20,4},{24,8},{28,12},{1,17},{... | collective-permute-start | bytes 221192 | tf_op jit(solution)/shard_map/ppermute | solution.py:97
  62.8 5.4 %collective-permute-done.11 = f32[16,1152]{1,0:T(8,128)S(1)} collective-permute-done((f32[16,1152]{1,0:T(8,128)S(1)}, f32[16,1152]{1,0:T(8,128)S(1)}, u32[]{:S(2)}, u32[]{:S(2)}) %collective-permute-start.11) | collective-permute-done | bytes 73760 | tf_op jit(solution)/shard_map/ppermute | solution.py:97
  69.2 3.8 %collective-permute-done.18 = bf16[2,4,36,128]{3,2,1,0:T(8,128)(2,1)S(1)} collective-permute-done((bf16[2,4,36,128]{3,2,1,0:T(8,128)(2,1)S(1)}, bf16[2,4,36,128]{3,2,1,0:T(8,128)(2,1)S(1)}, u32[]{:S(2)}, u32[]{:S(2)}) %collective-permute-start.18) | collective-permute-done | bytes 73760 | tf_op jit(solution)/shard_map/ppermute | solution.py:97
  75.8 3.9 %fusion.130 = (f32[4,8,16]{2,1,0:T(8,128)S(1)}, f32[4,8,16,512]{3,2,1,0:T(8,128)S(1)}) fusion(bf16[4,8,16,64]{3,2,1,0:T(8,128)(2,1)S(1)} %bitcast.82, bf16[4,8,16,64]{3,2,1,0:T(8,128)(2,1)S(1)} %bitcast.80, pred[4,512]{1,0:T(4,128)(4,1)S(1)} %iota_compare_fusion, bf16[4,512,1024]{2,1,0:T(8,128)(2,1)} %param.24), kind=kOutput, calls=%fused_computation.251 | convolution fusion | flops 68156928 | bytes 5378048 | tf_op jit(solution)/shard_map/rgqd,rlgd->rgql/dot_general | solution.py:59
  82.4 3.7 %collective-permute-done.20 = bf16[2,4,4096]{2,1,0:T(4,128)(2,1)S(1)} collective-permute-done((bf16[2,4,4096]{2,1,0:T(4,128)(2,1)S(1)}, bf16[2,4,4096]{2,1,0:T(4,128)(2,1)S(1)}, u32[]{:S(2)}, u32[]{:S(2)}) %collective-permute-start.20) | collective-permute-done | bytes 65568 | tf_op jit(solution)/shard_map/ppermute | solution.py:97
  89.8 2.8 %collective-permute-start.22 = (bf16[16,2048]{1,0:T(8,128)(2,1)S(1)}, bf16[16,2048]{1,0:T(8,128)(2,1)S(1)}, u32[]{:S(2)}, u32[]{:S(2)}) collective-permute-start(bf16[16,2048]{1,0:T(8,128)(2,1)S(1)} %pad_maximum_fusion.10.array_ref), channel_id=1, source_target_pairs={{0,16},{4,20},{8,24},{12,28},{16,0},{20,4},{24,8},{28,12},{1,17},{... | collective-permute-start | bytes 196616 | tf_op jit(solution)/shard_map/ppermute | solution.py:97
  98.8 2.9 %collective-permute-start.28 = (bf16[16,2048]{1,0:T(8,128)(2,1)S(1)}, bf16[16,2048]{1,0:T(8,128)(2,1)S(1)}, u32[]{:S(2)}, u32[]{:S(2)}) collective-permute-start(bf16[16,2048]{1,0:T(8,128)(2,1)S(1)} %collective-permute-done.24.refs_3_), channel_id=1, source_target_pairs={{0,4},{4,0},{8,12},{12,8},{16,20},{20,16},{24,28},{28,24},{1,5},{5... | collective-permute-start | bytes 196616 | tf_op jit(solution)/shard_map/ppermute | solution.py:97
  115.5 5.0 %collective-permute-done.37 = bf16[32,2048]{1,0:T(8,128)(2,1)S(1)} collective-permute-done((bf16[32,2048]{1,0:T(8,128)(2,1)S(1)}, bf16[32,2048]{1,0:T(8,128)(2,1)S(1)}, u32[]{:S(2)}, u32[]{:S(2)}) %collective-permute-start.37) | collective-permute-done | bytes 131104 | tf_op jit(solution)/shard_map/ppermute | solution.py:97
  121.3 9.2 %all_to_all.12 = f32[32,1,32]{2,1,0:T(1,128)S(1)} all-to-all(f32[32,1,32]{2,1,0:T(1,128)S(1)} %broadcast_in_dim.20), channel_id=1, replica_groups=mesh['wide'=8,'narrow'=4] {'wide','narrow'}, dimensions={0} | all-to-all | bytes 8192 | tf_op jit(solution)/shard_map/all_to_all | solution.py:325
  132.3 4.7 %shard_map.144 = (f32[64,2048]{1,0:T(8,128)S(1)}, f32[64,2048]{1,0:T(8,128)S(1)}) custom-call(bf16[64,2048]{1,0:T(8,128)(2,1)S(1)} %get-tuple-element.140.refs_0_, bf16[64,2048]{1,0:T(8,128)(2,1)S(1)} %get-tuple-element.139.refs_1_, bf16[128,128]{1,0:T(8,128)(2,1)S(1)} %get-tuple-element.143.refs_2_, bf16[2048,2048]{1,0:T(8,128)(2,1)} %refs_3_.13, ...), custom_call_target="tpu_custom_call" | custom-call | flops 1140850688 | bytes 9437184 | tf_op jit(solution)/shard_map/pallas_call | solution.py:181
  137.7 4.7 %shard_map.143 = (f32[64,2048]{1,0:T(8,128)S(1)}, f32[64,2048]{1,0:T(8,128)S(1)}) custom-call(bf16[64,2048]{1,0:T(8,128)(2,1)S(1)} %get-tuple-element.140.refs_0_, bf16[64,2048]{1,0:T(8,128)(2,1)S(1)} %get-tuple-element.139.refs_1_, bf16[128,128]{1,0:T(8,128)(2,1)S(1)} %get-tuple-element.143.refs_2_, bf16[2048,2048]{1,0:T(8,128)(2,1)} %refs_3_.13, ...), custom_call_target="tpu_custom_call" | custom-call | flops 1140850688 | bytes 9437184 | tf_op jit(solution)/shard_map/pallas_call | solution.py:181
  156.4 3.0 %collective-permute-done.41 = f16[16,2048]{1,0:T(8,128)(2,1)S(1)} collective-permute-done((f16[16,2048]{1,0:T(8,128)(2,1)S(1)}, f16[16,2048]{1,0:T(8,128)(2,1)S(1)}, u32[]{:S(2)}, u32[]{:S(2)}) %collective-permute-start.41) | collective-permute-done | bytes 65568 | tf_op jit(solution)/shard_map/ppermute | solution.py:97
  171.9 3.5 %shard_map.145.refs_4_ = f32[128,2048]{1,0:T(8,128)S(1)} custom-call(bf16[64,1024]{1,0:T(8,128)(2,1)S(1)} %pad_maximum_fusion.5.refs_0_, bf16[64,1024]{1,0:T(8,128)(2,1)S(1)} %collective-permute-done.53.refs_1_, bf16[128,128]{1,0:T(8,128)(2,1)S(1)} %get-tuple-element.143.refs_2_, bf16[2048,2048]{1,0:T(8,128)(2,1)} %refs_3_.15), custom_call_target="tpu_custom_call" | custom-call | flops 570425344 | bytes 5242880 | tf_op jit(solution)/shard_map/pallas_call | solution.py:181
  175.4 3.5 %shard_map.146 = (f32[64,2048]{1,0:T(8,128)S(1)}, f32[64,2048]{1,0:T(8,128)S(1)}) custom-call(bf16[64,1024]{1,0:T(8,128)(2,1)S(1)} %pad_maximum_fusion.4.refs_0_, bf16[64,1024]{1,0:T(8,128)(2,1)S(1)} %collective-permute-done.46.refs_1_, bf16[128,128]{1,0:T(8,128)(2,1)S(1)} %get-tuple-element.143.refs_2_, bf16[2048,2048]{1,0:T(8,128)(2,1)} %refs_3_.15, ...), custom_call_target="tpu_custom_call" | custom-call | flops 570425344 | bytes 5242880 | tf_op jit(solution)/shard_map/pallas_call | solution.py:181
  181.1 5.4 %collective-permute-done.55 = bf16[32,2048]{1,0:T(8,128)(2,1)S(1)} collective-permute-done((bf16[32,2048]{1,0:T(8,128)(2,1)S(1)}, bf16[32,2048]{1,0:T(8,128)(2,1)S(1)}, u32[]{:S(2)}, u32[]{:S(2)}) %collective-permute-start.55) | collective-permute-done | bytes 131104 | tf_op jit(solution)/shard_map/ppermute | solution.py:97
  (232 shorter events, 86.8 us)
Async XLA Ops:
  0.0 16.7 %collective-permute-start = (bf16[32,2048]{1,0:T(8,128)(2,1)}, bf16[32,2048]{1,0:T(8,128)(2,1)S(1)}, u32[]{:S(2)}, u32[]{:S(2)}) collective-permute-start(bf16[32,2048]{1,0:T(8,128)(2,1)} %param.14), channel_id=1, source_target_pairs={{0,2},{1,3},{2,0},{3,1},{4,6},{5,7},{6,4},{7,5},{8,10},{9,11},{10,... | collective-permute-start | bytes 393224 | tf_op jit(solution)/shard_map/ppermute | solution.py:97
  4.6 12.0 %all-to-all-start = ((f32[32,1,32]{2,1,0:T(1,128)}), f32[32,1,32]{2,1,0:T(1,128)S(1)}, u32[]{:S(2)}, u32[]{:S(2)}) async-start(f32[32,1,32]{2,1,0:T(1,128)} %broadcast_in_dim.17), calls=%async_computation | async-start | bytes 32768 | tf_op jit(solution)/shard_map/all_to_all | solution.py:325
  22.5 14.6 %collective-permute-start.2 = (f32[64,1152]{1,0:T(8,128)S(1)}, f32[64,1152]{1,0:T(8,128)S(1)}, u32[]{:S(2)}, u32[]{:S(2)}) collective-permute-start(f32[64,1152]{1,0:T(8,128)S(1)} %get-tuple-element.45), channel_id=1, source_target_pairs={{0,4},{4,0},{8,12},{12,8},{16,20},{20,16},{24,28},{28,24},{1,5},{5... | collective-permute-start | bytes 884744 | tf_op jit(solution)/shard_map/ppermute | solution.py:97
  26.6 13.7 %collective-permute-start.6 = (f32[64,1152]{1,0:T(8,128)S(1)}, f32[64,1152]{1,0:T(8,128)S(1)}, u32[]{:S(2)}, u32[]{:S(2)}) collective-permute-start(f32[64,1152]{1,0:T(8,128)S(1)} %get-tuple-element.50), channel_id=1, source_target_pairs={{0,4},{4,0},{8,12},{12,8},{16,20},{20,16},{24,28},{28,24},{1,5},{5... | collective-permute-start | bytes 884744 | tf_op jit(solution)/shard_map/ppermute | solution.py:97
  35.1 10.0 %collective-permute-start.14 = (f32[64,1152]{1,0:T(8,128)S(1)}, f32[64,1152]{1,0:T(8,128)S(1)}, u32[]{:S(2)}, u32[]{:S(2)}) collective-permute-start(f32[64,1152]{1,0:T(8,128)S(1)} %get-tuple-element.60), channel_id=1, source_target_pairs={{0,4},{4,0},{8,12},{12,8},{16,20},{20,16},{24,28},{28,24},{1,5},{5... | collective-permute-start | bytes 884744 | tf_op jit(solution)/shard_map/ppermute | solution.py:97
  35.7 14.9 %collective-permute-start.10 = (f32[64,1152]{1,0:T(8,128)S(1)}, f32[64,1152]{1,0:T(8,128)S(1)}, u32[]{:S(2)}, u32[]{:S(2)}) collective-permute-start(f32[64,1152]{1,0:T(8,128)S(1)} %get-tuple-element.55), channel_id=1, source_target_pairs={{0,4},{4,0},{8,12},{12,8},{16,20},{20,16},{24,28},{28,24},{1,5},{5... | collective-permute-start | bytes 884744 | tf_op jit(solution)/shard_map/ppermute | solution.py:97
  37.2 14.0 %collective-permute-start.3 = (f32[16,1152]{1,0:T(8,128)S(1)}, f32[16,1152]{1,0:T(8,128)S(1)}, u32[]{:S(2)}, u32[]{:S(2)}) collective-permute-start(f32[16,1152]{1,0:T(8,128)S(1)} %get-tuple-element.83), channel_id=1, source_target_pairs={{0,16},{4,20},{8,24},{12,28},{16,0},{20,4},{24,8},{28,12},{1,17},{... | collective-permute-start | bytes 221192 | tf_op jit(solution)/shard_map/ppermute | solution.py:97
  37.9 14.0 %collective-permute-start.5 = (f32[16,1152]{1,0:T(8,128)S(1)}, f32[16,1152]{1,0:T(8,128)S(1)}, u32[]{:S(2)}, u32[]{:S(2)}) collective-permute-start(f32[16,1152]{1,0:T(8,128)S(1)} %get-tuple-element.84), channel_id=1, source_target_pairs={{0,24},{4,28},{8,16},{12,20},{16,8},{20,12},{24,0},{28,4},{1,25},{... | collective-permute-start | bytes 221192 | tf_op jit(solution)/shard_map/ppermute | solution.py:97
  40.2 14.9 %collective-permute-start.4 = (f32[16,1152]{1,0:T(8,128)S(1)}, f32[16,1152]{1,0:T(8,128)S(1)}, u32[]{:S(2)}, u32[]{:S(2)}) collective-permute-start(f32[16,1152]{1,0:T(8,128)S(1)} %get-tuple-element.85), channel_id=1, source_target_pairs={{0,8},{4,12},{8,0},{12,4},{16,24},{20,28},{24,16},{28,20},{1,9},{5... | collective-permute-start | bytes 221192 | tf_op jit(solution)/shard_map/ppermute | solution.py:97
  45.1 10.7 %collective-permute-start.7 = (f32[16,1152]{1,0:T(8,128)S(1)}, f32[16,1152]{1,0:T(8,128)S(1)}, u32[]{:S(2)}, u32[]{:S(2)}) collective-permute-start(f32[16,1152]{1,0:T(8,128)S(1)} %get-tuple-element.86), channel_id=1, source_target_pairs={{0,16},{4,20},{8,24},{12,28},{16,0},{20,4},{24,8},{28,12},{1,17},{... | collective-permute-start | bytes 221192 | tf_op jit(solution)/shard_map/ppermute | solution.py:97
  51.3 8.4 %collective-permute-start.8 = (f32[16,1152]{1,0:T(8,128)S(1)}, f32[16,1152]{1,0:T(8,128)S(1)}, u32[]{:S(2)}, u32[]{:S(2)}) collective-permute-start(f32[16,1152]{1,0:T(8,128)S(1)} %get-tuple-element.88), channel_id=1, source_target_pairs={{0,8},{4,12},{8,0},{12,4},{16,24},{20,28},{24,16},{28,20},{1,9},{5... | collective-permute-start | bytes 221192 | tf_op jit(solution)/shard_map/ppermute | solution.py:97
  51.9 10.8 %collective-permute-start.15 = (f32[16,1152]{1,0:T(8,128)S(1)}, f32[16,1152]{1,0:T(8,128)S(1)}, u32[]{:S(2)}, u32[]{:S(2)}) collective-permute-start(f32[16,1152]{1,0:T(8,128)S(1)} %get-tuple-element.92), channel_id=1, source_target_pairs={{0,16},{4,20},{8,24},{12,28},{16,0},{20,4},{24,8},{28,12},{1,17},{... | collective-permute-start | bytes 221192 | tf_op jit(solution)/shard_map/ppermute | solution.py:97
  57.6 10.5 %collective-permute-start.11 = (f32[16,1152]{1,0:T(8,128)S(1)}, f32[16,1152]{1,0:T(8,128)S(1)}, u32[]{:S(2)}, u32[]{:S(2)}) collective-permute-start(f32[16,1152]{1,0:T(8,128)S(1)} %get-tuple-element.89), channel_id=1, source_target_pairs={{0,16},{4,20},{8,24},{12,28},{16,0},{20,4},{24,8},{28,12},{1,17},{... | collective-permute-start | bytes 221192 | tf_op jit(solution)/shard_map/ppermute | solution.py:97
  59.6 8.5 %collective-permute-start.13 = (f32[16,1152]{1,0:T(8,128)S(1)}, f32[16,1152]{1,0:T(8,128)S(1)}, u32[]{:S(2)}, u32[]{:S(2)}) collective-permute-start(f32[16,1152]{1,0:T(8,128)S(1)} %get-tuple-element.90), channel_id=1, source_target_pairs={{0,24},{4,28},{8,16},{12,20},{16,8},{20,12},{24,0},{28,4},{1,25},{... | collective-permute-start | bytes 221192 | tf_op jit(solution)/shard_map/ppermute | solution.py:97
  89.8 9.0 %collective-permute-start.22 = (bf16[16,2048]{1,0:T(8,128)(2,1)S(1)}, bf16[16,2048]{1,0:T(8,128)(2,1)S(1)}, u32[]{:S(2)}, u32[]{:S(2)}) collective-permute-start(bf16[16,2048]{1,0:T(8,128)(2,1)S(1)} %pad_maximum_fusion.10.array_ref), channel_id=1, source_target_pairs={{0,16},{4,20},{8,24},{12,28},{16,0},{20,4},{24,8},{28,12},{1,17},{... | collective-permute-start | bytes 196616 | tf_op jit(solution)/shard_map/ppermute | solution.py:97
  92.7 9.0 %collective-permute-start.32 = (bf16[16,2048]{1,0:T(8,128)(2,1)S(1)}, bf16[16,2048]{1,0:T(8,128)(2,1)S(1)}, u32[]{:S(2)}, u32[]{:S(2)}) collective-permute-start(bf16[16,2048]{1,0:T(8,128)(2,1)S(1)} %pad_maximum_fusion.11.array_ref), channel_id=1, source_target_pairs={{0,4},{4,0},{8,12},{12,8},{16,20},{20,16},{24,28},{28,24},{1,5},{5... | collective-permute-start | bytes 196616 | tf_op jit(solution)/shard_map/ppermute | solution.py:97
  94.2 7.6 %collective-permute-start.31 = (bf16[16,2048]{1,0:T(8,128)(2,1)S(1)}, bf16[16,2048]{1,0:T(8,128)(2,1)S(1)}, u32[]{:S(2)}, u32[]{:S(2)}) collective-permute-start(bf16[16,2048]{1,0:T(8,128)(2,1)S(1)} %pad_maximum_fusion.11.array_ref), channel_id=1, source_target_pairs={{0,24},{4,28},{8,16},{12,20},{16,8},{20,12},{24,0},{28,4},{1,25},{... | collective-permute-start | bytes 196616 | tf_op jit(solution)/shard_map/ppermute | solution.py:97
  95.8 8.1 %collective-permute-start.30 = (bf16[16,2048]{1,0:T(8,128)(2,1)S(1)}, bf16[16,2048]{1,0:T(8,128)(2,1)S(1)}, u32[]{:S(2)}, u32[]{:S(2)}) collective-permute-start(bf16[16,2048]{1,0:T(8,128)(2,1)S(1)} %pad_maximum_fusion.11.array_ref), channel_id=1, source_target_pairs={{0,8},{4,12},{8,0},{12,4},{16,24},{20,28},{24,16},{28,20},{1,9},{5... | collective-permute-start | bytes 196616 | tf_op jit(solution)/shard_map/ppermute | solution.py:97
  120.7 9.8 %collective-permute-start.38 = (bf16[32,2048]{1,0:T(8,128)(2,1)S(1)}, bf16[32,2048]{1,0:T(8,128)(2,1)S(1)}, u32[]{:S(2)}, u32[]{:S(2)}) collective-permute-start(bf16[32,2048]{1,0:T(8,128)(2,1)S(1)} %get-tuple-element.74), channel_id=1, source_target_pairs={{0,2},{1,3},{2,0},{3,1},{4,6},{5,7},{6,4},{7,5},{8,10},{9,11},{10,... | collective-permute-start | bytes 393224 | tf_op jit(solution)/shard_map/ppermute | solution.py:97
  137.1 8.8 %collective-permute-start.47 = (f16[64,2048]{1,0:T(8,128)(2,1)S(1)}, f16[64,2048]{1,0:T(8,128)(2,1)S(1)}, u32[]{:S(2)}, u32[]{:S(2)}) collective-permute-start(f16[64,2048]{1,0:T(8,128)(2,1)S(1)} %convert_element_type.172), channel_id=1, source_target_pairs={{0,4},{4,0},{8,12},{12,8},{16,20},{20,16},{24,28},{28,24},{1,5},{5... | collective-permute-start | bytes 786440 | tf_op jit(solution)/shard_map/ppermute | solution.py:97
  142.5 8.6 %collective-permute-start.40 = (f16[64,2048]{1,0:T(8,128)(2,1)S(1)}, f16[64,2048]{1,0:T(8,128)(2,1)S(1)}, u32[]{:S(2)}, u32[]{:S(2)}) collective-permute-start(f16[64,2048]{1,0:T(8,128)(2,1)S(1)} %convert_element_type.166), channel_id=1, source_target_pairs={{0,4},{4,0},{8,12},{12,8},{16,20},{20,16},{24,28},{28,24},{1,5},{5... | collective-permute-start | bytes 786440 | tf_op jit(solution)/shard_map/ppermute | solution.py:97
  146.1 8.2 %collective-permute-start.48 = (f16[16,2048]{1,0:T(8,128)(2,1)S(1)}, f16[16,2048]{1,0:T(8,128)(2,1)S(1)}, u32[]{:S(2)}, u32[]{:S(2)}) collective-permute-start(f16[16,2048]{1,0:T(8,128)(2,1)S(1)} %get-tuple-element.95), channel_id=1, source_target_pairs={{0,16},{4,20},{8,24},{12,28},{16,0},{20,4},{24,8},{28,12},{1,17},{... | collective-permute-start | bytes 196616 | tf_op jit(solution)/shard_map/ppermute | solution.py:97
  146.7 8.1 %collective-permute-start.50 = (f16[16,2048]{1,0:T(8,128)(2,1)S(1)}, f16[16,2048]{1,0:T(8,128)(2,1)S(1)}, u32[]{:S(2)}, u32[]{:S(2)}) collective-permute-start(f16[16,2048]{1,0:T(8,128)(2,1)S(1)} %get-tuple-element.96), channel_id=1, source_target_pairs={{0,24},{4,28},{8,16},{12,20},{16,8},{20,12},{24,0},{28,4},{1,25},{... | collective-permute-start | bytes 196616 | tf_op jit(solution)/shard_map/ppermute | solution.py:97
  151.2 8.2 %collective-permute-start.41 = (f16[16,2048]{1,0:T(8,128)(2,1)S(1)}, f16[16,2048]{1,0:T(8,128)(2,1)S(1)}, u32[]{:S(2)}, u32[]{:S(2)}) collective-permute-start(f16[16,2048]{1,0:T(8,128)(2,1)S(1)} %get-tuple-element.98), channel_id=1, source_target_pairs={{0,16},{4,20},{8,24},{12,28},{16,0},{20,4},{24,8},{28,12},{1,17},{... | collective-permute-start | bytes 196616 | tf_op jit(solution)/shard_map/ppermute | solution.py:97
  (43 other events, 294.8 us)

commit v6 on v5

--- a/solution.py
+++ b/solution.py
@@ -79,15 +79,17 @@
     return context.reshape(row_count, groups * group_size * HEAD_DIM).astype(jnp.bfloat16)
 
 
-QKV_CHUNKS = 4
+QKV_CHUNKS = 3
 FFN_CHUNKS = 2
 CONTEXT_CHUNKS = 2
 NARROW_KINDS = [jnp.float32] + [jnp.bfloat16] * 8
 TILE = 512
 ROOM = 24
 DIRECT_ROOM = 50
-DIRECT_TILE = 256
-IN_FLIGHT = 4
+IN_FLIGHT = 9
+LANES = 128
+TOP_CODE = 32700.0
+LOG_STEPS = 64.0
 STAND_IN = 4
 MIB = 1024 * 1024
 
@@ -109,15 +111,36 @@
     return order
 
 
-def project(groups, order, turned, segments, split, total=None, direct=False):
+def encoded(values):
+    top = jnp.max(jnp.abs(values), axis=1, keepdims=True)
+    steps = jnp.floor(jnp.log2(jnp.maximum(top, 1e-30)) * LOG_STEPS + 1.5)
+    return jnp.round(values * (TOP_CODE * jnp.exp2(steps * (-1.0 / LOG_STEPS)))), steps
+
+
+def write_codes(code_ref, place, values, steps_tile):
+    codes, steps = encoded(values)
+    code_ref[:, place * LANES : (place + 1) * LANES] = codes.astype(jnp.int32).astype(jnp.int16)
+    lanes = lax.broadcasted_iota(jnp.int32, (values.shape[0], LANES), 1)
+    return jnp.where(lanes == place, steps, steps_tile)
+
+
+def read_codes(code_ref, place):
+    codes = code_ref[:, place * LANES : (place + 1) * LANES]
+    steps = code_ref[:, code_ref.shape[1] - LANES :].astype(jnp.int32).astype(jnp.float32)
+    scale = jnp.exp2(steps[:, place : place + 1] * (1.0 / LOG_STEPS)) * (1.0 / TOP_CODE)
+    return codes.astype(jnp.int32).astype(jnp.float32) * scale
+
+
+def project(
+    groups, order, turned, segments, split, total=None, direct=False, coded=False
+):
     rows = order.shape[0]
-    width_of_tile = DIRECT_TILE if direct else TILE
     depth = groups[0][0].shape[1]
     tiles = []
     width = 0
     for index, (_, first_row, first, columns) in enumerate(segments):
-        for start in range(first, first + columns, width_of_tile):
-            tile = min(width_of_tile, first + columns - start)
+        for start in range(first, first + columns, TILE):
+            tile = min(TILE, first + columns - start)
             tiles.append((index, first_row, start, tile, width))
             width += tile
     part = rows // split
@@ -148,6 +171,7 @@
                 preferred_element_type=jnp.float32,
             )
             lefts.append(left.astype(jnp.bfloat16))
+        steps_tile = jnp.zeros((part, LANES), jnp.float32)
         for number, (index, first_row, start, tile, base) in enumerate(tiles):
             result = None
             for group, left in enumerate(lefts):
@@ -164,14 +188,24 @@
                 result = product if result is None else result + product
             if total is not None:
                 result = result + total_ref[:, base : base + tile]
-            for place, out_ref in enumerate(out_refs):
+            for place, out_ref in enumerate(out_refs[: 1 if coded else split]):
                 out_ref[:, base : base + tile] = result[place * part : (place + 1) * part]
+            if coded:
+                for column in range(0, tile, LANES):
+                    values = result[part:, column : column + LANES]
+                    place = (base + column) // LANES
+                    steps_tile = write_codes(out_refs[1], place, values, steps_tile)
+        if coded:
+            out_refs[1][:, width:] = steps_tile.astype(jnp.int32).astype(jnp.int16)
 
     operands = pieces + [order] + [segment[0] for segment in segments]
     if total is not None:
         operands.append(total)
     in_vmem = pl.BlockSpec(memory_space=pltpu.VMEM)
     specs = [in_vmem] * len(operands)
+    out_shape = [jax.ShapeDtypeStruct((part, width), jnp.float32)] * split
+    if coded:
+        out_shape[1] = jax.ShapeDtypeStruct((part, width + LANES), jnp.int16)
     scratch = []
     if direct:
         for place in range(count + 1, count + 1 + len(segments)):
@@ -183,7 +217,7 @@
         in_specs=specs,
         out_specs=[in_vmem] * split,
         scratch_shapes=scratch,
-        out_shape=[jax.ShapeDtypeStruct((part, width), jnp.float32)] * split,
+        out_shape=out_shape,
         compiler_params=pltpu.CompilerParams(vmem_limit_bytes=(DIRECT_ROOM if direct else ROOM) * MIB),
         cost_estimate=pl.CostEstimate(
             flops=2 * rows * len(groups) * depth * (width + rows),
@@ -210,14 +244,60 @@
     )(array)
 
 
-def wide_scatter(kept, sent, kind):
-    strides = strides_of("wide")
+def fold(kept, arrived, blocks):
+    rows = kept.shape[0] // blocks
+    width = kept.shape[1]
+
+    def body(kept_ref, arrived_ref, own_ref, *code_refs):
+        tiles = [jnp.zeros((rows, LANES), jnp.float32)] * (blocks - 1)
+        for place in range(width // LANES):
+            columns = slice(place * LANES, (place + 1) * LANES)
+            sums = kept_ref[:, columns] + read_codes(arrived_ref, place)
+            own_ref[:, columns] = sums[:rows]
+            for index, code_ref in enumerate(code_refs):
+                values = sums[(index + 1) * rows : (index + 2) * rows]
+                tiles[index] = write_codes(code_ref, place, values, tiles[index])
+        for tile, code_ref in zip(tiles, code_refs):
+            code_ref[:, width:] = tile.astype(jnp.int32).astype(jnp.int16)
+
+    codes = jax.ShapeDtypeStruct((rows, width + LANES), jnp.int16)
+    return pl.pallas_call(
+        body,
+        out_shape=[jax.ShapeDtypeStruct((rows, width), jnp.float32)] + [codes] * (blocks - 1),
+        compiler_params=pltpu.CompilerParams(vmem_limit_bytes=8 * MIB),
+    )(kept, arrived)
+
+
+def add_codes(own, arrived):
+    def body(own_ref, *refs):
+        for place in range(own.shape[1] // LANES):
+            columns = slice(place * LANES, (place + 1) * LANES)
+            sums = own_ref[:, columns]
+            for code_ref in refs[:-1]:
+                sums = sums + read_codes(code_ref, place)
+            refs[-1][:, columns] = sums.astype(jnp.bfloat16)
+
+    return pl.pallas_call(
+        body,
+        out_shape=jax.ShapeDtypeStruct(own.shape, jnp.bfloat16),
+        compiler_params=pltpu.CompilerParams(vmem_limit_bytes=8 * MIB),
+    )(own, *arrived)
+
+
+def coded_scatter(kept, sent):
+    blocks = lax.axis_size("wide") // 2
+    own, *codes = fold(kept, swap(sent, "wide", 1), blocks)
+    offsets = offsets_of("wide")[1:blocks]
+    return add_codes(own, [swap(code, "wide", o) for code, o in zip(codes, offsets)])
+
+
+def wide_scatter(kept, sent):
     rows = 2 * kept.shape[0] // lax.axis_size("wide")
-    kept = kept + swap(sent.astype(kind), "wide", strides[0]).astype(jnp.float32)
+    kept = kept + swap(sent.astype(jnp.float16), "wide", 1).astype(jnp.float32)
     total = kept[:rows]
     for place, offset in enumerate(offsets_of("wide")[: kept.shape[0] // rows]):
         if offset:
-            block = kept[place * rows : (place + 1) * rows].astype(kind)
+            block = kept[place * rows : (place + 1) * rows].astype(jnp.float16)
             total = total + swap(block, "wide", offset).astype(jnp.float32)
     return total
 
@@ -353,10 +433,10 @@
             if low < high:
                 segments.append((weight, 0, low - start, high - low))
             start += columns
-        sums = project([normed], ordered, True, segments, 2, direct=True)
+        sums = project([normed], ordered, True, segments, 2, direct=True, coded=True)
         sums, ordered = lax.optimization_barrier((sums, ordered))
-        pieces.append(wide_scatter(*sums, jnp.float32))
-    summed = jnp.concatenate(pieces, axis=1).astype(jnp.bfloat16)
+        pieces.append(coded_scatter(*sums))
+    summed = jnp.concatenate(pieces, axis=1)
     summed = summed.reshape(narrow_count, local_rows, -1, HEAD_DIM)
     turned = exchange([summed[j] for j in range(narrow_count)], "narrow")
     turned = jnp.stack(by_rank(turned, flags), axis=1)
@@ -390,7 +470,7 @@
     total = None
     for chunk in range(FFN_CHUNKS):
         segments = [(w_gate, 0, chunk * f_cols, f_cols), (w_up, 0, chunk * f_cols, f_cols)]
-        sums = wide_scatter(*project([normed_two], to_wide, False, segments, 2, direct=True), jnp.float16)
+        sums = wide_scatter(*project([normed_two], to_wide, False, segments, 2, direct=True))
         act = (jax.nn.silu(sums[:, :f_cols]) * sums[:, f_cols:]).astype(jnp.bfloat16)
         last = chunk == FFN_CHUNKS - 1
         total = project(

time: 188 us -> 172 us (0.915)
  waiting for transfers between devices: 67.5 us -> 55.9 us
  starting transfers between devices: 61.4 us -> 58.9 us
  Pallas kernels: 32.7 us -> 30.8 us
    ppermute x56 -> x52, waiting for transfers between devices: 63.3 us -> 51 us  [swap(): return lax.ppermute(block, axis, [(i, i ^ offset) for i in range(count)])]
    pallas_call x9 -> x8, Pallas kernels: 32.7 us -> 27.4 us  [project(): pl.pallas_call(body, in_specs=specs, out_specs=[in_vmem] * split, scratch...]
    pallas_call x0 -> x6, Pallas kernels: none -> 3.38 us  [the longest x3 2.85 us: fold(): pl.pallas_call(body, out_shape=[jax.ShapeDtypeStruct((rows, width), jnp.f...]
    ppermute x56 -> x52, starting transfers between devices: 56.5 us -> 53.9 us  [swap(): return lax.ppermute(block, axis, [(i, i ^ offset) for i in range(count)])]
  transfers between devices with their start and end apart: 57 -> 53, of which waited for: 30 -> 29; matrix products, arithmetic and copies ran while one was open for 3% -> 3% of each run, Pallas kernels for 10% -> 10%
where the time goes in v6:
time: 172 us
  starting transfers between devices  58.9 us (34%)
  waiting for transfers between devices  55.9 us (32%)
  Pallas kernels  30.8 us (18%)
  blocking collectives  10.5 us (6%)
  other arithmetic  7.11 us (4%)
  matrix products  5.17 us (3%)
  local copies, waits for them, and re-layouts  2.38 us (1%)
    ppermute x52, starting transfers between devices, swap(): return lax.ppermute(block, axis, [(i, i ^ offset) for i in range(count)])  53.9 us
    ppermute x52, waiting for transfers between devices, swap(): return lax.ppermute(block, axis, [(i, i ^ offset) for i in range(count)])  51 us
    pallas_call x8, Pallas kernels, project(): pl.pallas_call(body, in_specs=specs, out_specs=[in_vmem] * split, scratch...  27.4 us
    all_to_all x1, blocking collectives, normalized_rows(): landed = lax.all_to_all(sent, ('wide', 'narrow'), 0, 0, tiled=True)  10.5 us
    all_to_all x1, starting transfers between devices, normalized_rows(): landed = lax.all_to_all(sent, ('wide', 'narrow'), 0, 0, tiled=True)  4.92 us
    all_to_all x1, waiting for transfers between devices, normalized_rows(): landed = lax.all_to_all(sent, ('wide', 'narrow'), 0, 0, tiled=True)  4.92 us
    dot_general x1, matrix products, attend(): jnp.einsum('rgqd,rlgd->rgql', query_heads, cache_keys, preferred_element_...  3.86 us
  transfers between devices with their start and end apart: 53, of which 29 were waited for; matrix products, arithmetic and copies ran while one was open for 3% of the time, Pallas kernels for 10%

profile of v6, /device:TPU:0, one launch (start us, length us, event | category | flops | bytes accessed | tf_op | source)
XLA Modules:
  0.0 171.5 jit_solution(9497851772304485661)
XLA Ops:
  0.0 2.9 %collective-permute-start = (bf16[32,2048]{1,0:T(8,128)(2,1)}, bf16[32,2048]{1,0:T(8,128)(2,1)S(1)}, u32[]{:S(2)}, u32[]{:S(2)}) collective-permute-start(bf16[32,2048]{1,0:T(8,128)(2,1)} %param.14), channel_id=1, source_target_pairs={{0,2},{1,3},{2,0},{3,1},{4,6},{5,7},{6,4},{7,5},{8,10},{9,11},{10,... | collective-permute-start | bytes 393224 | tf_op jit(solution)/shard_map/ppermute | solution.py:99
  4.6 4.9 %all-to-all-start = ((f32[32,1,32]{2,1,0:T(1,128)}), f32[32,1,32]{2,1,0:T(1,128)S(1)}, u32[]{:S(2)}, u32[]{:S(2)}) async-start(f32[32,1,32]{2,1,0:T(1,128)} %broadcast_in_dim.17), calls=%async_computation | async-start | bytes 32768 | tf_op jit(solution)/shard_map/all_to_all | solution.py:405
  11.7 4.9 %all-to-all-done = f32[32,1,32]{2,1,0:T(1,128)S(1)} async-done(((f32[32,1,32]{2,1,0:T(1,128)}), f32[32,1,32]{2,1,0:T(1,128)S(1)}, u32[]{:S(2)}, u32[]{:S(2)}) %all-to-all-start) | async-done | bytes 4128 | tf_op jit(solution)/shard_map/all_to_all | solution.py:405
  19.2 3.6 %shard_map.136 = (f32[64,1536]{1,0:T(8,128)S(1)}, s16[64,1664]{1,0:T(8,128)(2,1)S(1)}) custom-call(bf16[64,2048]{1,0:T(8,128)(2,1)S(1)} %get-tuple-element.144.refs_0_, bf16[64,2048]{1,0:T(8,128)(2,1)S(1)} %get-tuple-element.143.refs_1_, bf16[128,128]{1,0:T(8,128)(2,1)S(1)} %get-tuple-element.66.refs_2_.refs_16_, bf16[2048,4096]{1,0:T(8,128)(2,1)} %refs_3_.9), custom_call_target="tpu_custom_call" | custom-call | flops 872415232 | bytes 7077888 | tf_op jit(solution)/shard_map/pallas_call | solution.py:215
  23.4 3.6 %shard_map.139 = (f32[64,1536]{1,0:T(8,128)S(1)}, s16[64,1664]{1,0:T(8,128)(2,1)S(1)}) custom-call(bf16[64,2048]{1,0:T(8,128)(2,1)S(1)} %get-tuple-element.144.refs_0_, bf16[64,2048]{1,0:T(8,128)(2,1)S(1)} %get-tuple-element.143.refs_1_, bf16[128,128]{1,0:T(8,128)(2,1)S(1)} %get-tuple-element.66.refs_2_.refs_16_, bf16[2048,4096]{1,0:T(8,128)(2,1)} %refs_3_.9), custom_call_target="tpu_custom_call" | custom-call | flops 872415232 | bytes 7077888 | tf_op jit(solution)/shard_map/pallas_call | solution.py:215
  27.1 3.9 %shard_map.142 = (f32[64,1536]{1,0:T(8,128)S(1)}, s16[64,1664]{1,0:T(8,128)(2,1)S(1)}) custom-call(bf16[64,2048]{1,0:T(8,128)(2,1)S(1)} %get-tuple-element.144.refs_0_, bf16[64,2048]{1,0:T(8,128)(2,1)S(1)} %get-tuple-element.143.refs_1_, bf16[128,128]{1,0:T(8,128)(2,1)S(1)} %get-tuple-element.66.refs_2_.refs_16_, bf16[2048,4096]{1,0:T(8,128)(2,1)} %refs_3_.9, ...), custom_call_target="tpu_custom_call" | custom-call | flops 872415232 | bytes 7077888 | tf_op jit(solution)/shard_map/pallas_call | solution.py:215
  35.2 3.3 %collective-permute-start.5 = (s16[16,1664]{1,0:T(8,128)(2,1)S(1)}, s16[16,1664]{1,0:T(8,128)(2,1)S(1)}, u32[]{:S(2)}, u32[]{:S(2)}) collective-permute-start(s16[16,1664]{1,0:T(8,128)(2,1)S(1)} %get-tuple-element.56), channel_id=1, source_target_pairs={{0,24},{4,28},{8,16},{12,20},{16,8},{20,12},{24,0},{28,4},{1,25},{... | collective-permute-start | bytes 159752 | tf_op jit(solution)/shard_map/ppermute | solution.py:99
  55.8 3.8 %collective-permute-done.14 = bf16[2,4,36,128]{3,2,1,0:T(8,128)(2,1)S(1)} collective-permute-done((bf16[2,4,36,128]{3,2,1,0:T(8,128)(2,1)S(1)}, bf16[2,4,36,128]{3,2,1,0:T(8,128)(2,1)S(1)}, u32[]{:S(2)}, u32[]{:S(2)}) %collective-permute-start.14) | collective-permute-done | bytes 73760 | tf_op jit(solution)/shard_map/ppermute | solution.py:99
  62.5 3.9 %fusion.114 = (f32[4,8,16]{2,1,0:T(8,128)S(1)}, f32[4,8,16,512]{3,2,1,0:T(8,128)S(1)}) fusion(bf16[4,8,16,64]{3,2,1,0:T(8,128)(2,1)S(1)} %bitcast.82, bf16[4,8,16,64]{3,2,1,0:T(8,128)(2,1)S(1)} %bitcast.80, pred[4,512]{1,0:T(4,128)(4,1)S(1)} %iota_compare_fusion, bf16[4,512,1024]{2,1,0:T(8,128)(2,1)} %param.24), kind=kOutput, calls=%fused_computation.231 | convolution fusion | flops 68156928 | bytes 5378048 | tf_op jit(solution)/shard_map/rgqd,rlgd->rgql/dot_general | solution.py:59
  69.0 3.7 %collective-permute-done.16 = bf16[2,4,4096]{2,1,0:T(4,128)(2,1)S(1)} collective-permute-done((bf16[2,4,4096]{2,1,0:T(4,128)(2,1)S(1)}, bf16[2,4,4096]{2,1,0:T(4,128)(2,1)S(1)}, u32[]{:S(2)}, u32[]{:S(2)}) %collective-permute-start.16) | collective-permute-done | bytes 65568 | tf_op jit(solution)/shard_map/ppermute | solution.py:99
  77.2 2.9 %collective-permute-start.18 = (bf16[16,2048]{1,0:T(8,128)(2,1)S(1)}, bf16[16,2048]{1,0:T(8,128)(2,1)S(1)}, u32[]{:S(2)}, u32[]{:S(2)}) collective-permute-start(bf16[16,2048]{1,0:T(8,128)(2,1)S(1)} %pad_maximum_fusion.10.array_ref), channel_id=1, source_target_pairs={{0,16},{4,20},{8,24},{12,28},{16,0},{20,4},{24,8},{28,12},{1,17},{... | collective-permute-start | bytes 196616 | tf_op jit(solution)/shard_map/ppermute | solution.py:99
  95.4 2.9 %shard_map.147 = (f32[64,2048]{1,0:T(8,128)S(1)}, f32[64,2048]{1,0:T(8,128)S(1)}) custom-call(bf16[16,2048]{1,0:T(8,128)(2,1)S(1)} %shard_map.145.refs_0_, bf16[16,2048]{1,0:T(8,128)(2,1)S(1)} %collective-permute-done.18.refs_1_, bf16[16,2048]{1,0:T(8,128)(2,1)S(1)} %collective-permute-done.19.refs_2_, bf16[16,2048]{1,0:T(8,128)(2,1)S(1)} %collective-permute-done.20.refs_3_, ...), custom_call_target="tpu_custom_call" | custom-call | flops 2281701376 | bytes 17825792 | tf_op jit(solution)/shard_map/pallas_call | solution.py:215
  100.9 5.0 %collective-permute-done.33 = bf16[32,2048]{1,0:T(8,128)(2,1)S(1)} collective-permute-done((bf16[32,2048]{1,0:T(8,128)(2,1)S(1)}, bf16[32,2048]{1,0:T(8,128)(2,1)S(1)}, u32[]{:S(2)}, u32[]{:S(2)}) %collective-permute-start.33) | collective-permute-done | bytes 131104 | tf_op jit(solution)/shard_map/ppermute | solution.py:99
  106.7 10.5 %all_to_all.12 = f32[32,1,32]{2,1,0:T(1,128)S(1)} all-to-all(f32[32,1,32]{2,1,0:T(1,128)S(1)} %broadcast_in_dim.20), channel_id=1, replica_groups=mesh['wide'=8,'narrow'=4] {'wide','narrow'}, dimensions={0} | all-to-all | bytes 8192 | tf_op jit(solution)/shard_map/all_to_all | solution.py:405
  119.1 4.1 %shard_map.149 = (f32[64,2048]{1,0:T(8,128)S(1)}, f32[64,2048]{1,0:T(8,128)S(1)}) custom-call(bf16[64,2048]{1,0:T(8,128)(2,1)S(1)} %get-tuple-element.142.refs_0_, bf16[64,2048]{1,0:T(8,128)(2,1)S(1)} %get-tuple-element.141.refs_1_, bf16[128,128]{1,0:T(8,128)(2,1)S(1)} %get-tuple-element.145.refs_2_, bf16[2048,2048]{1,0:T(8,128)(2,1)} %refs_3_.11, ...), custom_call_target="tpu_custom_call" | custom-call | flops 1140850688 | bytes 9437184 | tf_op jit(solution)/shard_map/pallas_call | solution.py:215
  123.8 4.1 %shard_map.148 = (f32[64,2048]{1,0:T(8,128)S(1)}, f32[64,2048]{1,0:T(8,128)S(1)}) custom-call(bf16[64,2048]{1,0:T(8,128)(2,1)S(1)} %get-tuple-element.142.refs_0_, bf16[64,2048]{1,0:T(8,128)(2,1)S(1)} %get-tuple-element.141.refs_1_, bf16[128,128]{1,0:T(8,128)(2,1)S(1)} %get-tuple-element.145.refs_2_, bf16[2048,2048]{1,0:T(8,128)(2,1)} %refs_3_.11, ...), custom_call_target="tpu_custom_call" | custom-call | flops 1140850688 | bytes 9437184 | tf_op jit(solution)/shard_map/pallas_call | solution.py:215
  129.5 2.9 %collective-permute-done.43 = f16[64,2048]{1,0:T(8,128)(2,1)S(1)} collective-permute-done((f16[64,2048]{1,0:T(8,128)(2,1)S(1)}, f16[64,2048]{1,0:T(8,128)(2,1)S(1)}, u32[]{:S(2)}, u32[]{:S(2)}) %collective-permute-start.43) | collective-permute-done | bytes 262176 | tf_op jit(solution)/shard_map/ppermute | solution.py:99
  133.2 2.3 %collective-permute-start.46 = (f16[16,2048]{1,0:T(8,128)(2,1)S(1)}, f16[16,2048]{1,0:T(8,128)(2,1)S(1)}, u32[]{:S(2)}, u32[]{:S(2)}) collective-permute-start(f16[16,2048]{1,0:T(8,128)(2,1)S(1)} %get-tuple-element.98), channel_id=1, source_target_pairs={{0,24},{4,28},{8,16},{12,20},{16,8},{20,12},{24,0},{28,4},{1,25},{... | collective-permute-start | bytes 196616 | tf_op jit(solution)/shard_map/ppermute | solution.py:99
  138.0 2.3 %collective-permute-start.39 = (f16[16,2048]{1,0:T(8,128)(2,1)S(1)}, f16[16,2048]{1,0:T(8,128)(2,1)S(1)}, u32[]{:S(2)}, u32[]{:S(2)}) collective-permute-start(f16[16,2048]{1,0:T(8,128)(2,1)S(1)} %get-tuple-element.101), channel_id=1, source_target_pairs={{0,24},{4,28},{8,16},{12,20},{16,8},{20,12},{24,0},{28,4},{1,25},{... | collective-permute-start | bytes 196616 | tf_op jit(solution)/shard_map/ppermute | solution.py:99
  142.6 2.8 %collective-permute-done.37 = f16[16,2048]{1,0:T(8,128)(2,1)S(1)} collective-permute-done((f16[16,2048]{1,0:T(8,128)(2,1)S(1)}, f16[16,2048]{1,0:T(8,128)(2,1)S(1)}, u32[]{:S(2)}, u32[]{:S(2)}) %collective-permute-start.37) | collective-permute-done | bytes 65568 | tf_op jit(solution)/shard_map/ppermute | solution.py:99
  147.8 2.6 %collective-permute-done.40 = bf16[16,1024]{1,0:T(8,128)(2,1)S(1)} collective-permute-done((bf16[16,1024]{1,0:T(8,128)(2,1)S(1)}, bf16[16,1024]{1,0:T(8,128)(2,1)S(1)}, u32[]{:S(2)}, u32[]{:S(2)}) %collective-permute-start.40) | collective-permute-done | bytes 32800 | tf_op jit(solution)/shard_map/ppermute | solution.py:99
  157.9 2.6 %shard_map.150.refs_4_ = f32[128,2048]{1,0:T(8,128)S(1)} custom-call(bf16[64,1024]{1,0:T(8,128)(2,1)S(1)} %pad_maximum_fusion.5.refs_0_, bf16[64,1024]{1,0:T(8,128)(2,1)S(1)} %collective-permute-done.49.refs_1_, bf16[128,128]{1,0:T(8,128)(2,1)S(1)} %get-tuple-element.145.refs_2_, bf16[2048,2048]{1,0:T(8,128)(2,1)} %refs_3_.13), custom_call_target="tpu_custom_call" | custom-call | flops 570425344 | bytes 5242880 | tf_op jit(solution)/shard_map/pallas_call | solution.py:215
  160.6 2.6 %shard_map.151 = (f32[64,2048]{1,0:T(8,128)S(1)}, f32[64,2048]{1,0:T(8,128)S(1)}) custom-call(bf16[64,1024]{1,0:T(8,128)(2,1)S(1)} %pad_maximum_fusion.4.refs_0_, bf16[64,1024]{1,0:T(8,128)(2,1)S(1)} %collective-permute-done.42.refs_1_, bf16[128,128]{1,0:T(8,128)(2,1)S(1)} %get-tuple-element.145.refs_2_, bf16[2048,2048]{1,0:T(8,128)(2,1)} %refs_3_.13, ...), custom_call_target="tpu_custom_call" | custom-call | flops 570425344 | bytes 5242880 | tf_op jit(solution)/shard_map/pallas_call | solution.py:215
  165.8 5.0 %collective-permute-done.51 = bf16[32,2048]{1,0:T(8,128)(2,1)S(1)} collective-permute-done((bf16[32,2048]{1,0:T(8,128)(2,1)S(1)}, bf16[32,2048]{1,0:T(8,128)(2,1)S(1)}, u32[]{:S(2)}, u32[]{:S(2)}) %collective-permute-start.51) | collective-permute-done | bytes 131104 | tf_op jit(solution)/shard_map/ppermute | solution.py:99
  (217 shorter events, 79.4 us)
Async XLA Ops:
  0.0 16.7 %collective-permute-start = (bf16[32,2048]{1,0:T(8,128)(2,1)}, bf16[32,2048]{1,0:T(8,128)(2,1)S(1)}, u32[]{:S(2)}, u32[]{:S(2)}) collective-permute-start(bf16[32,2048]{1,0:T(8,128)(2,1)} %param.14), channel_id=1, source_target_pairs={{0,2},{1,3},{2,0},{3,1},{4,6},{5,7},{6,4},{7,5},{8,10},{9,11},{10,... | collective-permute-start | bytes 393224 | tf_op jit(solution)/shard_map/ppermute | solution.py:99
  4.6 12.0 %all-to-all-start = ((f32[32,1,32]{2,1,0:T(1,128)}), f32[32,1,32]{2,1,0:T(1,128)S(1)}, u32[]{:S(2)}, u32[]{:S(2)}) async-start(f32[32,1,32]{2,1,0:T(1,128)} %broadcast_in_dim.17), calls=%async_computation | async-start | bytes 32768 | tf_op jit(solution)/shard_map/all_to_all | solution.py:405
  22.8 10.3 %collective-permute-start.2 = (s16[64,1664]{1,0:T(8,128)(2,1)S(1)}, s16[64,1664]{1,0:T(8,128)(2,1)S(1)}, u32[]{:S(2)}, u32[]{:S(2)}) collective-permute-start(s16[64,1664]{1,0:T(8,128)(2,1)S(1)} %get-tuple-element.52), channel_id=1, source_target_pairs={{0,4},{4,0},{8,12},{12,8},{16,20},{20,16},{24,28},{28,24},{1,5},{5... | collective-permute-start | bytes 638984 | tf_op jit(solution)/shard_map/ppermute | solution.py:99
  31.0 8.2 %collective-permute-start.10 = (s16[64,1664]{1,0:T(8,128)(2,1)S(1)}, s16[64,1664]{1,0:T(8,128)(2,1)S(1)}, u32[]{:S(2)}, u32[]{:S(2)}) collective-permute-start(s16[64,1664]{1,0:T(8,128)(2,1)S(1)} %get-tuple-element.70), channel_id=1, source_target_pairs={{0,4},{4,0},{8,12},{12,8},{16,20},{20,16},{24,28},{28,24},{1,5},{5... | collective-permute-start | bytes 638984 | tf_op jit(solution)/shard_map/ppermute | solution.py:99
  32.6 10.2 %collective-permute-start.6 = (s16[64,1664]{1,0:T(8,128)(2,1)S(1)}, s16[64,1664]{1,0:T(8,128)(2,1)S(1)}, u32[]{:S(2)}, u32[]{:S(2)}) collective-permute-start(s16[64,1664]{1,0:T(8,128)(2,1)S(1)} %get-tuple-element.61), channel_id=1, source_target_pairs={{0,4},{4,0},{8,12},{12,8},{16,20},{20,16},{24,28},{28,24},{1,5},{5... | collective-permute-start | bytes 638984 | tf_op jit(solution)/shard_map/ppermute | solution.py:99
  34.1 10.3 %collective-permute-start.3 = (s16[16,1664]{1,0:T(8,128)(2,1)S(1)}, s16[16,1664]{1,0:T(8,128)(2,1)S(1)}, u32[]{:S(2)}, u32[]{:S(2)}) collective-permute-start(s16[16,1664]{1,0:T(8,128)(2,1)S(1)} %get-tuple-element.54), channel_id=1, source_target_pairs={{0,16},{4,20},{8,24},{12,28},{16,0},{20,4},{24,8},{28,12},{1,17},{... | collective-permute-start | bytes 159752 | tf_op jit(solution)/shard_map/ppermute | solution.py:99
  34.7 11.2 %collective-permute-start.4 = (s16[16,1664]{1,0:T(8,128)(2,1)S(1)}, s16[16,1664]{1,0:T(8,128)(2,1)S(1)}, u32[]{:S(2)}, u32[]{:S(2)}) collective-permute-start(s16[16,1664]{1,0:T(8,128)(2,1)S(1)} %get-tuple-element.55), channel_id=1, source_target_pairs={{0,8},{4,12},{8,0},{12,4},{16,24},{20,28},{24,16},{28,20},{1,9},{5... | collective-permute-start | bytes 159752 | tf_op jit(solution)/shard_map/ppermute | solution.py:99
  35.2 12.1 %collective-permute-start.5 = (s16[16,1664]{1,0:T(8,128)(2,1)S(1)}, s16[16,1664]{1,0:T(8,128)(2,1)S(1)}, u32[]{:S(2)}, u32[]{:S(2)}) collective-permute-start(s16[16,1664]{1,0:T(8,128)(2,1)S(1)} %get-tuple-element.56), channel_id=1, source_target_pairs={{0,24},{4,28},{8,16},{12,20},{16,8},{20,12},{24,0},{28,4},{1,25},{... | collective-permute-start | bytes 159752 | tf_op jit(solution)/shard_map/ppermute | solution.py:99
  40.2 8.7 %collective-permute-start.11 = (s16[16,1664]{1,0:T(8,128)(2,1)S(1)}, s16[16,1664]{1,0:T(8,128)(2,1)S(1)}, u32[]{:S(2)}, u32[]{:S(2)}) collective-permute-start(s16[16,1664]{1,0:T(8,128)(2,1)S(1)} %get-tuple-element.72), channel_id=1, source_target_pairs={{0,16},{4,20},{8,24},{12,28},{16,0},{20,4},{24,8},{28,12},{1,17},{... | collective-permute-start | bytes 159752 | tf_op jit(solution)/shard_map/ppermute | solution.py:99
  42.8 7.7 %collective-permute-start.12 = (s16[16,1664]{1,0:T(8,128)(2,1)S(1)}, s16[16,1664]{1,0:T(8,128)(2,1)S(1)}, u32[]{:S(2)}, u32[]{:S(2)}) collective-permute-start(s16[16,1664]{1,0:T(8,128)(2,1)S(1)} %get-tuple-element.73), channel_id=1, source_target_pairs={{0,8},{4,12},{8,0},{12,4},{16,24},{20,28},{24,16},{28,20},{1,9},{5... | collective-permute-start | bytes 159752 | tf_op jit(solution)/shard_map/ppermute | solution.py:99
  45.9 6.9 %collective-permute-start.7 = (s16[16,1664]{1,0:T(8,128)(2,1)S(1)}, s16[16,1664]{1,0:T(8,128)(2,1)S(1)}, u32[]{:S(2)}, u32[]{:S(2)}) collective-permute-start(s16[16,1664]{1,0:T(8,128)(2,1)S(1)} %get-tuple-element.63), channel_id=1, source_target_pairs={{0,16},{4,20},{8,24},{12,28},{16,0},{20,4},{24,8},{28,12},{1,17},{... | collective-permute-start | bytes 159752 | tf_op jit(solution)/shard_map/ppermute | solution.py:99
  74.3 6.6 %collective-permute-start.21 = (bf16[16,2048]{1,0:T(8,128)(2,1)S(1)}, bf16[16,2048]{1,0:T(8,128)(2,1)S(1)}, u32[]{:S(2)}, u32[]{:S(2)}) collective-permute-start(bf16[16,2048]{1,0:T(8,128)(2,1)S(1)} %pad_maximum_fusion.10.array_ref), channel_id=1, source_target_pairs={{0,4},{4,0},{8,12},{12,8},{16,20},{20,16},{24,28},{28,24},{1,5},{5... | collective-permute-start | bytes 196616 | tf_op jit(solution)/shard_map/ppermute | solution.py:99
  75.7 6.8 %collective-permute-start.20 = (bf16[16,2048]{1,0:T(8,128)(2,1)S(1)}, bf16[16,2048]{1,0:T(8,128)(2,1)S(1)}, u32[]{:S(2)}, u32[]{:S(2)}) collective-permute-start(bf16[16,2048]{1,0:T(8,128)(2,1)S(1)} %pad_maximum_fusion.10.array_ref), channel_id=1, source_target_pairs={{0,24},{4,28},{8,16},{12,20},{16,8},{20,12},{24,0},{28,4},{1,25},{... | collective-permute-start | bytes 196616 | tf_op jit(solution)/shard_map/ppermute | solution.py:99
  77.2 8.4 %collective-permute-start.18 = (bf16[16,2048]{1,0:T(8,128)(2,1)S(1)}, bf16[16,2048]{1,0:T(8,128)(2,1)S(1)}, u32[]{:S(2)}, u32[]{:S(2)}) collective-permute-start(bf16[16,2048]{1,0:T(8,128)(2,1)S(1)} %pad_maximum_fusion.10.array_ref), channel_id=1, source_target_pairs={{0,16},{4,20},{8,24},{12,28},{16,0},{20,4},{24,8},{28,12},{1,17},{... | collective-permute-start | bytes 196616 | tf_op jit(solution)/shard_map/ppermute | solution.py:99
  80.1 6.5 %collective-permute-start.28 = (bf16[16,2048]{1,0:T(8,128)(2,1)S(1)}, bf16[16,2048]{1,0:T(8,128)(2,1)S(1)}, u32[]{:S(2)}, u32[]{:S(2)}) collective-permute-start(bf16[16,2048]{1,0:T(8,128)(2,1)S(1)} %pad_maximum_fusion.11.array_ref), channel_id=1, source_target_pairs={{0,4},{4,0},{8,12},{12,8},{16,20},{20,16},{24,28},{28,24},{1,5},{5... | collective-permute-start | bytes 196616 | tf_op jit(solution)/shard_map/ppermute | solution.py:99
  80.9 6.9 %collective-permute-start.27 = (bf16[16,2048]{1,0:T(8,128)(2,1)S(1)}, bf16[16,2048]{1,0:T(8,128)(2,1)S(1)}, u32[]{:S(2)}, u32[]{:S(2)}) collective-permute-start(bf16[16,2048]{1,0:T(8,128)(2,1)S(1)} %pad_maximum_fusion.11.array_ref), channel_id=1, source_target_pairs={{0,24},{4,28},{8,16},{12,20},{16,8},{20,12},{24,0},{28,4},{1,25},{... | collective-permute-start | bytes 196616 | tf_op jit(solution)/shard_map/ppermute | solution.py:99
  83.0 6.9 %collective-permute-start.25 = (bf16[16,2048]{1,0:T(8,128)(2,1)S(1)}, bf16[16,2048]{1,0:T(8,128)(2,1)S(1)}, u32[]{:S(2)}, u32[]{:S(2)}) collective-permute-start(bf16[16,2048]{1,0:T(8,128)(2,1)S(1)} %pad_maximum_fusion.11.array_ref), channel_id=1, source_target_pairs={{0,16},{4,20},{8,24},{12,28},{16,0},{20,4},{24,8},{28,12},{1,17},{... | collective-permute-start | bytes 196616 | tf_op jit(solution)/shard_map/ppermute | solution.py:99
  106.1 11.2 %collective-permute-start.34 = (bf16[32,2048]{1,0:T(8,128)(2,1)S(1)}, bf16[32,2048]{1,0:T(8,128)(2,1)S(1)}, u32[]{:S(2)}, u32[]{:S(2)}) collective-permute-start(bf16[32,2048]{1,0:T(8,128)(2,1)S(1)} %get-tuple-element.88), channel_id=1, source_target_pairs={{0,2},{1,3},{2,0},{3,1},{4,6},{5,7},{6,4},{7,5},{8,10},{9,11},{10,... | collective-permute-start | bytes 393224 | tf_op jit(solution)/shard_map/ppermute | solution.py:99
  123.2 9.2 %collective-permute-start.43 = (f16[64,2048]{1,0:T(8,128)(2,1)S(1)}, f16[64,2048]{1,0:T(8,128)(2,1)S(1)}, u32[]{:S(2)}, u32[]{:S(2)}) collective-permute-start(f16[64,2048]{1,0:T(8,128)(2,1)S(1)} %convert_element_type.171), channel_id=1, source_target_pairs={{0,4},{4,0},{8,12},{12,8},{16,20},{20,16},{24,28},{28,24},{1,5},{5... | collective-permute-start | bytes 786440 | tf_op jit(solution)/shard_map/ppermute | solution.py:99
  128.0 9.3 %collective-permute-start.36 = (f16[64,2048]{1,0:T(8,128)(2,1)S(1)}, f16[64,2048]{1,0:T(8,128)(2,1)S(1)}, u32[]{:S(2)}, u32[]{:S(2)}) collective-permute-start(f16[64,2048]{1,0:T(8,128)(2,1)S(1)} %convert_element_type.165), channel_id=1, source_target_pairs={{0,4},{4,0},{8,12},{12,8},{16,20},{20,16},{24,28},{28,24},{1,5},{5... | collective-permute-start | bytes 786440 | tf_op jit(solution)/shard_map/ppermute | solution.py:99
  132.6 7.8 %collective-permute-start.44 = (f16[16,2048]{1,0:T(8,128)(2,1)S(1)}, f16[16,2048]{1,0:T(8,128)(2,1)S(1)}, u32[]{:S(2)}, u32[]{:S(2)}) collective-permute-start(f16[16,2048]{1,0:T(8,128)(2,1)S(1)} %get-tuple-element.97), channel_id=1, source_target_pairs={{0,16},{4,20},{8,24},{12,28},{16,0},{20,4},{24,8},{28,12},{1,17},{... | collective-permute-start | bytes 196616 | tf_op jit(solution)/shard_map/ppermute | solution.py:99
  133.2 7.7 %collective-permute-start.46 = (f16[16,2048]{1,0:T(8,128)(2,1)S(1)}, f16[16,2048]{1,0:T(8,128)(2,1)S(1)}, u32[]{:S(2)}, u32[]{:S(2)}) collective-permute-start(f16[16,2048]{1,0:T(8,128)(2,1)S(1)} %get-tuple-element.98), channel_id=1, source_target_pairs={{0,24},{4,28},{8,16},{12,20},{16,8},{20,12},{24,0},{28,4},{1,25},{... | collective-permute-start | bytes 196616 | tf_op jit(solution)/shard_map/ppermute | solution.py:99
  137.4 8.0 %collective-permute-start.37 = (f16[16,2048]{1,0:T(8,128)(2,1)S(1)}, f16[16,2048]{1,0:T(8,128)(2,1)S(1)}, u32[]{:S(2)}, u32[]{:S(2)}) collective-permute-start(f16[16,2048]{1,0:T(8,128)(2,1)S(1)} %get-tuple-element.100), channel_id=1, source_target_pairs={{0,16},{4,20},{8,24},{12,28},{16,0},{20,4},{24,8},{28,12},{1,17},{... | collective-permute-start | bytes 196616 | tf_op jit(solution)/shard_map/ppermute | solution.py:99
  138.0 7.3 %collective-permute-start.39 = (f16[16,2048]{1,0:T(8,128)(2,1)S(1)}, f16[16,2048]{1,0:T(8,128)(2,1)S(1)}, u32[]{:S(2)}, u32[]{:S(2)}) collective-permute-start(f16[16,2048]{1,0:T(8,128)(2,1)S(1)} %get-tuple-element.101), channel_id=1, source_target_pairs={{0,24},{4,28},{8,16},{12,20},{16,8},{20,12},{24,0},{28,4},{1,25},{... | collective-permute-start | bytes 196616 | tf_op jit(solution)/shard_map/ppermute | solution.py:99
  (39 other events, 244.7 us)

commit v7 on v6

--- a/solution.py
+++ b/solution.py
@@ -80,7 +80,7 @@
 
 
 QKV_CHUNKS = 3
-FFN_CHUNKS = 2
+FFN_SPLIT = 0.625
 CONTEXT_CHUNKS = 2
 NARROW_KINDS = [jnp.float32] + [jnp.bfloat16] * 8
 TILE = 512
@@ -284,9 +284,9 @@
     )(own, *arrived)
 
 
-def coded_scatter(kept, sent):
+def coded_scatter(kept, arrived):
     blocks = lax.axis_size("wide") // 2
-    own, *codes = fold(kept, swap(sent, "wide", 1), blocks)
+    own, *codes = fold(kept, arrived, blocks)
     offsets = offsets_of("wide")[1:blocks]
     return add_codes(own, [swap(code, "wide", o) for code, o in zip(codes, offsets)])
 
@@ -311,10 +311,11 @@
     return kept
 
 
-def gather(block, axis):
+def gather(block, axis, paired=False):
     strides = strides_of(axis)[::-1]
     for stride in strides[:-1]:
-        block = jnp.concatenate([block, swap(block, axis, stride)], axis=0)
+        held = stand_in(block) if paired else block
+        block = jnp.concatenate([held, swap(block, axis, stride)], axis=0)
     return [block, swap(block, axis, strides[-1])]
 
 
@@ -423,6 +424,7 @@
     heads = (q_cols + 2 * k_cols) // HEAD_DIM
     edges = [heads * chunk // QKV_CHUNKS for chunk in range(QKV_CHUNKS)] + [heads]
     pieces = []
+    arrivals = []
     ordered = to_hypothesis
     for chunk in range(QKV_CHUNKS):
         first, last = edges[chunk] * HEAD_DIM, edges[chunk + 1] * HEAD_DIM
@@ -433,9 +435,14 @@
             if low < high:
                 segments.append((weight, 0, low - start, high - low))
             start += columns
-        sums = project([normed], ordered, True, segments, 2, direct=True, coded=True)
-        sums, ordered = lax.optimization_barrier((sums, ordered))
-        pieces.append(coded_scatter(*sums))
+        if chunk >= 2:
+            ordered, arrivals[chunk - 2] = lax.optimization_barrier((ordered, arrivals[chunk - 2]))
+        (kept, sent), ordered = lax.optimization_barrier(
+            (project([normed], ordered, True, segments, 2, direct=True, coded=True), ordered)
+        )
+        pieces.append(kept)
+        arrivals.append(swap(sent, "wide", 1))
+    pieces = [coded_scatter(kept, arrived) for kept, arrived in zip(pieces, arrivals)]
     summed = jnp.concatenate(pieces, axis=1)
     summed = summed.reshape(narrow_count, local_rows, -1, HEAD_DIM)
     turned = exchange([summed[j] for j in range(narrow_count)], "narrow")
@@ -466,21 +473,24 @@
     resid_wide = resid.astype(jnp.float32)
     normed_two = normalized_rows(resid, ffn_gain)
 
-    f_cols = w_gate.shape[1] // FFN_CHUNKS
+    f_total = w_gate.shape[1]
+    f_edge = int(f_total * FFN_SPLIT) // LANES * LANES
     total = None
-    for chunk in range(FFN_CHUNKS):
-        segments = [(w_gate, 0, chunk * f_cols, f_cols), (w_up, 0, chunk * f_cols, f_cols)]
-        sums = wide_scatter(*project([normed_two], to_wide, False, segments, 2, direct=True))
+    for first, last in ((0, f_edge), (f_edge, f_total)):
+        f_cols = last - first
+        segments = [(w_gate, 0, first, f_cols), (w_up, 0, first, f_cols)]
+        sums, normed_two = lax.optimization_barrier(
+            (project([normed_two], to_wide, False, segments, 2, direct=True), normed_two)
+        )
+        sums = wide_scatter(*sums)
         act = (jax.nn.silu(sums[:, :f_cols]) * sums[:, f_cols:]).astype(jnp.bfloat16)
-        last = chunk == FFN_CHUNKS - 1
         total = project(
-            [gather(act, "wide")],
+            [gather(act, "wide", paired=True)],
             to_wide,
             True,
-            [(w_down, chunk * f_cols, 0, w_down.shape[1])],
-            2 if last else 1,
+            [(w_down, first, 0, w_down.shape[1])],
+            2 if last == f_total else 1,
             total if total is None else total[0],
-            direct=True,
         )
     ffn_out = narrow_scatter(*total)
     return (resid_wide + ffn_out).astype(jnp.bfloat16)

time: 172 us -> 181 us (1.052)
  waiting for transfers between devices: 55.9 us -> 67 us
  Pallas kernels: 30.8 us -> 27.5 us
    ppermute x52, waiting for transfers between devices: 51 us -> 62.1 us  [swap(): return lax.ppermute(block, axis, [(i, i ^ offset) for i in range(count)])]
    pallas_call x8, Pallas kernels: 27.4 us -> 24.1 us  [project(): pl.pallas_call(body, in_specs=specs, out_specs=[in_vmem] * split, scratch...]
  transfers between devices with their start and end apart: 53 -> 53, of which waited for: 29 -> 31; matrix products, arithmetic and copies ran while one was open for 3% -> 3% of each run, Pallas kernels for 10% -> 6%
where the time goes in v7:
time: 181 us
  waiting for transfers between devices  67 us (37%)
  starting transfers between devices  60.3 us (33%)
  Pallas kernels  27.5 us (15%)
  blocking collectives  10.6 us (6%)
  other arithmetic  7.15 us (4%)
  matrix products  5.17 us (3%)
  local copies, waits for them, and re-layouts  2.39 us (1%)
    ppermute x52, waiting for transfers between devices, swap(): return lax.ppermute(block, axis, [(i, i ^ offset) for i in range(count)])  62.1 us
    ppermute x52, starting transfers between devices, swap(): return lax.ppermute(block, axis, [(i, i ^ offset) for i in range(count)])  55.4 us
    pallas_call x8, Pallas kernels, project(): pl.pallas_call(body, in_specs=specs, out_specs=[in_vmem] * split, scratch...  24.1 us
    all_to_all x1, blocking collectives, normalized_rows(): landed = lax.all_to_all(sent, ('wide', 'narrow'), 0, 0, tiled=True)  10.6 us
    all_to_all x1, starting transfers between devices, normalized_rows(): landed = lax.all_to_all(sent, ('wide', 'narrow'), 0, 0, tiled=True)  4.92 us
    all_to_all x1, waiting for transfers between devices, normalized_rows(): landed = lax.all_to_all(sent, ('wide', 'narrow'), 0, 0, tiled=True)  4.92 us
    dot_general x1, matrix products, attend(): jnp.einsum('rgqd,rlgd->rgql', query_heads, cache_keys, preferred_element_...  3.86 us
  transfers between devices with their start and end apart: 53, of which 31 were waited for; matrix products, arithmetic and copies ran while one was open for 3% of the time, Pallas kernels for 6%

profile of v7, /device:TPU:0, one launch (start us, length us, event | category | flops | bytes accessed | tf_op | source)
XLA Modules:
  0.0 181.1 jit_solution(16912417241866139702)
XLA Ops:
  0.0 2.9 %collective-permute-start = (bf16[32,2048]{1,0:T(8,128)(2,1)}, bf16[32,2048]{1,0:T(8,128)(2,1)S(1)}, u32[]{:S(2)}, u32[]{:S(2)}) collective-permute-start(bf16[32,2048]{1,0:T(8,128)(2,1)} %param.14), channel_id=1, source_target_pairs={{0,2},{1,3},{2,0},{3,1},{4,6},{5,7},{6,4},{7,5},{8,10},{9,11},{10,... | collective-permute-start | bytes 393224 | tf_op jit(solution)/shard_map/ppermute | solution.py:99
  4.6 4.9 %all-to-all-start = ((f32[32,1,32]{2,1,0:T(1,128)}), f32[32,1,32]{2,1,0:T(1,128)S(1)}, u32[]{:S(2)}, u32[]{:S(2)}) async-start(f32[32,1,32]{2,1,0:T(1,128)} %broadcast_in_dim.17), calls=%async_computation | async-start | bytes 32768 | tf_op jit(solution)/shard_map/all_to_all | solution.py:406
  11.7 4.9 %all-to-all-done = f32[32,1,32]{2,1,0:T(1,128)S(1)} async-done(((f32[32,1,32]{2,1,0:T(1,128)}), f32[32,1,32]{2,1,0:T(1,128)S(1)}, u32[]{:S(2)}, u32[]{:S(2)}) %all-to-all-start) | async-done | bytes 4128 | tf_op jit(solution)/shard_map/all_to_all | solution.py:406
  19.2 3.6 %shard_map.136 = (f32[64,1536]{1,0:T(8,128)S(1)}, s16[64,1664]{1,0:T(8,128)(2,1)S(1)}) custom-call(bf16[64,2048]{1,0:T(8,128)(2,1)S(1)} %get-tuple-element.160.refs_0_, bf16[64,2048]{1,0:T(8,128)(2,1)S(1)} %get-tuple-element.159.refs_1_, bf16[128,128]{1,0:T(8,128)(2,1)S(1)} %get-tuple-element.76.refs_2_.refs_16_, bf16[2048,4096]{1,0:T(8,128)(2,1)} %refs_3_.9), custom_call_target="tpu_custom_call" | custom-call | flops 872415232 | bytes 7077888 | tf_op jit(solution)/shard_map/pallas_call | solution.py:215
  23.4 3.6 %shard_map.137 = (f32[64,1536]{1,0:T(8,128)S(1)}, s16[64,1664]{1,0:T(8,128)(2,1)S(1)}) custom-call(bf16[64,2048]{1,0:T(8,128)(2,1)S(1)} %get-tuple-element.160.refs_0_, bf16[64,2048]{1,0:T(8,128)(2,1)S(1)} %get-tuple-element.159.refs_1_, bf16[128,128]{1,0:T(8,128)(2,1)S(1)} %get-tuple-element.76.refs_2_.refs_16_, bf16[2048,4096]{1,0:T(8,128)(2,1)} %refs_3_.9), custom_call_target="tpu_custom_call" | custom-call | flops 872415232 | bytes 7077888 | tf_op jit(solution)/shard_map/pallas_call | solution.py:215
  30.6 3.9 %shard_map.142 = (f32[64,1536]{1,0:T(8,128)S(1)}, s16[64,1664]{1,0:T(8,128)(2,1)S(1)}) custom-call(bf16[64,2048]{1,0:T(8,128)(2,1)S(1)} %get-tuple-element.160.refs_0_, bf16[64,2048]{1,0:T(8,128)(2,1)S(1)} %get-tuple-element.159.refs_1_, bf16[128,128]{1,0:T(8,128)(2,1)S(1)} %get-tuple-element.76.refs_2_.refs_16_, bf16[2048,4096]{1,0:T(8,128)(2,1)} %refs_3_.9, ...), custom_call_target="tpu_custom_call" | custom-call | flops 872415232 | bytes 7077888 | tf_op jit(solution)/shard_map/pallas_call | solution.py:215
  36.9 3.3 %collective-permute-start.5 = (s16[16,1664]{1,0:T(8,128)(2,1)S(1)}, s16[16,1664]{1,0:T(8,128)(2,1)S(1)}, u32[]{:S(2)}, u32[]{:S(2)}) collective-permute-start(s16[16,1664]{1,0:T(8,128)(2,1)S(1)} %get-tuple-element.69), channel_id=1, source_target_pairs={{0,24},{4,28},{8,16},{12,20},{16,8},{20,12},{24,0},{28,4},{1,25},{... | collective-permute-start | bytes 159752 | tf_op jit(solution)/shard_map/ppermute | solution.py:99
  43.2 3.3 %collective-permute-start.9 = (s16[16,1664]{1,0:T(8,128)(2,1)S(1)}, s16[16,1664]{1,0:T(8,128)(2,1)S(1)}, u32[]{:S(2)}, u32[]{:S(2)}) collective-permute-start(s16[16,1664]{1,0:T(8,128)(2,1)S(1)} %get-tuple-element.75), channel_id=1, source_target_pairs={{0,24},{4,28},{8,16},{12,20},{16,8},{20,12},{24,0},{28,4},{1,25},{... | collective-permute-start | bytes 159752 | tf_op jit(solution)/shard_map/ppermute | solution.py:99
  47.7 3.3 %collective-permute-start.13 = (s16[16,1664]{1,0:T(8,128)(2,1)S(1)}, s16[16,1664]{1,0:T(8,128)(2,1)S(1)}, u32[]{:S(2)}, u32[]{:S(2)}) collective-permute-start(s16[16,1664]{1,0:T(8,128)(2,1)S(1)} %get-tuple-element.84), channel_id=1, source_target_pairs={{0,24},{4,28},{8,16},{12,20},{16,8},{20,12},{24,0},{28,4},{1,25},{... | collective-permute-start | bytes 159752 | tf_op jit(solution)/shard_map/ppermute | solution.py:99
  54.8 3.7 %collective-permute-done.14 = bf16[2,4,36,128]{3,2,1,0:T(8,128)(2,1)S(1)} collective-permute-done((bf16[2,4,36,128]{3,2,1,0:T(8,128)(2,1)S(1)}, bf16[2,4,36,128]{3,2,1,0:T(8,128)(2,1)S(1)}, u32[]{:S(2)}, u32[]{:S(2)}) %collective-permute-start.14) | collective-permute-done | bytes 73760 | tf_op jit(solution)/shard_map/ppermute | solution.py:99
  61.4 3.9 %fusion.114 = (f32[4,8,16]{2,1,0:T(8,128)S(1)}, f32[4,8,16,512]{3,2,1,0:T(8,128)S(1)}) fusion(bf16[4,8,16,64]{3,2,1,0:T(8,128)(2,1)S(1)} %bitcast.84, bf16[4,8,16,64]{3,2,1,0:T(8,128)(2,1)S(1)} %bitcast.82, pred[4,512]{1,0:T(4,128)(4,1)S(1)} %iota_compare_fusion, bf16[4,512,1024]{2,1,0:T(8,128)(2,1)} %param.24), kind=kOutput, calls=%fused_computation.231 | convolution fusion | flops 68156928 | bytes 5378048 | tf_op jit(solution)/shard_map/rgqd,rlgd->rgql/dot_general | solution.py:59
  68.0 3.6 %collective-permute-done.16 = bf16[2,4,4096]{2,1,0:T(4,128)(2,1)S(1)} collective-permute-done((bf16[2,4,4096]{2,1,0:T(4,128)(2,1)S(1)}, bf16[2,4,4096]{2,1,0:T(4,128)(2,1)S(1)}, u32[]{:S(2)}, u32[]{:S(2)}) %collective-permute-start.16) | collective-permute-done | bytes 65568 | tf_op jit(solution)/shard_map/ppermute | solution.py:99
  75.1 3.2 %collective-permute-start.20 = (bf16[16,2048]{1,0:T(8,128)(2,1)S(1)}, bf16[16,2048]{1,0:T(8,128)(2,1)S(1)}, u32[]{:S(2)}, u32[]{:S(2)}) collective-permute-start(bf16[16,2048]{1,0:T(8,128)(2,1)S(1)} %pad_maximum_fusion.11.array_ref), channel_id=1, source_target_pairs={{0,24},{4,28},{8,16},{12,20},{16,8},{20,12},{24,0},{28,4},{1,25},{... | collective-permute-start | bytes 196616 | tf_op jit(solution)/shard_map/ppermute | solution.py:99
  79.8 3.3 %collective-permute-start.27 = (bf16[16,2048]{1,0:T(8,128)(2,1)S(1)}, bf16[16,2048]{1,0:T(8,128)(2,1)S(1)}, u32[]{:S(2)}, u32[]{:S(2)}) collective-permute-start(bf16[16,2048]{1,0:T(8,128)(2,1)S(1)} %pad_maximum_fusion.12.array_ref), channel_id=1, source_target_pairs={{0,24},{4,28},{8,16},{12,20},{16,8},{20,12},{24,0},{28,4},{1,25},{... | collective-permute-start | bytes 196616 | tf_op jit(solution)/shard_map/ppermute | solution.py:99
  101.5 5.0 %collective-permute-done.33 = bf16[32,2048]{1,0:T(8,128)(2,1)S(1)} collective-permute-done((bf16[32,2048]{1,0:T(8,128)(2,1)S(1)}, bf16[32,2048]{1,0:T(8,128)(2,1)S(1)}, u32[]{:S(2)}, u32[]{:S(2)}) %collective-permute-start.33) | collective-permute-done | bytes 131104 | tf_op jit(solution)/shard_map/ppermute | solution.py:99
  107.3 10.6 %all_to_all.12 = f32[32,1,32]{2,1,0:T(1,128)S(1)} all-to-all(f32[32,1,32]{2,1,0:T(1,128)S(1)} %broadcast_in_dim.20), channel_id=1, replica_groups=mesh['wide'=8,'narrow'=4] {'wide','narrow'}, dimensions={0} | all-to-all | bytes 8192 | tf_op jit(solution)/shard_map/all_to_all | solution.py:406
  119.8 4.8 %shard_map.148 = (f32[64,2560]{1,0:T(8,128)S(1)}, f32[64,2560]{1,0:T(8,128)S(1)}) custom-call(bf16[64,2048]{1,0:T(8,128)(2,1)S(1)} %get-tuple-element.89.refs_0_, bf16[64,2048]{1,0:T(8,128)(2,1)S(1)} %get-tuple-element.90.refs_1_, bf16[128,128]{1,0:T(8,128)(2,1)S(1)} %get-tuple-element.161.refs_2_, bf16[2048,2048]{1,0:T(8,128)(2,1)} %refs_3_.11, ...), custom_call_target="tpu_custom_call" | custom-call | flops 1409286144 | bytes 11796480 | tf_op jit(solution)/shard_map/pallas_call | solution.py:215
  124.6 3.6 %shard_map.149 = (f32[64,1536]{1,0:T(8,128)S(1)}, f32[64,1536]{1,0:T(8,128)S(1)}) custom-call(bf16[64,2048]{1,0:T(8,128)(2,1)S(1)} %get-tuple-element.89.refs_0_, bf16[64,2048]{1,0:T(8,128)(2,1)S(1)} %get-tuple-element.90.refs_1_, bf16[128,128]{1,0:T(8,128)(2,1)S(1)} %get-tuple-element.161.refs_2_, bf16[2048,2048]{1,0:T(8,128)(2,1)} %refs_3_.11, ...), custom_call_target="tpu_custom_call" | custom-call | flops 872415232 | bytes 7077888 | tf_op jit(solution)/shard_map/pallas_call | solution.py:215
  128.8 6.4 %collective-permute-done.36 = f16[64,1536]{1,0:T(8,128)(2,1)S(1)} collective-permute-done((f16[64,1536]{1,0:T(8,128)(2,1)S(1)}, f16[64,1536]{1,0:T(8,128)(2,1)S(1)}, u32[]{:S(2)}, u32[]{:S(2)}) %collective-permute-start.36) | collective-permute-done | bytes 196640 | tf_op jit(solution)/shard_map/ppermute | solution.py:99
  143.1 4.0 %collective-permute-done.43 = f16[64,2560]{1,0:T(8,128)(2,1)S(1)} collective-permute-done((f16[64,2560]{1,0:T(8,128)(2,1)S(1)}, f16[64,2560]{1,0:T(8,128)(2,1)S(1)}, u32[]{:S(2)}, u32[]{:S(2)}) %collective-permute-start.43) | collective-permute-done | bytes 327712 | tf_op jit(solution)/shard_map/ppermute | solution.py:99
  156.6 4.4 %collective-permute-done.47 = bf16[16,1280]{1,0:T(8,128)(2,1)S(1)} collective-permute-done((bf16[16,1280]{1,0:T(8,128)(2,1)S(1)}, bf16[16,1280]{1,0:T(8,128)(2,1)S(1)}, u32[]{:S(2)}, u32[]{:S(2)}) %collective-permute-start.47) | collective-permute-done | bytes 40992 | tf_op jit(solution)/shard_map/ppermute | solution.py:99
  162.0 3.4 %collective-permute-done.48 = bf16[32,1280]{1,0:T(8,128)(2,1)S(1)} collective-permute-done((bf16[32,1280]{1,0:T(8,128)(2,1)S(1)}, bf16[32,1280]{1,0:T(8,128)(2,1)S(1)}, u32[]{:S(2)}, u32[]{:S(2)}) %collective-permute-start.48) | collective-permute-done | bytes 81952 | tf_op jit(solution)/shard_map/ppermute | solution.py:99
  167.7 3.2 %collective-permute-done.49.refs_1_ = bf16[64,1280]{1,0:T(8,128)(2,1)S(1)} collective-permute-done((bf16[64,1280]{1,0:T(8,128)(2,1)S(1)}, bf16[64,1280]{1,0:T(8,128)(2,1)S(1)}, u32[]{:S(2)}, u32[]{:S(2)}) %collective-permute-start.49) | collective-permute-done | bytes 163872 | tf_op jit(solution)/shard_map/ppermute | solution.py:99
  175.3 5.0 %collective-permute-done.51 = bf16[32,2048]{1,0:T(8,128)(2,1)S(1)} collective-permute-done((bf16[32,2048]{1,0:T(8,128)(2,1)S(1)}, bf16[32,2048]{1,0:T(8,128)(2,1)S(1)}, u32[]{:S(2)}, u32[]{:S(2)}) %collective-permute-start.51) | collective-permute-done | bytes 131104 | tf_op jit(solution)/shard_map/ppermute | solution.py:99
  (226 shorter events, 78.2 us)
Async XLA Ops:
  0.0 16.7 %collective-permute-start = (bf16[32,2048]{1,0:T(8,128)(2,1)}, bf16[32,2048]{1,0:T(8,128)(2,1)S(1)}, u32[]{:S(2)}, u32[]{:S(2)}) collective-permute-start(bf16[32,2048]{1,0:T(8,128)(2,1)} %param.14), channel_id=1, source_target_pairs={{0,2},{1,3},{2,0},{3,1},{4,6},{5,7},{6,4},{7,5},{8,10},{9,11},{10,... | collective-permute-start | bytes 393224 | tf_op jit(solution)/shard_map/ppermute | solution.py:99
  4.6 12.0 %all-to-all-start = ((f32[32,1,32]{2,1,0:T(1,128)}), f32[32,1,32]{2,1,0:T(1,128)S(1)}, u32[]{:S(2)}, u32[]{:S(2)}) async-start(f32[32,1,32]{2,1,0:T(1,128)} %broadcast_in_dim.17), calls=%async_computation | async-start | bytes 32768 | tf_op jit(solution)/shard_map/all_to_all | solution.py:406
  22.8 7.7 %collective-permute-start.2 = (s16[64,1664]{1,0:T(8,128)(2,1)S(1)}, s16[64,1664]{1,0:T(8,128)(2,1)S(1)}, u32[]{:S(2)}, u32[]{:S(2)}) collective-permute-start(s16[64,1664]{1,0:T(8,128)(2,1)S(1)} %get-tuple-element.64), channel_id=1, source_target_pairs={{0,4},{4,0},{8,12},{12,8},{16,20},{20,16},{24,28},{28,24},{1,5},{5... | collective-permute-start | bytes 638984 | tf_op jit(solution)/shard_map/ppermute | solution.py:99
  27.1 13.1 %collective-permute-start.6 = (s16[64,1664]{1,0:T(8,128)(2,1)S(1)}, s16[64,1664]{1,0:T(8,128)(2,1)S(1)}, u32[]{:S(2)}, u32[]{:S(2)}) collective-permute-start(s16[64,1664]{1,0:T(8,128)(2,1)S(1)} %get-tuple-element.71), channel_id=1, source_target_pairs={{0,4},{4,0},{8,12},{12,8},{16,20},{20,16},{24,28},{28,24},{1,5},{5... | collective-permute-start | bytes 638984 | tf_op jit(solution)/shard_map/ppermute | solution.py:99
  34.5 6.7 %collective-permute-start.10 = (s16[64,1664]{1,0:T(8,128)(2,1)S(1)}, s16[64,1664]{1,0:T(8,128)(2,1)S(1)}, u32[]{:S(2)}, u32[]{:S(2)}) collective-permute-start(s16[64,1664]{1,0:T(8,128)(2,1)S(1)} %get-tuple-element.80), channel_id=1, source_target_pairs={{0,4},{4,0},{8,12},{12,8},{16,20},{20,16},{24,28},{28,24},{1,5},{5... | collective-permute-start | bytes 638984 | tf_op jit(solution)/shard_map/ppermute | solution.py:99
  35.7 7.5 %collective-permute-start.3 = (s16[16,1664]{1,0:T(8,128)(2,1)S(1)}, s16[16,1664]{1,0:T(8,128)(2,1)S(1)}, u32[]{:S(2)}, u32[]{:S(2)}) collective-permute-start(s16[16,1664]{1,0:T(8,128)(2,1)S(1)} %get-tuple-element.67), channel_id=1, source_target_pairs={{0,16},{4,20},{8,24},{12,28},{16,0},{20,4},{24,8},{28,12},{1,17},{... | collective-permute-start | bytes 159752 | tf_op jit(solution)/shard_map/ppermute | solution.py:99
  36.3 10.3 %collective-permute-start.4 = (s16[16,1664]{1,0:T(8,128)(2,1)S(1)}, s16[16,1664]{1,0:T(8,128)(2,1)S(1)}, u32[]{:S(2)}, u32[]{:S(2)}) collective-permute-start(s16[16,1664]{1,0:T(8,128)(2,1)S(1)} %get-tuple-element.68), channel_id=1, source_target_pairs={{0,8},{4,12},{8,0},{12,4},{16,24},{20,28},{24,16},{28,20},{1,9},{5... | collective-permute-start | bytes 159752 | tf_op jit(solution)/shard_map/ppermute | solution.py:99
  36.9 9.7 %collective-permute-start.5 = (s16[16,1664]{1,0:T(8,128)(2,1)S(1)}, s16[16,1664]{1,0:T(8,128)(2,1)S(1)}, u32[]{:S(2)}, u32[]{:S(2)}) collective-permute-start(s16[16,1664]{1,0:T(8,128)(2,1)S(1)} %get-tuple-element.69), channel_id=1, source_target_pairs={{0,24},{4,28},{8,16},{12,20},{16,8},{20,12},{24,0},{28,4},{1,25},{... | collective-permute-start | bytes 159752 | tf_op jit(solution)/shard_map/ppermute | solution.py:99
  41.1 6.6 %collective-permute-start.7 = (s16[16,1664]{1,0:T(8,128)(2,1)S(1)}, s16[16,1664]{1,0:T(8,128)(2,1)S(1)}, u32[]{:S(2)}, u32[]{:S(2)}) collective-permute-start(s16[16,1664]{1,0:T(8,128)(2,1)S(1)} %get-tuple-element.73), channel_id=1, source_target_pairs={{0,16},{4,20},{8,24},{12,28},{16,0},{20,4},{24,8},{28,12},{1,17},{... | collective-permute-start | bytes 159752 | tf_op jit(solution)/shard_map/ppermute | solution.py:99
  41.2 10.0 %collective-permute-start.8 = (s16[16,1664]{1,0:T(8,128)(2,1)S(1)}, s16[16,1664]{1,0:T(8,128)(2,1)S(1)}, u32[]{:S(2)}, u32[]{:S(2)}) collective-permute-start(s16[16,1664]{1,0:T(8,128)(2,1)S(1)} %get-tuple-element.74), channel_id=1, source_target_pairs={{0,8},{4,12},{8,0},{12,4},{16,24},{20,28},{24,16},{28,20},{1,9},{5... | collective-permute-start | bytes 159752 | tf_op jit(solution)/shard_map/ppermute | solution.py:99
  43.2 8.0 %collective-permute-start.9 = (s16[16,1664]{1,0:T(8,128)(2,1)S(1)}, s16[16,1664]{1,0:T(8,128)(2,1)S(1)}, u32[]{:S(2)}, u32[]{:S(2)}) collective-permute-start(s16[16,1664]{1,0:T(8,128)(2,1)S(1)} %get-tuple-element.75), channel_id=1, source_target_pairs={{0,24},{4,28},{8,16},{12,20},{16,8},{20,12},{24,0},{28,4},{1,25},{... | collective-permute-start | bytes 159752 | tf_op jit(solution)/shard_map/ppermute | solution.py:99
  73.2 6.6 %collective-permute-start.21 = (bf16[16,2048]{1,0:T(8,128)(2,1)S(1)}, bf16[16,2048]{1,0:T(8,128)(2,1)S(1)}, u32[]{:S(2)}, u32[]{:S(2)}) collective-permute-start(bf16[16,2048]{1,0:T(8,128)(2,1)S(1)} %pad_maximum_fusion.11.array_ref), channel_id=1, source_target_pairs={{0,4},{4,0},{8,12},{12,8},{16,20},{20,16},{24,28},{28,24},{1,5},{5... | collective-permute-start | bytes 196616 | tf_op jit(solution)/shard_map/ppermute | solution.py:99
  75.1 7.9 %collective-permute-start.20 = (bf16[16,2048]{1,0:T(8,128)(2,1)S(1)}, bf16[16,2048]{1,0:T(8,128)(2,1)S(1)}, u32[]{:S(2)}, u32[]{:S(2)}) collective-permute-start(bf16[16,2048]{1,0:T(8,128)(2,1)S(1)} %pad_maximum_fusion.11.array_ref), channel_id=1, source_target_pairs={{0,24},{4,28},{8,16},{12,20},{16,8},{20,12},{24,0},{28,4},{1,25},{... | collective-permute-start | bytes 196616 | tf_op jit(solution)/shard_map/ppermute | solution.py:99
  78.3 8.4 %collective-permute-start.18 = (bf16[16,2048]{1,0:T(8,128)(2,1)S(1)}, bf16[16,2048]{1,0:T(8,128)(2,1)S(1)}, u32[]{:S(2)}, u32[]{:S(2)}) collective-permute-start(bf16[16,2048]{1,0:T(8,128)(2,1)S(1)} %pad_maximum_fusion.11.array_ref), channel_id=1, source_target_pairs={{0,16},{4,20},{8,24},{12,28},{16,0},{20,4},{24,8},{28,12},{1,17},{... | collective-permute-start | bytes 196616 | tf_op jit(solution)/shard_map/ppermute | solution.py:99
  79.5 7.3 %collective-permute-start.28 = (bf16[16,2048]{1,0:T(8,128)(2,1)S(1)}, bf16[16,2048]{1,0:T(8,128)(2,1)S(1)}, u32[]{:S(2)}, u32[]{:S(2)}) collective-permute-start(bf16[16,2048]{1,0:T(8,128)(2,1)S(1)} %pad_maximum_fusion.12.array_ref), channel_id=1, source_target_pairs={{0,4},{4,0},{8,12},{12,8},{16,20},{20,16},{24,28},{28,24},{1,5},{5... | collective-permute-start | bytes 196616 | tf_op jit(solution)/shard_map/ppermute | solution.py:99
  79.8 9.2 %collective-permute-start.27 = (bf16[16,2048]{1,0:T(8,128)(2,1)S(1)}, bf16[16,2048]{1,0:T(8,128)(2,1)S(1)}, u32[]{:S(2)}, u32[]{:S(2)}) collective-permute-start(bf16[16,2048]{1,0:T(8,128)(2,1)S(1)} %pad_maximum_fusion.12.array_ref), channel_id=1, source_target_pairs={{0,24},{4,28},{8,16},{12,20},{16,8},{20,12},{24,0},{28,4},{1,25},{... | collective-permute-start | bytes 196616 | tf_op jit(solution)/shard_map/ppermute | solution.py:99
  83.3 7.6 %collective-permute-start.25 = (bf16[16,2048]{1,0:T(8,128)(2,1)S(1)}, bf16[16,2048]{1,0:T(8,128)(2,1)S(1)}, u32[]{:S(2)}, u32[]{:S(2)}) collective-permute-start(bf16[16,2048]{1,0:T(8,128)(2,1)S(1)} %pad_maximum_fusion.12.array_ref), channel_id=1, source_target_pairs={{0,16},{4,20},{8,24},{12,28},{16,0},{20,4},{24,8},{28,12},{1,17},{... | collective-permute-start | bytes 196616 | tf_op jit(solution)/shard_map/ppermute | solution.py:99
  86.8 6.2 %collective-permute-start.23 = (bf16[16,2048]{1,0:T(8,128)(2,1)S(1)}, bf16[16,2048]{1,0:T(8,128)(2,1)S(1)}, u32[]{:S(2)}, u32[]{:S(2)}) collective-permute-start(bf16[16,2048]{1,0:T(8,128)(2,1)S(1)} %collective-permute-done.19.refs_2_), channel_id=1, source_target_pairs={{0,4},{4,0},{8,12},{12,8},{16,20},{20,16},{24,28},{28,24},{1,5},{5... | collective-permute-start | bytes 196616 | tf_op jit(solution)/shard_map/ppermute | solution.py:99
  106.7 11.2 %collective-permute-start.34 = (bf16[32,2048]{1,0:T(8,128)(2,1)S(1)}, bf16[32,2048]{1,0:T(8,128)(2,1)S(1)}, u32[]{:S(2)}, u32[]{:S(2)}) collective-permute-start(bf16[32,2048]{1,0:T(8,128)(2,1)S(1)} %get-tuple-element.104), channel_id=1, source_target_pairs={{0,2},{1,3},{2,0},{3,1},{4,6},{5,7},{6,4},{7,5},{8,10},{9,11},{10,... | collective-permute-start | bytes 393224 | tf_op jit(solution)/shard_map/ppermute | solution.py:99
  128.2 7.0 %collective-permute-start.36 = (f16[64,1536]{1,0:T(8,128)(2,1)S(1)}, f16[64,1536]{1,0:T(8,128)(2,1)S(1)}, u32[]{:S(2)}, u32[]{:S(2)}) collective-permute-start(f16[64,1536]{1,0:T(8,128)(2,1)S(1)} %convert_element_type.165), channel_id=1, source_target_pairs={{0,4},{4,0},{8,12},{12,8},{16,20},{20,16},{24,28},{28,24},{1,5},{5... | collective-permute-start | bytes 589832 | tf_op jit(solution)/shard_map/ppermute | solution.py:99
  138.9 8.2 %collective-permute-start.43 = (f16[64,2560]{1,0:T(8,128)(2,1)S(1)}, f16[64,2560]{1,0:T(8,128)(2,1)S(1)}, u32[]{:S(2)}, u32[]{:S(2)}) collective-permute-start(f16[64,2560]{1,0:T(8,128)(2,1)S(1)} %convert_element_type.171), channel_id=1, source_target_pairs={{0,4},{4,0},{8,12},{12,8},{16,20},{20,16},{24,28},{28,24},{1,5},{5... | collective-permute-start | bytes 983048 | tf_op jit(solution)/shard_map/ppermute | solution.py:99
  142.6 8.6 %collective-permute-start.40 = (bf16[16,768]{1,0:T(8,128)(2,1)S(1)}, bf16[16,768]{1,0:T(8,128)(2,1)S(1)}, u32[]{:S(2)}, u32[]{:S(2)}) collective-permute-start(bf16[16,768]{1,0:T(8,128)(2,1)S(1)} %fusion.76.array_ref), channel_id=1, source_target_pairs={{0,16},{4,20},{8,24},{12,28},{16,0},{20,4},{24,8},{28,12},{1,17},{... | collective-permute-start | bytes 73736 | tf_op jit(solution)/shard_map/ppermute | solution.py:99
  148.8 6.3 %collective-permute-start.46 = (f16[16,2560]{1,0:T(8,128)(2,1)S(1)}, f16[16,2560]{1,0:T(8,128)(2,1)S(1)}, u32[]{:S(2)}, u32[]{:S(2)}) collective-permute-start(f16[16,2560]{1,0:T(8,128)(2,1)S(1)} %get-tuple-element.112), channel_id=1, source_target_pairs={{0,24},{4,28},{8,16},{12,20},{16,8},{20,12},{24,0},{28,4},{1,25},{... | collective-permute-start | bytes 245768 | tf_op jit(solution)/shard_map/ppermute | solution.py:99
  151.1 15.0 %collective-permute-start.41 = (bf16[32,768]{1,0:T(8,128)(2,1)S(1)}, bf16[32,768]{1,0:T(8,128)(2,1)S(1)}, u32[]{:S(2)}, u32[]{:S(2)}) collective-permute-start(bf16[32,768]{1,0:T(8,128)(2,1)S(1)} %pad_maximum_fusion.13.array_ref), channel_id=1, source_target_pairs={{0,8},{4,12},{8,0},{12,4},{16,24},{20,28},{24,16},{28,20},{1,9},{5... | collective-permute-start | bytes 147464 | tf_op jit(solution)/shard_map/ppermute | solution.py:99
  (41 other events, 260.6 us)

commit v8 on v7

--- a/solution.py
+++ b/solution.py
@@ -24,63 +24,8 @@
     return (scaled * gain_row[None, :]).astype(jnp.bfloat16)
 
 
-def rotate(head_rows, lengths):
-    head_size = head_rows.shape[-1]
-    half_size = head_size // 2
-    inverse_freq = jnp.exp(
-        jnp.arange(half_size, dtype=jnp.float32) * (-2.0 * math.log(ROPE_BASE) / head_size)
-    )
-    angles = lengths.astype(jnp.float32)[:, None] * inverse_freq[None, :]
-    cos_part = jnp.cos(angles)[:, None, :]
-    sin_part = jnp.sin(angles)[:, None, :]
-    front_half = head_rows[..., :half_size].astype(jnp.float32)
-    back_half = head_rows[..., half_size:].astype(jnp.float32)
-    turned = jnp.concatenate(
-        [
-            front_half * cos_part - back_half * sin_part,
-            back_half * cos_part + front_half * sin_part,
-        ],
-        axis=-1,
-    )
-    return turned.astype(jnp.bfloat16)
-
-
-def attend(queries, fresh_key, fresh_value, key_cache, value_cache, lengths):
-    row_count, length, kv_width = key_cache.shape
-    groups = kv_width // HEAD_DIM
-    group_size = queries.shape[1] // kv_width
-    score_scale = 1.0 / math.sqrt(HEAD_DIM)
-    query_heads = queries.reshape(row_count, groups, group_size, HEAD_DIM)
-    cache_keys = key_cache.reshape(row_count, length, groups, HEAD_DIM)
-    cache_values = value_cache.reshape(row_count, length, groups, HEAD_DIM)
-    own_key = fresh_key.reshape(row_count, groups, HEAD_DIM)
-    own_value = fresh_value.reshape(row_count, groups, HEAD_DIM)
-    scores = (
-        jnp.einsum("rgqd,rlgd->rgql", query_heads, cache_keys, preferred_element_type=jnp.float32)
-        * score_scale
-    )
-    own_score = (
-        jnp.einsum("rgqd,rgd->rgq", query_heads, own_key, preferred_element_type=jnp.float32)
-        * score_scale
-    )
-    valid_pos = jnp.arange(length, dtype=jnp.int32)[None, :] < lengths[:, None]
-    scores = jnp.where(valid_pos[:, None, None, :], scores, -jnp.inf)
-    row_max = jnp.maximum(jnp.max(scores, axis=3), own_score)
-    weights = jnp.exp(scores - row_max[..., None])
-    own_weight = jnp.exp(own_score - row_max)
-    weight_sum = jnp.sum(weights, axis=3) + own_weight
-    probs = (weights / weight_sum[..., None]).astype(jnp.bfloat16)
-    own_prob = (own_weight / weight_sum).astype(jnp.bfloat16)
-    context = jnp.einsum("rgql,rlgd->rgqd", probs, cache_values, preferred_element_type=jnp.float32)
-    context = (
-        context
-        + own_prob.astype(jnp.float32)[..., None] * own_value.astype(jnp.float32)[:, :, None, :]
-    )
-    return context.reshape(row_count, groups * group_size * HEAD_DIM).astype(jnp.bfloat16)
-
-
 QKV_CHUNKS = 3
-FFN_SPLIT = 0.625
+FFN_SPLIT = 0.5
 CONTEXT_CHUNKS = 2
 NARROW_KINDS = [jnp.float32] + [jnp.bfloat16] * 8
 TILE = 512
@@ -109,6 +54,77 @@
     for stride in reversed(strides_of(axis)):
         order = order + [offset ^ stride for offset in order]
     return order
+
+
+def attend(queries, fresh, key_cache, value_cache, lengths, me):
+    count, row_count, heads, _ = queries.shape
+    groups = fresh.shape[2] // 2
+    group_size = heads // groups
+    length = key_cache.shape[1]
+    half_size = HEAD_DIM // 2
+    score_scale = 1.0 / math.sqrt(HEAD_DIM)
+    inverse_freq = jnp.exp(
+        jnp.arange(half_size, dtype=jnp.float32) * (-2.0 * math.log(ROPE_BASE) / HEAD_DIM)
+    )
+    angles = lengths.astype(jnp.float32)[:, None] * inverse_freq[None, :]
+    cosines = jnp.concatenate([jnp.cos(angles)] * 2, axis=1)
+    sines = jnp.concatenate([-jnp.sin(angles), jnp.sin(angles)], axis=1)
+
+    def body(me_ref, length_ref, query_ref, fresh_ref, cos_ref, sin_ref, key_ref, value_ref, out_ref):
+        places = lax.broadcasted_iota(jnp.int32, (group_size, length), 1)
+        for row in range(row_count):
+            cos_row, sin_row = cos_ref[row : row + 1, :], sin_ref[row : row + 1, :]
+            valid = places < length_ref[row]
+
+            def turn(values):
+                turned = values * cos_row + pltpu.roll(values, half_size, 1) * sin_row
+                return turned.astype(jnp.bfloat16)
+
+            for offset in range(count):
+                fresh_rows = fresh_ref[offset, row]
+                own_keys = turn(jnp.concatenate([fresh_rows] * (8 // (2 * groups)), axis=0))
+                for group in range(groups):
+                    heads_of = slice(group * group_size, (group + 1) * group_size)
+                    query = turn(query_ref[offset, row, heads_of, :].astype(jnp.float32))
+                    first = ((me_ref[0] ^ offset) * groups + group) * HEAD_DIM
+                    columns = pl.ds(pl.multiple_of(first, HEAD_DIM), HEAD_DIM)
+                    scores = lax.dot_general(
+                        query,
+                        key_ref[row, :, columns],
+                        (((1,), (1,)), ((), ())),
+                        preferred_element_type=jnp.float32,
+                    )
+                    scores = jnp.where(valid, scores * score_scale, -jnp.inf)
+                    own_key = own_keys[group : group + 1].astype(jnp.float32)
+                    own_score = jnp.sum(query.astype(jnp.float32) * own_key, axis=1, keepdims=True)
+                    own_score = own_score * score_scale
+                    row_max = jnp.maximum(jnp.max(scores, axis=1, keepdims=True), own_score)
+                    weights = jnp.exp(scores - row_max)
+                    own_weight = jnp.exp(own_score - row_max)
+                    weight_sum = jnp.sum(weights, axis=1, keepdims=True) + own_weight
+                    probs = (weights / weight_sum).astype(jnp.bfloat16)
+                    own_prob = (own_weight / weight_sum).astype(jnp.bfloat16).astype(jnp.float32)
+                    context = jnp.dot(
+                        probs, value_ref[row, :, columns], preferred_element_type=jnp.float32
+                    )
+                    own_value = fresh_rows[groups + group : groups + group + 1]
+                    context = context + own_prob * own_value
+                    out_ref[offset, row, heads_of, :] = context.astype(jnp.bfloat16)
+
+    in_vmem = pl.BlockSpec(memory_space=pltpu.VMEM)
+    in_smem = pl.BlockSpec(memory_space=pltpu.SMEM)
+    return pl.pallas_call(
+        body,
+        in_specs=[in_smem, in_smem] + [in_vmem] * 6,
+        out_specs=in_vmem,
+        out_shape=jax.ShapeDtypeStruct(queries.shape, jnp.bfloat16),
+        compiler_params=pltpu.CompilerParams(vmem_limit_bytes=ROOM * MIB),
+        cost_estimate=pl.CostEstimate(
+            flops=4 * queries.size * length,
+            bytes_accessed=4 * key_cache.size,
+            transcendentals=queries.size * length // HEAD_DIM,
+        ),
+    )(me[None], lengths, queries, fresh, cosines, sines, key_cache, value_cache)
 
 
 def encoded(values):
@@ -445,21 +461,18 @@
     pieces = [coded_scatter(kept, arrived) for kept, arrived in zip(pieces, arrivals)]
     summed = jnp.concatenate(pieces, axis=1)
     summed = summed.reshape(narrow_count, local_rows, -1, HEAD_DIM)
-    turned = exchange([summed[j] for j in range(narrow_count)], "narrow")
-    turned = jnp.stack(by_rank(turned, flags), axis=1)
+    turned = jnp.stack(exchange([summed[j] for j in range(narrow_count)], "narrow"))
     q_heads = q_cols // HEAD_DIM
-    k_heads = k_cols // HEAD_DIM
-    query_rot = rotate(
-        turned[:, :, :q_heads].reshape(local_rows, -1, HEAD_DIM), cache_len
-    ).reshape(local_rows, -1)
-    key_rot = rotate(
-        turned[:, :, q_heads : q_heads + k_heads].reshape(local_rows, -1, HEAD_DIM), cache_len
-    ).reshape(local_rows, -1)
-    value_new = turned[:, :, q_heads + k_heads :].reshape(local_rows, -1)
-    context = attend(query_rot, key_rot, value_new, key_cache, value_cache, cache_len)
-    context = context.reshape(local_rows, narrow_count, -1)
-    context = by_rank([context[:, j] for j in range(narrow_count)], flags)
-    by_heads = exchange(context, "narrow")
+    context = attend(
+        turned[:, :, :q_heads],
+        turned[:, :, q_heads:].astype(jnp.float32),
+        key_cache,
+        value_cache,
+        cache_len,
+        me_narrow,
+    )
+    context = context.reshape(narrow_count, local_rows, -1)
+    by_heads = exchange([context[j] for j in range(narrow_count)], "narrow")
 
     depth = w_out.shape[0] // CONTEXT_CHUNKS
     groups = []
@@ -479,10 +492,7 @@
     for first, last in ((0, f_edge), (f_edge, f_total)):
         f_cols = last - first
         segments = [(w_gate, 0, first, f_cols), (w_up, 0, first, f_cols)]
-        sums, normed_two = lax.optimization_barrier(
-            (project([normed_two], to_wide, False, segments, 2, direct=True), normed_two)
-        )
-        sums = wide_scatter(*sums)
+        sums = wide_scatter(*project([normed_two], to_wide, False, segments, 2, direct=True))
         act = (jax.nn.silu(sums[:, :f_cols]) * sums[:, f_cols:]).astype(jnp.bfloat16)
         total = project(
             [gather(act, "wide", paired=True)],

time: 181 us -> 178 us (0.983)
  waiting for transfers between devices: 67 us -> 55.3 us
  Pallas kernels: 27.5 us -> 38.2 us
  matrix products: 5.17 us -> 0 us
  local copies, waits for them, and re-layouts: 2.39 us -> 6.44 us
    ppermute x52, waiting for transfers between devices: 62.1 us -> 50.3 us  [swap(): return lax.ppermute(block, axis, [(i, i ^ offset) for i in range(count)])]
    pallas_call x0 -> x1, Pallas kernels: none -> 11.1 us  [attend(): pl.pallas_call(body, in_specs=[in_smem, in_smem] + [in_vmem] * 6, out_spe...]
    dot_general x3 -> x0, matrix products: 5.17 us -> none  [the longest x1 3.86 us: attend(): jnp.einsum('rgqd,rlgd->rgql', query_heads, cache_keys, preferred_element_...]
    unnamed x25 -> x29, local copies, waits for them, and re-layouts: 0.98 us -> 5.37 us
  transfers between devices with their start and end apart: 53 -> 53, of which waited for: 31 -> 30; matrix products, arithmetic and copies ran while one was open for 3% -> 3% of each run, Pallas kernels for 6% -> 9%
where the time goes in v8:
time: 178 us
  starting transfers between devices  61.3 us (34%)
  waiting for transfers between devices  55.3 us (31%)
  Pallas kernels  38.2 us (21%)
  blocking collectives  10.6 us (6%)
  local copies, waits for them, and re-layouts  6.44 us (4%)
  other arithmetic  5.41 us (3%)
    ppermute x52, starting transfers between devices, swap(): return lax.ppermute(block, axis, [(i, i ^ offset) for i in range(count)])  56.3 us
    ppermute x52, waiting for transfers between devices, swap(): return lax.ppermute(block, axis, [(i, i ^ offset) for i in range(count)])  50.3 us
    pallas_call x8, Pallas kernels, project(): pl.pallas_call(body, in_specs=specs, out_specs=[in_vmem] * split, scratch...  23.7 us
    pallas_call x1, Pallas kernels, attend(): pl.pallas_call(body, in_specs=[in_smem, in_smem] + [in_vmem] * 6, out_spe...  11.1 us
    all_to_all x1, blocking collectives, normalized_rows(): landed = lax.all_to_all(sent, ('wide', 'narrow'), 0, 0, tiled=True)  10.6 us
    unnamed x29, local copies, waits for them, and re-layouts  5.37 us
    all_to_all x1, waiting for transfers between devices, normalized_rows(): landed = lax.all_to_all(sent, ('wide', 'narrow'), 0, 0, tiled=True)  4.98 us
    all_to_all x1, starting transfers between devices, normalized_rows(): landed = lax.all_to_all(sent, ('wide', 'narrow'), 0, 0, tiled=True)  4.92 us
  transfers between devices with their start and end apart: 53, of which 30 were waited for; matrix products, arithmetic and copies ran while one was open for 3% of the time, Pallas kernels for 9%

profile of v8, /device:TPU:0, one launch (start us, length us, event | category | flops | bytes accessed | tf_op | source)
XLA Modules:
  0.0 177.9 jit_solution(17946371994447280078)
XLA Ops:
  0.0 2.9 %collective-permute-start = (bf16[32,2048]{1,0:T(8,128)(2,1)}, bf16[32,2048]{1,0:T(8,128)(2,1)S(1)}, u32[]{:S(2)}, u32[]{:S(2)}) collective-permute-start(bf16[32,2048]{1,0:T(8,128)(2,1)} %param.14), channel_id=1, source_target_pairs={{0,2},{1,3},{2,0},{3,1},{4,6},{5,7},{6,4},{7,5},{8,10},{9,11},{10,... | collective-permute-start | bytes 393224 | tf_op jit(solution)/shard_map/ppermute | solution.py:44
  4.6 4.9 %all-to-all-start = ((f32[32,1,32]{2,1,0:T(1,128)}), f32[32,1,32]{2,1,0:T(1,128)S(1)}, u32[]{:S(2)}, u32[]{:S(2)}) async-start(f32[32,1,32]{2,1,0:T(1,128)} %broadcast_in_dim.11), calls=%async_computation | async-start | bytes 32768 | tf_op jit(solution)/shard_map/all_to_all | solution.py:422
  11.7 5.0 %all-to-all-done = f32[32,1,32]{2,1,0:T(1,128)S(1)} async-done(((f32[32,1,32]{2,1,0:T(1,128)}), f32[32,1,32]{2,1,0:T(1,128)S(1)}, u32[]{:S(2)}, u32[]{:S(2)}) %all-to-all-start) | async-done | bytes 4128 | tf_op jit(solution)/shard_map/all_to_all | solution.py:422
  19.2 3.6 %shard_map.136 = (f32[64,1536]{1,0:T(8,128)S(1)}, s16[64,1664]{1,0:T(8,128)(2,1)S(1)}) custom-call(bf16[64,2048]{1,0:T(8,128)(2,1)S(1)} %get-tuple-element.126.refs_0_, bf16[64,2048]{1,0:T(8,128)(2,1)S(1)} %get-tuple-element.125.refs_1_, bf16[128,128]{1,0:T(8,128)(2,1)S(1)} %get-tuple-element.70.refs_2_.refs_16_, bf16[2048,4096]{1,0:T(8,128)(2,1)} %refs_3_.9), custom_call_target="tpu_custom_call" | custom-call | flops 872415232 | bytes 7077888 | tf_op jit(solution)/shard_map/pallas_call | solution.py:231
  23.4 3.6 %shard_map.137 = (f32[64,1536]{1,0:T(8,128)S(1)}, s16[64,1664]{1,0:T(8,128)(2,1)S(1)}) custom-call(bf16[64,2048]{1,0:T(8,128)(2,1)S(1)} %get-tuple-element.126.refs_0_, bf16[64,2048]{1,0:T(8,128)(2,1)S(1)} %get-tuple-element.125.refs_1_, bf16[128,128]{1,0:T(8,128)(2,1)S(1)} %get-tuple-element.70.refs_2_.refs_16_, bf16[2048,4096]{1,0:T(8,128)(2,1)} %refs_3_.9), custom_call_target="tpu_custom_call" | custom-call | flops 872415232 | bytes 7077888 | tf_op jit(solution)/shard_map/pallas_call | solution.py:231
  30.6 3.9 %shard_map.142 = (f32[64,1536]{1,0:T(8,128)S(1)}, s16[64,1664]{1,0:T(8,128)(2,1)S(1)}) custom-call(bf16[64,2048]{1,0:T(8,128)(2,1)S(1)} %get-tuple-element.126.refs_0_, bf16[64,2048]{1,0:T(8,128)(2,1)S(1)} %get-tuple-element.125.refs_1_, bf16[128,128]{1,0:T(8,128)(2,1)S(1)} %get-tuple-element.70.refs_2_.refs_16_, bf16[2048,4096]{1,0:T(8,128)(2,1)} %refs_3_.9, ...), custom_call_target="tpu_custom_call" | custom-call | flops 872415232 | bytes 7077888 | tf_op jit(solution)/shard_map/pallas_call | solution.py:231
  36.9 3.3 %collective-permute-start.5 = (s16[16,1664]{1,0:T(8,128)(2,1)S(1)}, s16[16,1664]{1,0:T(8,128)(2,1)S(1)}, u32[]{:S(2)}, u32[]{:S(2)}) collective-permute-start(s16[16,1664]{1,0:T(8,128)(2,1)S(1)} %get-tuple-element.63), channel_id=1, source_target_pairs={{0,24},{4,28},{8,16},{12,20},{16,8},{20,12},{24,0},{28,4},{1,25},{... | collective-permute-start | bytes 159752 | tf_op jit(solution)/shard_map/ppermute | solution.py:44
  43.2 3.3 %collective-permute-start.9 = (s16[16,1664]{1,0:T(8,128)(2,1)S(1)}, s16[16,1664]{1,0:T(8,128)(2,1)S(1)}, u32[]{:S(2)}, u32[]{:S(2)}) collective-permute-start(s16[16,1664]{1,0:T(8,128)(2,1)S(1)} %get-tuple-element.69), channel_id=1, source_target_pairs={{0,24},{4,28},{8,16},{12,20},{16,8},{20,12},{24,0},{28,4},{1,25},{... | collective-permute-start | bytes 159752 | tf_op jit(solution)/shard_map/ppermute | solution.py:44
  47.7 3.3 %collective-permute-start.13 = (s16[16,1664]{1,0:T(8,128)(2,1)S(1)}, s16[16,1664]{1,0:T(8,128)(2,1)S(1)}, u32[]{:S(2)}, u32[]{:S(2)}) collective-permute-start(s16[16,1664]{1,0:T(8,128)(2,1)S(1)} %get-tuple-element.78), channel_id=1, source_target_pairs={{0,24},{4,28},{8,16},{12,20},{16,8},{20,12},{24,0},{28,4},{1,25},{... | collective-permute-start | bytes 159752 | tf_op jit(solution)/shard_map/ppermute | solution.py:44
  54.8 3.7 %collective-permute-done.14 = bf16[2,4,36,128]{3,2,1,0:T(8,128)(2,1)S(1)} collective-permute-done((bf16[2,4,36,128]{3,2,1,0:T(8,128)(2,1)S(1)}, bf16[2,4,36,128]{3,2,1,0:T(8,128)(2,1)S(1)}, u32[]{:S(2)}, u32[]{:S(2)}) %collective-permute-start.14) | collective-permute-done | bytes 73760 | tf_op jit(solution)/shard_map/ppermute | solution.py:44
  64.3 11.1 %shard_map.145 = bf16[4,4,32,128]{3,2,1,0:T(8,128)(2,1)S(1)} custom-call(s32[1]{0:T(128)} %bitcast.me_ref, s32[4]{0:T(128)S(1)} %copy-done.4, bf16[4,4,32,128]{3,2,1,0:T(8,128)(2,1)S(1)} %slice.245.query_ref, f32[4,4,4,128]{3,2,1,0:T(4,128)S(1)} %maximum_convert_fusion.fresh_ref, f32[4,128]{1,0:T(4,128)S(1)} %get-tuple-element.154.cos_ref, ...), custom_call_target="tpu_custom_call" | custom-call | flops 134217728 | bytes 8388608 | tf_op jit(solution)/shard_map/pallas_call | solution.py:116
  76.3 3.6 %collective-permute-done.16 = bf16[2,4,4096]{2,1,0:T(4,128)(2,1)S(1)} collective-permute-done((bf16[2,4,4096]{2,1,0:T(4,128)(2,1)S(1)}, bf16[2,4,4096]{2,1,0:T(4,128)(2,1)S(1)}, u32[]{:S(2)}, u32[]{:S(2)}) %collective-permute-start.16) | collective-permute-done | bytes 65568 | tf_op jit(solution)/shard_map/ppermute | solution.py:44
  83.3 3.2 %collective-permute-start.20 = (bf16[16,2048]{1,0:T(8,128)(2,1)S(1)}, bf16[16,2048]{1,0:T(8,128)(2,1)S(1)}, u32[]{:S(2)}, u32[]{:S(2)}) collective-permute-start(bf16[16,2048]{1,0:T(8,128)(2,1)S(1)} %pad_maximum_fusion.9.array_ref), channel_id=1, source_target_pairs={{0,24},{4,28},{8,16},{12,20},{16,8},{20,12},{24,0},{28,4},{1,25},{... | collective-permute-start | bytes 196616 | tf_op jit(solution)/shard_map/ppermute | solution.py:44
  88.0 3.3 %collective-permute-start.27 = (bf16[16,2048]{1,0:T(8,128)(2,1)S(1)}, bf16[16,2048]{1,0:T(8,128)(2,1)S(1)}, u32[]{:S(2)}, u32[]{:S(2)}) collective-permute-start(bf16[16,2048]{1,0:T(8,128)(2,1)S(1)} %pad_maximum_fusion.10.array_ref), channel_id=1, source_target_pairs={{0,24},{4,28},{8,16},{12,20},{16,8},{20,12},{24,0},{28,4},{1,25},{... | collective-permute-start | bytes 196616 | tf_op jit(solution)/shard_map/ppermute | solution.py:44
  104.2 2.6 %shard_map.148 = (f32[64,2048]{1,0:T(8,128)S(1)}, f32[64,2048]{1,0:T(8,128)S(1)}) custom-call(bf16[16,2048]{1,0:T(8,128)(2,1)S(1)} %shard_map.146.refs_0_, bf16[16,2048]{1,0:T(8,128)(2,1)S(1)} %collective-permute-done.18.refs_1_, bf16[16,2048]{1,0:T(8,128)(2,1)S(1)} %collective-permute-done.19.refs_2_, bf16[16,2048]{1,0:T(8,128)(2,1)S(1)} %collective-permute-done.20.refs_3_, ...), custom_call_target="tpu_custom_call" | custom-call | flops 2281701376 | bytes 17825792 | tf_op jit(solution)/shard_map/pallas_call | solution.py:231
  109.5 5.0 %collective-permute-done.33 = bf16[32,2048]{1,0:T(8,128)(2,1)S(1)} collective-permute-done((bf16[32,2048]{1,0:T(8,128)(2,1)S(1)}, bf16[32,2048]{1,0:T(8,128)(2,1)S(1)}, u32[]{:S(2)}, u32[]{:S(2)}) %collective-permute-start.33) | collective-permute-done | bytes 131104 | tf_op jit(solution)/shard_map/ppermute | solution.py:44
  115.5 10.6 %all_to_all.12 = f32[32,1,32]{2,1,0:T(1,128)S(1)} all-to-all(f32[32,1,32]{2,1,0:T(1,128)S(1)} %broadcast_in_dim.13), channel_id=1, replica_groups=mesh['wide'=8,'narrow'=4] {'wide','narrow'}, dimensions={0} | all-to-all | bytes 8192 | tf_op jit(solution)/shard_map/all_to_all | solution.py:422
  128.0 4.1 %shard_map.152 = (f32[64,2048]{1,0:T(8,128)S(1)}, f32[64,2048]{1,0:T(8,128)S(1)}) custom-call(bf16[64,2048]{1,0:T(8,128)(2,1)S(1)} %get-tuple-element.124.refs_0_, bf16[64,2048]{1,0:T(8,128)(2,1)S(1)} %get-tuple-element.123.refs_1_, bf16[128,128]{1,0:T(8,128)(2,1)S(1)} %get-tuple-element.127.refs_2_, bf16[2048,2048]{1,0:T(8,128)(2,1)} %refs_3_.11, ...), custom_call_target="tpu_custom_call" | custom-call | flops 1140850688 | bytes 9437184 | tf_op jit(solution)/shard_map/pallas_call | solution.py:231
  132.7 4.1 %shard_map.149 = (f32[64,2048]{1,0:T(8,128)S(1)}, f32[64,2048]{1,0:T(8,128)S(1)}) custom-call(bf16[64,2048]{1,0:T(8,128)(2,1)S(1)} %get-tuple-element.124.refs_0_, bf16[64,2048]{1,0:T(8,128)(2,1)S(1)} %get-tuple-element.123.refs_1_, bf16[128,128]{1,0:T(8,128)(2,1)S(1)} %get-tuple-element.127.refs_2_, bf16[2048,2048]{1,0:T(8,128)(2,1)} %refs_3_.11, ...), custom_call_target="tpu_custom_call" | custom-call | flops 1140850688 | bytes 9437184 | tf_op jit(solution)/shard_map/pallas_call | solution.py:231
  138.4 2.9 %collective-permute-done.43 = f16[64,2048]{1,0:T(8,128)(2,1)S(1)} collective-permute-done((f16[64,2048]{1,0:T(8,128)(2,1)S(1)}, f16[64,2048]{1,0:T(8,128)(2,1)S(1)}, u32[]{:S(2)}, u32[]{:S(2)}) %collective-permute-start.43) | collective-permute-done | bytes 262176 | tf_op jit(solution)/shard_map/ppermute | solution.py:44
  151.5 2.8 %collective-permute-done.37 = f16[16,2048]{1,0:T(8,128)(2,1)S(1)} collective-permute-done((f16[16,2048]{1,0:T(8,128)(2,1)S(1)}, f16[16,2048]{1,0:T(8,128)(2,1)S(1)}, u32[]{:S(2)}, u32[]{:S(2)}) %collective-permute-start.37) | collective-permute-done | bytes 65568 | tf_op jit(solution)/shard_map/ppermute | solution.py:44
  156.7 2.5 %collective-permute-done.40 = bf16[16,1024]{1,0:T(8,128)(2,1)S(1)} collective-permute-done((bf16[16,1024]{1,0:T(8,128)(2,1)S(1)}, bf16[16,1024]{1,0:T(8,128)(2,1)S(1)}, u32[]{:S(2)}, u32[]{:S(2)}) %collective-permute-start.40) | collective-permute-done | bytes 32800 | tf_op jit(solution)/shard_map/ppermute | solution.py:44
  164.1 2.7 %collective-permute-done.49.refs_1_ = bf16[64,1024]{1,0:T(8,128)(2,1)S(1)} collective-permute-done((bf16[64,1024]{1,0:T(8,128)(2,1)S(1)}, bf16[64,1024]{1,0:T(8,128)(2,1)S(1)}, u32[]{:S(2)}, u32[]{:S(2)}) %collective-permute-start.49) | collective-permute-done | bytes 131104 | tf_op jit(solution)/shard_map/ppermute | solution.py:44
  172.2 5.0 %collective-permute-done.51 = bf16[32,2048]{1,0:T(8,128)(2,1)S(1)} collective-permute-done((bf16[32,2048]{1,0:T(8,128)(2,1)S(1)}, bf16[32,2048]{1,0:T(8,128)(2,1)S(1)}, u32[]{:S(2)}, u32[]{:S(2)}) %collective-permute-start.51) | collective-permute-done | bytes 131104 | tf_op jit(solution)/shard_map/ppermute | solution.py:44
  (207 shorter events, 75.9 us)
Async XLA Ops:
  0.0 16.7 %collective-permute-start = (bf16[32,2048]{1,0:T(8,128)(2,1)}, bf16[32,2048]{1,0:T(8,128)(2,1)S(1)}, u32[]{:S(2)}, u32[]{:S(2)}) collective-permute-start(bf16[32,2048]{1,0:T(8,128)(2,1)} %param.14), channel_id=1, source_target_pairs={{0,2},{1,3},{2,0},{3,1},{4,6},{5,7},{6,4},{7,5},{8,10},{9,11},{10,... | collective-permute-start | bytes 393224 | tf_op jit(solution)/shard_map/ppermute | solution.py:44
  4.6 12.0 %all-to-all-start = ((f32[32,1,32]{2,1,0:T(1,128)}), f32[32,1,32]{2,1,0:T(1,128)S(1)}, u32[]{:S(2)}, u32[]{:S(2)}) async-start(f32[32,1,32]{2,1,0:T(1,128)} %broadcast_in_dim.11), calls=%async_computation | async-start | bytes 32768 | tf_op jit(solution)/shard_map/all_to_all | solution.py:422
  22.8 7.7 %collective-permute-start.2 = (s16[64,1664]{1,0:T(8,128)(2,1)S(1)}, s16[64,1664]{1,0:T(8,128)(2,1)S(1)}, u32[]{:S(2)}, u32[]{:S(2)}) collective-permute-start(s16[64,1664]{1,0:T(8,128)(2,1)S(1)} %get-tuple-element.58), channel_id=1, source_target_pairs={{0,4},{4,0},{8,12},{12,8},{16,20},{20,16},{24,28},{28,24},{1,5},{5... | collective-permute-start | bytes 638984 | tf_op jit(solution)/shard_map/ppermute | solution.py:44
  27.1 13.1 %collective-permute-start.6 = (s16[64,1664]{1,0:T(8,128)(2,1)S(1)}, s16[64,1664]{1,0:T(8,128)(2,1)S(1)}, u32[]{:S(2)}, u32[]{:S(2)}) collective-permute-start(s16[64,1664]{1,0:T(8,128)(2,1)S(1)} %get-tuple-element.65), channel_id=1, source_target_pairs={{0,4},{4,0},{8,12},{12,8},{16,20},{20,16},{24,28},{28,24},{1,5},{5... | collective-permute-start | bytes 638984 | tf_op jit(solution)/shard_map/ppermute | solution.py:44
  34.5 6.7 %collective-permute-start.10 = (s16[64,1664]{1,0:T(8,128)(2,1)S(1)}, s16[64,1664]{1,0:T(8,128)(2,1)S(1)}, u32[]{:S(2)}, u32[]{:S(2)}) collective-permute-start(s16[64,1664]{1,0:T(8,128)(2,1)S(1)} %get-tuple-element.74), channel_id=1, source_target_pairs={{0,4},{4,0},{8,12},{12,8},{16,20},{20,16},{24,28},{28,24},{1,5},{5... | collective-permute-start | bytes 638984 | tf_op jit(solution)/shard_map/ppermute | solution.py:44
  35.7 7.5 %collective-permute-start.3 = (s16[16,1664]{1,0:T(8,128)(2,1)S(1)}, s16[16,1664]{1,0:T(8,128)(2,1)S(1)}, u32[]{:S(2)}, u32[]{:S(2)}) collective-permute-start(s16[16,1664]{1,0:T(8,128)(2,1)S(1)} %get-tuple-element.61), channel_id=1, source_target_pairs={{0,16},{4,20},{8,24},{12,28},{16,0},{20,4},{24,8},{28,12},{1,17},{... | collective-permute-start | bytes 159752 | tf_op jit(solution)/shard_map/ppermute | solution.py:44
  36.3 10.3 %collective-permute-start.4 = (s16[16,1664]{1,0:T(8,128)(2,1)S(1)}, s16[16,1664]{1,0:T(8,128)(2,1)S(1)}, u32[]{:S(2)}, u32[]{:S(2)}) collective-permute-start(s16[16,1664]{1,0:T(8,128)(2,1)S(1)} %get-tuple-element.62), channel_id=1, source_target_pairs={{0,8},{4,12},{8,0},{12,4},{16,24},{20,28},{24,16},{28,20},{1,9},{5... | collective-permute-start | bytes 159752 | tf_op jit(solution)/shard_map/ppermute | solution.py:44
  36.9 9.7 %collective-permute-start.5 = (s16[16,1664]{1,0:T(8,128)(2,1)S(1)}, s16[16,1664]{1,0:T(8,128)(2,1)S(1)}, u32[]{:S(2)}, u32[]{:S(2)}) collective-permute-start(s16[16,1664]{1,0:T(8,128)(2,1)S(1)} %get-tuple-element.63), channel_id=1, source_target_pairs={{0,24},{4,28},{8,16},{12,20},{16,8},{20,12},{24,0},{28,4},{1,25},{... | collective-permute-start | bytes 159752 | tf_op jit(solution)/shard_map/ppermute | solution.py:44
  41.1 6.6 %collective-permute-start.7 = (s16[16,1664]{1,0:T(8,128)(2,1)S(1)}, s16[16,1664]{1,0:T(8,128)(2,1)S(1)}, u32[]{:S(2)}, u32[]{:S(2)}) collective-permute-start(s16[16,1664]{1,0:T(8,128)(2,1)S(1)} %get-tuple-element.67), channel_id=1, source_target_pairs={{0,16},{4,20},{8,24},{12,28},{16,0},{20,4},{24,8},{28,12},{1,17},{... | collective-permute-start | bytes 159752 | tf_op jit(solution)/shard_map/ppermute | solution.py:44
  41.2 10.0 %collective-permute-start.8 = (s16[16,1664]{1,0:T(8,128)(2,1)S(1)}, s16[16,1664]{1,0:T(8,128)(2,1)S(1)}, u32[]{:S(2)}, u32[]{:S(2)}) collective-permute-start(s16[16,1664]{1,0:T(8,128)(2,1)S(1)} %get-tuple-element.68), channel_id=1, source_target_pairs={{0,8},{4,12},{8,0},{12,4},{16,24},{20,28},{24,16},{28,20},{1,9},{5... | collective-permute-start | bytes 159752 | tf_op jit(solution)/shard_map/ppermute | solution.py:44
  43.2 8.0 %collective-permute-start.9 = (s16[16,1664]{1,0:T(8,128)(2,1)S(1)}, s16[16,1664]{1,0:T(8,128)(2,1)S(1)}, u32[]{:S(2)}, u32[]{:S(2)}) collective-permute-start(s16[16,1664]{1,0:T(8,128)(2,1)S(1)} %get-tuple-element.69), channel_id=1, source_target_pairs={{0,24},{4,28},{8,16},{12,20},{16,8},{20,12},{24,0},{28,4},{1,25},{... | collective-permute-start | bytes 159752 | tf_op jit(solution)/shard_map/ppermute | solution.py:44
  81.4 6.6 %collective-permute-start.21 = (bf16[16,2048]{1,0:T(8,128)(2,1)S(1)}, bf16[16,2048]{1,0:T(8,128)(2,1)S(1)}, u32[]{:S(2)}, u32[]{:S(2)}) collective-permute-start(bf16[16,2048]{1,0:T(8,128)(2,1)S(1)} %pad_maximum_fusion.9.array_ref), channel_id=1, source_target_pairs={{0,4},{4,0},{8,12},{12,8},{16,20},{20,16},{24,28},{28,24},{1,5},{5... | collective-permute-start | bytes 196616 | tf_op jit(solution)/shard_map/ppermute | solution.py:44
  83.3 7.9 %collective-permute-start.20 = (bf16[16,2048]{1,0:T(8,128)(2,1)S(1)}, bf16[16,2048]{1,0:T(8,128)(2,1)S(1)}, u32[]{:S(2)}, u32[]{:S(2)}) collective-permute-start(bf16[16,2048]{1,0:T(8,128)(2,1)S(1)} %pad_maximum_fusion.9.array_ref), channel_id=1, source_target_pairs={{0,24},{4,28},{8,16},{12,20},{16,8},{20,12},{24,0},{28,4},{1,25},{... | collective-permute-start | bytes 196616 | tf_op jit(solution)/shard_map/ppermute | solution.py:44
  86.6 8.4 %collective-permute-start.18 = (bf16[16,2048]{1,0:T(8,128)(2,1)S(1)}, bf16[16,2048]{1,0:T(8,128)(2,1)S(1)}, u32[]{:S(2)}, u32[]{:S(2)}) collective-permute-start(bf16[16,2048]{1,0:T(8,128)(2,1)S(1)} %pad_maximum_fusion.9.array_ref), channel_id=1, source_target_pairs={{0,16},{4,20},{8,24},{12,28},{16,0},{20,4},{24,8},{28,12},{1,17},{... | collective-permute-start | bytes 196616 | tf_op jit(solution)/shard_map/ppermute | solution.py:44
  87.8 7.3 %collective-permute-start.28 = (bf16[16,2048]{1,0:T(8,128)(2,1)S(1)}, bf16[16,2048]{1,0:T(8,128)(2,1)S(1)}, u32[]{:S(2)}, u32[]{:S(2)}) collective-permute-start(bf16[16,2048]{1,0:T(8,128)(2,1)S(1)} %pad_maximum_fusion.10.array_ref), channel_id=1, source_target_pairs={{0,4},{4,0},{8,12},{12,8},{16,20},{20,16},{24,28},{28,24},{1,5},{5... | collective-permute-start | bytes 196616 | tf_op jit(solution)/shard_map/ppermute | solution.py:44
  88.0 9.2 %collective-permute-start.27 = (bf16[16,2048]{1,0:T(8,128)(2,1)S(1)}, bf16[16,2048]{1,0:T(8,128)(2,1)S(1)}, u32[]{:S(2)}, u32[]{:S(2)}) collective-permute-start(bf16[16,2048]{1,0:T(8,128)(2,1)S(1)} %pad_maximum_fusion.10.array_ref), channel_id=1, source_target_pairs={{0,24},{4,28},{8,16},{12,20},{16,8},{20,12},{24,0},{28,4},{1,25},{... | collective-permute-start | bytes 196616 | tf_op jit(solution)/shard_map/ppermute | solution.py:44
  91.6 7.6 %collective-permute-start.25 = (bf16[16,2048]{1,0:T(8,128)(2,1)S(1)}, bf16[16,2048]{1,0:T(8,128)(2,1)S(1)}, u32[]{:S(2)}, u32[]{:S(2)}) collective-permute-start(bf16[16,2048]{1,0:T(8,128)(2,1)S(1)} %pad_maximum_fusion.10.array_ref), channel_id=1, source_target_pairs={{0,16},{4,20},{8,24},{12,28},{16,0},{20,4},{24,8},{28,12},{1,17},{... | collective-permute-start | bytes 196616 | tf_op jit(solution)/shard_map/ppermute | solution.py:44
  114.7 11.5 %collective-permute-start.34 = (bf16[32,2048]{1,0:T(8,128)(2,1)S(1)}, bf16[32,2048]{1,0:T(8,128)(2,1)S(1)}, u32[]{:S(2)}, u32[]{:S(2)}) collective-permute-start(bf16[32,2048]{1,0:T(8,128)(2,1)S(1)} %get-tuple-element.92), channel_id=1, source_target_pairs={{0,2},{1,3},{2,0},{3,1},{4,6},{5,7},{6,4},{7,5},{8,10},{9,11},{10,... | collective-permute-start | bytes 393224 | tf_op jit(solution)/shard_map/ppermute | solution.py:44
  132.1 9.2 %collective-permute-start.43 = (f16[64,2048]{1,0:T(8,128)(2,1)S(1)}, f16[64,2048]{1,0:T(8,128)(2,1)S(1)}, u32[]{:S(2)}, u32[]{:S(2)}) collective-permute-start(f16[64,2048]{1,0:T(8,128)(2,1)S(1)} %convert_element_type.122), channel_id=1, source_target_pairs={{0,4},{4,0},{8,12},{12,8},{16,20},{20,16},{24,28},{28,24},{1,5},{5... | collective-permute-start | bytes 786440 | tf_op jit(solution)/shard_map/ppermute | solution.py:44
  136.8 9.3 %collective-permute-start.36 = (f16[64,2048]{1,0:T(8,128)(2,1)S(1)}, f16[64,2048]{1,0:T(8,128)(2,1)S(1)}, u32[]{:S(2)}, u32[]{:S(2)}) collective-permute-start(f16[64,2048]{1,0:T(8,128)(2,1)S(1)} %convert_element_type.116), channel_id=1, source_target_pairs={{0,4},{4,0},{8,12},{12,8},{16,20},{20,16},{24,28},{28,24},{1,5},{5... | collective-permute-start | bytes 786440 | tf_op jit(solution)/shard_map/ppermute | solution.py:44
  141.4 7.8 %collective-permute-start.44 = (f16[16,2048]{1,0:T(8,128)(2,1)S(1)}, f16[16,2048]{1,0:T(8,128)(2,1)S(1)}, u32[]{:S(2)}, u32[]{:S(2)}) collective-permute-start(f16[16,2048]{1,0:T(8,128)(2,1)S(1)} %get-tuple-element.93), channel_id=1, source_target_pairs={{0,16},{4,20},{8,24},{12,28},{16,0},{20,4},{24,8},{28,12},{1,17},{... | collective-permute-start | bytes 196616 | tf_op jit(solution)/shard_map/ppermute | solution.py:44
  142.1 7.7 %collective-permute-start.46 = (f16[16,2048]{1,0:T(8,128)(2,1)S(1)}, f16[16,2048]{1,0:T(8,128)(2,1)S(1)}, u32[]{:S(2)}, u32[]{:S(2)}) collective-permute-start(f16[16,2048]{1,0:T(8,128)(2,1)S(1)} %get-tuple-element.94), channel_id=1, source_target_pairs={{0,24},{4,28},{8,16},{12,20},{16,8},{20,12},{24,0},{28,4},{1,25},{... | collective-permute-start | bytes 196616 | tf_op jit(solution)/shard_map/ppermute | solution.py:44
  146.3 8.0 %collective-permute-start.37 = (f16[16,2048]{1,0:T(8,128)(2,1)S(1)}, f16[16,2048]{1,0:T(8,128)(2,1)S(1)}, u32[]{:S(2)}, u32[]{:S(2)}) collective-permute-start(f16[16,2048]{1,0:T(8,128)(2,1)S(1)} %get-tuple-element.96), channel_id=1, source_target_pairs={{0,16},{4,20},{8,24},{12,28},{16,0},{20,4},{24,8},{28,12},{1,17},{... | collective-permute-start | bytes 196616 | tf_op jit(solution)/shard_map/ppermute | solution.py:44
  146.9 7.3 %collective-permute-start.39 = (f16[16,2048]{1,0:T(8,128)(2,1)S(1)}, f16[16,2048]{1,0:T(8,128)(2,1)S(1)}, u32[]{:S(2)}, u32[]{:S(2)}) collective-permute-start(f16[16,2048]{1,0:T(8,128)(2,1)S(1)} %get-tuple-element.97), channel_id=1, source_target_pairs={{0,24},{4,28},{8,16},{12,20},{16,8},{20,12},{24,0},{28,4},{1,25},{... | collective-permute-start | bytes 196616 | tf_op jit(solution)/shard_map/ppermute | solution.py:44
  (42 other events, 267.2 us)

commit v9 on v7

--- a/solution.py
+++ b/solution.py
@@ -80,7 +80,7 @@
 
 
 QKV_CHUNKS = 3
-FFN_SPLIT = 0.625
+FFN_SPLIT = 0.5
 CONTEXT_CHUNKS = 2
 NARROW_KINDS = [jnp.float32] + [jnp.bfloat16] * 8
 TILE = 512
@@ -285,10 +285,10 @@
 
 
 def coded_scatter(kept, arrived):
-    blocks = lax.axis_size("wide") // 2
-    own, *codes = fold(kept, arrived, blocks)
-    offsets = offsets_of("wide")[1:blocks]
-    return add_codes(own, [swap(code, "wide", o) for code, o in zip(codes, offsets)])
+    for stride in strides_of("wide")[1:]:
+        kept, codes = fold(kept, arrived, 2)
+        arrived = swap(codes, "wide", stride)
+    return add_codes(kept, [arrived])
 
 
 def wide_scatter(kept, sent):
@@ -319,10 +319,11 @@
     return [block, swap(block, axis, strides[-1])]
 
 
-def gather_direct(block, axis):
-    offsets = offsets_of(axis)
-    held = [block] + [swap(block, axis, o) for o in offsets[1 : len(offsets) // 2]]
-    return [stand_in(block)] + held[1:] + [swap(piece, axis, 1) for piece in held]
+def gather_pieces(block, axis):
+    held = [block]
+    for stride in strides_of(axis)[::-1]:
+        held = held + [swap(piece, axis, stride) for piece in held]
+    return [stand_in(block)] + held[1:]
 
 
 def exchange(blocks, axis):
@@ -466,7 +467,7 @@
     for chunk in range(CONTEXT_CHUNKS):
         columns = slice(chunk * depth, (chunk + 1) * depth)
         block = jnp.concatenate([piece[:, columns] for piece in by_heads], axis=0)
-        groups.append(gather_direct(block, "wide"))
+        groups.append(gather_pieces(block, "wide"))
     total = project(groups, to_hypothesis, False, [(w_out, 0, 0, w_out.shape[1])], 2)
     attn_out = narrow_scatter(*total)
     resid = (rows_in + attn_out).astype(jnp.bfloat16)
@@ -479,10 +480,7 @@
     for first, last in ((0, f_edge), (f_edge, f_total)):
         f_cols = last - first
         segments = [(w_gate, 0, first, f_cols), (w_up, 0, first, f_cols)]
-        sums, normed_two = lax.optimization_barrier(
-            (project([normed_two], to_wide, False, segments, 2, direct=True), normed_two)
-        )
-        sums = wide_scatter(*sums)
+        sums = wide_scatter(*project([normed_two], to_wide, False, segments, 2, direct=True))
         act = (jax.nn.silu(sums[:, :f_cols]) * sums[:, f_cols:]).astype(jnp.bfloat16)
         total = project(
             [gather(act, "wide", paired=True)],

time: 181 us -> 166 us (0.917)
  starting transfers between devices: 60.3 us -> 50.6 us
  waiting for transfers between devices: 67 us -> 60.4 us
    ppermute x52 -> x49, starting transfers between devices: 55.4 us -> 45.7 us  [swap(): return lax.ppermute(block, axis, [(i, i ^ offset) for i in range(count)])]
    ppermute x52 -> x49, waiting for transfers between devices: 62.1 us -> 55.5 us  [swap(): return lax.ppermute(block, axis, [(i, i ^ offset) for i in range(count)])]
    pallas_call x3 -> x6, Pallas kernels: 2.84 us -> 4.76 us  [fold(): pl.pallas_call(body, out_shape=[jax.ShapeDtypeStruct((rows, width), jnp.f...]
  transfers between devices with their start and end apart: 53 -> 50, of which waited for: 31 -> 30; matrix products, arithmetic and copies ran while one was open for 3% -> 3% of each run, Pallas kernels for 6% -> 11%
where the time goes in v9:
time: 166 us
  waiting for transfers between devices  60.4 us (36%)
  starting transfers between devices  50.6 us (30%)
  Pallas kernels  29.1 us (18%)
  blocking collectives  10.5 us (6%)
  other arithmetic  7.14 us (4%)
  matrix products  5.16 us (3%)
  local copies, waits for them, and re-layouts  2.39 us (1%)
    ppermute x49, waiting for transfers between devices, swap(): return lax.ppermute(block, axis, [(i, i ^ offset) for i in range(count)])  55.5 us
    ppermute x49, starting transfers between devices, swap(): return lax.ppermute(block, axis, [(i, i ^ offset) for i in range(count)])  45.7 us
    pallas_call x8, Pallas kernels, project(): pl.pallas_call(body, in_specs=specs, out_specs=[in_vmem] * split, scratch...  23.9 us
    all_to_all x1, blocking collectives, normalized_rows(): landed = lax.all_to_all(sent, ('wide', 'narrow'), 0, 0, tiled=True)  10.5 us
    all_to_all x1, starting transfers between devices, normalized_rows(): landed = lax.all_to_all(sent, ('wide', 'narrow'), 0, 0, tiled=True)  4.92 us
    all_to_all x1, waiting for transfers between devices, normalized_rows(): landed = lax.all_to_all(sent, ('wide', 'narrow'), 0, 0, tiled=True)  4.92 us
    pallas_call x6, Pallas kernels, fold(): pl.pallas_call(body, out_shape=[jax.ShapeDtypeStruct((rows, width), jnp.f...  4.76 us
    dot_general x1, matrix products, attend(): jnp.einsum('rgqd,rlgd->rgql', query_heads, cache_keys, preferred_element_...  3.86 us
  transfers between devices with their start and end apart: 50, of which 30 were waited for; matrix products, arithmetic and copies ran while one was open for 3% of the time, Pallas kernels for 11%

profile of v9, /device:TPU:0, one launch (start us, length us, event | category | flops | bytes accessed | tf_op | source)
XLA Modules:
  0.0 166.1 jit_solution(5253959872349476217)
XLA Ops:
  0.0 2.9 %collective-permute-start = (bf16[32,2048]{1,0:T(8,128)(2,1)}, bf16[32,2048]{1,0:T(8,128)(2,1)S(1)}, u32[]{:S(2)}, u32[]{:S(2)}) collective-permute-start(bf16[32,2048]{1,0:T(8,128)(2,1)} %param.14), channel_id=1, source_target_pairs={{0,2},{1,3},{2,0},{3,1},{4,6},{5,7},{6,4},{7,5},{8,10},{9,11},{10,... | collective-permute-start | bytes 393224 | tf_op jit(solution)/shard_map/ppermute | solution.py:99
  4.6 4.9 %all-to-all-start = ((f32[32,1,32]{2,1,0:T(1,128)}), f32[32,1,32]{2,1,0:T(1,128)S(1)}, u32[]{:S(2)}, u32[]{:S(2)}) async-start(f32[32,1,32]{2,1,0:T(1,128)} %broadcast_in_dim.17), calls=%async_computation | async-start | bytes 32768 | tf_op jit(solution)/shard_map/all_to_all | solution.py:407
  11.7 4.9 %all-to-all-done = f32[32,1,32]{2,1,0:T(1,128)S(1)} async-done(((f32[32,1,32]{2,1,0:T(1,128)}), f32[32,1,32]{2,1,0:T(1,128)S(1)}, u32[]{:S(2)}, u32[]{:S(2)}) %all-to-all-start) | async-done | bytes 4128 | tf_op jit(solution)/shard_map/all_to_all | solution.py:407
  19.2 3.6 %shard_map.136 = (f32[64,1536]{1,0:T(8,128)S(1)}, s16[64,1664]{1,0:T(8,128)(2,1)S(1)}) custom-call(bf16[64,2048]{1,0:T(8,128)(2,1)S(1)} %get-tuple-element.148.refs_0_, bf16[64,2048]{1,0:T(8,128)(2,1)S(1)} %get-tuple-element.147.refs_1_, bf16[128,128]{1,0:T(8,128)(2,1)S(1)} %get-tuple-element.70.refs_2_.refs_16_, bf16[2048,4096]{1,0:T(8,128)(2,1)} %refs_3_.9), custom_call_target="tpu_custom_call" | custom-call | flops 872415232 | bytes 7077888 | tf_op jit(solution)/shard_map/pallas_call | solution.py:215
  23.4 3.6 %shard_map.137 = (f32[64,1536]{1,0:T(8,128)S(1)}, s16[64,1664]{1,0:T(8,128)(2,1)S(1)}) custom-call(bf16[64,2048]{1,0:T(8,128)(2,1)S(1)} %get-tuple-element.148.refs_0_, bf16[64,2048]{1,0:T(8,128)(2,1)S(1)} %get-tuple-element.147.refs_1_, bf16[128,128]{1,0:T(8,128)(2,1)S(1)} %get-tuple-element.70.refs_2_.refs_16_, bf16[2048,4096]{1,0:T(8,128)(2,1)} %refs_3_.9), custom_call_target="tpu_custom_call" | custom-call | flops 872415232 | bytes 7077888 | tf_op jit(solution)/shard_map/pallas_call | solution.py:215
  30.6 3.9 %shard_map.144 = (f32[64,1536]{1,0:T(8,128)S(1)}, s16[64,1664]{1,0:T(8,128)(2,1)S(1)}) custom-call(bf16[64,2048]{1,0:T(8,128)(2,1)S(1)} %get-tuple-element.148.refs_0_, bf16[64,2048]{1,0:T(8,128)(2,1)S(1)} %get-tuple-element.147.refs_1_, bf16[128,128]{1,0:T(8,128)(2,1)S(1)} %get-tuple-element.70.refs_2_.refs_16_, bf16[2048,4096]{1,0:T(8,128)(2,1)} %refs_3_.9, ...), custom_call_target="tpu_custom_call" | custom-call | flops 872415232 | bytes 7077888 | tf_op jit(solution)/shard_map/pallas_call | solution.py:215
  44.2 2.4 %collective-permute-start.7 = (s16[16,1664]{1,0:T(8,128)(2,1)S(1)}, s16[16,1664]{1,0:T(8,128)(2,1)S(1)}, u32[]{:S(2)}, u32[]{:S(2)}) collective-permute-start(s16[16,1664]{1,0:T(8,128)(2,1)S(1)} %get-tuple-element.69), channel_id=1, source_target_pairs={{0,16},{4,20},{8,24},{12,28},{16,0},{20,4},{24,8},{28,12},{1,17},{... | collective-permute-start | bytes 159752 | tf_op jit(solution)/shard_map/ppermute | solution.py:99
  48.8 2.1 %collective-permute-done.7.refs_0_ = s16[16,1664]{1,0:T(8,128)(2,1)S(1)} collective-permute-done((s16[16,1664]{1,0:T(8,128)(2,1)S(1)}, s16[16,1664]{1,0:T(8,128)(2,1)S(1)}, u32[]{:S(2)}, u32[]{:S(2)}) %collective-permute-start.7) | collective-permute-done | bytes 53280 | tf_op jit(solution)/shard_map/ppermute | solution.py:99
  53.7 3.8 %collective-permute-done.11 = bf16[2,4,36,128]{3,2,1,0:T(8,128)(2,1)S(1)} collective-permute-done((bf16[2,4,36,128]{3,2,1,0:T(8,128)(2,1)S(1)}, bf16[2,4,36,128]{3,2,1,0:T(8,128)(2,1)S(1)}, u32[]{:S(2)}, u32[]{:S(2)}) %collective-permute-start.11) | collective-permute-done | bytes 73760 | tf_op jit(solution)/shard_map/ppermute | solution.py:99
  60.4 3.9 %fusion.114 = (f32[4,8,16]{2,1,0:T(8,128)S(1)}, f32[4,8,16,512]{3,2,1,0:T(8,128)S(1)}) fusion(bf16[4,8,16,64]{3,2,1,0:T(8,128)(2,1)S(1)} %bitcast.84, bf16[4,8,16,64]{3,2,1,0:T(8,128)(2,1)S(1)} %bitcast.82, pred[4,512]{1,0:T(4,128)(4,1)S(1)} %iota_compare_fusion, bf16[4,512,1024]{2,1,0:T(8,128)(2,1)} %param.24), kind=kOutput, calls=%fused_computation.231 | convolution fusion | flops 68156928 | bytes 5378048 | tf_op jit(solution)/shard_map/rgqd,rlgd->rgql/dot_general | solution.py:59
  66.9 3.7 %collective-permute-done.13 = bf16[2,4,4096]{2,1,0:T(4,128)(2,1)S(1)} collective-permute-done((bf16[2,4,4096]{2,1,0:T(4,128)(2,1)S(1)}, bf16[2,4,4096]{2,1,0:T(4,128)(2,1)S(1)}, u32[]{:S(2)}, u32[]{:S(2)}) %collective-permute-start.13) | collective-permute-done | bytes 65568 | tf_op jit(solution)/shard_map/ppermute | solution.py:99
  79.9 2.0 %collective-permute-done.15.refs_1_ = bf16[16,2048]{1,0:T(8,128)(2,1)S(1)} collective-permute-done((bf16[16,2048]{1,0:T(8,128)(2,1)S(1)}, bf16[16,2048]{1,0:T(8,128)(2,1)S(1)}, u32[]{:S(2)}, u32[]{:S(2)}) %collective-permute-start.15) | collective-permute-done | bytes 65568 | tf_op jit(solution)/shard_map/ppermute | solution.py:99
  92.5 2.9 %shard_map.150 = (f32[64,2048]{1,0:T(8,128)S(1)}, f32[64,2048]{1,0:T(8,128)S(1)}) custom-call(bf16[16,2048]{1,0:T(8,128)(2,1)S(1)} %shard_map.148.refs_0_, bf16[16,2048]{1,0:T(8,128)(2,1)S(1)} %collective-permute-done.15.refs_1_, bf16[16,2048]{1,0:T(8,128)(2,1)S(1)} %collective-permute-done.16.refs_2_, bf16[16,2048]{1,0:T(8,128)(2,1)S(1)} %collective-permute-done.17.refs_3_, ...), custom_call_target="tpu_custom_call" | custom-call | flops 2281701376 | bytes 17825792 | tf_op jit(solution)/shard_map/pallas_call | solution.py:215
  98.1 5.0 %collective-permute-done.30 = bf16[32,2048]{1,0:T(8,128)(2,1)S(1)} collective-permute-done((bf16[32,2048]{1,0:T(8,128)(2,1)S(1)}, bf16[32,2048]{1,0:T(8,128)(2,1)S(1)}, u32[]{:S(2)}, u32[]{:S(2)}) %collective-permute-start.30) | collective-permute-done | bytes 131104 | tf_op jit(solution)/shard_map/ppermute | solution.py:99
  103.8 10.5 %all_to_all.12 = f32[32,1,32]{2,1,0:T(1,128)S(1)} all-to-all(f32[32,1,32]{2,1,0:T(1,128)S(1)} %broadcast_in_dim.20), channel_id=1, replica_groups=mesh['wide'=8,'narrow'=4] {'wide','narrow'}, dimensions={0} | all-to-all | bytes 8192 | tf_op jit(solution)/shard_map/all_to_all | solution.py:407
  116.2 4.1 %shard_map.154 = (f32[64,2048]{1,0:T(8,128)S(1)}, f32[64,2048]{1,0:T(8,128)S(1)}) custom-call(bf16[64,2048]{1,0:T(8,128)(2,1)S(1)} %get-tuple-element.146.refs_0_, bf16[64,2048]{1,0:T(8,128)(2,1)S(1)} %get-tuple-element.145.refs_1_, bf16[128,128]{1,0:T(8,128)(2,1)S(1)} %get-tuple-element.149.refs_2_, bf16[2048,2048]{1,0:T(8,128)(2,1)} %refs_3_.11, ...), custom_call_target="tpu_custom_call" | custom-call | flops 1140850688 | bytes 9437184 | tf_op jit(solution)/shard_map/pallas_call | solution.py:215
  120.9 4.1 %shard_map.151 = (f32[64,2048]{1,0:T(8,128)S(1)}, f32[64,2048]{1,0:T(8,128)S(1)}) custom-call(bf16[64,2048]{1,0:T(8,128)(2,1)S(1)} %get-tuple-element.146.refs_0_, bf16[64,2048]{1,0:T(8,128)(2,1)S(1)} %get-tuple-element.145.refs_1_, bf16[128,128]{1,0:T(8,128)(2,1)S(1)} %get-tuple-element.149.refs_2_, bf16[2048,2048]{1,0:T(8,128)(2,1)} %refs_3_.11, ...), custom_call_target="tpu_custom_call" | custom-call | flops 1140850688 | bytes 9437184 | tf_op jit(solution)/shard_map/pallas_call | solution.py:215
  126.6 2.9 %collective-permute-done.40 = f16[64,2048]{1,0:T(8,128)(2,1)S(1)} collective-permute-done((f16[64,2048]{1,0:T(8,128)(2,1)S(1)}, f16[64,2048]{1,0:T(8,128)(2,1)S(1)}, u32[]{:S(2)}, u32[]{:S(2)}) %collective-permute-start.40) | collective-permute-done | bytes 262176 | tf_op jit(solution)/shard_map/ppermute | solution.py:99
  130.3 2.3 %collective-permute-start.43 = (f16[16,2048]{1,0:T(8,128)(2,1)S(1)}, f16[16,2048]{1,0:T(8,128)(2,1)S(1)}, u32[]{:S(2)}, u32[]{:S(2)}) collective-permute-start(f16[16,2048]{1,0:T(8,128)(2,1)S(1)} %get-tuple-element.102), channel_id=1, source_target_pairs={{0,24},{4,28},{8,16},{12,20},{16,8},{20,12},{24,0},{28,4},{1,25},{... | collective-permute-start | bytes 196616 | tf_op jit(solution)/shard_map/ppermute | solution.py:99
  135.1 2.3 %collective-permute-start.36 = (f16[16,2048]{1,0:T(8,128)(2,1)S(1)}, f16[16,2048]{1,0:T(8,128)(2,1)S(1)}, u32[]{:S(2)}, u32[]{:S(2)}) collective-permute-start(f16[16,2048]{1,0:T(8,128)(2,1)S(1)} %get-tuple-element.105), channel_id=1, source_target_pairs={{0,24},{4,28},{8,16},{12,20},{16,8},{20,12},{24,0},{28,4},{1,25},{... | collective-permute-start | bytes 196616 | tf_op jit(solution)/shard_map/ppermute | solution.py:99
  139.6 2.8 %collective-permute-done.34 = f16[16,2048]{1,0:T(8,128)(2,1)S(1)} collective-permute-done((f16[16,2048]{1,0:T(8,128)(2,1)S(1)}, f16[16,2048]{1,0:T(8,128)(2,1)S(1)}, u32[]{:S(2)}, u32[]{:S(2)}) %collective-permute-start.34) | collective-permute-done | bytes 65568 | tf_op jit(solution)/shard_map/ppermute | solution.py:99
  144.9 2.5 %collective-permute-done.37 = bf16[16,1024]{1,0:T(8,128)(2,1)S(1)} collective-permute-done((bf16[16,1024]{1,0:T(8,128)(2,1)S(1)}, bf16[16,1024]{1,0:T(8,128)(2,1)S(1)}, u32[]{:S(2)}, u32[]{:S(2)}) %collective-permute-start.37) | collective-permute-done | bytes 32800 | tf_op jit(solution)/shard_map/ppermute | solution.py:99
  152.3 2.7 %collective-permute-done.46.refs_1_ = bf16[64,1024]{1,0:T(8,128)(2,1)S(1)} collective-permute-done((bf16[64,1024]{1,0:T(8,128)(2,1)S(1)}, bf16[64,1024]{1,0:T(8,128)(2,1)S(1)}, u32[]{:S(2)}, u32[]{:S(2)}) %collective-permute-start.46) | collective-permute-done | bytes 131104 | tf_op jit(solution)/shard_map/ppermute | solution.py:99
  160.4 5.0 %collective-permute-done.48 = bf16[32,2048]{1,0:T(8,128)(2,1)S(1)} collective-permute-done((bf16[32,2048]{1,0:T(8,128)(2,1)S(1)}, bf16[32,2048]{1,0:T(8,128)(2,1)S(1)}, u32[]{:S(2)}, u32[]{:S(2)}) %collective-permute-start.48) | collective-permute-done | bytes 131104 | tf_op jit(solution)/shard_map/ppermute | solution.py:99
  (223 shorter events, 76.3 us)
Async XLA Ops:
  0.0 16.7 %collective-permute-start = (bf16[32,2048]{1,0:T(8,128)(2,1)}, bf16[32,2048]{1,0:T(8,128)(2,1)S(1)}, u32[]{:S(2)}, u32[]{:S(2)}) collective-permute-start(bf16[32,2048]{1,0:T(8,128)(2,1)} %param.14), channel_id=1, source_target_pairs={{0,2},{1,3},{2,0},{3,1},{4,6},{5,7},{6,4},{7,5},{8,10},{9,11},{10,... | collective-permute-start | bytes 393224 | tf_op jit(solution)/shard_map/ppermute | solution.py:99
  4.6 12.0 %all-to-all-start = ((f32[32,1,32]{2,1,0:T(1,128)}), f32[32,1,32]{2,1,0:T(1,128)S(1)}, u32[]{:S(2)}, u32[]{:S(2)}) async-start(f32[32,1,32]{2,1,0:T(1,128)} %broadcast_in_dim.17), calls=%async_computation | async-start | bytes 32768 | tf_op jit(solution)/shard_map/all_to_all | solution.py:407
  22.8 7.7 %collective-permute-start.2 = (s16[64,1664]{1,0:T(8,128)(2,1)S(1)}, s16[64,1664]{1,0:T(8,128)(2,1)S(1)}, u32[]{:S(2)}, u32[]{:S(2)}) collective-permute-start(s16[64,1664]{1,0:T(8,128)(2,1)S(1)} %get-tuple-element.58), channel_id=1, source_target_pairs={{0,4},{4,0},{8,12},{12,8},{16,20},{20,16},{24,28},{28,24},{1,5},{5... | collective-permute-start | bytes 638984 | tf_op jit(solution)/shard_map/ppermute | solution.py:99
  27.1 9.2 %collective-permute-start.5 = (s16[64,1664]{1,0:T(8,128)(2,1)S(1)}, s16[64,1664]{1,0:T(8,128)(2,1)S(1)}, u32[]{:S(2)}, u32[]{:S(2)}) collective-permute-start(s16[64,1664]{1,0:T(8,128)(2,1)S(1)} %get-tuple-element.65), channel_id=1, source_target_pairs={{0,4},{4,0},{8,12},{12,8},{16,20},{20,16},{24,28},{28,24},{1,5},{5... | collective-permute-start | bytes 638984 | tf_op jit(solution)/shard_map/ppermute | solution.py:99
  34.5 6.2 %collective-permute-start.8 = (s16[64,1664]{1,0:T(8,128)(2,1)S(1)}, s16[64,1664]{1,0:T(8,128)(2,1)S(1)}, u32[]{:S(2)}, u32[]{:S(2)}) collective-permute-start(s16[64,1664]{1,0:T(8,128)(2,1)S(1)} %get-tuple-element.74), channel_id=1, source_target_pairs={{0,4},{4,0},{8,12},{12,8},{16,20},{20,16},{24,28},{28,24},{1,5},{5... | collective-permute-start | bytes 638984 | tf_op jit(solution)/shard_map/ppermute | solution.py:99
  35.7 6.5 %collective-permute-start.3 = (s16[32,1664]{1,0:T(8,128)(2,1)S(1)}, s16[32,1664]{1,0:T(8,128)(2,1)S(1)}, u32[]{:S(2)}, u32[]{:S(2)}) collective-permute-start(s16[32,1664]{1,0:T(8,128)(2,1)S(1)} %get-tuple-element.61), channel_id=1, source_target_pairs={{0,8},{4,12},{8,0},{12,4},{16,24},{20,28},{24,16},{28,20},{1,9},{5... | collective-permute-start | bytes 319496 | tf_op jit(solution)/shard_map/ppermute | solution.py:99
  37.2 6.3 %collective-permute-start.6 = (s16[32,1664]{1,0:T(8,128)(2,1)S(1)}, s16[32,1664]{1,0:T(8,128)(2,1)S(1)}, u32[]{:S(2)}, u32[]{:S(2)}) collective-permute-start(s16[32,1664]{1,0:T(8,128)(2,1)S(1)} %get-tuple-element.67), channel_id=1, source_target_pairs={{0,8},{4,12},{8,0},{12,4},{16,24},{20,28},{24,16},{28,20},{1,9},{5... | collective-permute-start | bytes 319496 | tf_op jit(solution)/shard_map/ppermute | solution.py:99
  42.9 5.8 %collective-permute-start.4 = (s16[16,1664]{1,0:T(8,128)(2,1)S(1)}, s16[16,1664]{1,0:T(8,128)(2,1)S(1)}, u32[]{:S(2)}, u32[]{:S(2)}) collective-permute-start(s16[16,1664]{1,0:T(8,128)(2,1)S(1)} %get-tuple-element.63), channel_id=1, source_target_pairs={{0,16},{4,20},{8,24},{12,28},{16,0},{20,4},{24,8},{28,12},{1,17},{... | collective-permute-start | bytes 159752 | tf_op jit(solution)/shard_map/ppermute | solution.py:99
  44.2 6.7 %collective-permute-start.7 = (s16[16,1664]{1,0:T(8,128)(2,1)S(1)}, s16[16,1664]{1,0:T(8,128)(2,1)S(1)}, u32[]{:S(2)}, u32[]{:S(2)}) collective-permute-start(s16[16,1664]{1,0:T(8,128)(2,1)S(1)} %get-tuple-element.69), channel_id=1, source_target_pairs={{0,16},{4,20},{8,24},{12,28},{16,0},{20,4},{24,8},{28,12},{1,17},{... | collective-permute-start | bytes 159752 | tf_op jit(solution)/shard_map/ppermute | solution.py:99
  72.1 6.3 %collective-permute-start.18 = (bf16[16,2048]{1,0:T(8,128)(2,1)S(1)}, bf16[16,2048]{1,0:T(8,128)(2,1)S(1)}, u32[]{:S(2)}, u32[]{:S(2)}) collective-permute-start(bf16[16,2048]{1,0:T(8,128)(2,1)S(1)} %pad_maximum_fusion.10.array_ref), channel_id=1, source_target_pairs={{0,4},{4,0},{8,12},{12,8},{16,20},{20,16},{24,28},{28,24},{1,5},{5... | collective-permute-start | bytes 196616 | tf_op jit(solution)/shard_map/ppermute | solution.py:99
  72.8 6.6 %collective-permute-start.16 = (bf16[16,2048]{1,0:T(8,128)(2,1)S(1)}, bf16[16,2048]{1,0:T(8,128)(2,1)S(1)}, u32[]{:S(2)}, u32[]{:S(2)}) collective-permute-start(bf16[16,2048]{1,0:T(8,128)(2,1)S(1)} %pad_maximum_fusion.10.array_ref), channel_id=1, source_target_pairs={{0,8},{4,12},{8,0},{12,4},{16,24},{20,28},{24,16},{28,20},{1,9},{5... | collective-permute-start | bytes 196616 | tf_op jit(solution)/shard_map/ppermute | solution.py:99
  73.9 8.0 %collective-permute-start.15 = (bf16[16,2048]{1,0:T(8,128)(2,1)S(1)}, bf16[16,2048]{1,0:T(8,128)(2,1)S(1)}, u32[]{:S(2)}, u32[]{:S(2)}) collective-permute-start(bf16[16,2048]{1,0:T(8,128)(2,1)S(1)} %pad_maximum_fusion.10.array_ref), channel_id=1, source_target_pairs={{0,16},{4,20},{8,24},{12,28},{16,0},{20,4},{24,8},{28,12},{1,17},{... | collective-permute-start | bytes 196616 | tf_op jit(solution)/shard_map/ppermute | solution.py:99
  75.6 7.1 %collective-permute-start.22 = (bf16[16,2048]{1,0:T(8,128)(2,1)S(1)}, bf16[16,2048]{1,0:T(8,128)(2,1)S(1)}, u32[]{:S(2)}, u32[]{:S(2)}) collective-permute-start(bf16[16,2048]{1,0:T(8,128)(2,1)S(1)} %pad_maximum_fusion.11.array_ref), channel_id=1, source_target_pairs={{0,16},{4,20},{8,24},{12,28},{16,0},{20,4},{24,8},{28,12},{1,17},{... | collective-permute-start | bytes 196616 | tf_op jit(solution)/shard_map/ppermute | solution.py:99
  76.9 7.0 %collective-permute-start.25 = (bf16[16,2048]{1,0:T(8,128)(2,1)S(1)}, bf16[16,2048]{1,0:T(8,128)(2,1)S(1)}, u32[]{:S(2)}, u32[]{:S(2)}) collective-permute-start(bf16[16,2048]{1,0:T(8,128)(2,1)S(1)} %pad_maximum_fusion.11.array_ref), channel_id=1, source_target_pairs={{0,4},{4,0},{8,12},{12,8},{16,20},{20,16},{24,28},{28,24},{1,5},{5... | collective-permute-start | bytes 196616 | tf_op jit(solution)/shard_map/ppermute | solution.py:99
  78.4 7.0 %collective-permute-start.23 = (bf16[16,2048]{1,0:T(8,128)(2,1)S(1)}, bf16[16,2048]{1,0:T(8,128)(2,1)S(1)}, u32[]{:S(2)}, u32[]{:S(2)}) collective-permute-start(bf16[16,2048]{1,0:T(8,128)(2,1)S(1)} %pad_maximum_fusion.11.array_ref), channel_id=1, source_target_pairs={{0,8},{4,12},{8,0},{12,4},{16,24},{20,28},{24,16},{28,20},{1,9},{5... | collective-permute-start | bytes 196616 | tf_op jit(solution)/shard_map/ppermute | solution.py:99
  79.3 6.7 %collective-permute-start.20 = (bf16[16,2048]{1,0:T(8,128)(2,1)S(1)}, bf16[16,2048]{1,0:T(8,128)(2,1)S(1)}, u32[]{:S(2)}, u32[]{:S(2)}) collective-permute-start(bf16[16,2048]{1,0:T(8,128)(2,1)S(1)} %collective-permute-done.16.refs_2_), channel_id=1, source_target_pairs={{0,4},{4,0},{8,12},{12,8},{16,20},{20,16},{24,28},{28,24},{1,5},{5... | collective-permute-start | bytes 196616 | tf_op jit(solution)/shard_map/ppermute | solution.py:99
  103.3 11.1 %collective-permute-start.31 = (bf16[32,2048]{1,0:T(8,128)(2,1)S(1)}, bf16[32,2048]{1,0:T(8,128)(2,1)S(1)}, u32[]{:S(2)}, u32[]{:S(2)}) collective-permute-start(bf16[32,2048]{1,0:T(8,128)(2,1)S(1)} %get-tuple-element.92), channel_id=1, source_target_pairs={{0,2},{1,3},{2,0},{3,1},{4,6},{5,7},{6,4},{7,5},{8,10},{9,11},{10,... | collective-permute-start | bytes 393224 | tf_op jit(solution)/shard_map/ppermute | solution.py:99
  120.3 9.2 %collective-permute-start.40 = (f16[64,2048]{1,0:T(8,128)(2,1)S(1)}, f16[64,2048]{1,0:T(8,128)(2,1)S(1)}, u32[]{:S(2)}, u32[]{:S(2)}) collective-permute-start(f16[64,2048]{1,0:T(8,128)(2,1)S(1)} %convert_element_type.171), channel_id=1, source_target_pairs={{0,4},{4,0},{8,12},{12,8},{16,20},{20,16},{24,28},{28,24},{1,5},{5... | collective-permute-start | bytes 786440 | tf_op jit(solution)/shard_map/ppermute | solution.py:99
  125.0 9.3 %collective-permute-start.33 = (f16[64,2048]{1,0:T(8,128)(2,1)S(1)}, f16[64,2048]{1,0:T(8,128)(2,1)S(1)}, u32[]{:S(2)}, u32[]{:S(2)}) collective-permute-start(f16[64,2048]{1,0:T(8,128)(2,1)S(1)} %convert_element_type.165), channel_id=1, source_target_pairs={{0,4},{4,0},{8,12},{12,8},{16,20},{20,16},{24,28},{28,24},{1,5},{5... | collective-permute-start | bytes 786440 | tf_op jit(solution)/shard_map/ppermute | solution.py:99
  129.6 7.8 %collective-permute-start.41 = (f16[16,2048]{1,0:T(8,128)(2,1)S(1)}, f16[16,2048]{1,0:T(8,128)(2,1)S(1)}, u32[]{:S(2)}, u32[]{:S(2)}) collective-permute-start(f16[16,2048]{1,0:T(8,128)(2,1)S(1)} %get-tuple-element.101), channel_id=1, source_target_pairs={{0,16},{4,20},{8,24},{12,28},{16,0},{20,4},{24,8},{28,12},{1,17},{... | collective-permute-start | bytes 196616 | tf_op jit(solution)/shard_map/ppermute | solution.py:99
  130.3 7.7 %collective-permute-start.43 = (f16[16,2048]{1,0:T(8,128)(2,1)S(1)}, f16[16,2048]{1,0:T(8,128)(2,1)S(1)}, u32[]{:S(2)}, u32[]{:S(2)}) collective-permute-start(f16[16,2048]{1,0:T(8,128)(2,1)S(1)} %get-tuple-element.102), channel_id=1, source_target_pairs={{0,24},{4,28},{8,16},{12,20},{16,8},{20,12},{24,0},{28,4},{1,25},{... | collective-permute-start | bytes 196616 | tf_op jit(solution)/shard_map/ppermute | solution.py:99
  134.4 8.0 %collective-permute-start.34 = (f16[16,2048]{1,0:T(8,128)(2,1)S(1)}, f16[16,2048]{1,0:T(8,128)(2,1)S(1)}, u32[]{:S(2)}, u32[]{:S(2)}) collective-permute-start(f16[16,2048]{1,0:T(8,128)(2,1)S(1)} %get-tuple-element.104), channel_id=1, source_target_pairs={{0,16},{4,20},{8,24},{12,28},{16,0},{20,4},{24,8},{28,12},{1,17},{... | collective-permute-start | bytes 196616 | tf_op jit(solution)/shard_map/ppermute | solution.py:99
  135.1 7.3 %collective-permute-start.36 = (f16[16,2048]{1,0:T(8,128)(2,1)S(1)}, f16[16,2048]{1,0:T(8,128)(2,1)S(1)}, u32[]{:S(2)}, u32[]{:S(2)}) collective-permute-start(f16[16,2048]{1,0:T(8,128)(2,1)S(1)} %get-tuple-element.105), channel_id=1, source_target_pairs={{0,24},{4,28},{8,16},{12,20},{16,8},{20,12},{24,0},{28,4},{1,25},{... | collective-permute-start | bytes 196616 | tf_op jit(solution)/shard_map/ppermute | solution.py:99
  138.1 6.3 %collective-permute-start.44 = (bf16[16,1024]{1,0:T(8,128)(2,1)S(1)}, bf16[16,1024]{1,0:T(8,128)(2,1)S(1)}, u32[]{:S(2)}, u32[]{:S(2)}) collective-permute-start(bf16[16,1024]{1,0:T(8,128)(2,1)S(1)} %fusion.72.array_ref), channel_id=1, source_target_pairs={{0,16},{4,20},{8,24},{12,28},{16,0},{20,4},{24,8},{28,12},{1,17},{... | collective-permute-start | bytes 98312 | tf_op jit(solution)/shard_map/ppermute | solution.py:99
  (38 other events, 243.2 us)

commit v10 on v9

--- a/solution.py
+++ b/solution.py
@@ -80,8 +80,8 @@
 
 
 QKV_CHUNKS = 3
-FFN_SPLIT = 0.5
-CONTEXT_CHUNKS = 2
+FFN_EDGES = (0, 4, 10, 16)
+CONTEXT_CHUNKS = 1
 NARROW_KINDS = [jnp.float32] + [jnp.bfloat16] * 8
 TILE = 512
 ROOM = 24
@@ -291,9 +291,9 @@
     return add_codes(kept, [arrived])
 
 
-def wide_scatter(kept, sent):
+def wide_scatter(kept, arrived):
     rows = 2 * kept.shape[0] // lax.axis_size("wide")
-    kept = kept + swap(sent.astype(jnp.float16), "wide", 1).astype(jnp.float32)
+    kept = kept + arrived.astype(jnp.float32)
     total = kept[:rows]
     for place, offset in enumerate(offsets_of("wide")[: kept.shape[0] // rows]):
         if offset:
@@ -323,7 +323,7 @@
     held = [block]
     for stride in strides_of(axis)[::-1]:
         held = held + [swap(piece, axis, stride) for piece in held]
-    return [stand_in(block)] + held[1:]
+    return [stand_in(stand_in(block))] + held[1:]
 
 
 def exchange(blocks, axis):
@@ -475,12 +475,24 @@
     normed_two = normalized_rows(resid, ffn_gain)
 
     f_total = w_gate.shape[1]
-    f_edge = int(f_total * FFN_SPLIT) // LANES * LANES
+    f_edges = [f_total * edge // FFN_EDGES[-1] // LANES * LANES for edge in FFN_EDGES]
+    parts = []
+    arrivals = []
+    for chunk, (first, last) in enumerate(zip(f_edges[:-1], f_edges[1:])):
+        segments = [(w_gate, 0, first, last - first), (w_up, 0, first, last - first)]
+        if chunk >= 2:
+            normed_two, arrivals[chunk - 2] = lax.optimization_barrier(
+                (normed_two, arrivals[chunk - 2])
+            )
+        (kept, sent), normed_two = lax.optimization_barrier(
+            (project([normed_two], to_wide, False, segments, 2, direct=True), normed_two)
+        )
+        parts.append(kept)
+        arrivals.append(swap(sent.astype(jnp.float16), "wide", 1))
     total = None
-    for first, last in ((0, f_edge), (f_edge, f_total)):
+    for first, last, kept, arrived in zip(f_edges[:-1], f_edges[1:], parts, arrivals):
         f_cols = last - first
-        segments = [(w_gate, 0, first, f_cols), (w_up, 0, first, f_cols)]
-        sums = wide_scatter(*project([normed_two], to_wide, False, segments, 2, direct=True))
+        sums = wide_scatter(kept, arrived)
         act = (jax.nn.silu(sums[:, :f_cols]) * sums[:, f_cols:]).astype(jnp.bfloat16)
         total = project(
             [gather(act, "wide", paired=True)],

time: 166 us -> 187 us (1.13)
  waiting for transfers between devices: 60.4 us -> 80.2 us
  Pallas kernels: 29.1 us -> 31.1 us
    ppermute x49, waiting for transfers between devices: 55.5 us -> 75.3 us  [swap(): return lax.ppermute(block, axis, [(i, i ^ offset) for i in range(count)])]
    pallas_call x8 -> x10, Pallas kernels: 23.9 us -> 25.9 us  [project(): pl.pallas_call(body, in_specs=specs, out_specs=[in_vmem] * split, scratch...]
where the time goes in v10:
time: 187 us
  waiting for transfers between devices  80.2 us (43%)
  starting transfers between devices  49.5 us (26%)
  Pallas kernels  31.1 us (17%)
  blocking collectives  10.9 us (6%)
  other arithmetic  7.17 us (4%)
  matrix products  5.16 us (3%)
  local copies, waits for them, and re-layouts  2.34 us (1%)
    ppermute x49, waiting for transfers between devices, swap(): return lax.ppermute(block, axis, [(i, i ^ offset) for i in range(count)])  75.3 us
    ppermute x49, starting transfers between devices, swap(): return lax.ppermute(block, axis, [(i, i ^ offset) for i in range(count)])  44.6 us
    pallas_call x10, Pallas kernels, project(): pl.pallas_call(body, in_specs=specs, out_specs=[in_vmem] * split, scratch...  25.9 us
    all_to_all x1, blocking collectives, normalized_rows(): landed = lax.all_to_all(sent, ('wide', 'narrow'), 0, 0, tiled=True)  10.9 us
    all_to_all x1, starting transfers between devices, normalized_rows(): landed = lax.all_to_all(sent, ('wide', 'narrow'), 0, 0, tiled=True)  4.92 us
    all_to_all x1, waiting for transfers between devices, normalized_rows(): landed = lax.all_to_all(sent, ('wide', 'narrow'), 0, 0, tiled=True)  4.92 us
    pallas_call x6, Pallas kernels, fold(): pl.pallas_call(body, out_shape=[jax.ShapeDtypeStruct((rows, width), jnp.f...  4.76 us
    dot_general x1, matrix products, attend(): jnp.einsum('rgqd,rlgd->rgql', query_heads, cache_keys, preferred_element_...  3.86 us
  transfers between devices with their start and end apart: 50, of which 30 were waited for; matrix products, arithmetic and copies ran while one was open for 3% of the time, Pallas kernels for 11%

profile of v10, /device:TPU:0, one launch (start us, length us, event | category | flops | bytes accessed | tf_op | source)
XLA Modules:
  0.0 187.2 jit_solution(6029645950393328466)
XLA Ops:
  0.0 2.9 %collective-permute-start = (bf16[32,2048]{1,0:T(8,128)(2,1)}, bf16[32,2048]{1,0:T(8,128)(2,1)S(1)}, u32[]{:S(2)}, u32[]{:S(2)}) collective-permute-start(bf16[32,2048]{1,0:T(8,128)(2,1)} %param.14), channel_id=1, source_target_pairs={{0,2},{1,3},{2,0},{3,1},{4,6},{5,7},{6,4},{7,5},{8,10},{9,11},{10,... | collective-permute-start | bytes 393224 | tf_op jit(solution)/shard_map/ppermute | solution.py:99
  4.6 4.9 %all-to-all-start = ((f32[32,1,32]{2,1,0:T(1,128)}), f32[32,1,32]{2,1,0:T(1,128)S(1)}, u32[]{:S(2)}, u32[]{:S(2)}) async-start(f32[32,1,32]{2,1,0:T(1,128)} %broadcast_in_dim.17), calls=%async_computation | async-start | bytes 32768 | tf_op jit(solution)/shard_map/all_to_all | solution.py:407
  11.7 4.9 %all-to-all-done = f32[32,1,32]{2,1,0:T(1,128)S(1)} async-done(((f32[32,1,32]{2,1,0:T(1,128)}), f32[32,1,32]{2,1,0:T(1,128)S(1)}, u32[]{:S(2)}, u32[]{:S(2)}) %all-to-all-start) | async-done | bytes 4128 | tf_op jit(solution)/shard_map/all_to_all | solution.py:407
  19.2 3.6 %shard_map.136 = (f32[64,1536]{1,0:T(8,128)S(1)}, s16[64,1664]{1,0:T(8,128)(2,1)S(1)}) custom-call(bf16[64,2048]{1,0:T(8,128)(2,1)S(1)} %get-tuple-element.175.refs_0_, bf16[64,2048]{1,0:T(8,128)(2,1)S(1)} %get-tuple-element.174.refs_1_, bf16[128,128]{1,0:T(8,128)(2,1)S(1)} %get-tuple-element.85.refs_2_.refs_8_, bf16[2048,4096]{1,0:T(8,128)(2,1)} %refs_3_.11), custom_call_target="tpu_custom_call" | custom-call | flops 872415232 | bytes 7077888 | tf_op jit(solution)/shard_map/pallas_call | solution.py:215
  23.4 3.6 %shard_map.137 = (f32[64,1536]{1,0:T(8,128)S(1)}, s16[64,1664]{1,0:T(8,128)(2,1)S(1)}) custom-call(bf16[64,2048]{1,0:T(8,128)(2,1)S(1)} %get-tuple-element.175.refs_0_, bf16[64,2048]{1,0:T(8,128)(2,1)S(1)} %get-tuple-element.174.refs_1_, bf16[128,128]{1,0:T(8,128)(2,1)S(1)} %get-tuple-element.85.refs_2_.refs_8_, bf16[2048,4096]{1,0:T(8,128)(2,1)} %refs_3_.11), custom_call_target="tpu_custom_call" | custom-call | flops 872415232 | bytes 7077888 | tf_op jit(solution)/shard_map/pallas_call | solution.py:215
  30.6 3.9 %shard_map.144 = (f32[64,1536]{1,0:T(8,128)S(1)}, s16[64,1664]{1,0:T(8,128)(2,1)S(1)}) custom-call(bf16[64,2048]{1,0:T(8,128)(2,1)S(1)} %get-tuple-element.175.refs_0_, bf16[64,2048]{1,0:T(8,128)(2,1)S(1)} %get-tuple-element.174.refs_1_, bf16[128,128]{1,0:T(8,128)(2,1)S(1)} %get-tuple-element.85.refs_2_.refs_8_, bf16[2048,4096]{1,0:T(8,128)(2,1)} %refs_3_.11, ...), custom_call_target="tpu_custom_call" | custom-call | flops 872415232 | bytes 7077888 | tf_op jit(solution)/shard_map/pallas_call | solution.py:215
  44.2 2.4 %collective-permute-start.7 = (s16[16,1664]{1,0:T(8,128)(2,1)S(1)}, s16[16,1664]{1,0:T(8,128)(2,1)S(1)}, u32[]{:S(2)}, u32[]{:S(2)}) collective-permute-start(s16[16,1664]{1,0:T(8,128)(2,1)S(1)} %get-tuple-element.84), channel_id=1, source_target_pairs={{0,16},{4,20},{8,24},{12,28},{16,0},{20,4},{24,8},{28,12},{1,17},{... | collective-permute-start | bytes 159752 | tf_op jit(solution)/shard_map/ppermute | solution.py:99
  53.7 3.8 %collective-permute-done.11 = bf16[2,4,36,128]{3,2,1,0:T(8,128)(2,1)S(1)} collective-permute-done((bf16[2,4,36,128]{3,2,1,0:T(8,128)(2,1)S(1)}, bf16[2,4,36,128]{3,2,1,0:T(8,128)(2,1)S(1)}, u32[]{:S(2)}, u32[]{:S(2)}) %collective-permute-start.11) | collective-permute-done | bytes 73760 | tf_op jit(solution)/shard_map/ppermute | solution.py:99
  60.4 3.9 %fusion.115 = (f32[4,8,16]{2,1,0:T(8,128)S(1)}, f32[4,8,16,512]{3,2,1,0:T(8,128)S(1)}) fusion(bf16[4,8,16,64]{3,2,1,0:T(8,128)(2,1)S(1)} %bitcast.84, bf16[4,8,16,64]{3,2,1,0:T(8,128)(2,1)S(1)} %bitcast.82, pred[4,512]{1,0:T(4,128)(4,1)S(1)} %iota_compare_fusion, bf16[4,512,1024]{2,1,0:T(8,128)(2,1)} %param.24), kind=kOutput, calls=%fused_computation.236 | convolution fusion | flops 68156928 | bytes 5378048 | tf_op jit(solution)/shard_map/rgqd,rlgd->rgql/dot_general | solution.py:59
  66.9 3.8 %collective-permute-done.13 = bf16[2,4,4096]{2,1,0:T(4,128)(2,1)S(1)} collective-permute-done((bf16[2,4,4096]{2,1,0:T(4,128)(2,1)S(1)}, bf16[2,4,4096]{2,1,0:T(4,128)(2,1)S(1)}, u32[]{:S(2)}, u32[]{:S(2)}) %collective-permute-start.13) | collective-permute-done | bytes 65568 | tf_op jit(solution)/shard_map/ppermute | solution.py:99
  73.9 7.5 %collective-permute-done.15.refs_1_ = bf16[16,4096]{1,0:T(8,128)(2,1)S(1)} collective-permute-done((bf16[16,4096]{1,0:T(8,128)(2,1)S(1)}, bf16[16,4096]{1,0:T(8,128)(2,1)S(1)}, u32[]{:S(2)}, u32[]{:S(2)}) %collective-permute-start.15) | collective-permute-done | bytes 131104 | tf_op jit(solution)/shard_map/ppermute | solution.py:99
  88.0 5.5 %collective-permute-done.20.refs_6_ = bf16[16,4096]{1,0:T(8,128)(2,1)S(1)} collective-permute-done((bf16[16,4096]{1,0:T(8,128)(2,1)S(1)}, bf16[16,4096]{1,0:T(8,128)(2,1)S(1)}, u32[]{:S(2)}, u32[]{:S(2)}) %collective-permute-start.20) | collective-permute-done | bytes 131104 | tf_op jit(solution)/shard_map/ppermute | solution.py:99
  94.9 2.9 %shard_map.150 = (f32[64,2048]{1,0:T(8,128)S(1)}, f32[64,2048]{1,0:T(8,128)S(1)}) custom-call(bf16[16,4096]{1,0:T(8,128)(2,1)S(1)} %shard_map.149.refs_0_, bf16[16,4096]{1,0:T(8,128)(2,1)S(1)} %collective-permute-done.15.refs_1_, bf16[16,4096]{1,0:T(8,128)(2,1)S(1)} %collective-permute-done.16.refs_2_, bf16[16,4096]{1,0:T(8,128)(2,1)S(1)} %collective-permute-done.17.refs_3_, ...), custom_call_target="tpu_custom_call" | custom-call | flops 2281701376 | bytes 17825792 | tf_op jit(solution)/shard_map/pallas_call | solution.py:215
  100.4 5.0 %collective-permute-done.23 = bf16[32,2048]{1,0:T(8,128)(2,1)S(1)} collective-permute-done((bf16[32,2048]{1,0:T(8,128)(2,1)S(1)}, bf16[32,2048]{1,0:T(8,128)(2,1)S(1)}, u32[]{:S(2)}, u32[]{:S(2)}) %collective-permute-start.23) | collective-permute-done | bytes 131104 | tf_op jit(solution)/shard_map/ppermute | solution.py:99
  106.2 10.9 %all_to_all.12 = f32[32,1,32]{2,1,0:T(1,128)S(1)} all-to-all(f32[32,1,32]{2,1,0:T(1,128)S(1)} %broadcast_in_dim.20), channel_id=1, replica_groups=mesh['wide'=8,'narrow'=4] {'wide','narrow'}, dimensions={0} | all-to-all | bytes 8192 | tf_op jit(solution)/shard_map/all_to_all | solution.py:407
  118.9 2.8 %shard_map.151 = (f32[64,1024]{1,0:T(8,128)S(1)}, f32[64,1024]{1,0:T(8,128)S(1)}) custom-call(bf16[64,2048]{1,0:T(8,128)(2,1)S(1)} %get-tuple-element.105.refs_0_, bf16[64,2048]{1,0:T(8,128)(2,1)S(1)} %get-tuple-element.106.refs_1_, bf16[128,128]{1,0:T(8,128)(2,1)S(1)} %get-tuple-element.176.refs_2_, bf16[2048,2048]{1,0:T(8,128)(2,1)} %refs_3_.14, ...), custom_call_target="tpu_custom_call" | custom-call | flops 603979776 | bytes 4718592 | tf_op jit(solution)/shard_map/pallas_call | solution.py:215
  122.4 3.6 %shard_map.152 = (f32[64,1536]{1,0:T(8,128)S(1)}, f32[64,1536]{1,0:T(8,128)S(1)}) custom-call(bf16[64,2048]{1,0:T(8,128)(2,1)S(1)} %get-tuple-element.105.refs_0_, bf16[64,2048]{1,0:T(8,128)(2,1)S(1)} %get-tuple-element.106.refs_1_, bf16[128,128]{1,0:T(8,128)(2,1)S(1)} %get-tuple-element.176.refs_2_, bf16[2048,2048]{1,0:T(8,128)(2,1)} %refs_3_.14, ...), custom_call_target="tpu_custom_call" | custom-call | flops 872415232 | bytes 7077888 | tf_op jit(solution)/shard_map/pallas_call | solution.py:215
  131.1 3.6 %shard_map.153 = (f32[64,1536]{1,0:T(8,128)S(1)}, f32[64,1536]{1,0:T(8,128)S(1)}) custom-call(bf16[64,2048]{1,0:T(8,128)(2,1)S(1)} %get-tuple-element.105.refs_0_, bf16[64,2048]{1,0:T(8,128)(2,1)S(1)} %get-tuple-element.106.refs_1_, bf16[128,128]{1,0:T(8,128)(2,1)S(1)} %get-tuple-element.176.refs_2_, bf16[2048,2048]{1,0:T(8,128)(2,1)} %refs_3_.14, ...), custom_call_target="tpu_custom_call" | custom-call | flops 872415232 | bytes 7077888 | tf_op jit(solution)/shard_map/pallas_call | solution.py:215
  137.0 3.1 %collective-permute-done.44 = bf16[16,512]{1,0:T(8,128)(2,1)S(1)} collective-permute-done((bf16[16,512]{1,0:T(8,128)(2,1)S(1)}, bf16[16,512]{1,0:T(8,128)(2,1)S(1)}, u32[]{:S(2)}, u32[]{:S(2)}) %collective-permute-start.44) | collective-permute-done | bytes 16416 | tf_op jit(solution)/shard_map/ppermute | solution.py:99
  141.9 2.9 %collective-permute-start.37 = (f16[16,1536]{1,0:T(8,128)(2,1)S(1)}, f16[16,1536]{1,0:T(8,128)(2,1)S(1)}, u32[]{:S(2)}, u32[]{:S(2)}) collective-permute-start(f16[16,1536]{1,0:T(8,128)(2,1)S(1)} %get-tuple-element.137), channel_id=1, source_target_pairs={{0,24},{4,28},{8,16},{12,20},{16,8},{20,12},{24,0},{28,4},{1,25},{... | collective-permute-start | bytes 147464 | tf_op jit(solution)/shard_map/ppermute | solution.py:99
  149.9 4.9 %collective-permute-done.38 = bf16[16,768]{1,0:T(8,128)(2,1)S(1)} collective-permute-done((bf16[16,768]{1,0:T(8,128)(2,1)S(1)}, bf16[16,768]{1,0:T(8,128)(2,1)S(1)}, u32[]{:S(2)}, u32[]{:S(2)}) %collective-permute-start.38) | collective-permute-done | bytes 24608 | tf_op jit(solution)/shard_map/ppermute | solution.py:99
  165.0 4.2 %collective-permute-done.31 = bf16[16,768]{1,0:T(8,128)(2,1)S(1)} collective-permute-done((bf16[16,768]{1,0:T(8,128)(2,1)S(1)}, bf16[16,768]{1,0:T(8,128)(2,1)S(1)}, u32[]{:S(2)}, u32[]{:S(2)}) %collective-permute-start.31) | collective-permute-done | bytes 24608 | tf_op jit(solution)/shard_map/ppermute | solution.py:99
  169.6 3.8 %collective-permute-done.32 = bf16[32,768]{1,0:T(8,128)(2,1)S(1)} collective-permute-done((bf16[32,768]{1,0:T(8,128)(2,1)S(1)}, bf16[32,768]{1,0:T(8,128)(2,1)S(1)}, u32[]{:S(2)}, u32[]{:S(2)}) %collective-permute-start.32) | collective-permute-done | bytes 49184 | tf_op jit(solution)/shard_map/ppermute | solution.py:99
  181.6 4.9 %collective-permute-done.48 = bf16[32,2048]{1,0:T(8,128)(2,1)S(1)} collective-permute-done((bf16[32,2048]{1,0:T(8,128)(2,1)S(1)}, bf16[32,2048]{1,0:T(8,128)(2,1)S(1)}, u32[]{:S(2)}, u32[]{:S(2)}) %collective-permute-start.48) | collective-permute-done | bytes 131104 | tf_op jit(solution)/shard_map/ppermute | solution.py:99
  (229 shorter events, 83.0 us)
Async XLA Ops:
  0.0 16.7 %collective-permute-start = (bf16[32,2048]{1,0:T(8,128)(2,1)}, bf16[32,2048]{1,0:T(8,128)(2,1)S(1)}, u32[]{:S(2)}, u32[]{:S(2)}) collective-permute-start(bf16[32,2048]{1,0:T(8,128)(2,1)} %param.14), channel_id=1, source_target_pairs={{0,2},{1,3},{2,0},{3,1},{4,6},{5,7},{6,4},{7,5},{8,10},{9,11},{10,... | collective-permute-start | bytes 393224 | tf_op jit(solution)/shard_map/ppermute | solution.py:99
  4.6 12.0 %all-to-all-start = ((f32[32,1,32]{2,1,0:T(1,128)}), f32[32,1,32]{2,1,0:T(1,128)S(1)}, u32[]{:S(2)}, u32[]{:S(2)}) async-start(f32[32,1,32]{2,1,0:T(1,128)} %broadcast_in_dim.17), calls=%async_computation | async-start | bytes 32768 | tf_op jit(solution)/shard_map/all_to_all | solution.py:407
  22.8 7.7 %collective-permute-start.2 = (s16[64,1664]{1,0:T(8,128)(2,1)S(1)}, s16[64,1664]{1,0:T(8,128)(2,1)S(1)}, u32[]{:S(2)}, u32[]{:S(2)}) collective-permute-start(s16[64,1664]{1,0:T(8,128)(2,1)S(1)} %get-tuple-element.73), channel_id=1, source_target_pairs={{0,4},{4,0},{8,12},{12,8},{16,20},{20,16},{24,28},{28,24},{1,5},{5... | collective-permute-start | bytes 638984 | tf_op jit(solution)/shard_map/ppermute | solution.py:99
  27.1 9.2 %collective-permute-start.5 = (s16[64,1664]{1,0:T(8,128)(2,1)S(1)}, s16[64,1664]{1,0:T(8,128)(2,1)S(1)}, u32[]{:S(2)}, u32[]{:S(2)}) collective-permute-start(s16[64,1664]{1,0:T(8,128)(2,1)S(1)} %get-tuple-element.80), channel_id=1, source_target_pairs={{0,4},{4,0},{8,12},{12,8},{16,20},{20,16},{24,28},{28,24},{1,5},{5... | collective-permute-start | bytes 638984 | tf_op jit(solution)/shard_map/ppermute | solution.py:99
  34.5 6.2 %collective-permute-start.8 = (s16[64,1664]{1,0:T(8,128)(2,1)S(1)}, s16[64,1664]{1,0:T(8,128)(2,1)S(1)}, u32[]{:S(2)}, u32[]{:S(2)}) collective-permute-start(s16[64,1664]{1,0:T(8,128)(2,1)S(1)} %get-tuple-element.89), channel_id=1, source_target_pairs={{0,4},{4,0},{8,12},{12,8},{16,20},{20,16},{24,28},{28,24},{1,5},{5... | collective-permute-start | bytes 638984 | tf_op jit(solution)/shard_map/ppermute | solution.py:99
  35.7 6.5 %collective-permute-start.3 = (s16[32,1664]{1,0:T(8,128)(2,1)S(1)}, s16[32,1664]{1,0:T(8,128)(2,1)S(1)}, u32[]{:S(2)}, u32[]{:S(2)}) collective-permute-start(s16[32,1664]{1,0:T(8,128)(2,1)S(1)} %get-tuple-element.76), channel_id=1, source_target_pairs={{0,8},{4,12},{8,0},{12,4},{16,24},{20,28},{24,16},{28,20},{1,9},{5... | collective-permute-start | bytes 319496 | tf_op jit(solution)/shard_map/ppermute | solution.py:99
  37.2 6.3 %collective-permute-start.6 = (s16[32,1664]{1,0:T(8,128)(2,1)S(1)}, s16[32,1664]{1,0:T(8,128)(2,1)S(1)}, u32[]{:S(2)}, u32[]{:S(2)}) collective-permute-start(s16[32,1664]{1,0:T(8,128)(2,1)S(1)} %get-tuple-element.82), channel_id=1, source_target_pairs={{0,8},{4,12},{8,0},{12,4},{16,24},{20,28},{24,16},{28,20},{1,9},{5... | collective-permute-start | bytes 319496 | tf_op jit(solution)/shard_map/ppermute | solution.py:99
  44.2 6.7 %collective-permute-start.7 = (s16[16,1664]{1,0:T(8,128)(2,1)S(1)}, s16[16,1664]{1,0:T(8,128)(2,1)S(1)}, u32[]{:S(2)}, u32[]{:S(2)}) collective-permute-start(s16[16,1664]{1,0:T(8,128)(2,1)S(1)} %get-tuple-element.84), channel_id=1, source_target_pairs={{0,16},{4,20},{8,24},{12,28},{16,0},{20,4},{24,8},{28,12},{1,17},{... | collective-permute-start | bytes 159752 | tf_op jit(solution)/shard_map/ppermute | solution.py:99
  72.1 9.3 %collective-permute-start.15 = (bf16[16,4096]{1,0:T(8,128)(2,1)S(1)}, bf16[16,4096]{1,0:T(8,128)(2,1)S(1)}, u32[]{:S(2)}, u32[]{:S(2)}) collective-permute-start(bf16[16,4096]{1,0:T(8,128)(2,1)S(1)} %pad_maximum_fusion.4.array_ref), channel_id=1, source_target_pairs={{0,16},{4,20},{8,24},{12,28},{16,0},{20,4},{24,8},{28,12},{1,17},{... | collective-permute-start | bytes 393224 | tf_op jit(solution)/shard_map/ppermute | solution.py:99
  73.2 10.4 %collective-permute-start.16 = (bf16[16,4096]{1,0:T(8,128)(2,1)S(1)}, bf16[16,4096]{1,0:T(8,128)(2,1)S(1)}, u32[]{:S(2)}, u32[]{:S(2)}) collective-permute-start(bf16[16,4096]{1,0:T(8,128)(2,1)S(1)} %pad_maximum_fusion.4.array_ref), channel_id=1, source_target_pairs={{0,8},{4,12},{8,0},{12,4},{16,24},{20,28},{24,16},{28,20},{1,9},{5... | collective-permute-start | bytes 393224 | tf_op jit(solution)/shard_map/ppermute | solution.py:99
  81.5 6.5 %collective-permute-start.18 = (bf16[16,4096]{1,0:T(8,128)(2,1)S(1)}, bf16[16,4096]{1,0:T(8,128)(2,1)S(1)}, u32[]{:S(2)}, u32[]{:S(2)}) collective-permute-start(bf16[16,4096]{1,0:T(8,128)(2,1)S(1)} %pad_maximum_fusion.4.array_ref), channel_id=1, source_target_pairs={{0,4},{4,0},{8,12},{12,8},{16,20},{20,16},{24,28},{28,24},{1,5},{5... | collective-permute-start | bytes 393224 | tf_op jit(solution)/shard_map/ppermute | solution.py:99
  82.1 11.3 %collective-permute-start.19 = (bf16[16,4096]{1,0:T(8,128)(2,1)S(1)}, bf16[16,4096]{1,0:T(8,128)(2,1)S(1)}, u32[]{:S(2)}, u32[]{:S(2)}) collective-permute-start(bf16[16,4096]{1,0:T(8,128)(2,1)S(1)} %collective-permute-done.15.refs_1_), channel_id=1, source_target_pairs={{0,4},{4,0},{8,12},{12,8},{16,20},{20,16},{24,28},{28,24},{1,5},{5... | collective-permute-start | bytes 393224 | tf_op jit(solution)/shard_map/ppermute | solution.py:99
  83.6 9.9 %collective-permute-start.20 = (bf16[16,4096]{1,0:T(8,128)(2,1)S(1)}, bf16[16,4096]{1,0:T(8,128)(2,1)S(1)}, u32[]{:S(2)}, u32[]{:S(2)}) collective-permute-start(bf16[16,4096]{1,0:T(8,128)(2,1)S(1)} %collective-permute-done.16.refs_2_), channel_id=1, source_target_pairs={{0,4},{4,0},{8,12},{12,8},{16,20},{20,16},{24,28},{28,24},{1,5},{5... | collective-permute-start | bytes 393224 | tf_op jit(solution)/shard_map/ppermute | solution.py:99
  86.4 8.5 %collective-permute-start.21 = (bf16[16,4096]{1,0:T(8,128)(2,1)S(1)}, bf16[16,4096]{1,0:T(8,128)(2,1)S(1)}, u32[]{:S(2)}, u32[]{:S(2)}) collective-permute-start(bf16[16,4096]{1,0:T(8,128)(2,1)S(1)} %collective-permute-done.17.refs_3_), channel_id=1, source_target_pairs={{0,4},{4,0},{8,12},{12,8},{16,20},{20,16},{24,28},{28,24},{1,5},{5... | collective-permute-start | bytes 393224 | tf_op jit(solution)/shard_map/ppermute | solution.py:99
  105.6 11.4 %collective-permute-start.24 = (bf16[32,2048]{1,0:T(8,128)(2,1)S(1)}, bf16[32,2048]{1,0:T(8,128)(2,1)S(1)}, u32[]{:S(2)}, u32[]{:S(2)}) collective-permute-start(bf16[32,2048]{1,0:T(8,128)(2,1)S(1)} %get-tuple-element.124), channel_id=1, source_target_pairs={{0,2},{1,3},{2,0},{3,1},{4,6},{5,7},{6,4},{7,5},{8,10},{9,11},{10,... | collective-permute-start | bytes 393224 | tf_op jit(solution)/shard_map/ppermute | solution.py:99
  126.0 15.7 %collective-permute-start.34 = (f16[64,1536]{1,0:T(8,128)(2,1)S(1)}, f16[64,1536]{1,0:T(8,128)(2,1)S(1)}, u32[]{:S(2)}, u32[]{:S(2)}) collective-permute-start(f16[64,1536]{1,0:T(8,128)(2,1)S(1)} %convert_element_type.193), channel_id=1, source_target_pairs={{0,4},{4,0},{8,12},{12,8},{16,20},{20,16},{24,28},{28,24},{1,5},{5... | collective-permute-start | bytes 589832 | tf_op jit(solution)/shard_map/ppermute | solution.py:99
  127.6 7.8 %collective-permute-start.41 = (f16[16,1024]{1,0:T(8,128)(2,1)S(1)}, f16[16,1024]{1,0:T(8,128)(2,1)S(1)}, u32[]{:S(2)}, u32[]{:S(2)}) collective-permute-start(f16[16,1024]{1,0:T(8,128)(2,1)S(1)} %get-tuple-element.154), channel_id=1, source_target_pairs={{0,16},{4,20},{8,24},{12,28},{16,0},{20,4},{24,8},{28,12},{1,17},{... | collective-permute-start | bytes 98312 | tf_op jit(solution)/shard_map/ppermute | solution.py:99
  128.2 7.1 %collective-permute-start.43 = (f16[16,1024]{1,0:T(8,128)(2,1)S(1)}, f16[16,1024]{1,0:T(8,128)(2,1)S(1)}, u32[]{:S(2)}, u32[]{:S(2)}) collective-permute-start(f16[16,1024]{1,0:T(8,128)(2,1)S(1)} %get-tuple-element.155), channel_id=1, source_target_pairs={{0,24},{4,28},{8,16},{12,20},{16,8},{20,12},{24,0},{28,4},{1,25},{... | collective-permute-start | bytes 98312 | tf_op jit(solution)/shard_map/ppermute | solution.py:99
  134.7 20.2 %collective-permute-start.27 = (f16[64,1536]{1,0:T(8,128)(2,1)S(1)}, f16[64,1536]{1,0:T(8,128)(2,1)S(1)}, u32[]{:S(2)}, u32[]{:S(2)}) collective-permute-start(f16[64,1536]{1,0:T(8,128)(2,1)S(1)} %convert_element_type.187), channel_id=1, source_target_pairs={{0,4},{4,0},{8,12},{12,8},{16,20},{20,16},{24,28},{28,24},{1,5},{5... | collective-permute-start | bytes 589832 | tf_op jit(solution)/shard_map/ppermute | solution.py:99
  141.8 6.1 %collective-permute-start.35 = (f16[16,1536]{1,0:T(8,128)(2,1)S(1)}, f16[16,1536]{1,0:T(8,128)(2,1)S(1)}, u32[]{:S(2)}, u32[]{:S(2)}) collective-permute-start(f16[16,1536]{1,0:T(8,128)(2,1)S(1)} %get-tuple-element.136), channel_id=1, source_target_pairs={{0,16},{4,20},{8,24},{12,28},{16,0},{20,4},{24,8},{28,12},{1,17},{... | collective-permute-start | bytes 147464 | tf_op jit(solution)/shard_map/ppermute | solution.py:99
  141.9 6.0 %collective-permute-start.37 = (f16[16,1536]{1,0:T(8,128)(2,1)S(1)}, f16[16,1536]{1,0:T(8,128)(2,1)S(1)}, u32[]{:S(2)}, u32[]{:S(2)}) collective-permute-start(f16[16,1536]{1,0:T(8,128)(2,1)S(1)} %get-tuple-element.137), channel_id=1, source_target_pairs={{0,24},{4,28},{8,16},{12,20},{16,8},{20,12},{24,0},{28,4},{1,25},{... | collective-permute-start | bytes 147464 | tf_op jit(solution)/shard_map/ppermute | solution.py:99
  145.3 29.6 %collective-permute-start.46 = (bf16[64,512]{1,0:T(8,128)(2,1)S(1)}, bf16[64,512]{1,0:T(8,128)(2,1)S(1)}, u32[]{:S(2)}, u32[]{:S(2)}) collective-permute-start(bf16[64,512]{1,0:T(8,128)(2,1)S(1)} %pad_maximum_fusion.11.refs_0_), channel_id=1, source_target_pairs={{0,4},{4,0},{8,12},{12,8},{16,20},{20,16},{24,28},{28,24},{1,5},{5... | collective-permute-start | bytes 196616 | tf_op jit(solution)/shard_map/ppermute | solution.py:99
  155.1 6.0 %collective-permute-start.28 = (f16[16,1536]{1,0:T(8,128)(2,1)S(1)}, f16[16,1536]{1,0:T(8,128)(2,1)S(1)}, u32[]{:S(2)}, u32[]{:S(2)}) collective-permute-start(f16[16,1536]{1,0:T(8,128)(2,1)S(1)} %get-tuple-element.139), channel_id=1, source_target_pairs={{0,16},{4,20},{8,24},{12,28},{16,0},{20,4},{24,8},{28,12},{1,17},{... | collective-permute-start | bytes 147464 | tf_op jit(solution)/shard_map/ppermute | solution.py:99
  159.5 16.0 %collective-permute-start.40 = (bf16[64,768]{1,0:T(8,128)(2,1)S(1)}, bf16[64,768]{1,0:T(8,128)(2,1)S(1)}, u32[]{:S(2)}, u32[]{:S(2)}) collective-permute-start(bf16[64,768]{1,0:T(8,128)(2,1)S(1)} %pad_maximum_fusion.6.refs_0_), channel_id=1, source_target_pairs={{0,4},{4,0},{8,12},{12,8},{16,20},{20,16},{24,28},{28,24},{1,5},{5... | collective-permute-start | bytes 294920 | tf_op jit(solution)/shard_map/ppermute | solution.py:99
  (38 other events, 267.9 us)

commit v11 on v9

--- a/solution.py
+++ b/solution.py
@@ -311,12 +311,18 @@
     return kept
 
 
-def gather(block, axis, paired=False):
+def gather(block, axis):
     strides = strides_of(axis)[::-1]
     for stride in strides[:-1]:
-        held = stand_in(block) if paired else block
-        block = jnp.concatenate([held, swap(block, axis, stride)], axis=0)
+        block = jnp.concatenate([block, swap(block, axis, stride)], axis=0)
     return [block, swap(block, axis, strides[-1])]
+
+
+def gather_in_two(block, axis):
+    offsets = offsets_of(axis)
+    far = [swap(block, axis, offset) for offset in offsets[1 : len(offsets) // 2]]
+    block = jnp.concatenate([stand_in(block)] + far, axis=0)
+    return [block, swap(block, axis, 1)]
 
 
 def gather_pieces(block, axis):
@@ -483,7 +489,7 @@
         sums = wide_scatter(*project([normed_two], to_wide, False, segments, 2, direct=True))
         act = (jax.nn.silu(sums[:, :f_cols]) * sums[:, f_cols:]).astype(jnp.bfloat16)
         total = project(
-            [gather(act, "wide", paired=True)],
+            [gather_in_two(act, "wide")],
             to_wide,
             True,
             [(w_down, first, 0, w_down.shape[1])],

time: 166 us -> 166 us (level)
    ppermute x49 -> x51, waiting for transfers between devices: 55.5 us -> 54.3 us  [swap(): return lax.ppermute(block, axis, [(i, i ^ offset) for i in range(count)])]
    ppermute x49 -> x51, starting transfers between devices: 45.7 us -> 46.5 us  [swap(): return lax.ppermute(block, axis, [(i, i ^ offset) for i in range(count)])]
  transfers between devices with their start and end apart: 50 -> 52, of which waited for: 30 -> 30; matrix products, arithmetic and copies ran while one was open for 3% -> 3% of each run, Pallas kernels for 11% -> 11%
where the time goes in v11:
time: 166 us
  waiting for transfers between devices  59.2 us (36%)
  starting transfers between devices  51.4 us (31%)
  Pallas kernels  29 us (17%)
  blocking collectives  10.5 us (6%)
  other arithmetic  7.13 us (4%)
  matrix products  5.16 us (3%)
  local copies, waits for them, and re-layouts  2.4 us (1%)
    ppermute x51, waiting for transfers between devices, swap(): return lax.ppermute(block, axis, [(i, i ^ offset) for i in range(count)])  54.3 us
    ppermute x51, starting transfers between devices, swap(): return lax.ppermute(block, axis, [(i, i ^ offset) for i in range(count)])  46.5 us
    pallas_call x8, Pallas kernels, project(): pl.pallas_call(body, in_specs=specs, out_specs=[in_vmem] * split, scratch...  23.9 us
    all_to_all x1, blocking collectives, normalized_rows(): landed = lax.all_to_all(sent, ('wide', 'narrow'), 0, 0, tiled=True)  10.5 us
    all_to_all x1, starting transfers between devices, normalized_rows(): landed = lax.all_to_all(sent, ('wide', 'narrow'), 0, 0, tiled=True)  4.92 us
    all_to_all x1, waiting for transfers between devices, normalized_rows(): landed = lax.all_to_all(sent, ('wide', 'narrow'), 0, 0, tiled=True)  4.92 us
    pallas_call x6, Pallas kernels, fold(): pl.pallas_call(body, out_shape=[jax.ShapeDtypeStruct((rows, width), jnp.f...  4.76 us
    dot_general x1, matrix products, attend(): jnp.einsum('rgqd,rlgd->rgql', query_heads, cache_keys, preferred_element_...  3.86 us
  transfers between devices with their start and end apart: 52, of which 30 were waited for; matrix products, arithmetic and copies ran while one was open for 3% of the time, Pallas kernels for 11%

profile of v11, /device:TPU:0, one launch (start us, length us, event | category | flops | bytes accessed | tf_op | source)
XLA Modules:
  0.0 165.7 jit_solution(8347416171747926741)
XLA Ops:
  0.0 2.9 %collective-permute-start = (bf16[32,2048]{1,0:T(8,128)(2,1)}, bf16[32,2048]{1,0:T(8,128)(2,1)S(1)}, u32[]{:S(2)}, u32[]{:S(2)}) collective-permute-start(bf16[32,2048]{1,0:T(8,128)(2,1)} %param.14), channel_id=1, source_target_pairs={{0,2},{1,3},{2,0},{3,1},{4,6},{5,7},{6,4},{7,5},{8,10},{9,11},{10,... | collective-permute-start | bytes 393224 | tf_op jit(solution)/shard_map/ppermute | solution.py:99
  4.6 4.9 %all-to-all-start = ((f32[32,1,32]{2,1,0:T(1,128)}), f32[32,1,32]{2,1,0:T(1,128)S(1)}, u32[]{:S(2)}, u32[]{:S(2)}) async-start(f32[32,1,32]{2,1,0:T(1,128)} %broadcast_in_dim.17), calls=%async_computation | async-start | bytes 32768 | tf_op jit(solution)/shard_map/all_to_all | solution.py:413
  11.7 4.9 %all-to-all-done = f32[32,1,32]{2,1,0:T(1,128)S(1)} async-done(((f32[32,1,32]{2,1,0:T(1,128)}), f32[32,1,32]{2,1,0:T(1,128)S(1)}, u32[]{:S(2)}, u32[]{:S(2)}) %all-to-all-start) | async-done | bytes 4128 | tf_op jit(solution)/shard_map/all_to_all | solution.py:413
  19.2 3.6 %shard_map.136 = (f32[64,1536]{1,0:T(8,128)S(1)}, s16[64,1664]{1,0:T(8,128)(2,1)S(1)}) custom-call(bf16[64,2048]{1,0:T(8,128)(2,1)S(1)} %get-tuple-element.148.refs_0_, bf16[64,2048]{1,0:T(8,128)(2,1)S(1)} %get-tuple-element.147.refs_1_, bf16[128,128]{1,0:T(8,128)(2,1)S(1)} %get-tuple-element.70.refs_2_.refs_16_, bf16[2048,4096]{1,0:T(8,128)(2,1)} %refs_3_.9), custom_call_target="tpu_custom_call" | custom-call | flops 872415232 | bytes 7077888 | tf_op jit(solution)/shard_map/pallas_call | solution.py:215
  23.4 3.6 %shard_map.137 = (f32[64,1536]{1,0:T(8,128)S(1)}, s16[64,1664]{1,0:T(8,128)(2,1)S(1)}) custom-call(bf16[64,2048]{1,0:T(8,128)(2,1)S(1)} %get-tuple-element.148.refs_0_, bf16[64,2048]{1,0:T(8,128)(2,1)S(1)} %get-tuple-element.147.refs_1_, bf16[128,128]{1,0:T(8,128)(2,1)S(1)} %get-tuple-element.70.refs_2_.refs_16_, bf16[2048,4096]{1,0:T(8,128)(2,1)} %refs_3_.9), custom_call_target="tpu_custom_call" | custom-call | flops 872415232 | bytes 7077888 | tf_op jit(solution)/shard_map/pallas_call | solution.py:215
  30.6 3.9 %shard_map.144 = (f32[64,1536]{1,0:T(8,128)S(1)}, s16[64,1664]{1,0:T(8,128)(2,1)S(1)}) custom-call(bf16[64,2048]{1,0:T(8,128)(2,1)S(1)} %get-tuple-element.148.refs_0_, bf16[64,2048]{1,0:T(8,128)(2,1)S(1)} %get-tuple-element.147.refs_1_, bf16[128,128]{1,0:T(8,128)(2,1)S(1)} %get-tuple-element.70.refs_2_.refs_16_, bf16[2048,4096]{1,0:T(8,128)(2,1)} %refs_3_.9, ...), custom_call_target="tpu_custom_call" | custom-call | flops 872415232 | bytes 7077888 | tf_op jit(solution)/shard_map/pallas_call | solution.py:215
  44.2 2.4 %collective-permute-start.7 = (s16[16,1664]{1,0:T(8,128)(2,1)S(1)}, s16[16,1664]{1,0:T(8,128)(2,1)S(1)}, u32[]{:S(2)}, u32[]{:S(2)}) collective-permute-start(s16[16,1664]{1,0:T(8,128)(2,1)S(1)} %get-tuple-element.69), channel_id=1, source_target_pairs={{0,16},{4,20},{8,24},{12,28},{16,0},{20,4},{24,8},{28,12},{1,17},{... | collective-permute-start | bytes 159752 | tf_op jit(solution)/shard_map/ppermute | solution.py:99
  48.8 2.1 %collective-permute-done.7.refs_0_ = s16[16,1664]{1,0:T(8,128)(2,1)S(1)} collective-permute-done((s16[16,1664]{1,0:T(8,128)(2,1)S(1)}, s16[16,1664]{1,0:T(8,128)(2,1)S(1)}, u32[]{:S(2)}, u32[]{:S(2)}) %collective-permute-start.7) | collective-permute-done | bytes 53280 | tf_op jit(solution)/shard_map/ppermute | solution.py:99
  53.7 3.8 %collective-permute-done.11 = bf16[2,4,36,128]{3,2,1,0:T(8,128)(2,1)S(1)} collective-permute-done((bf16[2,4,36,128]{3,2,1,0:T(8,128)(2,1)S(1)}, bf16[2,4,36,128]{3,2,1,0:T(8,128)(2,1)S(1)}, u32[]{:S(2)}, u32[]{:S(2)}) %collective-permute-start.11) | collective-permute-done | bytes 73760 | tf_op jit(solution)/shard_map/ppermute | solution.py:99
  60.4 3.9 %fusion.114 = (f32[4,8,16]{2,1,0:T(8,128)S(1)}, f32[4,8,16,512]{3,2,1,0:T(8,128)S(1)}) fusion(bf16[4,8,16,64]{3,2,1,0:T(8,128)(2,1)S(1)} %bitcast.84, bf16[4,8,16,64]{3,2,1,0:T(8,128)(2,1)S(1)} %bitcast.82, pred[4,512]{1,0:T(4,128)(4,1)S(1)} %iota_compare_fusion, bf16[4,512,1024]{2,1,0:T(8,128)(2,1)} %param.24), kind=kOutput, calls=%fused_computation.229 | convolution fusion | flops 68156928 | bytes 5378048 | tf_op jit(solution)/shard_map/rgqd,rlgd->rgql/dot_general | solution.py:59
  66.9 3.7 %collective-permute-done.13 = bf16[2,4,4096]{2,1,0:T(4,128)(2,1)S(1)} collective-permute-done((bf16[2,4,4096]{2,1,0:T(4,128)(2,1)S(1)}, bf16[2,4,4096]{2,1,0:T(4,128)(2,1)S(1)}, u32[]{:S(2)}, u32[]{:S(2)}) %collective-permute-start.13) | collective-permute-done | bytes 65568 | tf_op jit(solution)/shard_map/ppermute | solution.py:99
  79.9 2.0 %collective-permute-done.15.refs_1_ = bf16[16,2048]{1,0:T(8,128)(2,1)S(1)} collective-permute-done((bf16[16,2048]{1,0:T(8,128)(2,1)S(1)}, bf16[16,2048]{1,0:T(8,128)(2,1)S(1)}, u32[]{:S(2)}, u32[]{:S(2)}) %collective-permute-start.15) | collective-permute-done | bytes 65568 | tf_op jit(solution)/shard_map/ppermute | solution.py:99
  92.5 2.9 %shard_map.150 = (f32[64,2048]{1,0:T(8,128)S(1)}, f32[64,2048]{1,0:T(8,128)S(1)}) custom-call(bf16[16,2048]{1,0:T(8,128)(2,1)S(1)} %shard_map.148.refs_0_, bf16[16,2048]{1,0:T(8,128)(2,1)S(1)} %collective-permute-done.15.refs_1_, bf16[16,2048]{1,0:T(8,128)(2,1)S(1)} %collective-permute-done.16.refs_2_, bf16[16,2048]{1,0:T(8,128)(2,1)S(1)} %collective-permute-done.17.refs_3_, ...), custom_call_target="tpu_custom_call" | custom-call | flops 2281701376 | bytes 17825792 | tf_op jit(solution)/shard_map/pallas_call | solution.py:215
  98.1 5.0 %collective-permute-done.30 = bf16[32,2048]{1,0:T(8,128)(2,1)S(1)} collective-permute-done((bf16[32,2048]{1,0:T(8,128)(2,1)S(1)}, bf16[32,2048]{1,0:T(8,128)(2,1)S(1)}, u32[]{:S(2)}, u32[]{:S(2)}) %collective-permute-start.30) | collective-permute-done | bytes 131104 | tf_op jit(solution)/shard_map/ppermute | solution.py:99
  103.8 10.5 %all_to_all.12 = f32[32,1,32]{2,1,0:T(1,128)S(1)} all-to-all(f32[32,1,32]{2,1,0:T(1,128)S(1)} %broadcast_in_dim.20), channel_id=1, replica_groups=mesh['wide'=8,'narrow'=4] {'wide','narrow'}, dimensions={0} | all-to-all | bytes 8192 | tf_op jit(solution)/shard_map/all_to_all | solution.py:413
  116.2 4.1 %shard_map.153 = (f32[64,2048]{1,0:T(8,128)S(1)}, f32[64,2048]{1,0:T(8,128)S(1)}) custom-call(bf16[64,2048]{1,0:T(8,128)(2,1)S(1)} %get-tuple-element.146.refs_0_, bf16[64,2048]{1,0:T(8,128)(2,1)S(1)} %get-tuple-element.145.refs_1_, bf16[128,128]{1,0:T(8,128)(2,1)S(1)} %get-tuple-element.149.refs_2_, bf16[2048,2048]{1,0:T(8,128)(2,1)} %refs_3_.11, ...), custom_call_target="tpu_custom_call" | custom-call | flops 1140850688 | bytes 9437184 | tf_op jit(solution)/shard_map/pallas_call | solution.py:215
  120.9 4.1 %shard_map.151 = (f32[64,2048]{1,0:T(8,128)S(1)}, f32[64,2048]{1,0:T(8,128)S(1)}) custom-call(bf16[64,2048]{1,0:T(8,128)(2,1)S(1)} %get-tuple-element.146.refs_0_, bf16[64,2048]{1,0:T(8,128)(2,1)S(1)} %get-tuple-element.145.refs_1_, bf16[128,128]{1,0:T(8,128)(2,1)S(1)} %get-tuple-element.149.refs_2_, bf16[2048,2048]{1,0:T(8,128)(2,1)} %refs_3_.11, ...), custom_call_target="tpu_custom_call" | custom-call | flops 1140850688 | bytes 9437184 | tf_op jit(solution)/shard_map/pallas_call | solution.py:215
  126.6 2.9 %collective-permute-done.41 = f16[64,2048]{1,0:T(8,128)(2,1)S(1)} collective-permute-done((f16[64,2048]{1,0:T(8,128)(2,1)S(1)}, f16[64,2048]{1,0:T(8,128)(2,1)S(1)}, u32[]{:S(2)}, u32[]{:S(2)}) %collective-permute-start.41) | collective-permute-done | bytes 262176 | tf_op jit(solution)/shard_map/ppermute | solution.py:99
  130.3 2.3 %collective-permute-start.44 = (f16[16,2048]{1,0:T(8,128)(2,1)S(1)}, f16[16,2048]{1,0:T(8,128)(2,1)S(1)}, u32[]{:S(2)}, u32[]{:S(2)}) collective-permute-start(f16[16,2048]{1,0:T(8,128)(2,1)S(1)} %get-tuple-element.102), channel_id=1, source_target_pairs={{0,24},{4,28},{8,16},{12,20},{16,8},{20,12},{24,0},{28,4},{1,25},{... | collective-permute-start | bytes 196616 | tf_op jit(solution)/shard_map/ppermute | solution.py:99
  135.1 2.3 %collective-permute-start.36 = (f16[16,2048]{1,0:T(8,128)(2,1)S(1)}, f16[16,2048]{1,0:T(8,128)(2,1)S(1)}, u32[]{:S(2)}, u32[]{:S(2)}) collective-permute-start(f16[16,2048]{1,0:T(8,128)(2,1)S(1)} %get-tuple-element.105), channel_id=1, source_target_pairs={{0,24},{4,28},{8,16},{12,20},{16,8},{20,12},{24,0},{28,4},{1,25},{... | collective-permute-start | bytes 196616 | tf_op jit(solution)/shard_map/ppermute | solution.py:99
  140.2 2.3 %collective-permute-done.34 = f16[16,2048]{1,0:T(8,128)(2,1)S(1)} collective-permute-done((f16[16,2048]{1,0:T(8,128)(2,1)S(1)}, f16[16,2048]{1,0:T(8,128)(2,1)S(1)}, u32[]{:S(2)}, u32[]{:S(2)}) %collective-permute-start.34) | collective-permute-done | bytes 65568 | tf_op jit(solution)/shard_map/ppermute | solution.py:99
  149.2 2.2 %collective-permute-done.37 = bf16[16,1024]{1,0:T(8,128)(2,1)S(1)} collective-permute-done((bf16[16,1024]{1,0:T(8,128)(2,1)S(1)}, bf16[16,1024]{1,0:T(8,128)(2,1)S(1)}, u32[]{:S(2)}, u32[]{:S(2)}) %collective-permute-start.37) | collective-permute-done | bytes 32800 | tf_op jit(solution)/shard_map/ppermute | solution.py:99
  154.0 2.4 %collective-permute-done.40.refs_1_ = bf16[64,1024]{1,0:T(8,128)(2,1)S(1)} collective-permute-done((bf16[64,1024]{1,0:T(8,128)(2,1)S(1)}, bf16[64,1024]{1,0:T(8,128)(2,1)S(1)}, u32[]{:S(2)}, u32[]{:S(2)}) %collective-permute-start.40) | collective-permute-done | bytes 131104 | tf_op jit(solution)/shard_map/ppermute | solution.py:99
  160.0 5.0 %collective-permute-done.50 = bf16[32,2048]{1,0:T(8,128)(2,1)S(1)} collective-permute-done((bf16[32,2048]{1,0:T(8,128)(2,1)S(1)}, bf16[32,2048]{1,0:T(8,128)(2,1)S(1)}, u32[]{:S(2)}, u32[]{:S(2)}) %collective-permute-start.50) | collective-permute-done | bytes 131104 | tf_op jit(solution)/shard_map/ppermute | solution.py:99
  (223 shorter events, 76.9 us)
Async XLA Ops:
  0.0 16.7 %collective-permute-start = (bf16[32,2048]{1,0:T(8,128)(2,1)}, bf16[32,2048]{1,0:T(8,128)(2,1)S(1)}, u32[]{:S(2)}, u32[]{:S(2)}) collective-permute-start(bf16[32,2048]{1,0:T(8,128)(2,1)} %param.14), channel_id=1, source_target_pairs={{0,2},{1,3},{2,0},{3,1},{4,6},{5,7},{6,4},{7,5},{8,10},{9,11},{10,... | collective-permute-start | bytes 393224 | tf_op jit(solution)/shard_map/ppermute | solution.py:99
  4.6 12.0 %all-to-all-start = ((f32[32,1,32]{2,1,0:T(1,128)}), f32[32,1,32]{2,1,0:T(1,128)S(1)}, u32[]{:S(2)}, u32[]{:S(2)}) async-start(f32[32,1,32]{2,1,0:T(1,128)} %broadcast_in_dim.17), calls=%async_computation | async-start | bytes 32768 | tf_op jit(solution)/shard_map/all_to_all | solution.py:413
  22.8 7.7 %collective-permute-start.2 = (s16[64,1664]{1,0:T(8,128)(2,1)S(1)}, s16[64,1664]{1,0:T(8,128)(2,1)S(1)}, u32[]{:S(2)}, u32[]{:S(2)}) collective-permute-start(s16[64,1664]{1,0:T(8,128)(2,1)S(1)} %get-tuple-element.58), channel_id=1, source_target_pairs={{0,4},{4,0},{8,12},{12,8},{16,20},{20,16},{24,28},{28,24},{1,5},{5... | collective-permute-start | bytes 638984 | tf_op jit(solution)/shard_map/ppermute | solution.py:99
  27.1 9.2 %collective-permute-start.5 = (s16[64,1664]{1,0:T(8,128)(2,1)S(1)}, s16[64,1664]{1,0:T(8,128)(2,1)S(1)}, u32[]{:S(2)}, u32[]{:S(2)}) collective-permute-start(s16[64,1664]{1,0:T(8,128)(2,1)S(1)} %get-tuple-element.65), channel_id=1, source_target_pairs={{0,4},{4,0},{8,12},{12,8},{16,20},{20,16},{24,28},{28,24},{1,5},{5... | collective-permute-start | bytes 638984 | tf_op jit(solution)/shard_map/ppermute | solution.py:99
  34.5 6.2 %collective-permute-start.8 = (s16[64,1664]{1,0:T(8,128)(2,1)S(1)}, s16[64,1664]{1,0:T(8,128)(2,1)S(1)}, u32[]{:S(2)}, u32[]{:S(2)}) collective-permute-start(s16[64,1664]{1,0:T(8,128)(2,1)S(1)} %get-tuple-element.74), channel_id=1, source_target_pairs={{0,4},{4,0},{8,12},{12,8},{16,20},{20,16},{24,28},{28,24},{1,5},{5... | collective-permute-start | bytes 638984 | tf_op jit(solution)/shard_map/ppermute | solution.py:99
  35.7 6.5 %collective-permute-start.3 = (s16[32,1664]{1,0:T(8,128)(2,1)S(1)}, s16[32,1664]{1,0:T(8,128)(2,1)S(1)}, u32[]{:S(2)}, u32[]{:S(2)}) collective-permute-start(s16[32,1664]{1,0:T(8,128)(2,1)S(1)} %get-tuple-element.61), channel_id=1, source_target_pairs={{0,8},{4,12},{8,0},{12,4},{16,24},{20,28},{24,16},{28,20},{1,9},{5... | collective-permute-start | bytes 319496 | tf_op jit(solution)/shard_map/ppermute | solution.py:99
  37.2 6.3 %collective-permute-start.6 = (s16[32,1664]{1,0:T(8,128)(2,1)S(1)}, s16[32,1664]{1,0:T(8,128)(2,1)S(1)}, u32[]{:S(2)}, u32[]{:S(2)}) collective-permute-start(s16[32,1664]{1,0:T(8,128)(2,1)S(1)} %get-tuple-element.67), channel_id=1, source_target_pairs={{0,8},{4,12},{8,0},{12,4},{16,24},{20,28},{24,16},{28,20},{1,9},{5... | collective-permute-start | bytes 319496 | tf_op jit(solution)/shard_map/ppermute | solution.py:99
  44.2 6.7 %collective-permute-start.7 = (s16[16,1664]{1,0:T(8,128)(2,1)S(1)}, s16[16,1664]{1,0:T(8,128)(2,1)S(1)}, u32[]{:S(2)}, u32[]{:S(2)}) collective-permute-start(s16[16,1664]{1,0:T(8,128)(2,1)S(1)} %get-tuple-element.69), channel_id=1, source_target_pairs={{0,16},{4,20},{8,24},{12,28},{16,0},{20,4},{24,8},{28,12},{1,17},{... | collective-permute-start | bytes 159752 | tf_op jit(solution)/shard_map/ppermute | solution.py:99
  72.1 6.3 %collective-permute-start.18 = (bf16[16,2048]{1,0:T(8,128)(2,1)S(1)}, bf16[16,2048]{1,0:T(8,128)(2,1)S(1)}, u32[]{:S(2)}, u32[]{:S(2)}) collective-permute-start(bf16[16,2048]{1,0:T(8,128)(2,1)S(1)} %pad_maximum_fusion.10.array_ref), channel_id=1, source_target_pairs={{0,4},{4,0},{8,12},{12,8},{16,20},{20,16},{24,28},{28,24},{1,5},{5... | collective-permute-start | bytes 196616 | tf_op jit(solution)/shard_map/ppermute | solution.py:99
  72.8 6.6 %collective-permute-start.16 = (bf16[16,2048]{1,0:T(8,128)(2,1)S(1)}, bf16[16,2048]{1,0:T(8,128)(2,1)S(1)}, u32[]{:S(2)}, u32[]{:S(2)}) collective-permute-start(bf16[16,2048]{1,0:T(8,128)(2,1)S(1)} %pad_maximum_fusion.10.array_ref), channel_id=1, source_target_pairs={{0,8},{4,12},{8,0},{12,4},{16,24},{20,28},{24,16},{28,20},{1,9},{5... | collective-permute-start | bytes 196616 | tf_op jit(solution)/shard_map/ppermute | solution.py:99
  73.9 8.0 %collective-permute-start.15 = (bf16[16,2048]{1,0:T(8,128)(2,1)S(1)}, bf16[16,2048]{1,0:T(8,128)(2,1)S(1)}, u32[]{:S(2)}, u32[]{:S(2)}) collective-permute-start(bf16[16,2048]{1,0:T(8,128)(2,1)S(1)} %pad_maximum_fusion.10.array_ref), channel_id=1, source_target_pairs={{0,16},{4,20},{8,24},{12,28},{16,0},{20,4},{24,8},{28,12},{1,17},{... | collective-permute-start | bytes 196616 | tf_op jit(solution)/shard_map/ppermute | solution.py:99
  75.6 7.1 %collective-permute-start.22 = (bf16[16,2048]{1,0:T(8,128)(2,1)S(1)}, bf16[16,2048]{1,0:T(8,128)(2,1)S(1)}, u32[]{:S(2)}, u32[]{:S(2)}) collective-permute-start(bf16[16,2048]{1,0:T(8,128)(2,1)S(1)} %pad_maximum_fusion.11.array_ref), channel_id=1, source_target_pairs={{0,16},{4,20},{8,24},{12,28},{16,0},{20,4},{24,8},{28,12},{1,17},{... | collective-permute-start | bytes 196616 | tf_op jit(solution)/shard_map/ppermute | solution.py:99
  76.9 7.0 %collective-permute-start.25 = (bf16[16,2048]{1,0:T(8,128)(2,1)S(1)}, bf16[16,2048]{1,0:T(8,128)(2,1)S(1)}, u32[]{:S(2)}, u32[]{:S(2)}) collective-permute-start(bf16[16,2048]{1,0:T(8,128)(2,1)S(1)} %pad_maximum_fusion.11.array_ref), channel_id=1, source_target_pairs={{0,4},{4,0},{8,12},{12,8},{16,20},{20,16},{24,28},{28,24},{1,5},{5... | collective-permute-start | bytes 196616 | tf_op jit(solution)/shard_map/ppermute | solution.py:99
  78.4 7.0 %collective-permute-start.23 = (bf16[16,2048]{1,0:T(8,128)(2,1)S(1)}, bf16[16,2048]{1,0:T(8,128)(2,1)S(1)}, u32[]{:S(2)}, u32[]{:S(2)}) collective-permute-start(bf16[16,2048]{1,0:T(8,128)(2,1)S(1)} %pad_maximum_fusion.11.array_ref), channel_id=1, source_target_pairs={{0,8},{4,12},{8,0},{12,4},{16,24},{20,28},{24,16},{28,20},{1,9},{5... | collective-permute-start | bytes 196616 | tf_op jit(solution)/shard_map/ppermute | solution.py:99
  79.3 6.7 %collective-permute-start.20 = (bf16[16,2048]{1,0:T(8,128)(2,1)S(1)}, bf16[16,2048]{1,0:T(8,128)(2,1)S(1)}, u32[]{:S(2)}, u32[]{:S(2)}) collective-permute-start(bf16[16,2048]{1,0:T(8,128)(2,1)S(1)} %collective-permute-done.16.refs_2_), channel_id=1, source_target_pairs={{0,4},{4,0},{8,12},{12,8},{16,20},{20,16},{24,28},{28,24},{1,5},{5... | collective-permute-start | bytes 196616 | tf_op jit(solution)/shard_map/ppermute | solution.py:99
  103.3 11.1 %collective-permute-start.31 = (bf16[32,2048]{1,0:T(8,128)(2,1)S(1)}, bf16[32,2048]{1,0:T(8,128)(2,1)S(1)}, u32[]{:S(2)}, u32[]{:S(2)}) collective-permute-start(bf16[32,2048]{1,0:T(8,128)(2,1)S(1)} %get-tuple-element.92), channel_id=1, source_target_pairs={{0,2},{1,3},{2,0},{3,1},{4,6},{5,7},{6,4},{7,5},{8,10},{9,11},{10,... | collective-permute-start | bytes 393224 | tf_op jit(solution)/shard_map/ppermute | solution.py:99
  120.3 9.2 %collective-permute-start.41 = (f16[64,2048]{1,0:T(8,128)(2,1)S(1)}, f16[64,2048]{1,0:T(8,128)(2,1)S(1)}, u32[]{:S(2)}, u32[]{:S(2)}) collective-permute-start(f16[64,2048]{1,0:T(8,128)(2,1)S(1)} %convert_element_type.171), channel_id=1, source_target_pairs={{0,4},{4,0},{8,12},{12,8},{16,20},{20,16},{24,28},{28,24},{1,5},{5... | collective-permute-start | bytes 786440 | tf_op jit(solution)/shard_map/ppermute | solution.py:99
  125.0 9.3 %collective-permute-start.33 = (f16[64,2048]{1,0:T(8,128)(2,1)S(1)}, f16[64,2048]{1,0:T(8,128)(2,1)S(1)}, u32[]{:S(2)}, u32[]{:S(2)}) collective-permute-start(f16[64,2048]{1,0:T(8,128)(2,1)S(1)} %convert_element_type.165), channel_id=1, source_target_pairs={{0,4},{4,0},{8,12},{12,8},{16,20},{20,16},{24,28},{28,24},{1,5},{5... | collective-permute-start | bytes 786440 | tf_op jit(solution)/shard_map/ppermute | solution.py:99
  129.6 7.8 %collective-permute-start.42 = (f16[16,2048]{1,0:T(8,128)(2,1)S(1)}, f16[16,2048]{1,0:T(8,128)(2,1)S(1)}, u32[]{:S(2)}, u32[]{:S(2)}) collective-permute-start(f16[16,2048]{1,0:T(8,128)(2,1)S(1)} %get-tuple-element.101), channel_id=1, source_target_pairs={{0,16},{4,20},{8,24},{12,28},{16,0},{20,4},{24,8},{28,12},{1,17},{... | collective-permute-start | bytes 196616 | tf_op jit(solution)/shard_map/ppermute | solution.py:99
  130.3 7.7 %collective-permute-start.44 = (f16[16,2048]{1,0:T(8,128)(2,1)S(1)}, f16[16,2048]{1,0:T(8,128)(2,1)S(1)}, u32[]{:S(2)}, u32[]{:S(2)}) collective-permute-start(f16[16,2048]{1,0:T(8,128)(2,1)S(1)} %get-tuple-element.102), channel_id=1, source_target_pairs={{0,24},{4,28},{8,16},{12,20},{16,8},{20,12},{24,0},{28,4},{1,25},{... | collective-permute-start | bytes 196616 | tf_op jit(solution)/shard_map/ppermute | solution.py:99
  134.4 8.1 %collective-permute-start.34 = (f16[16,2048]{1,0:T(8,128)(2,1)S(1)}, f16[16,2048]{1,0:T(8,128)(2,1)S(1)}, u32[]{:S(2)}, u32[]{:S(2)}) collective-permute-start(f16[16,2048]{1,0:T(8,128)(2,1)S(1)} %get-tuple-element.104), channel_id=1, source_target_pairs={{0,16},{4,20},{8,24},{12,28},{16,0},{20,4},{24,8},{28,12},{1,17},{... | collective-permute-start | bytes 196616 | tf_op jit(solution)/shard_map/ppermute | solution.py:99
  135.1 7.5 %collective-permute-start.36 = (f16[16,2048]{1,0:T(8,128)(2,1)S(1)}, f16[16,2048]{1,0:T(8,128)(2,1)S(1)}, u32[]{:S(2)}, u32[]{:S(2)}) collective-permute-start(f16[16,2048]{1,0:T(8,128)(2,1)S(1)} %get-tuple-element.105), channel_id=1, source_target_pairs={{0,24},{4,28},{8,16},{12,20},{16,8},{20,12},{24,0},{28,4},{1,25},{... | collective-permute-start | bytes 196616 | tf_op jit(solution)/shard_map/ppermute | solution.py:99
  138.1 8.1 %collective-permute-start.47 = (bf16[16,1024]{1,0:T(8,128)(2,1)S(1)}, bf16[16,1024]{1,0:T(8,128)(2,1)S(1)}, u32[]{:S(2)}, u32[]{:S(2)}) collective-permute-start(bf16[16,1024]{1,0:T(8,128)(2,1)S(1)} %fusion.72.array_ref), channel_id=1, source_target_pairs={{0,24},{4,28},{8,16},{12,20},{16,8},{20,12},{24,0},{28,4},{1,25},{... | collective-permute-start | bytes 98312 | tf_op jit(solution)/shard_map/ppermute | solution.py:99
  139.9 7.6 %collective-permute-start.46 = (bf16[16,1024]{1,0:T(8,128)(2,1)S(1)}, bf16[16,1024]{1,0:T(8,128)(2,1)S(1)}, u32[]{:S(2)}, u32[]{:S(2)}) collective-permute-start(bf16[16,1024]{1,0:T(8,128)(2,1)S(1)} %fusion.72.array_ref), channel_id=1, source_target_pairs={{0,8},{4,12},{8,0},{12,4},{16,24},{20,28},{24,16},{28,20},{1,9},{5... | collective-permute-start | bytes 98312 | tf_op jit(solution)/shard_map/ppermute | solution.py:99
  (40 other events, 260.7 us)

commit v12 on v11

--- a/solution.py
+++ b/solution.py
@@ -474,8 +474,12 @@
         columns = slice(chunk * depth, (chunk + 1) * depth)
         block = jnp.concatenate([piece[:, columns] for piece in by_heads], axis=0)
         groups.append(gather_pieces(block, "wide"))
-    total = project(groups, to_hypothesis, False, [(w_out, 0, 0, w_out.shape[1])], 2)
-    attn_out = narrow_scatter(*total)
+    half = w_out.shape[1] // 2
+    halves = [
+        project(groups, to_hypothesis, False, [(w_out, 0, first, half)], 2)
+        for first in (0, half)
+    ]
+    attn_out = jnp.concatenate([narrow_scatter(*sums) for sums in halves], axis=1)
     resid = (rows_in + attn_out).astype(jnp.bfloat16)
     resid_wide = resid.astype(jnp.float32)
     normed_two = normalized_rows(resid, ffn_gain)

time: 166 us -> 165 us (level)
  waiting for transfers between devices: 59.2 us -> 56.3 us
  starting transfers between devices: 51.4 us -> 53.3 us
    ppermute x51 -> x53, waiting for transfers between devices: 54.3 us -> 51.4 us  [swap(): return lax.ppermute(block, axis, [(i, i ^ offset) for i in range(count)])]
    ppermute x51 -> x53, starting transfers between devices: 46.5 us -> 48.4 us  [swap(): return lax.ppermute(block, axis, [(i, i ^ offset) for i in range(count)])]
    pallas_call x8 -> x9, Pallas kernels: 23.9 us -> 24.3 us  [project(): pl.pallas_call(body, in_specs=specs, out_specs=[in_vmem] * split, scratch...]
  transfers between devices with their start and end apart: 52 -> 54, of which waited for: 30 -> 31; matrix products, arithmetic and copies ran while one was open for 3% -> 3% of each run, Pallas kernels for 11% -> 12%
where the time goes in v12:
time: 165 us
  waiting for transfers between devices  56.3 us (34%)
  starting transfers between devices  53.3 us (32%)
  Pallas kernels  29.5 us (18%)
  blocking collectives  10.2 us (6%)
  other arithmetic  7.13 us (4%)
  matrix products  5.16 us (3%)
  local copies, waits for them, and re-layouts  2.4 us (1%)
    ppermute x53, waiting for transfers between devices, swap(): return lax.ppermute(block, axis, [(i, i ^ offset) for i in range(count)])  51.4 us
    ppermute x53, starting transfers between devices, swap(): return lax.ppermute(block, axis, [(i, i ^ offset) for i in range(count)])  48.4 us
    pallas_call x9, Pallas kernels, project(): pl.pallas_call(body, in_specs=specs, out_specs=[in_vmem] * split, scratch...  24.3 us
    all_to_all x1, blocking collectives, normalized_rows(): landed = lax.all_to_all(sent, ('wide', 'narrow'), 0, 0, tiled=True)  10.2 us
    all_to_all x1, starting transfers between devices, normalized_rows(): landed = lax.all_to_all(sent, ('wide', 'narrow'), 0, 0, tiled=True)  4.92 us
    all_to_all x1, waiting for transfers between devices, normalized_rows(): landed = lax.all_to_all(sent, ('wide', 'narrow'), 0, 0, tiled=True)  4.92 us
    pallas_call x6, Pallas kernels, fold(): pl.pallas_call(body, out_shape=[jax.ShapeDtypeStruct((rows, width), jnp.f...  4.76 us
    dot_general x1, matrix products, attend(): jnp.einsum('rgqd,rlgd->rgql', query_heads, cache_keys, preferred_element_...  3.86 us
  transfers between devices with their start and end apart: 54, of which 31 were waited for; matrix products, arithmetic and copies ran while one was open for 3% of the time, Pallas kernels for 12%

profile of v12, /device:TPU:0, one launch (start us, length us, event | category | flops | bytes accessed | tf_op | source)
XLA Modules:
  0.0 164.9 jit_solution(9679848880230076138)
XLA Ops:
  0.0 2.9 %collective-permute-start = (bf16[32,2048]{1,0:T(8,128)(2,1)}, bf16[32,2048]{1,0:T(8,128)(2,1)S(1)}, u32[]{:S(2)}, u32[]{:S(2)}) collective-permute-start(bf16[32,2048]{1,0:T(8,128)(2,1)} %param.14), channel_id=1, source_target_pairs={{0,2},{1,3},{2,0},{3,1},{4,6},{5,7},{6,4},{7,5},{8,10},{9,11},{10,... | collective-permute-start | bytes 393224 | tf_op jit(solution)/shard_map/ppermute | solution.py:99
  4.6 4.9 %all-to-all-start = ((f32[32,1,32]{2,1,0:T(1,128)}), f32[32,1,32]{2,1,0:T(1,128)S(1)}, u32[]{:S(2)}, u32[]{:S(2)}) async-start(f32[32,1,32]{2,1,0:T(1,128)} %broadcast_in_dim.17), calls=%async_computation | async-start | bytes 32768 | tf_op jit(solution)/shard_map/all_to_all | solution.py:413
  11.7 4.9 %all-to-all-done = f32[32,1,32]{2,1,0:T(1,128)S(1)} async-done(((f32[32,1,32]{2,1,0:T(1,128)}), f32[32,1,32]{2,1,0:T(1,128)S(1)}, u32[]{:S(2)}, u32[]{:S(2)}) %all-to-all-start) | async-done | bytes 4128 | tf_op jit(solution)/shard_map/all_to_all | solution.py:413
  19.2 3.6 %shard_map.136 = (f32[64,1536]{1,0:T(8,128)S(1)}, s16[64,1664]{1,0:T(8,128)(2,1)S(1)}) custom-call(bf16[64,2048]{1,0:T(8,128)(2,1)S(1)} %get-tuple-element.152.refs_0_, bf16[64,2048]{1,0:T(8,128)(2,1)S(1)} %get-tuple-element.151.refs_1_, bf16[128,128]{1,0:T(8,128)(2,1)S(1)} %get-tuple-element.72.refs_2_.refs_16_, bf16[2048,4096]{1,0:T(8,128)(2,1)} %refs_3_.9), custom_call_target="tpu_custom_call" | custom-call | flops 872415232 | bytes 7077888 | tf_op jit(solution)/shard_map/pallas_call | solution.py:215
  23.4 3.6 %shard_map.137 = (f32[64,1536]{1,0:T(8,128)S(1)}, s16[64,1664]{1,0:T(8,128)(2,1)S(1)}) custom-call(bf16[64,2048]{1,0:T(8,128)(2,1)S(1)} %get-tuple-element.152.refs_0_, bf16[64,2048]{1,0:T(8,128)(2,1)S(1)} %get-tuple-element.151.refs_1_, bf16[128,128]{1,0:T(8,128)(2,1)S(1)} %get-tuple-element.72.refs_2_.refs_16_, bf16[2048,4096]{1,0:T(8,128)(2,1)} %refs_3_.9), custom_call_target="tpu_custom_call" | custom-call | flops 872415232 | bytes 7077888 | tf_op jit(solution)/shard_map/pallas_call | solution.py:215
  28.6 1.9 %collective-permute-done.2.arrived_ref = s16[64,1664]{1,0:T(8,128)(2,1)S(1)} collective-permute-done((s16[64,1664]{1,0:T(8,128)(2,1)S(1)}, s16[64,1664]{1,0:T(8,128)(2,1)S(1)}, u32[]{:S(2)}, u32[]{:S(2)}) %collective-permute-start.2) | collective-permute-done | bytes 213024 | tf_op jit(solution)/shard_map/ppermute | solution.py:99
  30.6 3.9 %shard_map.144 = (f32[64,1536]{1,0:T(8,128)S(1)}, s16[64,1664]{1,0:T(8,128)(2,1)S(1)}) custom-call(bf16[64,2048]{1,0:T(8,128)(2,1)S(1)} %get-tuple-element.152.refs_0_, bf16[64,2048]{1,0:T(8,128)(2,1)S(1)} %get-tuple-element.151.refs_1_, bf16[128,128]{1,0:T(8,128)(2,1)S(1)} %get-tuple-element.72.refs_2_.refs_16_, bf16[2048,4096]{1,0:T(8,128)(2,1)} %refs_3_.9, ...), custom_call_target="tpu_custom_call" | custom-call | flops 872415232 | bytes 7077888 | tf_op jit(solution)/shard_map/pallas_call | solution.py:215
  44.2 2.4 %collective-permute-start.7 = (s16[16,1664]{1,0:T(8,128)(2,1)S(1)}, s16[16,1664]{1,0:T(8,128)(2,1)S(1)}, u32[]{:S(2)}, u32[]{:S(2)}) collective-permute-start(s16[16,1664]{1,0:T(8,128)(2,1)S(1)} %get-tuple-element.71), channel_id=1, source_target_pairs={{0,16},{4,20},{8,24},{12,28},{16,0},{20,4},{24,8},{28,12},{1,17},{... | collective-permute-start | bytes 159752 | tf_op jit(solution)/shard_map/ppermute | solution.py:99
  48.8 2.1 %collective-permute-done.7.refs_0_ = s16[16,1664]{1,0:T(8,128)(2,1)S(1)} collective-permute-done((s16[16,1664]{1,0:T(8,128)(2,1)S(1)}, s16[16,1664]{1,0:T(8,128)(2,1)S(1)}, u32[]{:S(2)}, u32[]{:S(2)}) %collective-permute-start.7) | collective-permute-done | bytes 53280 | tf_op jit(solution)/shard_map/ppermute | solution.py:99
  53.7 3.8 %collective-permute-done.11 = bf16[2,4,36,128]{3,2,1,0:T(8,128)(2,1)S(1)} collective-permute-done((bf16[2,4,36,128]{3,2,1,0:T(8,128)(2,1)S(1)}, bf16[2,4,36,128]{3,2,1,0:T(8,128)(2,1)S(1)}, u32[]{:S(2)}, u32[]{:S(2)}) %collective-permute-start.11) | collective-permute-done | bytes 73760 | tf_op jit(solution)/shard_map/ppermute | solution.py:99
  60.4 3.9 %fusion.114 = (f32[4,8,16]{2,1,0:T(8,128)S(1)}, f32[4,8,16,512]{3,2,1,0:T(8,128)S(1)}) fusion(bf16[4,8,16,64]{3,2,1,0:T(8,128)(2,1)S(1)} %bitcast.84, bf16[4,8,16,64]{3,2,1,0:T(8,128)(2,1)S(1)} %bitcast.82, pred[4,512]{1,0:T(4,128)(4,1)S(1)} %iota_compare_fusion, bf16[4,512,1024]{2,1,0:T(8,128)(2,1)} %param.24), kind=kOutput, calls=%fused_computation.231 | convolution fusion | flops 68156928 | bytes 5378048 | tf_op jit(solution)/shard_map/rgqd,rlgd->rgql/dot_general | solution.py:59
  66.9 3.7 %collective-permute-done.13 = bf16[2,4,4096]{2,1,0:T(4,128)(2,1)S(1)} collective-permute-done((bf16[2,4,4096]{2,1,0:T(4,128)(2,1)S(1)}, bf16[2,4,4096]{2,1,0:T(4,128)(2,1)S(1)}, u32[]{:S(2)}, u32[]{:S(2)}) %collective-permute-start.13) | collective-permute-done | bytes 65568 | tf_op jit(solution)/shard_map/ppermute | solution.py:99
  79.9 2.0 %collective-permute-done.15.refs_1_ = bf16[16,2048]{1,0:T(8,128)(2,1)S(1)} collective-permute-done((bf16[16,2048]{1,0:T(8,128)(2,1)S(1)}, bf16[16,2048]{1,0:T(8,128)(2,1)S(1)}, u32[]{:S(2)}, u32[]{:S(2)}) %collective-permute-start.15) | collective-permute-done | bytes 65568 | tf_op jit(solution)/shard_map/ppermute | solution.py:99
  98.8 2.3 %collective-permute-done.32 = bf16[32,1024]{1,0:T(8,128)(2,1)S(1)} collective-permute-done((bf16[32,1024]{1,0:T(8,128)(2,1)S(1)}, bf16[32,1024]{1,0:T(8,128)(2,1)S(1)}, u32[]{:S(2)}, u32[]{:S(2)}) %collective-permute-start.32) | collective-permute-done | bytes 65568 | tf_op jit(solution)/shard_map/ppermute | solution.py:99
  103.3 10.2 %all_to_all.12 = f32[32,1,32]{2,1,0:T(1,128)S(1)} all-to-all(f32[32,1,32]{2,1,0:T(1,128)S(1)} %broadcast_in_dim.20), channel_id=1, replica_groups=mesh['wide'=8,'narrow'=4] {'wide','narrow'}, dimensions={0} | all-to-all | bytes 8192 | tf_op jit(solution)/shard_map/all_to_all | solution.py:413
  115.4 4.1 %shard_map.154 = (f32[64,2048]{1,0:T(8,128)S(1)}, f32[64,2048]{1,0:T(8,128)S(1)}) custom-call(bf16[64,2048]{1,0:T(8,128)(2,1)S(1)} %get-tuple-element.150.refs_0_, bf16[64,2048]{1,0:T(8,128)(2,1)S(1)} %get-tuple-element.149.refs_1_, bf16[128,128]{1,0:T(8,128)(2,1)S(1)} %get-tuple-element.153.refs_2_, bf16[2048,2048]{1,0:T(8,128)(2,1)} %refs_3_.11, ...), custom_call_target="tpu_custom_call" | custom-call | flops 1140850688 | bytes 9437184 | tf_op jit(solution)/shard_map/pallas_call | solution.py:215
  120.1 4.1 %shard_map.152 = (f32[64,2048]{1,0:T(8,128)S(1)}, f32[64,2048]{1,0:T(8,128)S(1)}) custom-call(bf16[64,2048]{1,0:T(8,128)(2,1)S(1)} %get-tuple-element.150.refs_0_, bf16[64,2048]{1,0:T(8,128)(2,1)S(1)} %get-tuple-element.149.refs_1_, bf16[128,128]{1,0:T(8,128)(2,1)S(1)} %get-tuple-element.153.refs_2_, bf16[2048,2048]{1,0:T(8,128)(2,1)} %refs_3_.11, ...), custom_call_target="tpu_custom_call" | custom-call | flops 1140850688 | bytes 9437184 | tf_op jit(solution)/shard_map/pallas_call | solution.py:215
  125.8 2.9 %collective-permute-done.43 = f16[64,2048]{1,0:T(8,128)(2,1)S(1)} collective-permute-done((f16[64,2048]{1,0:T(8,128)(2,1)S(1)}, f16[64,2048]{1,0:T(8,128)(2,1)S(1)}, u32[]{:S(2)}, u32[]{:S(2)}) %collective-permute-start.43) | collective-permute-done | bytes 262176 | tf_op jit(solution)/shard_map/ppermute | solution.py:99
  129.5 2.3 %collective-permute-start.46 = (f16[16,2048]{1,0:T(8,128)(2,1)S(1)}, f16[16,2048]{1,0:T(8,128)(2,1)S(1)}, u32[]{:S(2)}, u32[]{:S(2)}) collective-permute-start(f16[16,2048]{1,0:T(8,128)(2,1)S(1)} %get-tuple-element.106), channel_id=1, source_target_pairs={{0,24},{4,28},{8,16},{12,20},{16,8},{20,12},{24,0},{28,4},{1,25},{... | collective-permute-start | bytes 196616 | tf_op jit(solution)/shard_map/ppermute | solution.py:99
  134.3 2.3 %collective-permute-start.38 = (f16[16,2048]{1,0:T(8,128)(2,1)S(1)}, f16[16,2048]{1,0:T(8,128)(2,1)S(1)}, u32[]{:S(2)}, u32[]{:S(2)}) collective-permute-start(f16[16,2048]{1,0:T(8,128)(2,1)S(1)} %get-tuple-element.109), channel_id=1, source_target_pairs={{0,24},{4,28},{8,16},{12,20},{16,8},{20,12},{24,0},{28,4},{1,25},{... | collective-permute-start | bytes 196616 | tf_op jit(solution)/shard_map/ppermute | solution.py:99
  139.4 2.3 %collective-permute-done.36 = f16[16,2048]{1,0:T(8,128)(2,1)S(1)} collective-permute-done((f16[16,2048]{1,0:T(8,128)(2,1)S(1)}, f16[16,2048]{1,0:T(8,128)(2,1)S(1)}, u32[]{:S(2)}, u32[]{:S(2)}) %collective-permute-start.36) | collective-permute-done | bytes 65568 | tf_op jit(solution)/shard_map/ppermute | solution.py:99
  148.4 2.2 %collective-permute-done.39 = bf16[16,1024]{1,0:T(8,128)(2,1)S(1)} collective-permute-done((bf16[16,1024]{1,0:T(8,128)(2,1)S(1)}, bf16[16,1024]{1,0:T(8,128)(2,1)S(1)}, u32[]{:S(2)}, u32[]{:S(2)}) %collective-permute-start.39) | collective-permute-done | bytes 32800 | tf_op jit(solution)/shard_map/ppermute | solution.py:99
  153.1 2.5 %collective-permute-done.42.refs_1_ = bf16[64,1024]{1,0:T(8,128)(2,1)S(1)} collective-permute-done((bf16[64,1024]{1,0:T(8,128)(2,1)S(1)}, bf16[64,1024]{1,0:T(8,128)(2,1)S(1)}, u32[]{:S(2)}, u32[]{:S(2)}) %collective-permute-start.42) | collective-permute-done | bytes 131104 | tf_op jit(solution)/shard_map/ppermute | solution.py:99
  159.2 5.0 %collective-permute-done.52 = bf16[32,2048]{1,0:T(8,128)(2,1)S(1)} collective-permute-done((bf16[32,2048]{1,0:T(8,128)(2,1)S(1)}, bf16[32,2048]{1,0:T(8,128)(2,1)S(1)}, u32[]{:S(2)}, u32[]{:S(2)}) %collective-permute-start.52) | collective-permute-done | bytes 131104 | tf_op jit(solution)/shard_map/ppermute | solution.py:99
  (232 shorter events, 80.0 us)
Async XLA Ops:
  0.0 16.7 %collective-permute-start = (bf16[32,2048]{1,0:T(8,128)(2,1)}, bf16[32,2048]{1,0:T(8,128)(2,1)S(1)}, u32[]{:S(2)}, u32[]{:S(2)}) collective-permute-start(bf16[32,2048]{1,0:T(8,128)(2,1)} %param.14), channel_id=1, source_target_pairs={{0,2},{1,3},{2,0},{3,1},{4,6},{5,7},{6,4},{7,5},{8,10},{9,11},{10,... | collective-permute-start | bytes 393224 | tf_op jit(solution)/shard_map/ppermute | solution.py:99
  4.6 12.0 %all-to-all-start = ((f32[32,1,32]{2,1,0:T(1,128)}), f32[32,1,32]{2,1,0:T(1,128)S(1)}, u32[]{:S(2)}, u32[]{:S(2)}) async-start(f32[32,1,32]{2,1,0:T(1,128)} %broadcast_in_dim.17), calls=%async_computation | async-start | bytes 32768 | tf_op jit(solution)/shard_map/all_to_all | solution.py:413
  22.8 7.7 %collective-permute-start.2 = (s16[64,1664]{1,0:T(8,128)(2,1)S(1)}, s16[64,1664]{1,0:T(8,128)(2,1)S(1)}, u32[]{:S(2)}, u32[]{:S(2)}) collective-permute-start(s16[64,1664]{1,0:T(8,128)(2,1)S(1)} %get-tuple-element.60), channel_id=1, source_target_pairs={{0,4},{4,0},{8,12},{12,8},{16,20},{20,16},{24,28},{28,24},{1,5},{5... | collective-permute-start | bytes 638984 | tf_op jit(solution)/shard_map/ppermute | solution.py:99
  27.1 9.2 %collective-permute-start.5 = (s16[64,1664]{1,0:T(8,128)(2,1)S(1)}, s16[64,1664]{1,0:T(8,128)(2,1)S(1)}, u32[]{:S(2)}, u32[]{:S(2)}) collective-permute-start(s16[64,1664]{1,0:T(8,128)(2,1)S(1)} %get-tuple-element.67), channel_id=1, source_target_pairs={{0,4},{4,0},{8,12},{12,8},{16,20},{20,16},{24,28},{28,24},{1,5},{5... | collective-permute-start | bytes 638984 | tf_op jit(solution)/shard_map/ppermute | solution.py:99
  34.5 6.2 %collective-permute-start.8 = (s16[64,1664]{1,0:T(8,128)(2,1)S(1)}, s16[64,1664]{1,0:T(8,128)(2,1)S(1)}, u32[]{:S(2)}, u32[]{:S(2)}) collective-permute-start(s16[64,1664]{1,0:T(8,128)(2,1)S(1)} %get-tuple-element.76), channel_id=1, source_target_pairs={{0,4},{4,0},{8,12},{12,8},{16,20},{20,16},{24,28},{28,24},{1,5},{5... | collective-permute-start | bytes 638984 | tf_op jit(solution)/shard_map/ppermute | solution.py:99
  35.7 6.5 %collective-permute-start.3 = (s16[32,1664]{1,0:T(8,128)(2,1)S(1)}, s16[32,1664]{1,0:T(8,128)(2,1)S(1)}, u32[]{:S(2)}, u32[]{:S(2)}) collective-permute-start(s16[32,1664]{1,0:T(8,128)(2,1)S(1)} %get-tuple-element.63), channel_id=1, source_target_pairs={{0,8},{4,12},{8,0},{12,4},{16,24},{20,28},{24,16},{28,20},{1,9},{5... | collective-permute-start | bytes 319496 | tf_op jit(solution)/shard_map/ppermute | solution.py:99
  37.2 6.3 %collective-permute-start.6 = (s16[32,1664]{1,0:T(8,128)(2,1)S(1)}, s16[32,1664]{1,0:T(8,128)(2,1)S(1)}, u32[]{:S(2)}, u32[]{:S(2)}) collective-permute-start(s16[32,1664]{1,0:T(8,128)(2,1)S(1)} %get-tuple-element.69), channel_id=1, source_target_pairs={{0,8},{4,12},{8,0},{12,4},{16,24},{20,28},{24,16},{28,20},{1,9},{5... | collective-permute-start | bytes 319496 | tf_op jit(solution)/shard_map/ppermute | solution.py:99
  44.2 6.7 %collective-permute-start.7 = (s16[16,1664]{1,0:T(8,128)(2,1)S(1)}, s16[16,1664]{1,0:T(8,128)(2,1)S(1)}, u32[]{:S(2)}, u32[]{:S(2)}) collective-permute-start(s16[16,1664]{1,0:T(8,128)(2,1)S(1)} %get-tuple-element.71), channel_id=1, source_target_pairs={{0,16},{4,20},{8,24},{12,28},{16,0},{20,4},{24,8},{28,12},{1,17},{... | collective-permute-start | bytes 159752 | tf_op jit(solution)/shard_map/ppermute | solution.py:99
  72.1 6.3 %collective-permute-start.18 = (bf16[16,2048]{1,0:T(8,128)(2,1)S(1)}, bf16[16,2048]{1,0:T(8,128)(2,1)S(1)}, u32[]{:S(2)}, u32[]{:S(2)}) collective-permute-start(bf16[16,2048]{1,0:T(8,128)(2,1)S(1)} %pad_maximum_fusion.10.array_ref), channel_id=1, source_target_pairs={{0,4},{4,0},{8,12},{12,8},{16,20},{20,16},{24,28},{28,24},{1,5},{5... | collective-permute-start | bytes 196616 | tf_op jit(solution)/shard_map/ppermute | solution.py:99
  72.8 6.6 %collective-permute-start.16 = (bf16[16,2048]{1,0:T(8,128)(2,1)S(1)}, bf16[16,2048]{1,0:T(8,128)(2,1)S(1)}, u32[]{:S(2)}, u32[]{:S(2)}) collective-permute-start(bf16[16,2048]{1,0:T(8,128)(2,1)S(1)} %pad_maximum_fusion.10.array_ref), channel_id=1, source_target_pairs={{0,8},{4,12},{8,0},{12,4},{16,24},{20,28},{24,16},{28,20},{1,9},{5... | collective-permute-start | bytes 196616 | tf_op jit(solution)/shard_map/ppermute | solution.py:99
  73.9 8.0 %collective-permute-start.15 = (bf16[16,2048]{1,0:T(8,128)(2,1)S(1)}, bf16[16,2048]{1,0:T(8,128)(2,1)S(1)}, u32[]{:S(2)}, u32[]{:S(2)}) collective-permute-start(bf16[16,2048]{1,0:T(8,128)(2,1)S(1)} %pad_maximum_fusion.10.array_ref), channel_id=1, source_target_pairs={{0,16},{4,20},{8,24},{12,28},{16,0},{20,4},{24,8},{28,12},{1,17},{... | collective-permute-start | bytes 196616 | tf_op jit(solution)/shard_map/ppermute | solution.py:99
  75.6 7.1 %collective-permute-start.22 = (bf16[16,2048]{1,0:T(8,128)(2,1)S(1)}, bf16[16,2048]{1,0:T(8,128)(2,1)S(1)}, u32[]{:S(2)}, u32[]{:S(2)}) collective-permute-start(bf16[16,2048]{1,0:T(8,128)(2,1)S(1)} %pad_maximum_fusion.11.array_ref), channel_id=1, source_target_pairs={{0,16},{4,20},{8,24},{12,28},{16,0},{20,4},{24,8},{28,12},{1,17},{... | collective-permute-start | bytes 196616 | tf_op jit(solution)/shard_map/ppermute | solution.py:99
  76.9 7.0 %collective-permute-start.25 = (bf16[16,2048]{1,0:T(8,128)(2,1)S(1)}, bf16[16,2048]{1,0:T(8,128)(2,1)S(1)}, u32[]{:S(2)}, u32[]{:S(2)}) collective-permute-start(bf16[16,2048]{1,0:T(8,128)(2,1)S(1)} %pad_maximum_fusion.11.array_ref), channel_id=1, source_target_pairs={{0,4},{4,0},{8,12},{12,8},{16,20},{20,16},{24,28},{28,24},{1,5},{5... | collective-permute-start | bytes 196616 | tf_op jit(solution)/shard_map/ppermute | solution.py:99
  78.4 7.0 %collective-permute-start.23 = (bf16[16,2048]{1,0:T(8,128)(2,1)S(1)}, bf16[16,2048]{1,0:T(8,128)(2,1)S(1)}, u32[]{:S(2)}, u32[]{:S(2)}) collective-permute-start(bf16[16,2048]{1,0:T(8,128)(2,1)S(1)} %pad_maximum_fusion.11.array_ref), channel_id=1, source_target_pairs={{0,8},{4,12},{8,0},{12,4},{16,24},{20,28},{24,16},{28,20},{1,9},{5... | collective-permute-start | bytes 196616 | tf_op jit(solution)/shard_map/ppermute | solution.py:99
  79.3 6.7 %collective-permute-start.20 = (bf16[16,2048]{1,0:T(8,128)(2,1)S(1)}, bf16[16,2048]{1,0:T(8,128)(2,1)S(1)}, u32[]{:S(2)}, u32[]{:S(2)}) collective-permute-start(bf16[16,2048]{1,0:T(8,128)(2,1)S(1)} %collective-permute-done.16.refs_2_), channel_id=1, source_target_pairs={{0,4},{4,0},{8,12},{12,8},{16,20},{20,16},{24,28},{28,24},{1,5},{5... | collective-permute-start | bytes 196616 | tf_op jit(solution)/shard_map/ppermute | solution.py:99
  102.5 11.1 %collective-permute-start.33 = (bf16[32,2048]{1,0:T(8,128)(2,1)S(1)}, bf16[32,2048]{1,0:T(8,128)(2,1)S(1)}, u32[]{:S(2)}, u32[]{:S(2)}) collective-permute-start(bf16[32,2048]{1,0:T(8,128)(2,1)S(1)} %get-tuple-element.96), channel_id=1, source_target_pairs={{0,2},{1,3},{2,0},{3,1},{4,6},{5,7},{6,4},{7,5},{8,10},{9,11},{10,... | collective-permute-start | bytes 393224 | tf_op jit(solution)/shard_map/ppermute | solution.py:99
  119.5 9.2 %collective-permute-start.43 = (f16[64,2048]{1,0:T(8,128)(2,1)S(1)}, f16[64,2048]{1,0:T(8,128)(2,1)S(1)}, u32[]{:S(2)}, u32[]{:S(2)}) collective-permute-start(f16[64,2048]{1,0:T(8,128)(2,1)S(1)} %convert_element_type.176), channel_id=1, source_target_pairs={{0,4},{4,0},{8,12},{12,8},{16,20},{20,16},{24,28},{28,24},{1,5},{5... | collective-permute-start | bytes 786440 | tf_op jit(solution)/shard_map/ppermute | solution.py:99
  124.2 9.3 %collective-permute-start.35 = (f16[64,2048]{1,0:T(8,128)(2,1)S(1)}, f16[64,2048]{1,0:T(8,128)(2,1)S(1)}, u32[]{:S(2)}, u32[]{:S(2)}) collective-permute-start(f16[64,2048]{1,0:T(8,128)(2,1)S(1)} %convert_element_type.170), channel_id=1, source_target_pairs={{0,4},{4,0},{8,12},{12,8},{16,20},{20,16},{24,28},{28,24},{1,5},{5... | collective-permute-start | bytes 786440 | tf_op jit(solution)/shard_map/ppermute | solution.py:99
  128.8 7.8 %collective-permute-start.44 = (f16[16,2048]{1,0:T(8,128)(2,1)S(1)}, f16[16,2048]{1,0:T(8,128)(2,1)S(1)}, u32[]{:S(2)}, u32[]{:S(2)}) collective-permute-start(f16[16,2048]{1,0:T(8,128)(2,1)S(1)} %get-tuple-element.105), channel_id=1, source_target_pairs={{0,16},{4,20},{8,24},{12,28},{16,0},{20,4},{24,8},{28,12},{1,17},{... | collective-permute-start | bytes 196616 | tf_op jit(solution)/shard_map/ppermute | solution.py:99
  129.5 7.7 %collective-permute-start.46 = (f16[16,2048]{1,0:T(8,128)(2,1)S(1)}, f16[16,2048]{1,0:T(8,128)(2,1)S(1)}, u32[]{:S(2)}, u32[]{:S(2)}) collective-permute-start(f16[16,2048]{1,0:T(8,128)(2,1)S(1)} %get-tuple-element.106), channel_id=1, source_target_pairs={{0,24},{4,28},{8,16},{12,20},{16,8},{20,12},{24,0},{28,4},{1,25},{... | collective-permute-start | bytes 196616 | tf_op jit(solution)/shard_map/ppermute | solution.py:99
  133.7 8.1 %collective-permute-start.36 = (f16[16,2048]{1,0:T(8,128)(2,1)S(1)}, f16[16,2048]{1,0:T(8,128)(2,1)S(1)}, u32[]{:S(2)}, u32[]{:S(2)}) collective-permute-start(f16[16,2048]{1,0:T(8,128)(2,1)S(1)} %get-tuple-element.108), channel_id=1, source_target_pairs={{0,16},{4,20},{8,24},{12,28},{16,0},{20,4},{24,8},{28,12},{1,17},{... | collective-permute-start | bytes 196616 | tf_op jit(solution)/shard_map/ppermute | solution.py:99
  134.3 7.5 %collective-permute-start.38 = (f16[16,2048]{1,0:T(8,128)(2,1)S(1)}, f16[16,2048]{1,0:T(8,128)(2,1)S(1)}, u32[]{:S(2)}, u32[]{:S(2)}) collective-permute-start(f16[16,2048]{1,0:T(8,128)(2,1)S(1)} %get-tuple-element.109), channel_id=1, source_target_pairs={{0,24},{4,28},{8,16},{12,20},{16,8},{20,12},{24,0},{28,4},{1,25},{... | collective-permute-start | bytes 196616 | tf_op jit(solution)/shard_map/ppermute | solution.py:99
  137.3 8.1 %collective-permute-start.49 = (bf16[16,1024]{1,0:T(8,128)(2,1)S(1)}, bf16[16,1024]{1,0:T(8,128)(2,1)S(1)}, u32[]{:S(2)}, u32[]{:S(2)}) collective-permute-start(bf16[16,1024]{1,0:T(8,128)(2,1)S(1)} %fusion.72.array_ref), channel_id=1, source_target_pairs={{0,24},{4,28},{8,16},{12,20},{16,8},{20,12},{24,0},{28,4},{1,25},{... | collective-permute-start | bytes 98312 | tf_op jit(solution)/shard_map/ppermute | solution.py:99
  139.1 7.6 %collective-permute-start.48 = (bf16[16,1024]{1,0:T(8,128)(2,1)S(1)}, bf16[16,1024]{1,0:T(8,128)(2,1)S(1)}, u32[]{:S(2)}, u32[]{:S(2)}) collective-permute-start(bf16[16,1024]{1,0:T(8,128)(2,1)S(1)} %fusion.72.array_ref), channel_id=1, source_target_pairs={{0,8},{4,12},{8,0},{12,4},{16,24},{20,28},{24,16},{28,20},{1,9},{5... | collective-permute-start | bytes 98312 | tf_op jit(solution)/shard_map/ppermute | solution.py:99
  (42 other events, 255.3 us)

commit v13 on v12

--- a/solution.py
+++ b/solution.py
@@ -486,21 +486,26 @@
 
     f_total = w_gate.shape[1]
     f_edge = int(f_total * FFN_SPLIT) // LANES * LANES
-    total = None
+    total = [None, None]
     for first, last in ((0, f_edge), (f_edge, f_total)):
         f_cols = last - first
         segments = [(w_gate, 0, first, f_cols), (w_up, 0, first, f_cols)]
         sums = wide_scatter(*project([normed_two], to_wide, False, segments, 2, direct=True))
         act = (jax.nn.silu(sums[:, :f_cols]) * sums[:, f_cols:]).astype(jnp.bfloat16)
-        total = project(
-            [gather_in_two(act, "wide")],
-            to_wide,
-            True,
-            [(w_down, first, 0, w_down.shape[1])],
-            2 if last == f_total else 1,
-            total if total is None else total[0],
-        )
-    ffn_out = narrow_scatter(*total)
+        gathered = gather_in_two(act, "wide")
+        half = w_down.shape[1] // 2
+        total = [
+            project(
+                [gathered],
+                to_wide,
+                True,
+                [(w_down, first, place * half, half)],
+                2 if last == f_total else 1,
+                earlier if earlier is None else earlier[0],
+            )
+            for place, earlier in enumerate(total)
+        ]
+    ffn_out = jnp.concatenate([narrow_scatter(*sums) for sums in total], axis=1)
     return (resid_wide + ffn_out).astype(jnp.bfloat16)
 
 

time: 165 us -> 167 us (1.012)
  starting transfers between devices: 53.3 us -> 56.3 us
    ppermute x53 -> x55, starting transfers between devices: 48.4 us -> 51.4 us  [swap(): return lax.ppermute(block, axis, [(i, i ^ offset) for i in range(count)])]
    ppermute x53 -> x55, waiting for transfers between devices: 51.4 us -> 50 us  [swap(): return lax.ppermute(block, axis, [(i, i ^ offset) for i in range(count)])]
    pallas_call x9 -> x11, Pallas kernels: 24.3 us -> 25 us  [project(): pl.pallas_call(body, in_specs=specs, out_specs=[in_vmem] * split, scratch...]
  transfers between devices with their start and end apart: 54 -> 56, of which waited for: 31 -> 34; matrix products, arithmetic and copies ran while one was open for 3% -> 3% of each run, Pallas kernels for 12% -> 12%
where the time goes in v13:
time: 167 us
  starting transfers between devices  56.3 us (34%)
  waiting for transfers between devices  54.9 us (33%)
  Pallas kernels  30.1 us (18%)
  blocking collectives  9.87 us (6%)
  other arithmetic  7.13 us (4%)
  matrix products  5.15 us (3%)
  local copies, waits for them, and re-layouts  2.41 us (1%)
    ppermute x55, starting transfers between devices, swap(): return lax.ppermute(block, axis, [(i, i ^ offset) for i in range(count)])  51.4 us
    ppermute x55, waiting for transfers between devices, swap(): return lax.ppermute(block, axis, [(i, i ^ offset) for i in range(count)])  50 us
    pallas_call x11, Pallas kernels, project(): pl.pallas_call(body, in_specs=specs, out_specs=[in_vmem] * split, scratch...  25 us
    all_to_all x1, blocking collectives, normalized_rows(): landed = lax.all_to_all(sent, ('wide', 'narrow'), 0, 0, tiled=True)  9.87 us
    all_to_all x1, starting transfers between devices, normalized_rows(): landed = lax.all_to_all(sent, ('wide', 'narrow'), 0, 0, tiled=True)  4.92 us
    all_to_all x1, waiting for transfers between devices, normalized_rows(): landed = lax.all_to_all(sent, ('wide', 'narrow'), 0, 0, tiled=True)  4.92 us
    pallas_call x6, Pallas kernels, fold(): pl.pallas_call(body, out_shape=[jax.ShapeDtypeStruct((rows, width), jnp.f...  4.76 us
    dot_general x1, matrix products, attend(): jnp.einsum('rgqd,rlgd->rgql', query_heads, cache_keys, preferred_element_...  3.85 us
  transfers between devices with their start and end apart: 56, of which 34 were waited for; matrix products, arithmetic and copies ran while one was open for 3% of the time, Pallas kernels for 12%

profile of v13, /device:TPU:0, one launch (start us, length us, event | category | flops | bytes accessed | tf_op | source)
XLA Modules:
  0.0 166.8 jit_solution(11062933397730168301)
XLA Ops:
  0.0 2.9 %collective-permute-start = (bf16[32,2048]{1,0:T(8,128)(2,1)}, bf16[32,2048]{1,0:T(8,128)(2,1)S(1)}, u32[]{:S(2)}, u32[]{:S(2)}) collective-permute-start(bf16[32,2048]{1,0:T(8,128)(2,1)} %param.14), channel_id=1, source_target_pairs={{0,2},{1,3},{2,0},{3,1},{4,6},{5,7},{6,4},{7,5},{8,10},{9,11},{10,... | collective-permute-start | bytes 393224 | tf_op jit(solution)/shard_map/ppermute | solution.py:99
  4.6 4.9 %all-to-all-start = ((f32[32,1,32]{2,1,0:T(1,128)}), f32[32,1,32]{2,1,0:T(1,128)S(1)}, u32[]{:S(2)}, u32[]{:S(2)}) async-start(f32[32,1,32]{2,1,0:T(1,128)} %broadcast_in_dim.17), calls=%async_computation | async-start | bytes 32768 | tf_op jit(solution)/shard_map/all_to_all | solution.py:413
  11.7 4.9 %all-to-all-done = f32[32,1,32]{2,1,0:T(1,128)S(1)} async-done(((f32[32,1,32]{2,1,0:T(1,128)}), f32[32,1,32]{2,1,0:T(1,128)S(1)}, u32[]{:S(2)}, u32[]{:S(2)}) %all-to-all-start) | async-done | bytes 4128 | tf_op jit(solution)/shard_map/all_to_all | solution.py:413
  19.2 3.6 %shard_map.136 = (f32[64,1536]{1,0:T(8,128)S(1)}, s16[64,1664]{1,0:T(8,128)(2,1)S(1)}) custom-call(bf16[64,2048]{1,0:T(8,128)(2,1)S(1)} %get-tuple-element.156.refs_0_, bf16[64,2048]{1,0:T(8,128)(2,1)S(1)} %get-tuple-element.155.refs_1_, bf16[128,128]{1,0:T(8,128)(2,1)S(1)} %get-tuple-element.74.refs_2_.refs_16_, bf16[2048,4096]{1,0:T(8,128)(2,1)} %refs_3_.11), custom_call_target="tpu_custom_call" | custom-call | flops 872415232 | bytes 7077888 | tf_op jit(solution)/shard_map/pallas_call | solution.py:215
  23.4 3.6 %shard_map.137 = (f32[64,1536]{1,0:T(8,128)S(1)}, s16[64,1664]{1,0:T(8,128)(2,1)S(1)}) custom-call(bf16[64,2048]{1,0:T(8,128)(2,1)S(1)} %get-tuple-element.156.refs_0_, bf16[64,2048]{1,0:T(8,128)(2,1)S(1)} %get-tuple-element.155.refs_1_, bf16[128,128]{1,0:T(8,128)(2,1)S(1)} %get-tuple-element.74.refs_2_.refs_16_, bf16[2048,4096]{1,0:T(8,128)(2,1)} %refs_3_.11), custom_call_target="tpu_custom_call" | custom-call | flops 872415232 | bytes 7077888 | tf_op jit(solution)/shard_map/pallas_call | solution.py:215
  28.6 1.9 %collective-permute-done.2.arrived_ref = s16[64,1664]{1,0:T(8,128)(2,1)S(1)} collective-permute-done((s16[64,1664]{1,0:T(8,128)(2,1)S(1)}, s16[64,1664]{1,0:T(8,128)(2,1)S(1)}, u32[]{:S(2)}, u32[]{:S(2)}) %collective-permute-start.2) | collective-permute-done | bytes 213024 | tf_op jit(solution)/shard_map/ppermute | solution.py:99
  30.6 3.9 %shard_map.144 = (f32[64,1536]{1,0:T(8,128)S(1)}, s16[64,1664]{1,0:T(8,128)(2,1)S(1)}) custom-call(bf16[64,2048]{1,0:T(8,128)(2,1)S(1)} %get-tuple-element.156.refs_0_, bf16[64,2048]{1,0:T(8,128)(2,1)S(1)} %get-tuple-element.155.refs_1_, bf16[128,128]{1,0:T(8,128)(2,1)S(1)} %get-tuple-element.74.refs_2_.refs_16_, bf16[2048,4096]{1,0:T(8,128)(2,1)} %refs_3_.11, ...), custom_call_target="tpu_custom_call" | custom-call | flops 872415232 | bytes 7077888 | tf_op jit(solution)/shard_map/pallas_call | solution.py:215
  44.2 2.4 %collective-permute-start.4 = (s16[16,1664]{1,0:T(8,128)(2,1)S(1)}, s16[16,1664]{1,0:T(8,128)(2,1)S(1)}, u32[]{:S(2)}, u32[]{:S(2)}) collective-permute-start(s16[16,1664]{1,0:T(8,128)(2,1)S(1)} %get-tuple-element.67), channel_id=1, source_target_pairs={{0,16},{4,20},{8,24},{12,28},{16,0},{20,4},{24,8},{28,12},{1,17},{... | collective-permute-start | bytes 159752 | tf_op jit(solution)/shard_map/ppermute | solution.py:99
  48.8 2.1 %collective-permute-done.4.refs_0_ = s16[16,1664]{1,0:T(8,128)(2,1)S(1)} collective-permute-done((s16[16,1664]{1,0:T(8,128)(2,1)S(1)}, s16[16,1664]{1,0:T(8,128)(2,1)S(1)}, u32[]{:S(2)}, u32[]{:S(2)}) %collective-permute-start.4) | collective-permute-done | bytes 53280 | tf_op jit(solution)/shard_map/ppermute | solution.py:99
  53.7 3.8 %collective-permute-done.11 = bf16[2,4,36,128]{3,2,1,0:T(8,128)(2,1)S(1)} collective-permute-done((bf16[2,4,36,128]{3,2,1,0:T(8,128)(2,1)S(1)}, bf16[2,4,36,128]{3,2,1,0:T(8,128)(2,1)S(1)}, u32[]{:S(2)}, u32[]{:S(2)}) %collective-permute-start.11) | collective-permute-done | bytes 73760 | tf_op jit(solution)/shard_map/ppermute | solution.py:99
  60.3 3.9 %fusion.114 = (f32[4,8,16]{2,1,0:T(8,128)S(1)}, f32[4,8,16,512]{3,2,1,0:T(8,128)S(1)}) fusion(bf16[4,8,16,64]{3,2,1,0:T(8,128)(2,1)S(1)} %bitcast.84, bf16[4,8,16,64]{3,2,1,0:T(8,128)(2,1)S(1)} %bitcast.82, pred[4,512]{1,0:T(4,128)(4,1)S(1)} %iota_compare_fusion, bf16[4,512,1024]{2,1,0:T(8,128)(2,1)} %param.24), kind=kOutput, calls=%fused_computation.233 | convolution fusion | flops 68156928 | bytes 5378048 | tf_op jit(solution)/shard_map/rgqd,rlgd->rgql/dot_general | solution.py:59
  66.9 3.7 %collective-permute-done.13 = bf16[2,4,4096]{2,1,0:T(4,128)(2,1)S(1)} collective-permute-done((bf16[2,4,4096]{2,1,0:T(4,128)(2,1)S(1)}, bf16[2,4,4096]{2,1,0:T(4,128)(2,1)S(1)}, u32[]{:S(2)}, u32[]{:S(2)}) %collective-permute-start.13) | collective-permute-done | bytes 65568 | tf_op jit(solution)/shard_map/ppermute | solution.py:99
  97.8 2.3 %collective-permute-done.32 = bf16[32,1024]{1,0:T(8,128)(2,1)S(1)} collective-permute-done((bf16[32,1024]{1,0:T(8,128)(2,1)S(1)}, bf16[32,1024]{1,0:T(8,128)(2,1)S(1)}, u32[]{:S(2)}, u32[]{:S(2)}) %collective-permute-start.32) | collective-permute-done | bytes 65568 | tf_op jit(solution)/shard_map/ppermute | solution.py:99
  102.3 9.9 %all_to_all.12 = f32[32,1,32]{2,1,0:T(1,128)S(1)} all-to-all(f32[32,1,32]{2,1,0:T(1,128)S(1)} %broadcast_in_dim.20), channel_id=1, replica_groups=mesh['wide'=8,'narrow'=4] {'wide','narrow'}, dimensions={0} | all-to-all | bytes 8192 | tf_op jit(solution)/shard_map/all_to_all | solution.py:413
  114.1 4.1 %shard_map.152 = (f32[64,2048]{1,0:T(8,128)S(1)}, f32[64,2048]{1,0:T(8,128)S(1)}) custom-call(bf16[64,2048]{1,0:T(8,128)(2,1)S(1)} %get-tuple-element.154.refs_0_, bf16[64,2048]{1,0:T(8,128)(2,1)S(1)} %get-tuple-element.153.refs_1_, bf16[128,128]{1,0:T(8,128)(2,1)S(1)} %get-tuple-element.157.refs_2_, bf16[2048,2048]{1,0:T(8,128)(2,1)} %refs_3_.13, ...), custom_call_target="tpu_custom_call" | custom-call | flops 1140850688 | bytes 9437184 | tf_op jit(solution)/shard_map/pallas_call | solution.py:215
  118.8 4.1 %shard_map.154 = (f32[64,2048]{1,0:T(8,128)S(1)}, f32[64,2048]{1,0:T(8,128)S(1)}) custom-call(bf16[64,2048]{1,0:T(8,128)(2,1)S(1)} %get-tuple-element.154.refs_0_, bf16[64,2048]{1,0:T(8,128)(2,1)S(1)} %get-tuple-element.153.refs_1_, bf16[128,128]{1,0:T(8,128)(2,1)S(1)} %get-tuple-element.157.refs_2_, bf16[2048,2048]{1,0:T(8,128)(2,1)} %refs_3_.13, ...), custom_call_target="tpu_custom_call" | custom-call | flops 1140850688 | bytes 9437184 | tf_op jit(solution)/shard_map/pallas_call | solution.py:215
  124.5 2.9 %collective-permute-done.35 = f16[64,2048]{1,0:T(8,128)(2,1)S(1)} collective-permute-done((f16[64,2048]{1,0:T(8,128)(2,1)S(1)}, f16[64,2048]{1,0:T(8,128)(2,1)S(1)}, u32[]{:S(2)}, u32[]{:S(2)}) %collective-permute-start.35) | collective-permute-done | bytes 262176 | tf_op jit(solution)/shard_map/ppermute | solution.py:99
  128.7 3.2 %collective-permute-start.36 = (f16[16,2048]{1,0:T(8,128)(2,1)S(1)}, f16[16,2048]{1,0:T(8,128)(2,1)S(1)}, u32[]{:S(2)}, u32[]{:S(2)}) collective-permute-start(f16[16,2048]{1,0:T(8,128)(2,1)S(1)} %get-tuple-element.112), channel_id=1, source_target_pairs={{0,16},{4,20},{8,24},{12,28},{16,0},{20,4},{24,8},{28,12},{1,17},{... | collective-permute-start | bytes 196616 | tf_op jit(solution)/shard_map/ppermute | solution.py:99
  133.7 3.1 %collective-permute-start.44 = (f16[16,2048]{1,0:T(8,128)(2,1)S(1)}, f16[16,2048]{1,0:T(8,128)(2,1)S(1)}, u32[]{:S(2)}, u32[]{:S(2)}) collective-permute-start(f16[16,2048]{1,0:T(8,128)(2,1)S(1)} %get-tuple-element.109), channel_id=1, source_target_pairs={{0,16},{4,20},{8,24},{12,28},{16,0},{20,4},{24,8},{28,12},{1,17},{... | collective-permute-start | bytes 196616 | tf_op jit(solution)/shard_map/ppermute | solution.py:99
  139.0 2.9 %collective-permute-done.44 = f16[16,2048]{1,0:T(8,128)(2,1)S(1)} collective-permute-done((f16[16,2048]{1,0:T(8,128)(2,1)S(1)}, f16[16,2048]{1,0:T(8,128)(2,1)S(1)}, u32[]{:S(2)}, u32[]{:S(2)}) %collective-permute-start.44) | collective-permute-done | bytes 65568 | tf_op jit(solution)/shard_map/ppermute | solution.py:99
  143.7 2.8 %collective-permute-start.47 = (bf16[16,1024]{1,0:T(8,128)(2,1)S(1)}, bf16[16,1024]{1,0:T(8,128)(2,1)S(1)}, u32[]{:S(2)}, u32[]{:S(2)}) collective-permute-start(bf16[16,1024]{1,0:T(8,128)(2,1)S(1)} %fusion.72.array_ref), channel_id=1, source_target_pairs={{0,16},{4,20},{8,24},{12,28},{16,0},{20,4},{24,8},{28,12},{1,17},{... | collective-permute-start | bytes 98312 | tf_op jit(solution)/shard_map/ppermute | solution.py:99
  149.7 3.1 %collective-permute-done.39 = bf16[16,1024]{1,0:T(8,128)(2,1)S(1)} collective-permute-done((bf16[16,1024]{1,0:T(8,128)(2,1)S(1)}, bf16[16,1024]{1,0:T(8,128)(2,1)S(1)}, u32[]{:S(2)}, u32[]{:S(2)}) %collective-permute-start.39) | collective-permute-done | bytes 32800 | tf_op jit(solution)/shard_map/ppermute | solution.py:99
  155.1 2.8 %collective-permute-done.42.refs_1_ = bf16[64,1024]{1,0:T(8,128)(2,1)S(1)} collective-permute-done((bf16[64,1024]{1,0:T(8,128)(2,1)S(1)}, bf16[64,1024]{1,0:T(8,128)(2,1)S(1)}, u32[]{:S(2)}, u32[]{:S(2)}) %collective-permute-start.42) | collective-permute-done | bytes 131104 | tf_op jit(solution)/shard_map/ppermute | solution.py:99
  162.6 2.3 %collective-permute-done.54 = bf16[32,1024]{1,0:T(8,128)(2,1)S(1)} collective-permute-done((bf16[32,1024]{1,0:T(8,128)(2,1)S(1)}, bf16[32,1024]{1,0:T(8,128)(2,1)S(1)}, u32[]{:S(2)}, u32[]{:S(2)}) %collective-permute-start.54) | collective-permute-done | bytes 65568 | tf_op jit(solution)/shard_map/ppermute | solution.py:99
  (242 shorter events, 80.6 us)
Async XLA Ops:
  0.0 16.7 %collective-permute-start = (bf16[32,2048]{1,0:T(8,128)(2,1)}, bf16[32,2048]{1,0:T(8,128)(2,1)S(1)}, u32[]{:S(2)}, u32[]{:S(2)}) collective-permute-start(bf16[32,2048]{1,0:T(8,128)(2,1)} %param.14), channel_id=1, source_target_pairs={{0,2},{1,3},{2,0},{3,1},{4,6},{5,7},{6,4},{7,5},{8,10},{9,11},{10,... | collective-permute-start | bytes 393224 | tf_op jit(solution)/shard_map/ppermute | solution.py:99
  4.6 12.0 %all-to-all-start = ((f32[32,1,32]{2,1,0:T(1,128)}), f32[32,1,32]{2,1,0:T(1,128)S(1)}, u32[]{:S(2)}, u32[]{:S(2)}) async-start(f32[32,1,32]{2,1,0:T(1,128)} %broadcast_in_dim.17), calls=%async_computation | async-start | bytes 32768 | tf_op jit(solution)/shard_map/all_to_all | solution.py:413
  22.8 7.7 %collective-permute-start.2 = (s16[64,1664]{1,0:T(8,128)(2,1)S(1)}, s16[64,1664]{1,0:T(8,128)(2,1)S(1)}, u32[]{:S(2)}, u32[]{:S(2)}) collective-permute-start(s16[64,1664]{1,0:T(8,128)(2,1)S(1)} %get-tuple-element.62), channel_id=1, source_target_pairs={{0,4},{4,0},{8,12},{12,8},{16,20},{20,16},{24,28},{28,24},{1,5},{5... | collective-permute-start | bytes 638984 | tf_op jit(solution)/shard_map/ppermute | solution.py:99
  27.1 7.7 %collective-permute-start.5 = (s16[64,1664]{1,0:T(8,128)(2,1)S(1)}, s16[64,1664]{1,0:T(8,128)(2,1)S(1)}, u32[]{:S(2)}, u32[]{:S(2)}) collective-permute-start(s16[64,1664]{1,0:T(8,128)(2,1)S(1)} %get-tuple-element.69), channel_id=1, source_target_pairs={{0,4},{4,0},{8,12},{12,8},{16,20},{20,16},{24,28},{28,24},{1,5},{5... | collective-permute-start | bytes 638984 | tf_op jit(solution)/shard_map/ppermute | solution.py:99
  34.5 6.2 %collective-permute-start.8 = (s16[64,1664]{1,0:T(8,128)(2,1)S(1)}, s16[64,1664]{1,0:T(8,128)(2,1)S(1)}, u32[]{:S(2)}, u32[]{:S(2)}) collective-permute-start(s16[64,1664]{1,0:T(8,128)(2,1)S(1)} %get-tuple-element.78), channel_id=1, source_target_pairs={{0,4},{4,0},{8,12},{12,8},{16,20},{20,16},{24,28},{28,24},{1,5},{5... | collective-permute-start | bytes 638984 | tf_op jit(solution)/shard_map/ppermute | solution.py:99
  35.7 6.5 %collective-permute-start.6 = (s16[32,1664]{1,0:T(8,128)(2,1)S(1)}, s16[32,1664]{1,0:T(8,128)(2,1)S(1)}, u32[]{:S(2)}, u32[]{:S(2)}) collective-permute-start(s16[32,1664]{1,0:T(8,128)(2,1)S(1)} %get-tuple-element.71), channel_id=1, source_target_pairs={{0,8},{4,12},{8,0},{12,4},{16,24},{20,28},{24,16},{28,20},{1,9},{5... | collective-permute-start | bytes 319496 | tf_op jit(solution)/shard_map/ppermute | solution.py:99
  37.3 6.2 %collective-permute-start.3 = (s16[32,1664]{1,0:T(8,128)(2,1)S(1)}, s16[32,1664]{1,0:T(8,128)(2,1)S(1)}, u32[]{:S(2)}, u32[]{:S(2)}) collective-permute-start(s16[32,1664]{1,0:T(8,128)(2,1)S(1)} %get-tuple-element.65), channel_id=1, source_target_pairs={{0,8},{4,12},{8,0},{12,4},{16,24},{20,28},{24,16},{28,20},{1,9},{5... | collective-permute-start | bytes 319496 | tf_op jit(solution)/shard_map/ppermute | solution.py:99
  44.2 6.7 %collective-permute-start.4 = (s16[16,1664]{1,0:T(8,128)(2,1)S(1)}, s16[16,1664]{1,0:T(8,128)(2,1)S(1)}, u32[]{:S(2)}, u32[]{:S(2)}) collective-permute-start(s16[16,1664]{1,0:T(8,128)(2,1)S(1)} %get-tuple-element.67), channel_id=1, source_target_pairs={{0,16},{4,20},{8,24},{12,28},{16,0},{20,4},{24,8},{28,12},{1,17},{... | collective-permute-start | bytes 159752 | tf_op jit(solution)/shard_map/ppermute | solution.py:99
  72.1 6.9 %collective-permute-start.15 = (bf16[16,2048]{1,0:T(8,128)(2,1)S(1)}, bf16[16,2048]{1,0:T(8,128)(2,1)S(1)}, u32[]{:S(2)}, u32[]{:S(2)}) collective-permute-start(bf16[16,2048]{1,0:T(8,128)(2,1)S(1)} %pad_maximum_fusion.10.array_ref), channel_id=1, source_target_pairs={{0,16},{4,20},{8,24},{12,28},{16,0},{20,4},{24,8},{28,12},{1,17},{... | collective-permute-start | bytes 196616 | tf_op jit(solution)/shard_map/ppermute | solution.py:99
  73.2 6.2 %collective-permute-start.16 = (bf16[16,2048]{1,0:T(8,128)(2,1)S(1)}, bf16[16,2048]{1,0:T(8,128)(2,1)S(1)}, u32[]{:S(2)}, u32[]{:S(2)}) collective-permute-start(bf16[16,2048]{1,0:T(8,128)(2,1)S(1)} %pad_maximum_fusion.10.array_ref), channel_id=1, source_target_pairs={{0,8},{4,12},{8,0},{12,4},{16,24},{20,28},{24,16},{28,20},{1,9},{5... | collective-permute-start | bytes 196616 | tf_op jit(solution)/shard_map/ppermute | solution.py:99
  73.9 6.5 %collective-permute-start.18 = (bf16[16,2048]{1,0:T(8,128)(2,1)S(1)}, bf16[16,2048]{1,0:T(8,128)(2,1)S(1)}, u32[]{:S(2)}, u32[]{:S(2)}) collective-permute-start(bf16[16,2048]{1,0:T(8,128)(2,1)S(1)} %pad_maximum_fusion.10.array_ref), channel_id=1, source_target_pairs={{0,4},{4,0},{8,12},{12,8},{16,20},{20,16},{24,28},{28,24},{1,5},{5... | collective-permute-start | bytes 196616 | tf_op jit(solution)/shard_map/ppermute | solution.py:99
  76.9 6.2 %collective-permute-start.23 = (bf16[16,2048]{1,0:T(8,128)(2,1)S(1)}, bf16[16,2048]{1,0:T(8,128)(2,1)S(1)}, u32[]{:S(2)}, u32[]{:S(2)}) collective-permute-start(bf16[16,2048]{1,0:T(8,128)(2,1)S(1)} %pad_maximum_fusion.11.array_ref), channel_id=1, source_target_pairs={{0,8},{4,12},{8,0},{12,4},{16,24},{20,28},{24,16},{28,20},{1,9},{5... | collective-permute-start | bytes 196616 | tf_op jit(solution)/shard_map/ppermute | solution.py:99
  101.5 10.7 %collective-permute-start.33 = (bf16[32,2048]{1,0:T(8,128)(2,1)S(1)}, bf16[32,2048]{1,0:T(8,128)(2,1)S(1)}, u32[]{:S(2)}, u32[]{:S(2)}) collective-permute-start(bf16[32,2048]{1,0:T(8,128)(2,1)S(1)} %get-tuple-element.100), channel_id=1, source_target_pairs={{0,2},{1,3},{2,0},{3,1},{4,6},{5,7},{6,4},{7,5},{8,10},{9,11},{10,... | collective-permute-start | bytes 393224 | tf_op jit(solution)/shard_map/ppermute | solution.py:99
  118.2 9.2 %collective-permute-start.35 = (f16[64,2048]{1,0:T(8,128)(2,1)S(1)}, f16[64,2048]{1,0:T(8,128)(2,1)S(1)}, u32[]{:S(2)}, u32[]{:S(2)}) collective-permute-start(f16[64,2048]{1,0:T(8,128)(2,1)S(1)} %convert_element_type.174), channel_id=1, source_target_pairs={{0,4},{4,0},{8,12},{12,8},{16,20},{20,16},{24,28},{28,24},{1,5},{5... | collective-permute-start | bytes 786440 | tf_op jit(solution)/shard_map/ppermute | solution.py:99
  122.9 9.3 %collective-permute-start.43 = (f16[64,2048]{1,0:T(8,128)(2,1)S(1)}, f16[64,2048]{1,0:T(8,128)(2,1)S(1)}, u32[]{:S(2)}, u32[]{:S(2)}) collective-permute-start(f16[64,2048]{1,0:T(8,128)(2,1)S(1)} %convert_element_type.180), channel_id=1, source_target_pairs={{0,4},{4,0},{8,12},{12,8},{16,20},{20,16},{24,28},{28,24},{1,5},{5... | collective-permute-start | bytes 786440 | tf_op jit(solution)/shard_map/ppermute | solution.py:99
  127.5 6.1 %collective-permute-start.38 = (f16[16,2048]{1,0:T(8,128)(2,1)S(1)}, f16[16,2048]{1,0:T(8,128)(2,1)S(1)}, u32[]{:S(2)}, u32[]{:S(2)}) collective-permute-start(f16[16,2048]{1,0:T(8,128)(2,1)S(1)} %get-tuple-element.113), channel_id=1, source_target_pairs={{0,24},{4,28},{8,16},{12,20},{16,8},{20,12},{24,0},{28,4},{1,25},{... | collective-permute-start | bytes 196616 | tf_op jit(solution)/shard_map/ppermute | solution.py:99
  128.2 8.6 %collective-permute-start.37 = (f16[16,2048]{1,0:T(8,128)(2,1)S(1)}, f16[16,2048]{1,0:T(8,128)(2,1)S(1)}, u32[]{:S(2)}, u32[]{:S(2)}) collective-permute-start(f16[16,2048]{1,0:T(8,128)(2,1)S(1)} %get-tuple-element.114), channel_id=1, source_target_pairs={{0,8},{4,12},{8,0},{12,4},{16,24},{20,28},{24,16},{28,20},{1,9},{5... | collective-permute-start | bytes 196616 | tf_op jit(solution)/shard_map/ppermute | solution.py:99
  128.7 8.1 %collective-permute-start.36 = (f16[16,2048]{1,0:T(8,128)(2,1)S(1)}, f16[16,2048]{1,0:T(8,128)(2,1)S(1)}, u32[]{:S(2)}, u32[]{:S(2)}) collective-permute-start(f16[16,2048]{1,0:T(8,128)(2,1)S(1)} %get-tuple-element.112), channel_id=1, source_target_pairs={{0,16},{4,20},{8,24},{12,28},{16,0},{20,4},{24,8},{28,12},{1,17},{... | collective-permute-start | bytes 196616 | tf_op jit(solution)/shard_map/ppermute | solution.py:99
  132.3 6.7 %collective-permute-start.46 = (f16[16,2048]{1,0:T(8,128)(2,1)S(1)}, f16[16,2048]{1,0:T(8,128)(2,1)S(1)}, u32[]{:S(2)}, u32[]{:S(2)}) collective-permute-start(f16[16,2048]{1,0:T(8,128)(2,1)S(1)} %get-tuple-element.110), channel_id=1, source_target_pairs={{0,24},{4,28},{8,16},{12,20},{16,8},{20,12},{24,0},{28,4},{1,25},{... | collective-permute-start | bytes 196616 | tf_op jit(solution)/shard_map/ppermute | solution.py:99
  133.0 6.1 %collective-permute-start.45 = (f16[16,2048]{1,0:T(8,128)(2,1)S(1)}, f16[16,2048]{1,0:T(8,128)(2,1)S(1)}, u32[]{:S(2)}, u32[]{:S(2)}) collective-permute-start(f16[16,2048]{1,0:T(8,128)(2,1)S(1)} %get-tuple-element.111), channel_id=1, source_target_pairs={{0,8},{4,12},{8,0},{12,4},{16,24},{20,28},{24,16},{28,20},{1,9},{5... | collective-permute-start | bytes 196616 | tf_op jit(solution)/shard_map/ppermute | solution.py:99
  133.7 8.3 %collective-permute-start.44 = (f16[16,2048]{1,0:T(8,128)(2,1)S(1)}, f16[16,2048]{1,0:T(8,128)(2,1)S(1)}, u32[]{:S(2)}, u32[]{:S(2)}) collective-permute-start(f16[16,2048]{1,0:T(8,128)(2,1)S(1)} %get-tuple-element.109), channel_id=1, source_target_pairs={{0,16},{4,20},{8,24},{12,28},{16,0},{20,4},{24,8},{28,12},{1,17},{... | collective-permute-start | bytes 196616 | tf_op jit(solution)/shard_map/ppermute | solution.py:99
  136.9 12.8 %collective-permute-start.41 = (bf16[16,1024]{1,0:T(8,128)(2,1)S(1)}, bf16[16,1024]{1,0:T(8,128)(2,1)S(1)}, u32[]{:S(2)}, u32[]{:S(2)}) collective-permute-start(bf16[16,1024]{1,0:T(8,128)(2,1)S(1)} %fusion.73.array_ref), channel_id=1, source_target_pairs={{0,24},{4,28},{8,16},{12,20},{16,8},{20,12},{24,0},{28,4},{1,25},{... | collective-permute-start | bytes 98312 | tf_op jit(solution)/shard_map/ppermute | solution.py:99
  138.6 11.1 %collective-permute-start.40 = (bf16[16,1024]{1,0:T(8,128)(2,1)S(1)}, bf16[16,1024]{1,0:T(8,128)(2,1)S(1)}, u32[]{:S(2)}, u32[]{:S(2)}) collective-permute-start(bf16[16,1024]{1,0:T(8,128)(2,1)S(1)} %fusion.73.array_ref), channel_id=1, source_target_pairs={{0,8},{4,12},{8,0},{12,4},{16,24},{20,28},{24,16},{28,20},{1,9},{5... | collective-permute-start | bytes 98312 | tf_op jit(solution)/shard_map/ppermute | solution.py:99
  142.1 5.9 %collective-permute-start.49 = (bf16[16,1024]{1,0:T(8,128)(2,1)S(1)}, bf16[16,1024]{1,0:T(8,128)(2,1)S(1)}, u32[]{:S(2)}, u32[]{:S(2)}) collective-permute-start(bf16[16,1024]{1,0:T(8,128)(2,1)S(1)} %fusion.72.array_ref), channel_id=1, source_target_pairs={{0,24},{4,28},{8,16},{12,20},{16,8},{20,12},{24,0},{28,4},{1,25},{... | collective-permute-start | bytes 98312 | tf_op jit(solution)/shard_map/ppermute | solution.py:99
  (44 other events, 263.2 us)
